TPU v7x, 32 devices: a whole 2x2x4 slice. The times are simulated.
32 devices in a mesh: island: 16 (over z, x, core), fsdp: 2 (over y).
Axes of the slice: x: 2, y: 2, z: 4, core: 2. Of those that a mesh axis runs over, the one named last changes fastest.
Arguments:
- activations: bfloat16 [4096, 8192], P(('island', 'fsdp')), may hold values from -6 to 6
- cotangent: bfloat16 [4096, 1024], P(('island', 'fsdp')), may hold values from -6 to 6
- inner_weight: bfloat16 [16, 8192, 1024], P('island', 'fsdp'), may hold values from -0.09375 to 0.09375
- outer_weight: float32 [8192, 1024], P(('fsdp', 'island')), may hold values from -0.0625 to 0.0625
- outer_momentum: float32 [8192, 1024], P(('fsdp', 'island')), may hold values from -0.06 to 0.06
- next_activations: bfloat16 [4096, 8192], P(('island', 'fsdp')), may hold values from -6 to 6
Outputs:
- input_grad: bfloat16 [4096, 8192], P(('island', 'fsdp'))
- next_keys: bfloat16 [4096, 1024], P(('island', 'fsdp'))
- new_outer: float32 [8192, 1024], P(('fsdp', 'island'))
- new_momentum: float32 [8192, 1024], P(('fsdp', 'island'))
All inputs are finite; a program needn't handle non-finite values.
Results may differ from a plain program's by a relative error of at most 0.0049.
Values may be sent and summed in bfloat16 or wider, within the bound.
No kernel may reach another device: no remote copies, remote signals or barrier semaphores. Data moves between devices by JAX's collectives and lax.ppermute only.
A program may use at most 128 MiB of HBM per device.

v0:
```python
import jax
import jax.numpy as jnp
from jax import lax
from jax.sharding import PartitionSpec as P

inner_rate = 1.2
outer_rate = 0.7
nesterov = 0.9


def local(activations, cotangent, inner_weight, outer_weight, outer_momentum, next_activations):
    fsdp_count = lax.axis_size("fsdp")
    island_count = lax.axis_size("island")
    tok_rows = activations.shape[0]
    own_weight = inner_weight[0]
    island_cotangent = lax.all_gather(cotangent, "fsdp", axis=0, tiled=True)
    column_block = lax.all_to_all(activations, "fsdp", split_axis=1, concat_axis=0, tiled=True)
    weight_grad = lax.dot_general(
        column_block, island_cotangent, (((0,), (0,)), ((), ())), preferred_element_type=jnp.float32
    ) / (tok_rows * fsdp_count)
    input_grad = lax.dot_general(
        cotangent,
        lax.all_gather(own_weight, "fsdp", axis=0, tiled=True),
        (((1,), (1,)), ((), ())),
        preferred_element_type=jnp.float32,
    ).astype(jnp.bfloat16)
    inner_new = own_weight.astype(jnp.float32) - inner_rate * weight_grad
    summed = lax.psum_scatter(inner_new, "island", scatter_dimension=0, tiled=True)
    pseudo_grad = outer_weight - summed / island_count
    new_momentum = nesterov * outer_momentum + pseudo_grad
    new_outer = outer_weight - outer_rate * (pseudo_grad + nesterov * new_momentum)
    new_share = new_outer.astype(jnp.bfloat16)
    island_block = lax.all_gather(new_share, "island", axis=0, tiled=True)
    next_keys = jnp.dot(
        next_activations,
        lax.all_gather(island_block, "fsdp", axis=0, tiled=True),
        preferred_element_type=jnp.float32,
    )
    return (input_grad, next_keys.astype(jnp.bfloat16), new_outer, new_momentum)


def solution(mesh):
    in_specs = (
        P(("island", "fsdp"), None),
        P(("island", "fsdp"), None),
        P("island", "fsdp", None),
        P(("fsdp", "island"), None),
        P(("fsdp", "island"), None),
        P(("island", "fsdp"), None),
    )
    out_specs = (
        P(("island", "fsdp"), None),
        P(("island", "fsdp"), None),
        P(("fsdp", "island"), None),
        P(("fsdp", "island"), None),
    )
    return jax.shard_map(local, mesh=mesh, in_specs=in_specs, out_specs=out_specs, check_vma=False)
```

profile of v0, /device:TPU:0, one launch (start us, length us, event | category | flops | bytes accessed | tf_op | source)
XLA Modules:
  0.0 736.2 jit_solution(6185854028525201765)
XLA Ops:
  7.2 0.0 copy-start
  7.2 0.0 copy-start.1
  7.2 4.2 copy.12
  11.4 4.8 all-to-all-start
  16.2 0.0 reduce-scatter.2.cloned.1.call-start
  16.3 0.0 copy-done.1
  16.3 31.9 %all_gather.13 = bf16[256,1024]{1,0:T(8,128)(2,1)S(1)} all-gather(bf16[128,1024]{1,0:T(8,128)(2,1)S(1)} %copy-done.1), channel_id=1, replica_groups=mesh['island'=16,'fsdp'=2] {'fsdp'}, dimensions={0}, use_global_device_ids=true | all-gather | bytes 786432 | tf_op jit(solution)/shard_map/all_gather | solution.py:16
  48.2 0.0 all-to-all-done
  48.2 4.1 copy.13
  52.3 12.2 %convert_subtract_fusion = f32[4096,1024]{1,0:T(8,128)} fusion(bf16[256,4096]{1,0:T(8,128)(2,1)} %bitcast.18, bf16[256,1024]{1,0:T(8,128)(2,1)S(1)} %all_gather.13, bf16[1,4096,1024]{2,1,0:T(8,128)(2,1)} %param.8), kind=kOutput, calls=%fused_computation | convolution fusion | flops 2160066560 | bytes 27787264 | tf_op jit(solution)/shard_map/dot_general | solution.py:18
  64.4 0.0 reduce-scatter.2.cloned.1.call-update
  64.4 0.0 all-gather.5.cloned.1.call-start
  64.5 179.2 %reduce-scatter.2.cloned.1.call-done = f32[256,1024]{1,0:T(8,128)} async-done(((f32[4096,1024]{1,0:T(8,128)}), f32[256,1024]{1,0:T(8,128)}) %reduce-scatter.2.cloned.1.call-update) | async-done | bytes 1048592 | tf_op jit(solution)/shard_map/reduce_scatter | solution.py:28
  243.7 3.9 fusion.6
  247.6 0.0 all-gather.5.cloned.1.call-update
  247.6 0.0 all-gather.9.cloned.1.call-start
  247.7 0.7 all-gather.9.cloned.1.call-update
  248.4 0.0 all-gather.7.cloned.1.call-start
  248.4 73.3 %all-gather.5.cloned.1.call-done = bf16[4096,1024]{1,0:T(8,128)(2,1)} async-done(((bf16[256,1024]{1,0:T(8,128)(2,1)}), bf16[4096,1024]{1,0:T(8,128)(2,1)}) %all-gather.5.cloned.1.call-update) | async-done | bytes 8388624 | tf_op jit(solution)/shard_map/all_gather | solution.py:33
  321.7 0.0 all-gather.7.cloned.1.call-update
  321.7 198.7 %all-gather.9.cloned.1.call-done = bf16[1,8192,1024]{2,1,0:T(8,128)(2,1)} async-done(((bf16[1,4096,1024]{2,1,0:T(8,128)(2,1)}), bf16[1,8192,1024]{2,1,0:T(8,128)(2,1)}) %all-gather.9.cloned.1.call-update) | async-done | bytes 16777232 | tf_op jit(solution)/shard_map/all_gather | solution.py:23
  520.4 12.9 %fusion.2 = bf16[128,8192]{1,0:T(8,128)(2,1)} fusion(bf16[128,1024]{1,0:T(8,128)(2,1)S(1)} %copy-done.1, bf16[1,8192,1024]{2,1,0:T(8,128)(2,1)} %all-gather.9.cloned.1.call-done), kind=kOutput, calls=%fused_computation.3 | convolution fusion | flops 2148532224 | bytes 19136512 | tf_op jit(solution)/shard_map/dot_general | solution.py:21
  533.3 187.4 %all-gather.7.cloned.1.call-done = bf16[8192,1024]{1,0:T(8,128)(2,1)} async-done(((bf16[4096,1024]{1,0:T(8,128)(2,1)}), bf16[8192,1024]{1,0:T(8,128)(2,1)}) %all-gather.7.cloned.1.call-update) | async-done | bytes 16777232 | tf_op jit(solution)/shard_map/all_gather | solution.py:36
  720.7 0.0 copy-done
  720.7 8.2 %fusion.5 = bf16[128,1024]{0,1:T(8,128)(2,1)S(1)} fusion(bf16[8192,1024]{1,0:T(8,128)(2,1)} %all-gather.7.cloned.1.call-done, bf16[128,8192]{1,0:T(8,128)(2,1)S(1)} %copy-done), kind=kOutput, calls=%fused_computation.5 | convolution fusion | flops 2147614720 | bytes 19136512 | tf_op jit(solution)/shard_map/dot_general | solution.py:34
  728.8 0.9 copy.14
Async XLA Ops:
  7.2 713.5 %copy-start = (bf16[128,8192]{1,0:T(8,128)(2,1)S(1)}, bf16[128,8192]{1,0:T(8,128)(2,1)}, u32[]{:S(2)}) copy-start(bf16[128,8192]{1,0:T(8,128)(2,1)} %param.11) | copy-start | bytes 6291460
  7.2 9.1 %copy-start.1 = (bf16[128,1024]{1,0:T(8,128)(2,1)S(1)}, bf16[128,1024]{1,0:T(8,128)(2,1)}, u32[]{:S(2)}) copy-start(bf16[128,1024]{1,0:T(8,128)(2,1)} %param.7) | copy-start | bytes 786436
  11.4 36.8 %all-to-all-start = ((bf16[128,2,4096]{0,2,1:T(8,128)(2,1)}), bf16[128,2,4096]{0,2,1:T(8,128)(2,1)}, u32[]{:S(2)}, u32[]{:S(2)}) async-start(bf16[128,2,4096]{0,2,1:T(8,128)(2,1)} %bitcast.19), calls=%async_computation | async-start | bytes 4194304 | tf_op jit(solution)/shard_map/all_to_all | solution.py:17
  16.2 227.4 %reduce-scatter.2.cloned.1.call-start = ((), (), s32[]{:S(2)}) async-start(), calls=%async_computation.2 | async-start | bytes 17825792 | tf_op jit(solution)/shard_map/reduce_scatter | solution.py:28
  64.4 257.2 %all-gather.5.cloned.1.call-start = ((), (), s32[]{:S(2)}) async-start(), calls=%async_computation.3 | async-start | bytes 8912896 | tf_op jit(solution)/shard_map/all_gather | solution.py:33
  247.6 272.8 %all-gather.9.cloned.1.call-start = ((), (), s32[]{:S(2)}) async-start(), calls=%async_computation.5 | async-start | bytes 25165824 | tf_op jit(solution)/shard_map/all_gather | solution.py:23
  248.4 472.3 %all-gather.7.cloned.1.call-start = ((), (), s32[]{:S(2)}) async-start(), calls=%async_computation.4 | async-start | bytes 25165824 | tf_op jit(solution)/shard_map/all_gather | solution.py:36
Sparse Core Ops, SparseCore 0:
  64.6 179.0 reduce-scatter.1
  247.8 73.8 all-gather.4
  323.2 197.1 all-gather.8
  521.8 198.8 all-gather.6
where the time goes:
time: 737 us; the launch traced here: 736 us
  waiting for transfers between devices  639 us (87%)
  matrix products  33.2 us (5%)
  blocking collectives  31.9 us (4%)
  between operations  13.8 us (2%)
  local copies, waits for them, and re-layouts  9.17 us (1%)
    all_gather x1, waiting for transfers between devices, local(): lax.all_gather(own_weight, 'fsdp', axis=0, tiled=True)  199 us
    all_gather x1, waiting for transfers between devices, local(): lax.all_gather(island_block, 'fsdp', axis=0, tiled=True)  187 us
    reduce_scatter x1, waiting for transfers between devices, local(): lax.psum_scatter(inner_new, 'island', scatter_dimension=0, tiled=True)  179 us
    all_gather x1, waiting for transfers between devices, local(): island_block = lax.all_gather(new_share, 'island', axis=0, tiled=True)  73.3 us
    all_gather x1, blocking collectives, local(): island_cotangent = lax.all_gather(cotangent, 'fsdp', axis=0, tiled=True)  31.9 us
  transfers between devices with their start and end apart: 5, of which 4 were waited for; matrix products, arithmetic and copies ran while one was open for 2% of the time, Pallas kernels for 0%

commit v1 on v0

v1 whole, which is shorter than its diff:
```python
import functools

import jax
import jax.numpy as jnp
from jax import lax
from jax.experimental import pallas as pl
from jax.experimental.pallas import tpu as pltpu
from jax.sharding import Mesh, PartitionSpec as P

inner_rate = 1.2
outer_rate = 0.7
nesterov = 0.9
CORES = 2
PAIR = 2

bf16, f32 = jnp.bfloat16, jnp.float32


def ring(count, shift):
    return [(i, (i + shift) % count) for i in range(count)]


def inner_kernel(fsdp, share, scale, place, *refs):
    acts, cots = refs[:fsdp], refs[fsdp : 2 * fsdp]
    weight, give, keep, total = refs[2 * fsdp :]
    core = place[2]
    grad = None
    for a, g in zip(acts, cots):
        term = lax.dot_general(a[...], g[...], (((0,), (0,)), ((), ())), preferred_element_type=f32)
        grad = term if grad is None else grad + term
    total[...] = weight[...].astype(f32) - scale * grad
    for x in range(PAIR):
        here = pl.ds(x * share, share)
        theirs = pl.multiple_of((x * CORES + 1 - core) * share, share)
        ours = pl.multiple_of((x * CORES + core) * share, share)
        give[here, :] = total[pl.ds(theirs, share), :].astype(bf16)
        keep[here, :] = total[pl.ds(ours, share), :]


def inner_block(place, acts, cots, weight, share, tile=256):
    fsdp = len(acts)
    tok, kv = cots[0].shape
    block = PAIR * CORES * share
    half = PAIR * share
    spec = pltpu.PrefetchScalarGridSpec(
        num_scalar_prefetch=1,
        grid=(kv // tile,),
        in_specs=[pl.BlockSpec((tok, block), lambda i, p: (0, p[0]))]
        + [pl.BlockSpec((tok, block), lambda i, p: (0, 0))] * (fsdp - 1)
        + [pl.BlockSpec((tok, tile), lambda i, p: (0, i))] * fsdp
        + [pl.BlockSpec((block, tile), lambda i, p: (p[1], i))],
        out_specs=[pl.BlockSpec((half, tile), lambda i, p: (0, i))] * 2,
        scratch_shapes=[pltpu.VMEM((block, tile), f32)],
    )
    return pl.pallas_call(
        functools.partial(inner_kernel, fsdp, share, inner_rate / (tok * fsdp)),
        out_shape=[jax.ShapeDtypeStruct((half, kv), bf16), jax.ShapeDtypeStruct((half, kv), f32)],
        grid_spec=spec,
        compiler_params=pltpu.CompilerParams(vmem_limit_bytes=32 * 1024 * 1024),
        cost_estimate=pl.CostEstimate(
            flops=2 * tok * fsdp * block * kv, bytes_accessed=block * kv * 5 + 2 * tok * fsdp * (block + kv), transcendentals=0
        ),
    )(place, *acts, *cots, weight)


def local(activations, cotangent, inner_weight, outer_weight, outer_momentum, next_activations):
    fsdp, nz = lax.axis_size("fsdp"), lax.axis_size("z")
    f, z, x, c = (lax.axis_index(a) for a in ("fsdp", "z", "x", "core"))
    tok, d = activations.shape
    kv = cotangent.shape[1]
    width = d // fsdp
    block = width // nz
    share = block // (PAIR * CORES)
    own_weight = inner_weight[0]

    def columns(array, start, size):
        return lax.dynamic_slice_in_dim(array, start, size, axis=1)

    cots = [cotangent] + [lax.ppermute(cotangent, "fsdp", ring(fsdp, s)) for s in range(1, fsdp)]

    kept = []
    for j in range(nz):
        b = z ^ (nz - 1 - j)
        acts = [activations]
        for s in range(1, fsdp):
            mine = columns(activations, ((f + s) % fsdp) * width + b * block, block)
            acts.append(lax.ppermute(mine, "fsdp", ring(fsdp, s)))
        place = jnp.stack([f * nz + b, b, c]).astype(jnp.int32)
        give, keep = inner_block(place, acts, cots, own_weight, share)
        other = lax.ppermute(give, "core", ring(CORES, 1))

        def rows(array, index):
            return lax.dynamic_slice_in_dim(array, index * share, share, axis=0).astype(f32)

        over_x = (rows(keep, 1 - x) + rows(other, 1 - x)).astype(bf16)
        here = rows(keep, x) + rows(other, x)
        kept.append(here + lax.ppermute(over_x, "x", ring(PAIR, 1)).astype(f32))

    def kept_at(b, slots):
        chosen = kept[slots[0]]
        for j in slots[1:]:
            chosen = jnp.where(b == z ^ (nz - 1 - j), kept[j], chosen)
        return chosen

    up = down = None
    for t in range(1, nz):
        dist = nz - t
        slots_up = sorted({nz - 1 - ((i + dist) ^ i) for i in range(t)})
        slots_down = sorted({nz - 1 - ((i - dist) ^ i) for i in range(dist, nz)})
        send_up, send_down = kept_at(z + dist, slots_up), kept_at(z - dist, slots_down)
        if up is not None:
            send_up, send_down = send_up + up.astype(f32), send_down + down.astype(f32)
        up = lax.ppermute(send_up.astype(bf16), "z", [(i, i + 1) for i in range(t)])
        down = lax.ppermute(send_down.astype(bf16), "z", [(i, i - 1) for i in range(dist, nz)])
    summed = kept[nz - 1] + (up.astype(f32) + down.astype(f32))

    grad_rows = lax.dot_general(
        jnp.concatenate(cots, axis=0), own_weight, (((1,), (1,)), ((), ())), preferred_element_type=f32
    ).astype(bf16)
    input_grad = jnp.zeros((tok, d), bf16)
    for s in range(fsdp):
        part = grad_rows[s * tok : (s + 1) * tok]
        if s:
            part = lax.ppermute(part, "fsdp", ring(fsdp, -s))
        input_grad = lax.dynamic_update_slice_in_dim(input_grad, part, ((f + s) % fsdp) * width, axis=1)

    nexts = [columns(next_activations, f * width, width)]
    for s in range(1, fsdp):
        mine = columns(next_activations, ((f + s) % fsdp) * width, width)
        nexts.append(lax.ppermute(mine, "fsdp", ring(fsdp, s)))
    nexts = jnp.concatenate(nexts, axis=0).reshape(fsdp * tok, nz * PAIR, CORES, share)

    def of_core(core):
        return lax.dynamic_index_in_dim(nexts, core, 2, keepdims=False).reshape(fsdp * tok, nz * PAIR * share)

    nexts = jnp.concatenate([of_core(c), lax.ppermute(of_core(1 - c), "core", ring(CORES, 1))], axis=0)

    pseudo_grad = outer_weight - summed / (nz * PAIR * CORES)
    new_momentum = nesterov * outer_momentum + pseudo_grad
    new_outer = outer_weight - outer_rate * (pseudo_grad + nesterov * new_momentum)
    weight_rows = lax.all_gather(new_outer.astype(bf16), ("z", "x"), axis=0, tiled=True)

    partial = jnp.dot(nexts, weight_rows, preferred_element_type=f32)
    rows = fsdp * tok
    mine = partial[:rows] + lax.ppermute(partial[rows:].astype(bf16), "core", ring(CORES, 1)).astype(f32)
    keys = mine[:tok]
    for s in range(1, fsdp):
        keys = keys + lax.ppermute(mine[s * tok : (s + 1) * tok].astype(bf16), "fsdp", ring(fsdp, -s)).astype(f32)
    return (input_grad, keys.astype(bf16), new_outer, new_momentum)


def solution(mesh):
    fsdp = mesh.shape["fsdp"]
    nz = mesh.shape["island"] // (PAIR * CORES)
    split = Mesh(mesh.devices.reshape(nz, PAIR, CORES, fsdp), ("z", "x", "core", "fsdp"))
    island = ("z", "x", "core")
    tokens = P(island + ("fsdp",), None)
    width = P(("fsdp",) + island, None)
    in_specs = (tokens, tokens, P(island, "fsdp", None), width, width, tokens)
    out_specs = (tokens, tokens, width, width)
    return jax.shard_map(local, mesh=split, in_specs=in_specs, out_specs=out_specs, check_vma=False)
```

time: 737 us -> 233 us (0.32)
  waiting for transfers between devices: 639 us -> 104 us
  blocking collectives: 31.9 us -> 0 us
  starting transfers between devices: 4.98 us -> 36.5 us
  matrix products: 33.2 us -> 11.4 us
  other arithmetic: 3.94 us -> 22.5 us
  local copies, waits for them, and re-layouts: 9.17 us -> 27.4 us
  Pallas kernels: 0 us -> 16.1 us
    all_gather x3 -> x1, waiting for transfers between devices: 459 us -> 35.5 us  [local(): lax.all_gather(new_outer.astype(bf16), ('z', 'x'), axis=0, tiled=True)]
    reduce_scatter x1 -> x0, waiting for transfers between devices: 179 us -> none  [local(): lax.psum_scatter(inner_new, 'island', scatter_dimension=0, tiled=True)]
    ppermute x0 -> x24, waiting for transfers between devices: none -> 68.5 us  [the longest x1 20.9 us: local(): nexts.append(lax.ppermute(mine, 'fsdp', ring(fsdp, s)))]
    ppermute x0 -> x24, starting transfers between devices: none -> 36.4 us  [the longest x3 17.4 us: local(): up = lax.ppermute(send_up.astype(bf16), 'z', [(i, i + 1) for i in range(t)])]
    all_gather x1 -> x0, blocking collectives: 31.9 us -> none  [local(): island_cotangent = lax.all_gather(cotangent, 'fsdp', axis=0, tiled=True)]
    dot_general x3 -> x2, matrix products: 33.2 us -> 11.4 us  [the longest x1 6.21 us: local(): lax.dot_general(jnp.concatenate(cots, axis=0), own_weight, (((1,), (1,)),...]
    convert_element_type x1 -> x9, other arithmetic: 3.94 us -> 20.6 us  [the longest x4 8.81 us: local(): over_x = (rows(keep, 1 - x) + rows(other, 1 - x)).astype(bf16)]
    pallas_call x0 -> x4, Pallas kernels: none -> 16.1 us  [inner_block(): pl.pallas_call(functools.partial(inner_kernel, fsdp, share, inner_rate /...]
  transfers between devices with their start and end apart: 5 -> 25, of which waited for: 4 -> 12; matrix products, arithmetic and copies ran while one was open for 2% -> 16% of each run, Pallas kernels for 0% -> 5%
where the time goes in v1:
time: 233 us; the launch traced here: 232 us
  waiting for transfers between devices  104 us (45%)
  starting transfers between devices  36.5 us (16%)
  local copies, waits for them, and re-layouts  27.4 us (12%)
  other arithmetic  22.5 us (10%)
  Pallas kernels  16.1 us (7%)
  between operations  14.3 us (6%)
  matrix products  11.4 us (5%)
    all_gather x1, waiting for transfers between devices, local(): lax.all_gather(new_outer.astype(bf16), ('z', 'x'), axis=0, tiled=True)  35.5 us
    ppermute x1, waiting for transfers between devices, local(): nexts.append(lax.ppermute(mine, 'fsdp', ring(fsdp, s)))  20.9 us
    unnamed x40, local copies, waits for them, and re-layouts  20.5 us
    ppermute x3, starting transfers between devices, local(): up = lax.ppermute(send_up.astype(bf16), 'z', [(i, i + 1) for i in range(t)])  17.4 us
    ppermute x4, waiting for transfers between devices, local(): acts.append(lax.ppermute(mine, 'fsdp', ring(fsdp, s)))  17.2 us
    pallas_call x4, Pallas kernels, inner_block(): pl.pallas_call(functools.partial(inner_kernel, fsdp, share, inner_rate /...  16.1 us
    ppermute x3, waiting for transfers between devices, local(): up = lax.ppermute(send_up.astype(bf16), 'z', [(i, i + 1) for i in range(t)])  10.2 us
    convert_element_type x4, other arithmetic, local(): over_x = (rows(keep, 1 - x) + rows(other, 1 - x)).astype(bf16)  8.81 us
  transfers between devices with their start and end apart: 25, of which 12 were waited for; matrix products, arithmetic and copies ran while one was open for 16% of the time, Pallas kernels for 5%

profile of v1, /device:TPU:0, one launch (start us, length us, event | category | flops | bytes accessed | tf_op | source)
XLA Modules:
  0.0 232.2 jit_solution(7515620605429463795)
XLA Ops:
  7.3 2.3 constant_dynamic-slice_fusion.3
  9.5 3.0 %collective-permute-start.10 = (bf16[128,1024]{1,0:T(8,128)(2,1)S(1)}, bf16[128,1024]{1,0:T(8,128)(2,1)S(1)}, u32[]{:S(2)}, u32[]{:S(2)}) collective-permute-start(bf16[128,1024]{1,0:T(8,128)(2,1)S(1)} %get-tuple-element.32), channel_id=1, source_target_pairs={{0,1},{1,0},{2,3},{3,2},{4,5},{5,4},{6,7},{7,6},{8,9},{9,8},{10,11... | collective-permute-start | bytes 786440 | tf_op jit(solution)/shard_map/ppermute | solution.py:87
  12.6 7.0 %collective-permute-done.10.refs_1_ = bf16[128,1024]{1,0:T(8,128)(2,1)S(1)} collective-permute-done((bf16[128,1024]{1,0:T(8,128)(2,1)S(1)}, bf16[128,1024]{1,0:T(8,128)(2,1)S(1)}, u32[]{:S(2)}, u32[]{:S(2)}) %collective-permute-start.10) | collective-permute-done | bytes 262176 | tf_op jit(solution)/shard_map/ppermute | solution.py:87
  19.6 4.8 %collective-permute-done.refs_3_ = bf16[128,1024]{1,0:T(8,128)(2,1)S(1)} collective-permute-done((bf16[128,1024]{1,0:T(8,128)(2,1)}, bf16[128,1024]{1,0:T(8,128)(2,1)S(1)}, u32[]{:S(2)}, u32[]{:S(2)}) %collective-permute-start) | collective-permute-done | bytes 262176 | tf_op jit(solution)/shard_map/ppermute | solution.py:79
  24.4 3.4 %copy-done = bf16[1,4096,1024]{2,1,0:T(8,128)(2,1)S(1)} copy-done((bf16[1,4096,1024]{2,1,0:T(8,128)(2,1)S(1)}, bf16[1,4096,1024]{2,1,0:T(8,128)(2,1)}, u32[]{:S(2)}) %copy-start) | copy-done | bytes 8388632
  28.8 4.0 %shard_map.95 = (bf16[512,1024]{1,0:T(8,128)(2,1)}, f32[512,1024]{1,0:T(8,128)S(1)}) custom-call(s32[3]{0:T(128)S(1)} %add_add_fusion.2.place, bf16[128,8192]{1,0:T(8,128)(2,1)S(1)} %copy-done.4, bf16[128,1024]{1,0:T(8,128)(2,1)S(1)} %collective-permute-done.10.refs_1_, bf16[128,1024]{1,0:T(8,128)(2,1)S(1)} %copy-done.8, ...), custom_call_target="tpu_custom_call" | custom-call | flops 536870912 | bytes 6291456 | tf_op jit(solution)/shard_map/pallas_call | solution.py:55
  35.9 6.9 %collective-permute-done.13.refs_1_ = bf16[128,1024]{1,0:T(8,128)(2,1)S(1)} collective-permute-done((bf16[128,1024]{1,0:T(8,128)(2,1)S(1)}, bf16[128,1024]{1,0:T(8,128)(2,1)S(1)}, u32[]{:S(2)}, u32[]{:S(2)}) %collective-permute-start.13) | collective-permute-done | bytes 262176 | tf_op jit(solution)/shard_map/ppermute | solution.py:87
  42.8 3.4 %copy-done.1 = bf16[1,4096,1024]{2,1,0:T(8,128)(2,1)S(1)} copy-done((bf16[1,4096,1024]{2,1,0:T(8,128)(2,1)S(1)}, bf16[1,4096,1024]{2,1,0:T(8,128)(2,1)}, u32[]{:S(2)}) %copy-start.1) | copy-done | bytes 8388632
  46.2 4.0 %shard_map.96 = (bf16[512,1024]{1,0:T(8,128)(2,1)}, f32[512,1024]{1,0:T(8,128)S(1)}) custom-call(s32[3]{0:T(128)S(1)} %add_add_fusion.3.place, bf16[128,8192]{1,0:T(8,128)(2,1)S(1)} %copy-done.4, bf16[128,1024]{1,0:T(8,128)(2,1)S(1)} %collective-permute-done.13.refs_1_, bf16[128,1024]{1,0:T(8,128)(2,1)S(1)} %copy-done.9, ...), custom_call_target="tpu_custom_call" | custom-call | flops 536870912 | bytes 6291456 | tf_op jit(solution)/shard_map/pallas_call | solution.py:55
  53.3 2.3 add_convert_fusion.5
  57.2 3.3 %collective-permute-done.7.refs_1_ = bf16[128,1024]{1,0:T(8,128)(2,1)S(1)} collective-permute-done((bf16[128,1024]{1,0:T(8,128)(2,1)}, bf16[128,1024]{1,0:T(8,128)(2,1)S(1)}, u32[]{:S(2)}, u32[]{:S(2)}) %collective-permute-start.7) | collective-permute-done | bytes 262176 | tf_op jit(solution)/shard_map/ppermute | solution.py:87
  60.5 3.4 %copy-done.2 = bf16[1,4096,1024]{2,1,0:T(8,128)(2,1)S(1)} copy-done((bf16[1,4096,1024]{2,1,0:T(8,128)(2,1)S(1)}, bf16[1,4096,1024]{2,1,0:T(8,128)(2,1)}, u32[]{:S(2)}) %copy-start.2) | copy-done | bytes 8388632
  63.9 4.0 %shard_map.94 = (bf16[512,1024]{1,0:T(8,128)(2,1)}, f32[512,1024]{1,0:T(8,128)S(1)}) custom-call(s32[3]{0:T(128)S(1)} %add_add_fusion.1.place, bf16[128,8192]{1,0:T(8,128)(2,1)S(1)} %copy-done.4, bf16[128,1024]{1,0:T(8,128)(2,1)S(1)} %collective-permute-done.7.refs_1_, bf16[128,1024]{1,0:T(8,128)(2,1)S(1)} %copy-done.9, ...), custom_call_target="tpu_custom_call" | custom-call | flops 536870912 | bytes 6291456 | tf_op jit(solution)/shard_map/pallas_call | solution.py:55
  71.0 2.5 %add_convert_fusion.4 = bf16[256,1024]{1,0:T(8,128)(2,1)} fusion(f32[512,1024]{1,0:T(8,128)} %copy-done.10, s32[]{:T(128)S(6)} %select_n.93, bf16[512,1024]{1,0:T(8,128)(2,1)} %collective-permute-done.14), kind=kLoop, calls=%fused_computation.17 | loop fusion | flops 786432 | bytes 2097156 | tf_op jit(solution)/shard_map/convert_element_type | solution.py:95
  77.1 4.3 %collective-permute-start.16 = (bf16[256,1024]{1,0:T(8,128)(2,1)}, bf16[256,1024]{1,0:T(8,128)(2,1)}, u32[]{:S(2)}, u32[]{:S(2)}) collective-permute-start(bf16[256,1024]{1,0:T(8,128)(2,1)} %fusion.11), channel_id=1, source_target_pairs={{0,8},{1,9},{2,10},{3,11},{4,12},{5,13},{6,14},{7,15}} | collective-permute-start | bytes 1572872 | tf_op jit(solution)/shard_map/ppermute | solution.py:113
  82.9 3.4 %copy-done.3 = bf16[1,4096,1024]{2,1,0:T(8,128)(2,1)S(1)} copy-done((bf16[1,4096,1024]{2,1,0:T(8,128)(2,1)S(1)}, bf16[1,4096,1024]{2,1,0:T(8,128)(2,1)}, u32[]{:S(2)}) %copy-start.3) | copy-done | bytes 8388632
  86.3 4.0 %shard_map.93 = (bf16[512,1024]{1,0:T(8,128)(2,1)}, f32[512,1024]{1,0:T(8,128)S(1)}) custom-call(s32[3]{0:T(128)S(1)} %add_add_fusion.place, bf16[128,8192]{1,0:T(8,128)(2,1)S(1)} %copy-done.4, bf16[128,1024]{1,0:T(8,128)(2,1)S(1)} %collective-permute-done.4.refs_1_, bf16[128,1024]{1,0:T(8,128)(2,1)S(1)} %copy-done.9, ...), custom_call_target="tpu_custom_call" | custom-call | flops 536870912 | bytes 6291456 | tf_op jit(solution)/shard_map/pallas_call | solution.py:55
  90.4 2.5 %add_convert_fusion.6 = bf16[256,1024]{1,0:T(8,128)(2,1)} fusion(f32[512,1024]{1,0:T(8,128)S(1)} %copy-done.15, s32[]{:T(128)S(6)} %select_n.93, bf16[512,1024]{1,0:T(8,128)(2,1)} %collective-permute-done.8), kind=kLoop, calls=%fused_computation.21 | loop fusion | flops 786432 | bytes 2097156 | tf_op jit(solution)/shard_map/convert_element_type | solution.py:95
  93.5 3.0 %add_convert_fusion.3 = (bf16[256,1024]{1,0:T(8,128)(2,1)}, bf16[256,1024]{1,0:T(8,128)(2,1)}) fusion(bf16[256,1024]{1,0:T(8,128)(2,1)} %collective-permute-done.16, bf16[256,1024]{1,0:T(8,128)(2,1)} %collective-permute-done.15, bf16[512,1024]{1,0:T(8,128)(2,1)} %collective-permute-done.14, s32[]{:T(128)S(6)} %select_n.92, f32[512,1024]{1,0:T(8,128)S(1)} %copy-done.11, ...), kind=kLoop, calls=%fused_computation.15 | loop fusion | flops 2621440 | bytes 4194308 | tf_op jit(solution)/shard_map/convert_element_type | solution.py:113
  96.5 4.0 %collective-permute-start.17 = (bf16[256,1024]{1,0:T(8,128)(2,1)}, bf16[256,1024]{1,0:T(8,128)(2,1)}, u32[]{:S(2)}, u32[]{:S(2)}) collective-permute-start(bf16[256,1024]{1,0:T(8,128)(2,1)} %get-tuple-element.25), channel_id=1, source_target_pairs={{0,8},{8,16},{1,9},{9,17},{2,10},{10,18},{3,11},{11,19},{4,12},{12... | collective-permute-start | bytes 1572872 | tf_op jit(solution)/shard_map/ppermute | solution.py:113
  104.1 3.8 %collective-permute-done.9 = bf16[256,1024]{1,0:T(8,128)(2,1)} collective-permute-done((bf16[256,1024]{1,0:T(8,128)(2,1)}, bf16[256,1024]{1,0:T(8,128)(2,1)}, u32[]{:S(2)}, u32[]{:S(2)}) %collective-permute-start.9) | collective-permute-done | bytes 524320 | tf_op jit(solution)/shard_map/ppermute | solution.py:97
  108.0 2.5 %collective-permute-done.17 = bf16[256,1024]{1,0:T(8,128)(2,1)} collective-permute-done((bf16[256,1024]{1,0:T(8,128)(2,1)}, bf16[256,1024]{1,0:T(8,128)(2,1)}, u32[]{:S(2)}, u32[]{:S(2)}) %collective-permute-start.17) | collective-permute-done | bytes 524320 | tf_op jit(solution)/shard_map/ppermute | solution.py:113
  110.4 2.8 %add_convert_fusion.2 = (bf16[256,1024]{1,0:T(8,128)(2,1)S(1)}, bf16[256,1024]{1,0:T(8,128)(2,1)S(1)}) fusion(bf16[256,1024]{1,0:T(8,128)(2,1)} %collective-permute-done.17, pred[]{:T(512)S(6)} %eq.14, bf16[256,1024]{1,0:T(8,128)(2,1)} %collective-permute-done.9, bf16[512,1024]{1,0:T(8,128)(2,1)} %collective-permute-done.8, s32[]{:T(128)S(6)} %select_n.92, ...), kind=kLoop, calls=%fused_computation.14 | loop fusion | flops 4194304 | bytes 6291462 | tf_op jit(solution)/shard_map/convert_element_type | solution.py:113
  113.2 9.1 %collective-permute-start.18 = (bf16[256,1024]{1,0:T(8,128)(2,1)S(1)}, bf16[256,1024]{1,0:T(8,128)(2,1)S(1)}, u32[]{:S(2)}, u32[]{:S(2)}) collective-permute-start(bf16[256,1024]{1,0:T(8,128)(2,1)S(1)} %get-tuple-element.23), channel_id=1, source_target_pairs={{0,8},{8,16},{16,24},{1,9},{9,17},{17,25},{2,10},{10,18},{18,26},{... | collective-permute-start | bytes 1572872 | tf_op jit(solution)/shard_map/ppermute | solution.py:113
  123.8 7.7 %collective-permute-done.18 = bf16[256,1024]{1,0:T(8,128)(2,1)S(1)} collective-permute-done((bf16[256,1024]{1,0:T(8,128)(2,1)S(1)}, bf16[256,1024]{1,0:T(8,128)(2,1)S(1)}, u32[]{:S(2)}, u32[]{:S(2)}) %collective-permute-start.18) | collective-permute-done | bytes 524320 | tf_op jit(solution)/shard_map/ppermute | solution.py:113
  131.5 4.1 %collective-permute-done.21 = bf16[256,1024]{1,0:T(8,128)(2,1)S(1)} collective-permute-done((bf16[256,1024]{1,0:T(8,128)(2,1)S(1)}, bf16[256,1024]{1,0:T(8,128)(2,1)S(1)}, u32[]{:S(2)}, u32[]{:S(2)}) %collective-permute-start.21) | collective-permute-done | bytes 524320 | tf_op jit(solution)/shard_map/ppermute | solution.py:114
  135.7 3.2 %fusion.12 = (bf16[256,1024]{1,0:T(8,128)(2,1)}, f32[256,1024]{1,0:T(8,128)}, f32[256,1024]{1,0:T(8,128)}) fusion(f32[256,1024]{1,0:T(8,128)S(1)} %copy-done.17, f32[256,1024]{1,0:T(8,128)S(1)} %copy-done.18, bf16[256,1024]{1,0:T(8,128)(2,1)S(1)} %collective-permute-done.21, bf16[256,1024]{1,0:T(8,128)(2,1)S(1)} %collective-permute-done.18, ...), kind=kLoop, calls=%fused_computation.46 | loop fusion | flops 4456448 | bytes 7864324 | tf_op jit(solution)/shard_map/convert_element_type | solution.py:141
  143.1 20.9 %collective-permute-done.2 = bf16[128,4096]{0,1:T(8,128)(2,1)} collective-permute-done((bf16[128,4096]{0,1:T(8,128)(2,1)}, bf16[128,4096]{0,1:T(8,128)(2,1)}, u32[]{:S(2)}, u32[]{:S(2)}) %collective-permute-start.2) | collective-permute-done | bytes 1048608 | tf_op jit(solution)/shard_map/ppermute | solution.py:130
  166.5 6.2 %convolution_convert_fusion = bf16[256,4096]{1,0:T(8,128)(2,1)S(1)} fusion(bf16[128,1024]{1,0:T(8,128)(2,1)S(1)} %collective-permute-done.refs_3_, bf16[128,1024]{1,0:T(8,128)(2,1)S(1)} %copy-done.9, bf16[1,4096,1024]{2,1,0:T(8,128)(2,1)} %param.8), kind=kOutput, calls=%fused_computation | convolution fusion | flops 2149580800 | bytes 11010048 | tf_op jit(solution)/shard_map/dot_general | solution.py:117
  173.3 35.5 %all-gather.2.cloned.1.call-done = bf16[2048,1024]{1,0:T(8,128)(2,1)} async-done(((bf16[256,1024]{1,0:T(8,128)(2,1)}), bf16[2048,1024]{1,0:T(8,128)(2,1)}) %all-gather.2.cloned.1.call-update) | async-done | bytes 4194320 | tf_op jit(solution)/shard_map/all_gather | solution.py:141
  208.7 5.2 %fusion = f32[512,1024]{1,0:T(8,128)S(1)} fusion(bf16[2048,1024]{1,0:T(8,128)(2,1)} %all-gather.2.cloned.1.call-done, bf16[256,2048]{0,1:T(8,128)(2,1)} %collective-permute-done.3, bf16[256,2048]{0,1:T(8,128)(2,1)} %bitcast.21), kind=kOutput, calls=%fused_computation.2 | convolution fusion | flops 2151677952 | bytes 8388608 | tf_op jit(solution)/shard_map/dot_general | solution.py:143
  219.1 5.5 %collective-permute-done.23 = bf16[128,1024]{1,0:T(8,128)(2,1)S(1)} collective-permute-done((bf16[128,1024]{1,0:T(8,128)(2,1)S(1)}, bf16[128,1024]{1,0:T(8,128)(2,1)S(1)}, u32[]{:S(2)}, u32[]{:S(2)}) %collective-permute-start.23) | collective-permute-done | bytes 262176 | tf_op jit(solution)/shard_map/ppermute | solution.py:148
  (88 shorter events, 35.9 us)
Async XLA Ops:
  7.2 17.3 %copy-start.4 = (bf16[128,8192]{1,0:T(8,128)(2,1)S(1)}, bf16[128,8192]{1,0:T(8,128)(2,1)}, u32[]{:S(2)}) copy-start(bf16[128,8192]{1,0:T(8,128)(2,1)} %refs_0_.7) | copy-start | bytes 6291460
  7.2 201.6 %all-gather.2.cloned.1.call-start = ((), (), s32[]{:S(2)}) async-start(), calls=%async_computation | async-start | bytes 4718592 | tf_op jit(solution)/shard_map/all_gather | solution.py:141
  9.5 10.1 %collective-permute-start.10 = (bf16[128,1024]{1,0:T(8,128)(2,1)S(1)}, bf16[128,1024]{1,0:T(8,128)(2,1)S(1)}, u32[]{:S(2)}, u32[]{:S(2)}) collective-permute-start(bf16[128,1024]{1,0:T(8,128)(2,1)S(1)} %get-tuple-element.32), channel_id=1, source_target_pairs={{0,1},{1,0},{2,3},{3,2},{4,5},{5,4},{6,7},{7,6},{8,9},{9,8},{10,11... | collective-permute-start | bytes 786440 | tf_op jit(solution)/shard_map/ppermute | solution.py:87
  12.5 11.9 %collective-permute-start = (bf16[128,1024]{1,0:T(8,128)(2,1)}, bf16[128,1024]{1,0:T(8,128)(2,1)S(1)}, u32[]{:S(2)}, u32[]{:S(2)}) collective-permute-start(bf16[128,1024]{1,0:T(8,128)(2,1)} %refs_2_.7), channel_id=1, source_target_pairs={{0,1},{1,0},{2,3},{3,2},{4,5},{5,4},{6,7},{7,6},{8,9},{9,8},{10,11... | collective-permute-start | bytes 786440 | tf_op jit(solution)/shard_map/ppermute | solution.py:79
  28.8 14.1 %copy-start.9 = (bf16[128,1024]{1,0:T(8,128)(2,1)S(1)}, bf16[128,1024]{1,0:T(8,128)(2,1)}, u32[]{:S(2)}) copy-start(bf16[128,1024]{1,0:T(8,128)(2,1)} %refs_2_.7) | copy-start | bytes 786436
  34.1 19.2 %collective-permute-start.11 = (bf16[512,1024]{1,0:T(8,128)(2,1)}, bf16[512,1024]{1,0:T(8,128)(2,1)}, u32[]{:S(2)}, u32[]{:S(2)}) collective-permute-start(bf16[512,1024]{1,0:T(8,128)(2,1)} %get-tuple-element.17), channel_id=1, source_target_pairs={{0,2},{2,0},{1,3},{3,1},{4,6},{6,4},{5,7},{7,5},{8,10},{10,8},{9,1... | collective-permute-start | bytes 3145736 | tf_op jit(solution)/shard_map/ppermute | solution.py:90
  34.1 8.7 %collective-permute-start.13 = (bf16[128,1024]{1,0:T(8,128)(2,1)S(1)}, bf16[128,1024]{1,0:T(8,128)(2,1)S(1)}, u32[]{:S(2)}, u32[]{:S(2)}) collective-permute-start(bf16[128,1024]{1,0:T(8,128)(2,1)S(1)} %get-tuple-element.34), channel_id=1, source_target_pairs={{0,1},{1,0},{2,3},{3,2},{4,5},{5,4},{6,7},{7,6},{8,9},{9,8},{10,11... | collective-permute-start | bytes 786440 | tf_op jit(solution)/shard_map/ppermute | solution.py:87
  51.6 19.4 %collective-permute-start.14 = (bf16[512,1024]{1,0:T(8,128)(2,1)}, bf16[512,1024]{1,0:T(8,128)(2,1)}, u32[]{:S(2)}, u32[]{:S(2)}) collective-permute-start(bf16[512,1024]{1,0:T(8,128)(2,1)} %get-tuple-element.19), channel_id=1, source_target_pairs={{0,2},{2,0},{1,3},{3,1},{4,6},{6,4},{5,7},{7,5},{8,10},{10,8},{9,1... | collective-permute-start | bytes 3145736 | tf_op jit(solution)/shard_map/ppermute | solution.py:90
  51.6 8.9 %collective-permute-start.7 = (bf16[128,1024]{1,0:T(8,128)(2,1)}, bf16[128,1024]{1,0:T(8,128)(2,1)S(1)}, u32[]{:S(2)}, u32[]{:S(2)}) collective-permute-start(bf16[128,1024]{1,0:T(8,128)(2,1)} %get-tuple-element.33), channel_id=1, source_target_pairs={{0,1},{1,0},{2,3},{3,2},{4,5},{5,4},{6,7},{7,6},{8,9},{9,8},{10,11... | collective-permute-start | bytes 786440 | tf_op jit(solution)/shard_map/ppermute | solution.py:87
  55.6 19.3 %collective-permute-start.12 = (bf16[256,1024]{1,0:T(8,128)(2,1)}, bf16[256,1024]{1,0:T(8,128)(2,1)S(1)}, u32[]{:S(2)}, u32[]{:S(2)}) collective-permute-start(bf16[256,1024]{1,0:T(8,128)(2,1)} %add_convert_fusion.5), channel_id=1, source_target_pairs={{0,4},{4,0},{1,5},{5,1},{2,6},{6,2},{3,7},{7,3},{8,12},{12,8},{9,1... | collective-permute-start | bytes 1572872 | tf_op jit(solution)/shard_map/ppermute | solution.py:97
  69.3 21.1 %collective-permute-start.8 = (bf16[512,1024]{1,0:T(8,128)(2,1)}, bf16[512,1024]{1,0:T(8,128)(2,1)}, u32[]{:S(2)}, u32[]{:S(2)}) collective-permute-start(bf16[512,1024]{1,0:T(8,128)(2,1)} %get-tuple-element.15), channel_id=1, source_target_pairs={{0,2},{2,0},{1,3},{3,1},{4,6},{6,4},{5,7},{7,5},{8,10},{10,8},{9,1... | collective-permute-start | bytes 3145736 | tf_op jit(solution)/shard_map/ppermute | solution.py:90
  69.3 13.6 %collective-permute-start.4 = (bf16[128,1024]{1,0:T(8,128)(2,1)}, bf16[128,1024]{1,0:T(8,128)(2,1)S(1)}, u32[]{:S(2)}, u32[]{:S(2)}) collective-permute-start(bf16[128,1024]{1,0:T(8,128)(2,1)} %get-tuple-element.31), channel_id=1, source_target_pairs={{0,1},{1,0},{2,3},{3,2},{4,5},{5,4},{6,7},{7,6},{8,9},{9,8},{10,11... | collective-permute-start | bytes 786440 | tf_op jit(solution)/shard_map/ppermute | solution.py:87
  73.5 20.0 %collective-permute-start.15 = (bf16[256,1024]{1,0:T(8,128)(2,1)}, bf16[256,1024]{1,0:T(8,128)(2,1)}, u32[]{:S(2)}, u32[]{:S(2)}) collective-permute-start(bf16[256,1024]{1,0:T(8,128)(2,1)} %add_convert_fusion.4), channel_id=1, source_target_pairs={{0,4},{4,0},{1,5},{5,1},{2,6},{6,2},{3,7},{7,3},{8,12},{12,8},{9,1... | collective-permute-start | bytes 1572872 | tf_op jit(solution)/shard_map/ppermute | solution.py:97
  77.1 16.4 %collective-permute-start.16 = (bf16[256,1024]{1,0:T(8,128)(2,1)}, bf16[256,1024]{1,0:T(8,128)(2,1)}, u32[]{:S(2)}, u32[]{:S(2)}) collective-permute-start(bf16[256,1024]{1,0:T(8,128)(2,1)} %fusion.11), channel_id=1, source_target_pairs={{0,8},{1,9},{2,10},{3,11},{4,12},{5,13},{6,14},{7,15}} | collective-permute-start | bytes 1572872 | tf_op jit(solution)/shard_map/ppermute | solution.py:113
  81.4 12.0 %collective-permute-start.19 = (bf16[256,1024]{1,0:T(8,128)(2,1)}, bf16[256,1024]{1,0:T(8,128)(2,1)}, u32[]{:S(2)}, u32[]{:S(2)}) collective-permute-start(bf16[256,1024]{1,0:T(8,128)(2,1)} %fusion.11), channel_id=1, source_target_pairs={{24,16},{25,17},{26,18},{27,19},{28,20},{29,21},{30,22},{31,23}} | collective-permute-start | bytes 1572872 | tf_op jit(solution)/shard_map/ppermute | solution.py:114
  90.4 11.6 %collective-permute-start.5 = (bf16[512,1024]{1,0:T(8,128)(2,1)}, bf16[512,1024]{1,0:T(8,128)(2,1)}, u32[]{:S(2)}, u32[]{:S(2)}) collective-permute-start(bf16[512,1024]{1,0:T(8,128)(2,1)} %get-tuple-element.13), channel_id=1, source_target_pairs={{0,2},{2,0},{1,3},{3,1},{4,6},{6,4},{5,7},{7,5},{8,10},{10,8},{9,1... | collective-permute-start | bytes 3145736 | tf_op jit(solution)/shard_map/ppermute | solution.py:90
  92.9 15.0 %collective-permute-start.9 = (bf16[256,1024]{1,0:T(8,128)(2,1)}, bf16[256,1024]{1,0:T(8,128)(2,1)}, u32[]{:S(2)}, u32[]{:S(2)}) collective-permute-start(bf16[256,1024]{1,0:T(8,128)(2,1)} %add_convert_fusion.6), channel_id=1, source_target_pairs={{0,4},{4,0},{1,5},{5,1},{2,6},{6,2},{3,7},{7,3},{8,12},{12,8},{9,1... | collective-permute-start | bytes 1572872 | tf_op jit(solution)/shard_map/ppermute | solution.py:97
  96.5 13.9 %copy-start.7 = (f32[512,1024]{1,0:T(8,128)S(1)}, f32[512,1024]{1,0:T(8,128)}, u32[]{:S(2)}) copy-start(f32[512,1024]{1,0:T(8,128)} %copy-done.5) | copy-start | bytes 6291460
  96.5 13.9 %collective-permute-start.17 = (bf16[256,1024]{1,0:T(8,128)(2,1)}, bf16[256,1024]{1,0:T(8,128)(2,1)}, u32[]{:S(2)}, u32[]{:S(2)}) collective-permute-start(bf16[256,1024]{1,0:T(8,128)(2,1)} %get-tuple-element.25), channel_id=1, source_target_pairs={{0,8},{8,16},{1,9},{9,17},{2,10},{10,18},{3,11},{11,19},{4,12},{12... | collective-permute-start | bytes 1572872 | tf_op jit(solution)/shard_map/ppermute | solution.py:113
  100.5 9.9 %collective-permute-start.20 = (bf16[256,1024]{1,0:T(8,128)(2,1)}, bf16[256,1024]{1,0:T(8,128)(2,1)}, u32[]{:S(2)}, u32[]{:S(2)}) collective-permute-start(bf16[256,1024]{1,0:T(8,128)(2,1)} %get-tuple-element.26), channel_id=1, source_target_pairs={{16,8},{24,16},{17,9},{25,17},{18,10},{26,18},{19,11},{27,19},{20,... | collective-permute-start | bytes 1572872 | tf_op jit(solution)/shard_map/ppermute | solution.py:114
  103.5 32.2 %copy-start.13 = (f32[512,1024]{1,0:T(8,128)S(1)}, f32[512,1024]{1,0:T(8,128)}, u32[]{:S(2)}) copy-start(f32[512,1024]{1,0:T(8,128)} %copy-done.12) | copy-start | bytes 6291460
  103.5 32.2 %copy-start.17 = (f32[256,1024]{1,0:T(8,128)S(1)}, f32[256,1024]{1,0:T(8,128)}, u32[]{:S(2)}) copy-start(f32[256,1024]{1,0:T(8,128)} %param.9) | copy-start | bytes 3145732
  103.5 32.2 %copy-start.18 = (f32[256,1024]{1,0:T(8,128)S(1)}, f32[256,1024]{1,0:T(8,128)}, u32[]{:S(2)}) copy-start(f32[256,1024]{1,0:T(8,128)} %param.10) | copy-start | bytes 3145732
  103.5 20.3 %collective-permute-start.6 = (bf16[256,1024]{1,0:T(8,128)(2,1)S(1)}, bf16[256,1024]{1,0:T(8,128)(2,1)S(1)}, u32[]{:S(2)}, u32[]{:S(2)}) collective-permute-start(bf16[256,1024]{1,0:T(8,128)(2,1)S(1)} %add_convert_fusion.7), channel_id=1, source_target_pairs={{0,4},{4,0},{1,5},{5,1},{2,6},{6,2},{3,7},{7,3},{8,12},{12,8},{9,1... | collective-permute-start | bytes 1572872 | tf_op jit(solution)/shard_map/ppermute | solution.py:97
  113.2 18.3 %collective-permute-start.18 = (bf16[256,1024]{1,0:T(8,128)(2,1)S(1)}, bf16[256,1024]{1,0:T(8,128)(2,1)S(1)}, u32[]{:S(2)}, u32[]{:S(2)}) collective-permute-start(bf16[256,1024]{1,0:T(8,128)(2,1)S(1)} %get-tuple-element.23), channel_id=1, source_target_pairs={{0,8},{8,16},{16,24},{1,9},{9,17},{17,25},{2,10},{10,18},{18,26},{... | collective-permute-start | bytes 1572872 | tf_op jit(solution)/shard_map/ppermute | solution.py:113
  122.3 13.3 %collective-permute-start.21 = (bf16[256,1024]{1,0:T(8,128)(2,1)S(1)}, bf16[256,1024]{1,0:T(8,128)(2,1)S(1)}, u32[]{:S(2)}, u32[]{:S(2)}) collective-permute-start(bf16[256,1024]{1,0:T(8,128)(2,1)S(1)} %get-tuple-element.24), channel_id=1, source_target_pairs={{8,0},{16,8},{24,16},{9,1},{17,9},{25,17},{10,2},{18,10},{26,18},{... | collective-permute-start | bytes 1572872 | tf_op jit(solution)/shard_map/ppermute | solution.py:114
  141.9 22.1 %collective-permute-start.2 = (bf16[128,4096]{0,1:T(8,128)(2,1)}, bf16[128,4096]{0,1:T(8,128)(2,1)}, u32[]{:S(2)}, u32[]{:S(2)}) collective-permute-start(bf16[128,4096]{0,1:T(8,128)(2,1)} %copy.13), channel_id=1, source_target_pairs={{0,1},{1,0},{2,3},{3,2},{4,5},{5,4},{6,7},{7,6},{8,9},{9,8},{10,11... | collective-permute-start | bytes 3145736 | tf_op jit(solution)/shard_map/ppermute | solution.py:130
  166.5 6.8 %collective-permute-start.3 = (bf16[256,2048]{0,1:T(8,128)(2,1)S(1)}, bf16[256,2048]{0,1:T(8,128)(2,1)}, u32[]{:S(2)}, u32[]{:S(2)}) collective-permute-start(bf16[256,2048]{0,1:T(8,128)(2,1)S(1)} %bitcast.22), channel_id=1, source_target_pairs={{0,2},{2,0},{1,3},{3,1},{4,6},{6,4},{5,7},{7,5},{8,10},{10,8},{9,1... | collective-permute-start | bytes 3145736 | tf_op jit(solution)/shard_map/ppermute | solution.py:136
  173.2 44.5 %collective-permute-start.1 = (bf16[128,4096]{1,0:T(8,128)(2,1)S(1)}, bf16[128,4096]{1,0:T(8,128)(2,1)}, u32[]{:S(2)}, u32[]{:S(2)}) collective-permute-start(bf16[128,4096]{1,0:T(8,128)(2,1)S(1)} %get-tuple-element.35), channel_id=1, source_target_pairs={{0,1},{1,0},{2,3},{3,2},{4,5},{5,4},{6,7},{7,6},{8,9},{9,8},{10,11... | collective-permute-start | bytes 3145736 | tf_op jit(solution)/shard_map/ppermute | solution.py:124
  214.0 2.0 collective-permute-start.22
  216.2 8.4 %collective-permute-start.23 = (bf16[128,1024]{1,0:T(8,128)(2,1)S(1)}, bf16[128,1024]{1,0:T(8,128)(2,1)S(1)}, u32[]{:S(2)}, u32[]{:S(2)}) collective-permute-start(bf16[128,1024]{1,0:T(8,128)(2,1)S(1)} %slice.40), channel_id=1, source_target_pairs={{0,1},{1,0},{2,3},{3,2},{4,5},{5,4},{6,7},{7,6},{8,9},{9,8},{10,11... | collective-permute-start | bytes 786440 | tf_op jit(solution)/shard_map/ppermute | solution.py:148
  219.1 6.3 %copy-start.16 = (bf16[128,8192]{1,0:T(8,128)(2,1)}, bf16[128,8192]{1,0:T(8,128)(2,1)S(1)}, u32[]{:S(2)}) copy-start(bf16[128,8192]{1,0:T(8,128)(2,1)S(1)} %constant_dynamic-update-slice_fusion) | copy-start | bytes 6291460
  (12 other events, 35.8 us)
Sparse Core Ops, SparseCore 0:
  139.0 69.6 all-gather.1

commit v2 on v0

v2 whole, which is shorter than its diff:
```python
import functools

import jax
import jax.numpy as jnp
from jax import lax
from jax.experimental import pallas as pl
from jax.experimental.pallas import tpu as pltpu
from jax.sharding import Mesh, PartitionSpec as P

inner_rate = 1.2
outer_rate = 0.7
nesterov = 0.9
CORES = 2
PAIR = 2
LANES = 128

bf16, f32 = jnp.bfloat16, jnp.float32
VMEM, HBM = pl.BlockSpec(memory_space=pltpu.VMEM), pl.BlockSpec(memory_space=pltpu.HBM)
SMEM = pl.BlockSpec(memory_space=pltpu.SMEM)
MIB = 1024 * 1024


def ring(count, shift):
    return [(i, (i + shift) % count) for i in range(count)]


def strip(axis, start, size):
    return (pl.ds(start, size), slice(None)) if axis == 0 else (slice(None), pl.ds(start, size))


def in_hbm(array):
    return pltpu.with_memory_space_constraint(array, pltpu.HBM)


def pack_kernel(plan, starts, *refs):
    sources, outs, done = refs[: len(plan)], refs[len(plan) : -1], refs[-1]
    copies, o = [], 0
    for source, (axis, size, counts) in zip(sources, plan):
        for count in counts:
            for i in range(count):
                n = len(copies)
                part = source.at[strip(axis, pl.multiple_of(starts[n], size), size)]
                copies.append(pltpu.make_async_copy(part, outs[o].at[strip(axis, i * size, size)], done.at[n]))
            o += 1
    for copy in copies:
        copy.start()
    for copy in copies:
        copy.wait()


def pack(items, after=()):
    result, rest = {}, []
    for n, (array, axis, size, groups) in enumerate(items):
        if axis == 1 and size % LANES:
            strips = [[lax.dynamic_slice_in_dim(array, at, size, axis=axis) for at in group] for group in groups]
            result[n] = [jnp.concatenate(group, axis=axis) for group in strips]
        else:
            rest.append((n, array, axis, size, groups))
    if not rest:
        return [result[n] for n in range(len(items))], list(after)
    starts = jnp.stack([at for item in rest for group in item[4] for at in group]).astype(jnp.int32)
    if after:
        starts, *after = lax.optimization_barrier((starts, *after))
    plan, shapes = [], []
    for _, array, axis, size, groups in rest:
        counts = [len(group) for group in groups]
        plan.append((axis, size, counts))
        for n in counts:
            shape = (n * size, array.shape[1]) if axis == 0 else (array.shape[0], n * size)
            shapes.append(jax.ShapeDtypeStruct(shape, array.dtype))
    moved = sum(4 * shape.size for shape in shapes)
    outs = pl.pallas_call(
        functools.partial(pack_kernel, plan),
        out_shape=shapes,
        in_specs=[SMEM] + [HBM] * len(rest),
        out_specs=[pl.BlockSpec(memory_space=pl.ANY)] * len(shapes),
        scratch_shapes=[pltpu.SemaphoreType.DMA((starts.shape[0],))],
        compiler_params=pltpu.CompilerParams(vmem_limit_bytes=4 * MIB),
        cost_estimate=pl.CostEstimate(flops=0, bytes_accessed=moved, transcendentals=0),
    )(starts, *[in_hbm(item[1]) for item in rest])
    for n, *_, groups in rest:
        result[n], outs = outs[: len(groups)], outs[len(groups) :]
    return [result[n] for n in range(len(items))], list(after)


def inner_kernel(pieces, share, scale, act_at, other_at, place, *refs):
    acts, cots = refs[:pieces], refs[pieces : 2 * pieces]
    own, other, give, keep, rows, total, done = refs[2 * pieces :]
    copies = []
    for i in range(PAIR):
        for n, (weight, at) in enumerate(((own, place[i] * share), (other, other_at + i * share))):
            source = weight.at[pl.ds(pl.multiple_of(at, share), share), :]
            copies.append(pltpu.make_async_copy(source, rows.at[n, i], done.at[n, i]))
    for copy in copies:
        copy.start()
    left = jnp.concatenate([a[:, act_at : act_at + PAIR * share] for a in acts], axis=0)
    right = jnp.concatenate([g[...] for g in cots], axis=0)
    total[...] = lax.dot_general(left, right, (((0,), (0,)), ((), ())), preferred_element_type=f32)
    for copy in copies:
        copy.wait()
    x = place[PAIR]

    def inner_new(i):
        grad = total[pl.ds(pl.multiple_of(i * share, share), share), :]
        return (rows[0, i].astype(f32) + rows[1, i].astype(f32)) - scale * grad

    give[...] = inner_new(1 - x).astype(bf16)
    keep[...] = inner_new(x)


def inner_block(place, acts, act_at, cots, own, other, other_at, share):
    pieces = len(acts)
    tok, kv = cots[0].shape
    if act_at % LANES or PAIR * share % LANES:
        acts, act_at = [a[:, act_at : act_at + PAIR * share] for a in acts], 0
    return pl.pallas_call(
        functools.partial(inner_kernel, pieces, share, inner_rate / (tok * pieces // CORES), act_at, other_at),
        out_shape=[jax.ShapeDtypeStruct((share, kv), bf16), jax.ShapeDtypeStruct((share, kv), f32)],
        in_specs=[SMEM] + [VMEM] * (2 * pieces) + [HBM] * 2,
        out_specs=[VMEM] * 2,
        scratch_shapes=[
            pltpu.VMEM((CORES, PAIR, share, kv), bf16),
            pltpu.VMEM((PAIR * share, kv), f32),
            pltpu.SemaphoreType.DMA((CORES, PAIR)),
        ],
        compiler_params=pltpu.CompilerParams(vmem_limit_bytes=24 * MIB),
        cost_estimate=pl.CostEstimate(flops=pieces * tok * share * kv, bytes_accessed=share * kv, transcendentals=0),
    )(place, *acts, *cots, in_hbm(own), other)


def keys_kernel(acts_count, at, *refs):
    acts, (*blocks, out) = refs[:acts_count], refs[acts_count:]
    if at:
        *blocks, before = blocks
    weight = jnp.concatenate([w[...] for w in blocks], axis=0)
    left = jnp.concatenate([a[:, at : at + weight.shape[0]] for a in acts], axis=0)
    product = jnp.dot(left, weight, preferred_element_type=f32)
    out[...] = before[...] + product if at else product


def keys_part(acts, blocks, at, before=()):
    rows, kv = len(acts) * acts[0].shape[0], blocks[0].shape[1]
    depth = sum(w.shape[0] for w in blocks)
    if at % LANES:
        acts = [a[:, at:] for a in acts]
        return before[0] + keys_part(acts, blocks, 0)
    return pl.pallas_call(
        functools.partial(keys_kernel, len(acts), at),
        out_shape=jax.ShapeDtypeStruct((rows, kv), f32),
        in_specs=[VMEM] * (len(acts) + len(blocks) + len(before)),
        out_specs=VMEM,
        compiler_params=pltpu.CompilerParams(vmem_limit_bytes=24 * MIB),
        cost_estimate=pl.CostEstimate(flops=2 * rows * depth * kv, bytes_accessed=rows * kv, transcendentals=0),
    )(*acts, *blocks, *before)


def core_sum_kernel(fsdp, tok, keep, came, to_x, stay_x, stay_f, *to_f):
    half = keep.shape[1] // 2
    total = keep[...] + came[...]
    rows = fsdp * tok
    stay_x[...] = total[:rows, :half]
    to_x[...] = total[rows:, :half].astype(bf16)
    for i in range(PAIR):
        here = slice(i * tok, (i + 1) * tok)
        stay_f[here, :] = total[i * rows : i * rows + tok, half:]
        for s in range(1, fsdp):
            to_f[s - 1][here, :] = total[i * rows + s * tok : i * rows + (s + 1) * tok, half:].astype(bf16)


def second_sum_kernel(fsdp, tok, *refs):
    stay_x, stay_f, from_x, *from_f = refs[: fsdp + 2]
    left, right, to_x, *to_f = refs[fsdp + 2 :]
    first = stay_x[...] + from_x[...].astype(f32)
    left[...] = first[:tok]
    for s in range(1, fsdp):
        to_f[s - 1][...] = first[s * tok : (s + 1) * tok].astype(bf16)
    second = stay_f[...]
    for came in from_f:
        second = second + came[...].astype(f32)
    right[...] = second[:tok]
    to_x[...] = second[tok:].astype(bf16)


def last_sum_kernel(left, right, from_x, *refs):
    *from_f, keys = refs
    half = left.shape[1]
    first = left[...]
    for came in from_f:
        first = first + came[...].astype(f32)
    keys[:, :half] = first.astype(bf16)
    keys[:, half:] = (right[...] + from_x[...].astype(f32)).astype(bf16)


def small_call(kernel, shapes, *args):
    size = sum(shape.size for shape in shapes)
    return pl.pallas_call(
        kernel,
        out_shape=shapes,
        in_specs=[VMEM] * len(args),
        out_specs=[VMEM] * len(shapes),
        compiler_params=pltpu.CompilerParams(vmem_limit_bytes=24 * MIB),
        cost_estimate=pl.CostEstimate(flops=size, bytes_accessed=8 * size, transcendentals=0),
    )(*args)


def join_kernel(starts, *refs):
    *parts, out, done = refs
    copies = []
    for n, part in enumerate(parts):
        width = part.shape[1]
        here = out.at[:, pl.ds(pl.multiple_of(starts[n], width), width)]
        copies.append(pltpu.make_async_copy(part, here, done.at[n]))
    for copy in copies:
        copy.start()
    for copy in copies:
        copy.wait()


def join(parts, starts):
    rows, width = parts[0].shape
    return pl.pallas_call(
        join_kernel,
        out_shape=jax.ShapeDtypeStruct((rows, width * len(parts)), parts[0].dtype),
        in_specs=[SMEM] + [pl.BlockSpec(memory_space=pl.ANY)] * len(parts),
        out_specs=HBM,
        scratch_shapes=[pltpu.SemaphoreType.DMA((len(parts),))],
        compiler_params=pltpu.CompilerParams(vmem_limit_bytes=4 * MIB),
        cost_estimate=pl.CostEstimate(flops=0, bytes_accessed=4 * rows * width * len(parts), transcendentals=0),
    )(jnp.stack(starts).astype(jnp.int32), *parts)


def local(activations, cotangent, inner_weight, outer_weight, outer_momentum, next_activations):
    fsdp, nz = lax.axis_size("fsdp"), lax.axis_size("z")
    f, z, x, c = (lax.axis_index(a) for a in ("fsdp", "z", "x", "core"))
    tok, d = activations.shape
    kv = cotangent.shape[1]
    width = d // fsdp
    block = width // nz
    share = block // (PAIR * CORES)
    own_weight = inner_weight[0]
    swap = ring(CORES, 1)

    def column(b, i, k, s):
        return ((f + s) % fsdp) * width + b * block + i * CORES * share + ((c + k) % CORES) * share

    def pair_ring(k, s):
        at = lambda i, j: (i % CORES) * fsdp + j % fsdp
        return [(at(i, j), at(i + k, j + s)) for i in range(CORES) for j in range(fsdp)]

    shifts = [(k, s) for s in range(fsdp) for k in range(CORES)]
    stages = [[nz - 1], list(range(nz - 2, -1, -1))]

    cots = {(0, 0): cotangent}
    for s in range(1, fsdp):
        cots[0, s] = lax.ppermute(cotangent, "fsdp", ring(fsdp, s))
    packed, after = [], []
    for ms in stages:
        columns = [[column(z ^ m, i, k, s) for m in ms for i in range(PAIR)] for k, s in shifts]
        rows = [((z ^ m) * PAIR * CORES + i * CORES + 1 - c) * share for m in ms for i in range(PAIR)]
        (mine, (weight,)), after = pack([(activations, 1, share, columns), (own_weight, 0, share, [rows])], after)
        if packed:
            packed[-1] = (after[:-1], after[-1])
        packed.append((mine, weight))
        after = [*mine, weight]
    acts, other = [], []
    for mine, weight in packed:
        came = []
        for (k, s), part in zip(shifts, mine):
            came.append(part if (k, s) == (0, 0) else lax.ppermute(part, ("core", "fsdp"), pair_ring(k, s)))
        acts.append(came)
        other.append(lax.ppermute(weight, "core", swap))
    cots[1, 0] = lax.ppermute(cotangent, "core", swap)
    for s in range(1, fsdp):
        cots[1, s] = lax.ppermute(cots[0, s], "core", swap)

    total = {}
    given = None
    for stage, ms in enumerate(stages):
        for n, m in enumerate(ms):
            place = jnp.stack([((z ^ m) * PAIR + i) * CORES + c for i in range(PAIR)] + [x]).astype(jnp.int32)
            at = n * PAIR * share
            ordered = [cots[k, s] for k, s in shifts]
            if given is not None:
                place, _ = lax.optimization_barrier((place, given))
            given, keep = inner_block(place, acts[stage], at, ordered, own_weight, other[stage], at, share)
            held = keep + lax.ppermute(given, "x", ring(PAIR, 1)).astype(f32)
            total[m] = held if m not in total else held + total[m]
            if m:
                low = m & -m
                came = lax.ppermute(total[m].astype(bf16), "z", [(i, i ^ low) for i in range(nz)]).astype(f32)
                total[m ^ low] = came if m ^ low not in total else total[m ^ low] + came
    summed = total[0]

    grad_rows = lax.dot_general(
        jnp.concatenate([cots[0, s] for s in range(fsdp)], axis=0),
        own_weight,
        (((1,), (1,)), ((), ())),
        preferred_element_type=f32,
    ).astype(bf16)
    parts = [grad_rows[:tok]]
    for s in range(1, fsdp):
        parts.append(lax.ppermute(grad_rows[s * tok : (s + 1) * tok], "fsdp", ring(fsdp, -s)))

    far = [(i, k, s) for k in range(CORES) for i in range(PAIR) for s in range(fsdp)]
    at = lambda i, k, s: ((i % PAIR) * CORES + k % CORES) * fsdp + s % fsdp
    every = [(i, k, s) for i in range(PAIR) for k in range(CORES) for s in range(fsdp)]
    groups = [[column(z ^ m, (x + i) % PAIR, k, s) for m in range(nz)] for i, k, s in far]
    (mine,), _ = pack([(next_activations, 1, share, groups)])
    mine = dict(zip(far, mine))
    nexts = {}

    def send_next(i, k, s):
        pairs = [(at(*e), at(e[0] + i, e[1] + k, e[2] + s)) for e in every]
        nexts[i, k, s] = lax.ppermute(mine[i, k, s], ("x", "core", "fsdp"), pairs) if i or k or s else mine[i, k, s]

    near, away = [e for e in far if e[0] == 0], [e for e in far if e[0]]
    for e in near:
        send_next(*e)
    held = [summed, *parts, *[nexts[e] for e in near], *[mine[e] for e in away]]
    summed, *held = lax.optimization_barrier(held)
    parts, held = held[: len(parts)], held[len(parts) :]
    nexts.update(zip(near, held))
    mine.update(zip(away, held[len(near) :]))

    pseudo_grad = outer_weight - summed / (nz * PAIR * CORES)
    new_momentum = nesterov * outer_momentum + pseudo_grad
    new_outer = outer_weight - outer_rate * (pseudo_grad + nesterov * new_momentum)

    rows = [new_outer.astype(bf16)]
    for m in range(1, nz):
        low = m & -m
        source = rows[m ^ low]
        if m == nz - 1:
            input_grad = join(parts, [((f + s) % fsdp) * width for s in range(fsdp)])
            for e in away:
                send_next(*e)
            source, input_grad, *came = lax.optimization_barrier((source, input_grad, *[nexts[e] for e in away]))
            nexts.update(zip(away, came))
        rows.append(lax.ppermute(source, "z", [(i, i ^ low) for i in range(nz)]))

    half = len(far) // CORES
    near, away = [nexts[e] for e in far[:half]], [nexts[e] for e in far[half:]]
    give, keep = keys_part(away, rows[:-1], 0), keys_part(near, rows[:-1], 0)
    last = (nz - 1) * share
    give = keys_part(away, rows[-1:], last, [give])
    keep = keys_part(near, rows[-1:], last, [keep])
    came = lax.ppermute(give, "core", swap)
    shape = lambda n, kind: jax.ShapeDtypeStruct((n, kv // 2), kind)
    to_x, stay_x, stay_f, *to_f = small_call(
        functools.partial(core_sum_kernel, fsdp, tok),
        [shape(fsdp * tok, bf16), shape(fsdp * tok, f32), shape(PAIR * tok, f32)] + [shape(PAIR * tok, bf16)] * (fsdp - 1),
        keep,
        came,
    )

    def home(to_x, to_f):
        from_x = lax.ppermute(to_x, "x", ring(PAIR, 1))
        return [from_x] + [lax.ppermute(part, "fsdp", ring(fsdp, -s - 1)) for s, part in enumerate(to_f)]

    left, right, to_x, *to_f = small_call(
        functools.partial(second_sum_kernel, fsdp, tok),
        [shape(tok, f32)] * 2 + [shape(tok, bf16)] * fsdp,
        stay_x,
        stay_f,
        *home(to_x, to_f),
    )
    (keys,) = small_call(
        last_sum_kernel, [jax.ShapeDtypeStruct((tok, kv), bf16)], left, right, *home(to_x, to_f)
    )
    return (input_grad, keys, new_outer, new_momentum)


def solution(mesh):
    fsdp = mesh.shape["fsdp"]
    nz = mesh.shape["island"] // (PAIR * CORES)
    split = Mesh(mesh.devices.reshape(nz, PAIR, CORES, fsdp), ("z", "x", "core", "fsdp"))
    island = ("z", "x", "core")
    tokens = P(island + ("fsdp",), None)
    width = P(("fsdp",) + island, None)
    in_specs = (tokens, tokens, P(island, "fsdp", None), width, width, tokens)
    out_specs = (tokens, tokens, width, width)
    return jax.shard_map(local, mesh=split, in_specs=in_specs, out_specs=out_specs, check_vma=False)
```

time: 737 us -> 280 us (0.38)
  waiting for transfers between devices: 639 us -> 77.8 us
  Pallas kernels: 0 us -> 155 us
  blocking collectives: 31.9 us -> 0 us
  matrix products: 33.2 us -> 5.85 us
  starting transfers between devices: 4.98 us -> 28.2 us
  between operations: 13.8 us -> 1.16 us
    all_gather x3 -> x0, waiting for transfers between devices: 459 us -> none  [the longest x1 199 us: local(): lax.all_gather(own_weight, 'fsdp', axis=0, tiled=True)]
    reduce_scatter x1 -> x0, waiting for transfers between devices: 179 us -> none  [local(): lax.psum_scatter(inner_new, 'island', scatter_dimension=0, tiled=True)]
    pallas_call x0 -> x15, Pallas kernels: none -> 155 us  [the longest x3 105 us: pack(): pl.pallas_call(functools.partial(pack_kernel, plan), out_shape=shapes, in...]
    ppermute x0 -> x34, waiting for transfers between devices: none -> 77.8 us  [the longest x4 22.5 us: local(): held = keep + lax.ppermute(given, 'x', ring(PAIR, 1)).astype(f32)]
    all_gather x1 -> x0, blocking collectives: 31.9 us -> none  [local(): island_cotangent = lax.all_gather(cotangent, 'fsdp', axis=0, tiled=True)]
    ppermute x0 -> x34, starting transfers between devices: none -> 28.2 us  [the longest x7 5.78 us: send_next(): lax.ppermute(mine[i, k, s], ('x', 'core', 'fsdp'), pairs)]
    dot_general x3 -> x1, matrix products: 33.2 us -> 5.85 us  [local(): lax.dot_general(jnp.concatenate([cots[0, s] for s in range(fsdp)], axis=0...]
  transfers between devices with their start and end apart: 5 -> 34, of which waited for: 4 -> 17; matrix products, arithmetic and copies ran while one was open for 2% -> 3% of each run, Pallas kernels for 0% -> 18%
where the time goes in v2:
time: 280 us
  Pallas kernels  155 us (55%)
  waiting for transfers between devices  77.8 us (28%)
  starting transfers between devices  28.2 us (10%)
  local copies, waits for them, and re-layouts  7.71 us (3%)
  matrix products  5.85 us (2%)
  other arithmetic  3.81 us (1%)
    pallas_call x3, Pallas kernels, pack(): pl.pallas_call(functools.partial(pack_kernel, plan), out_shape=shapes, in...  105 us
    pallas_call x1, Pallas kernels, join(): pl.pallas_call(join_kernel, out_shape=jax.ShapeDtypeStruct((rows, width *...  33.4 us
    ppermute x4, waiting for transfers between devices, local(): held = keep + lax.ppermute(given, 'x', ring(PAIR, 1)).astype(f32)  22.5 us
    ppermute x3, waiting for transfers between devices, local(): lax.ppermute(total[m].astype(bf16), 'z', [(i, i ^ low) for i in range(nz)])  13.4 us
    pallas_call x4, Pallas kernels, inner_block(): pl.pallas_call(functools.partial(inner_kernel, pieces, share, inner_rate...  12.4 us
    ppermute x2, waiting for transfers between devices, home(): from_x = lax.ppermute(to_x, 'x', ring(PAIR, 1))  10.6 us
    ppermute x6, waiting for transfers between devices, local(): lax.ppermute(part, ('core', 'fsdp'), pair_ring(k, s))  9.74 us
    ppermute x3, waiting for transfers between devices, local(): rows.append(lax.ppermute(source, 'z', [(i, i ^ low) for i in range(nz)]))  8.56 us
  transfers between devices with their start and end apart: 34, of which 17 were waited for; matrix products, arithmetic and copies ran while one was open for 3% of the time, Pallas kernels for 18%

profile of v2, /device:TPU:0, one launch (start us, length us, event | category | flops | bytes accessed | tf_op | source)
XLA Modules:
  0.0 279.6 jit_solution(17907776465430871953)
XLA Ops:
  0.9 5.7 %shard_map.93 = (bf16[128,512]{1,0:T(8,128)(2,1)S(1)}, bf16[128,512]{1,0:T(8,128)(2,1)S(1)}, bf16[128,512]{1,0:T(8,128)(2,1)}, bf16[128,512]{1,0:T(8,128)(2,1)S(1)}, bf16[512,1024]{1,0:T(8,128)(2,1)S(1)}) custom-call(s32[10]{0:T(128)S(1)} %stack.330.starts, bf16[128,8192]{1,0:T(8,128)(2,1)} %refs_0_.4, bf16[4096,1024]{1,0:T(8,128)(2,1)} %bitcast.86), custom_call_target="tpu_custom_call" | custom-call | bytes 3145728 | tf_op jit(solution)/shard_map/pallas_call | solution.py:72
  8.0 97.3 %shard_map.95 = (bf16[128,1536]{1,0:T(8,128)(2,1)S(1)}, bf16[128,1536]{1,0:T(8,128)(2,1)S(1)}, bf16[128,1536]{1,0:T(8,128)(2,1)S(1)}, bf16[128,1536]{1,0:T(8,128)(2,1)S(1)}, bf16[1536,1024]{1,0:T(8,128)(2,1)}) custom-call(s32[30]{0:T(128)S(1)} %stack.319.starts, bf16[128,8192]{1,0:T(8,128)(2,1)} %refs_0_.4, bf16[4096,1024]{1,0:T(8,128)(2,1)} %bitcast.87), custom_call_target="tpu_custom_call" | custom-call | bytes 9437184 | tf_op jit(solution)/shard_map/pallas_call | solution.py:72
  108.8 3.0 %collective-permute-start.4 = (bf16[128,1024]{1,0:T(8,128)(2,1)S(1)}, bf16[128,1024]{1,0:T(8,128)(2,1)}, u32[]{:S(2)}, u32[]{:S(2)}) collective-permute-start(bf16[128,1024]{1,0:T(8,128)(2,1)S(1)} %copy-done), channel_id=1, source_target_pairs={{0,1},{1,0},{2,3},{3,2},{4,5},{5,4},{6,7},{7,6},{8,9},{9,8},{10,11... | collective-permute-start | bytes 786440 | tf_op jit(solution)/shard_map/ppermute | solution.py:255
  111.9 2.4 collective-permute-done.refs_1_
  115.1 3.9 %collective-permute-done.4.refs_6_ = bf16[128,1024]{1,0:T(8,128)(2,1)} collective-permute-done((bf16[128,1024]{1,0:T(8,128)(2,1)S(1)}, bf16[128,1024]{1,0:T(8,128)(2,1)}, u32[]{:S(2)}, u32[]{:S(2)}) %collective-permute-start.4) | collective-permute-done | bytes 262176 | tf_op jit(solution)/shard_map/ppermute | solution.py:255
  119.0 2.2 collective-permute-done.1.refs_2_
  121.8 5.2 %collective-permute-done.2.refs_3_ = bf16[128,512]{1,0:T(8,128)(2,1)} collective-permute-done((bf16[128,512]{1,0:T(8,128)(2,1)}, bf16[128,512]{1,0:T(8,128)(2,1)}, u32[]{:S(2)}, u32[]{:S(2)}) %collective-permute-start.2) | collective-permute-done | bytes 131104 | tf_op jit(solution)/shard_map/ppermute | solution.py:269
  129.8 3.4 %shard_map.94 = (bf16[256,1024]{1,0:T(8,128)(2,1)S(1)}, f32[256,1024]{1,0:T(8,128)S(1)}) custom-call(s32[3]{0:T(128)S(1)} %get-tuple-element.132.place, bf16[128,512]{1,0:T(8,128)(2,1)S(1)} %get-tuple-element.69.refs_0_, bf16[128,512]{1,0:T(8,128)(2,1)S(1)} %copy-done.7, bf16[128,512]{1,0:T(8,128)(2,1)} %collective-permute-done.1.refs_2_, ...), custom_call_target="tpu_custom_call" | custom-call | flops 134217728 | bytes 262144 | tf_op jit(solution)/shard_map/pallas_call | solution.py:116
  133.2 2.0 collective-permute-start.13
  135.2 5.8 %convolution_convert_fusion = bf16[256,4096]{1,0:T(8,128)(2,1)S(1)} fusion(bf16[128,1024]{1,0:T(8,128)(2,1)} %collective-permute-done.4.refs_6_, bf16[128,1024]{1,0:T(8,128)(2,1)S(1)} %copy-done, bf16[1,4096,1024]{2,1,0:T(8,128)(2,1)} %param.8), kind=kOutput, calls=%fused_computation | convolution fusion | flops 2149580800 | bytes 11010048 | tf_op jit(solution)/shard_map/dot_general | solution.py:294
  141.0 6.7 %collective-permute-done.13 = bf16[256,1024]{1,0:T(8,128)(2,1)S(1)} collective-permute-done((bf16[256,1024]{1,0:T(8,128)(2,1)S(1)}, bf16[256,1024]{1,0:T(8,128)(2,1)S(1)}, u32[]{:S(2)}, u32[]{:S(2)}) %collective-permute-start.13) | collective-permute-done | bytes 524320 | tf_op jit(solution)/shard_map/ppermute | solution.py:286
  147.8 1.9 collective-permute-start.14
  149.8 2.8 %shard_map.96 = (bf16[256,1024]{1,0:T(8,128)(2,1)S(1)}, f32[256,1024]{1,0:T(8,128)S(1)}) custom-call(s32[3]{0:T(128)S(1)} %get-tuple-element.75.place, bf16[128,1536]{1,0:T(8,128)(2,1)S(1)} %copy-done.3, bf16[128,1536]{1,0:T(8,128)(2,1)S(1)} %collective-permute-done.7.refs_1_, bf16[128,1536]{1,0:T(8,128)(2,1)S(1)} %collective-permute-done.8.refs_2_, ...), custom_call_target="tpu_custom_call" | custom-call | flops 134217728 | bytes 262144 | tf_op jit(solution)/shard_map/pallas_call | solution.py:116
  154.2 2.7 shard_map.97
  159.8 3.4 %shard_map.98 = (bf16[256,1024]{1,0:T(8,128)(2,1)}, f32[256,1024]{1,0:T(8,128)S(1)}) custom-call(s32[3]{0:T(128)S(1)} %get-tuple-element.85.place, bf16[128,1536]{1,0:T(8,128)(2,1)S(1)} %copy-done.3, bf16[128,1536]{1,0:T(8,128)(2,1)S(1)} %collective-permute-done.7.refs_1_, bf16[128,1536]{1,0:T(8,128)(2,1)S(1)} %collective-permute-done.8.refs_2_, ...), custom_call_target="tpu_custom_call" | custom-call | flops 134217728 | bytes 262144 | tf_op jit(solution)/shard_map/pallas_call | solution.py:116
  164.8 2.7 collective-permute-done.12
  167.8 2.6 collective-permute-start.15
  170.4 8.3 %collective-permute-done.16 = bf16[256,1024]{1,0:T(8,128)(2,1)S(1)} collective-permute-done((bf16[256,1024]{1,0:T(8,128)(2,1)S(1)}, bf16[256,1024]{1,0:T(8,128)(2,1)S(1)}, u32[]{:S(2)}, u32[]{:S(2)}) %collective-permute-start.16) | collective-permute-done | bytes 524320 | tf_op jit(solution)/shard_map/ppermute | solution.py:286
  180.0 2.4 shard_map.99
  183.6 4.8 %collective-permute-done.11 = bf16[256,1024]{1,0:T(8,128)(2,1)S(1)} collective-permute-done((bf16[256,1024]{1,0:T(8,128)(2,1)}, bf16[256,1024]{1,0:T(8,128)(2,1)S(1)}, u32[]{:S(2)}, u32[]{:S(2)}) %collective-permute-start.11) | collective-permute-done | bytes 524320 | tf_op jit(solution)/shard_map/ppermute | solution.py:286
  188.4 2.5 collective-permute-done.15
  190.8 10.9 %collective-permute-done.17 = bf16[256,1024]{1,0:T(8,128)(2,1)S(1)} collective-permute-done((bf16[256,1024]{1,0:T(8,128)(2,1)}, bf16[256,1024]{1,0:T(8,128)(2,1)S(1)}, u32[]{:S(2)}, u32[]{:S(2)}) %collective-permute-start.17) | collective-permute-done | bytes 524320 | tf_op jit(solution)/shard_map/ppermute | solution.py:290
  202.2 1.9 fusion.5
  206.4 2.4 collective-permute-start.26
  208.8 4.5 %collective-permute-done.23.refs_2_ = bf16[128,1024]{1,0:T(8,128)(2,1)S(1)} collective-permute-done((bf16[128,1024]{1,0:T(8,128)(2,1)S(1)}, bf16[128,1024]{1,0:T(8,128)(2,1)S(1)}, u32[]{:S(2)}, u32[]{:S(2)}) %collective-permute-start.23) | collective-permute-done | bytes 262176 | tf_op jit(solution)/shard_map/ppermute | solution.py:314
  213.3 2.1 collective-permute-start.28
  215.4 33.4 %shard_map.100 = bf16[128,8192]{1,0:T(8,128)(2,1)} custom-call(s32[2]{0:T(128)S(1)} %pad_add_fusion.starts, bf16[128,4096]{1,0:T(8,128)(2,1)S(1)} %copy-done.1, bf16[128,4096]{1,0:T(8,128)(2,1)} %collective-permute-done.18.refs_1_), custom_call_target="tpu_custom_call" | custom-call | bytes 4194304 | tf_op jit(solution)/shard_map/pallas_call | solution.py:221
  250.0 8.6 %collective-permute-done.27.refs_4_ = bf16[256,1024]{1,0:T(8,128)(2,1)S(1)} collective-permute-done((bf16[256,1024]{1,0:T(8,128)(2,1)S(1)}, bf16[256,1024]{1,0:T(8,128)(2,1)S(1)}, u32[]{:S(2)}, u32[]{:S(2)}) %collective-permute-start.27) | collective-permute-done | bytes 524320 | tf_op jit(solution)/shard_map/ppermute | solution.py:339
  260.5 2.7 collective-permute-done.29.came
  263.4 1.9 collective-permute-start.30
  265.5 6.4 %collective-permute-done.30.refs_2_ = bf16[256,512]{1,0:T(8,128)(2,1)S(1)} collective-permute-done((bf16[256,512]{1,0:T(8,128)(2,1)S(1)}, bf16[256,512]{1,0:T(8,128)(2,1)S(1)}, u32[]{:S(2)}, u32[]{:S(2)}) %collective-permute-start.30) | collective-permute-done | bytes 262176 | tf_op jit(solution)/shard_map/ppermute | solution.py:357
  274.3 4.2 %collective-permute-done.32.from_x = bf16[128,512]{1,0:T(8,128)(2,1)S(1)} collective-permute-done((bf16[128,512]{1,0:T(8,128)(2,1)S(1)}, bf16[128,512]{1,0:T(8,128)(2,1)S(1)}, u32[]{:S(2)}, u32[]{:S(2)}) %collective-permute-start.32) | collective-permute-done | bytes 131104 | tf_op jit(solution)/shard_map/ppermute | solution.py:357
  (98 shorter events, 27.7 us)
Async XLA Ops:
  108.3 41.5 %collective-permute-start.10 = (bf16[1536,1024]{1,0:T(8,128)(2,1)}, bf16[1536,1024]{1,0:T(8,128)(2,1)S(1)}, u32[]{:S(2)}, u32[]{:S(2)}) collective-permute-start(bf16[1536,1024]{1,0:T(8,128)(2,1)} %get-tuple-element.81), channel_id=1, source_target_pairs={{0,2},{2,0},{1,3},{3,1},{4,6},{6,4},{5,7},{7,5},{8,10},{10,8},{9,1... | collective-permute-start | bytes 9437192 | tf_op jit(solution)/shard_map/ppermute | solution.py:271
  108.8 20.1 %collective-permute-start.6 = (bf16[512,1024]{1,0:T(8,128)(2,1)}, bf16[512,1024]{1,0:T(8,128)(2,1)}, u32[]{:S(2)}, u32[]{:S(2)}) collective-permute-start(bf16[512,1024]{1,0:T(8,128)(2,1)} %copy-done.8), channel_id=1, source_target_pairs={{0,2},{2,0},{1,3},{3,1},{4,6},{6,4},{5,7},{7,5},{8,10},{10,8},{9,1... | collective-permute-start | bytes 3145736 | tf_op jit(solution)/shard_map/ppermute | solution.py:271
  108.8 10.2 %collective-permute-start.4 = (bf16[128,1024]{1,0:T(8,128)(2,1)S(1)}, bf16[128,1024]{1,0:T(8,128)(2,1)}, u32[]{:S(2)}, u32[]{:S(2)}) collective-permute-start(bf16[128,1024]{1,0:T(8,128)(2,1)S(1)} %copy-done), channel_id=1, source_target_pairs={{0,1},{1,0},{2,3},{3,2},{4,5},{5,4},{6,7},{7,6},{8,9},{9,8},{10,11... | collective-permute-start | bytes 786440 | tf_op jit(solution)/shard_map/ppermute | solution.py:255
  111.8 9.4 %collective-permute-start.1 = (bf16[128,512]{1,0:T(8,128)(2,1)}, bf16[128,512]{1,0:T(8,128)(2,1)}, u32[]{:S(2)}, u32[]{:S(2)}) collective-permute-start(bf16[128,512]{1,0:T(8,128)(2,1)} %get-tuple-element.71), channel_id=1, source_target_pairs={{0,1},{1,0},{2,3},{3,2},{4,5},{5,4},{6,7},{7,6},{8,9},{9,8},{10,11... | collective-permute-start | bytes 393224 | tf_op jit(solution)/shard_map/ppermute | solution.py:269
  115.0 12.1 %collective-permute-start.3 = (bf16[128,1024]{1,0:T(8,128)(2,1)S(1)}, bf16[128,1024]{1,0:T(8,128)(2,1)}, u32[]{:S(2)}, u32[]{:S(2)}) collective-permute-start(bf16[128,1024]{1,0:T(8,128)(2,1)S(1)} %copy-done), channel_id=1, source_target_pairs={{0,2},{2,0},{1,3},{3,1},{4,6},{6,4},{5,7},{7,5},{8,10},{10,8},{9,1... | collective-permute-start | bytes 786440 | tf_op jit(solution)/shard_map/ppermute | solution.py:272
  119.0 9.4 %collective-permute-start.5 = (bf16[128,1024]{1,0:T(8,128)(2,1)}, bf16[128,1024]{1,0:T(8,128)(2,1)}, u32[]{:S(2)}, u32[]{:S(2)}) collective-permute-start(bf16[128,1024]{1,0:T(8,128)(2,1)} %collective-permute-done.4.refs_6_), channel_id=1, source_target_pairs={{0,2},{2,0},{1,3},{3,1},{4,6},{6,4},{5,7},{7,5},{8,10},{10,8},{9,1... | collective-permute-start | bytes 786440 | tf_op jit(solution)/shard_map/ppermute | solution.py:274
  121.2 5.8 %collective-permute-start.2 = (bf16[128,512]{1,0:T(8,128)(2,1)}, bf16[128,512]{1,0:T(8,128)(2,1)}, u32[]{:S(2)}, u32[]{:S(2)}) collective-permute-start(bf16[128,512]{1,0:T(8,128)(2,1)} %copy-done.12), channel_id=1, source_target_pairs={{0,3},{1,2},{2,1},{3,0},{4,7},{5,6},{6,5},{7,4},{8,11},{9,10},{10,... | collective-permute-start | bytes 393224 | tf_op jit(solution)/shard_map/ppermute | solution.py:269
  127.0 22.8 %collective-permute-start.7 = (bf16[128,1536]{1,0:T(8,128)(2,1)}, bf16[128,1536]{1,0:T(8,128)(2,1)S(1)}, u32[]{:S(2)}, u32[]{:S(2)}) collective-permute-start(bf16[128,1536]{1,0:T(8,128)(2,1)} %copy-done.11), channel_id=1, source_target_pairs={{0,2},{1,3},{2,0},{3,1},{4,6},{5,7},{6,4},{7,5},{8,10},{9,11},{10,... | collective-permute-start | bytes 1179656 | tf_op jit(solution)/shard_map/ppermute | solution.py:269
  127.1 22.6 %collective-permute-start.8 = (bf16[128,1536]{1,0:T(8,128)(2,1)}, bf16[128,1536]{1,0:T(8,128)(2,1)S(1)}, u32[]{:S(2)}, u32[]{:S(2)}) collective-permute-start(bf16[128,1536]{1,0:T(8,128)(2,1)} %copy-done.10), channel_id=1, source_target_pairs={{0,1},{1,0},{2,3},{3,2},{4,5},{5,4},{6,7},{7,6},{8,9},{9,8},{10,11... | collective-permute-start | bytes 1179656 | tf_op jit(solution)/shard_map/ppermute | solution.py:269
  128.4 21.4 %collective-permute-start.9 = (bf16[128,1536]{1,0:T(8,128)(2,1)}, bf16[128,1536]{1,0:T(8,128)(2,1)S(1)}, u32[]{:S(2)}, u32[]{:S(2)}) collective-permute-start(bf16[128,1536]{1,0:T(8,128)(2,1)} %copy-done.9), channel_id=1, source_target_pairs={{0,3},{1,2},{2,1},{3,0},{4,7},{5,6},{6,5},{7,4},{8,11},{9,10},{10,... | collective-permute-start | bytes 1179656 | tf_op jit(solution)/shard_map/ppermute | solution.py:269
  133.2 14.5 %collective-permute-start.13 = (bf16[256,1024]{1,0:T(8,128)(2,1)S(1)}, bf16[256,1024]{1,0:T(8,128)(2,1)S(1)}, u32[]{:S(2)}, u32[]{:S(2)}) collective-permute-start(bf16[256,1024]{1,0:T(8,128)(2,1)S(1)} %get-tuple-element.74), channel_id=1, source_target_pairs={{0,4},{4,0},{1,5},{5,1},{2,6},{6,2},{3,7},{7,3},{8,12},{12,8},{9,1... | collective-permute-start | bytes 1572872 | tf_op jit(solution)/shard_map/ppermute | solution.py:286
  147.8 17.0 %collective-permute-start.14 = (bf16[256,1024]{1,0:T(8,128)(2,1)S(1)}, bf16[256,1024]{1,0:T(8,128)(2,1)S(1)}, u32[]{:S(2)}, u32[]{:S(2)}) collective-permute-start(bf16[256,1024]{1,0:T(8,128)(2,1)S(1)} %add_convert_fusion.2), channel_id=1, source_target_pairs={{0,8},{8,0},{16,24},{24,16},{1,9},{9,1},{17,25},{25,17},{2,10},{10... | collective-permute-start | bytes 1572872 | tf_op jit(solution)/shard_map/ppermute | solution.py:290
  152.6 14.9 %collective-permute-start.12 = (bf16[256,1024]{1,0:T(8,128)(2,1)S(1)}, bf16[256,1024]{1,0:T(8,128)(2,1)S(1)}, u32[]{:S(2)}, u32[]{:S(2)}) collective-permute-start(bf16[256,1024]{1,0:T(8,128)(2,1)S(1)} %get-tuple-element.82), channel_id=1, source_target_pairs={{0,4},{4,0},{1,5},{5,1},{2,6},{6,2},{3,7},{7,3},{8,12},{12,8},{9,1... | collective-permute-start | bytes 1572872 | tf_op jit(solution)/shard_map/ppermute | solution.py:286
  156.9 21.9 %collective-permute-start.16 = (bf16[256,1024]{1,0:T(8,128)(2,1)S(1)}, bf16[256,1024]{1,0:T(8,128)(2,1)S(1)}, u32[]{:S(2)}, u32[]{:S(2)}) collective-permute-start(bf16[256,1024]{1,0:T(8,128)(2,1)S(1)} %get-tuple-element.84), channel_id=1, source_target_pairs={{0,4},{4,0},{1,5},{5,1},{2,6},{6,2},{3,7},{7,3},{8,12},{12,8},{9,1... | collective-permute-start | bytes 1572872 | tf_op jit(solution)/shard_map/ppermute | solution.py:286
  159.0 43.1 %collective-permute-start.18 = (bf16[128,4096]{1,0:T(8,128)(2,1)}, bf16[128,4096]{1,0:T(8,128)(2,1)}, u32[]{:S(2)}, u32[]{:S(2)}) collective-permute-start(bf16[128,4096]{1,0:T(8,128)(2,1)} %get-tuple-element.127), channel_id=1, source_target_pairs={{0,1},{1,0},{2,3},{3,2},{4,5},{5,4},{6,7},{7,6},{8,9},{9,8},{10,11... | collective-permute-start | bytes 3145736 | tf_op jit(solution)/shard_map/ppermute | solution.py:302
  163.3 25.1 %collective-permute-start.11 = (bf16[256,1024]{1,0:T(8,128)(2,1)}, bf16[256,1024]{1,0:T(8,128)(2,1)S(1)}, u32[]{:S(2)}, u32[]{:S(2)}) collective-permute-start(bf16[256,1024]{1,0:T(8,128)(2,1)} %get-tuple-element.87), channel_id=1, source_target_pairs={{0,4},{4,0},{1,5},{5,1},{2,6},{6,2},{3,7},{7,3},{8,12},{12,8},{9,1... | collective-permute-start | bytes 1572872 | tf_op jit(solution)/shard_map/ppermute | solution.py:286
  167.8 23.0 %collective-permute-start.15 = (bf16[256,1024]{1,0:T(8,128)(2,1)S(1)}, bf16[256,1024]{1,0:T(8,128)(2,1)S(1)}, u32[]{:S(2)}, u32[]{:S(2)}) collective-permute-start(bf16[256,1024]{1,0:T(8,128)(2,1)S(1)} %add_convert_fusion.1), channel_id=1, source_target_pairs={{0,16},{8,24},{16,0},{24,8},{1,17},{9,25},{17,1},{25,9},{2,18},{10... | collective-permute-start | bytes 1572872 | tf_op jit(solution)/shard_map/ppermute | solution.py:290
  179.7 22.1 %collective-permute-start.17 = (bf16[256,1024]{1,0:T(8,128)(2,1)}, bf16[256,1024]{1,0:T(8,128)(2,1)S(1)}, u32[]{:S(2)}, u32[]{:S(2)}) collective-permute-start(bf16[256,1024]{1,0:T(8,128)(2,1)} %add_convert_fusion), channel_id=1, source_target_pairs={{0,8},{8,0},{16,24},{24,16},{1,9},{9,1},{17,25},{25,17},{2,10},{10... | collective-permute-start | bytes 1572872 | tf_op jit(solution)/shard_map/ppermute | solution.py:290
  182.5 19.6 %collective-permute-start.19 = (bf16[128,1024]{1,0:T(8,128)(2,1)S(1)}, bf16[128,1024]{1,0:T(8,128)(2,1)S(1)}, u32[]{:S(2)}, u32[]{:S(2)}) collective-permute-start(bf16[128,1024]{1,0:T(8,128)(2,1)S(1)} %get-tuple-element.92), channel_id=1, source_target_pairs={{0,1},{1,0},{2,3},{3,2},{4,5},{5,4},{6,7},{7,6},{8,9},{9,8},{10,11... | collective-permute-start | bytes 786440 | tf_op jit(solution)/shard_map/ppermute | solution.py:314
  188.4 13.8 %collective-permute-start.20 = (bf16[128,1024]{1,0:T(8,128)(2,1)S(1)}, bf16[128,1024]{1,0:T(8,128)(2,1)S(1)}, u32[]{:S(2)}, u32[]{:S(2)}) collective-permute-start(bf16[128,1024]{1,0:T(8,128)(2,1)S(1)} %get-tuple-element.93), channel_id=1, source_target_pairs={{0,2},{1,3},{2,0},{3,1},{4,6},{5,7},{6,4},{7,5},{8,10},{9,11},{10,... | collective-permute-start | bytes 786440 | tf_op jit(solution)/shard_map/ppermute | solution.py:314
  190.8 11.3 %collective-permute-start.21 = (bf16[128,1024]{1,0:T(8,128)(2,1)S(1)}, bf16[128,1024]{1,0:T(8,128)(2,1)S(1)}, u32[]{:S(2)}, u32[]{:S(2)}) collective-permute-start(bf16[128,1024]{1,0:T(8,128)(2,1)S(1)} %get-tuple-element.94), channel_id=1, source_target_pairs={{0,3},{1,2},{2,1},{3,0},{4,7},{5,6},{6,5},{7,4},{8,11},{9,10},{10,... | collective-permute-start | bytes 786440 | tf_op jit(solution)/shard_map/ppermute | solution.py:314
  204.1 44.8 %collective-permute-start.22 = (bf16[256,1024]{1,0:T(8,128)(2,1)S(1)}, bf16[256,1024]{1,0:T(8,128)(2,1)S(1)}, u32[]{:S(2)}, u32[]{:S(2)}) collective-permute-start(bf16[256,1024]{1,0:T(8,128)(2,1)S(1)} %get-tuple-element.124.refs_4_), channel_id=1, source_target_pairs={{0,16},{8,24},{16,0},{24,8},{1,17},{9,25},{17,1},{25,9},{2,18},{10... | collective-permute-start | bytes 1572872 | tf_op jit(solution)/shard_map/ppermute | solution.py:339
  204.1 9.2 %collective-permute-start.23 = (bf16[128,1024]{1,0:T(8,128)(2,1)S(1)}, bf16[128,1024]{1,0:T(8,128)(2,1)S(1)}, u32[]{:S(2)}, u32[]{:S(2)}) collective-permute-start(bf16[128,1024]{1,0:T(8,128)(2,1)S(1)} %get-tuple-element.102), channel_id=1, source_target_pairs={{0,4},{1,5},{2,6},{3,7},{4,0},{5,1},{6,2},{7,3},{8,12},{9,13},{10,... | collective-permute-start | bytes 786440 | tf_op jit(solution)/shard_map/ppermute | solution.py:314
  205.6 43.3 %collective-permute-start.24 = (bf16[128,1024]{1,0:T(8,128)(2,1)S(1)}, bf16[128,1024]{1,0:T(8,128)(2,1)S(1)}, u32[]{:S(2)}, u32[]{:S(2)}) collective-permute-start(bf16[128,1024]{1,0:T(8,128)(2,1)S(1)} %get-tuple-element.103), channel_id=1, source_target_pairs={{0,5},{1,4},{2,7},{3,6},{4,1},{5,0},{6,3},{7,2},{8,13},{9,12},{10,... | collective-permute-start | bytes 786440 | tf_op jit(solution)/shard_map/ppermute | solution.py:314
  206.0 42.9 %collective-permute-start.25 = (bf16[128,1024]{1,0:T(8,128)(2,1)S(1)}, bf16[128,1024]{1,0:T(8,128)(2,1)S(1)}, u32[]{:S(2)}, u32[]{:S(2)}) collective-permute-start(bf16[128,1024]{1,0:T(8,128)(2,1)S(1)} %get-tuple-element.104), channel_id=1, source_target_pairs={{0,6},{1,7},{2,4},{3,5},{4,2},{5,3},{6,0},{7,1},{8,14},{9,15},{10,... | collective-permute-start | bytes 786440 | tf_op jit(solution)/shard_map/ppermute | solution.py:314
  206.4 42.5 %collective-permute-start.26 = (bf16[128,1024]{1,0:T(8,128)(2,1)S(1)}, bf16[128,1024]{1,0:T(8,128)(2,1)S(1)}, u32[]{:S(2)}, u32[]{:S(2)}) collective-permute-start(bf16[128,1024]{1,0:T(8,128)(2,1)S(1)} %get-tuple-element.105), channel_id=1, source_target_pairs={{0,7},{1,6},{2,5},{3,4},{4,3},{5,2},{6,1},{7,0},{8,15},{9,14},{10,... | collective-permute-start | bytes 786440 | tf_op jit(solution)/shard_map/ppermute | solution.py:314
  213.3 35.7 %collective-permute-start.28 = (bf16[256,1024]{1,0:T(8,128)(2,1)S(1)}, bf16[256,1024]{1,0:T(8,128)(2,1)S(1)}, u32[]{:S(2)}, u32[]{:S(2)}) collective-permute-start(bf16[256,1024]{1,0:T(8,128)(2,1)S(1)} %get-tuple-element.124.refs_4_), channel_id=1, source_target_pairs={{0,8},{8,0},{16,24},{24,16},{1,9},{9,1},{17,25},{25,17},{2,10},{10... | collective-permute-start | bytes 1572872 | tf_op jit(solution)/shard_map/ppermute | solution.py:339
  248.9 9.6 %collective-permute-start.27 = (bf16[256,1024]{1,0:T(8,128)(2,1)S(1)}, bf16[256,1024]{1,0:T(8,128)(2,1)S(1)}, u32[]{:S(2)}, u32[]{:S(2)}) collective-permute-start(bf16[256,1024]{1,0:T(8,128)(2,1)S(1)} %collective-permute-done.22.refs_6_), channel_id=1, source_target_pairs={{0,8},{8,0},{16,24},{24,16},{1,9},{9,1},{17,25},{25,17},{2,10},{10... | collective-permute-start | bytes 1572872 | tf_op jit(solution)/shard_map/ppermute | solution.py:339
  263.4 8.5 %collective-permute-start.30 = (bf16[256,512]{1,0:T(8,128)(2,1)S(1)}, bf16[256,512]{1,0:T(8,128)(2,1)S(1)}, u32[]{:S(2)}, u32[]{:S(2)}) collective-permute-start(bf16[256,512]{1,0:T(8,128)(2,1)S(1)} %get-tuple-element.118), channel_id=1, source_target_pairs={{0,4},{4,0},{1,5},{5,1},{2,6},{6,2},{3,7},{7,3},{8,12},{12,8},{9,1... | collective-permute-start | bytes 786440 | tf_op jit(solution)/shard_map/ppermute | solution.py:357
  265.3 8.1 %collective-permute-start.31 = (bf16[256,512]{1,0:T(8,128)(2,1)S(1)}, bf16[256,512]{1,0:T(8,128)(2,1)S(1)}, u32[]{:S(2)}, u32[]{:S(2)}) collective-permute-start(bf16[256,512]{1,0:T(8,128)(2,1)S(1)} %get-tuple-element.119), channel_id=1, source_target_pairs={{0,1},{1,0},{2,3},{3,2},{4,5},{5,4},{6,7},{7,6},{8,9},{9,8},{10,11... | collective-permute-start | bytes 786440 | tf_op jit(solution)/shard_map/ppermute | solution.py:358
  273.5 5.0 %collective-permute-start.32 = (bf16[128,512]{1,0:T(8,128)(2,1)S(1)}, bf16[128,512]{1,0:T(8,128)(2,1)S(1)}, u32[]{:S(2)}, u32[]{:S(2)}) collective-permute-start(bf16[128,512]{1,0:T(8,128)(2,1)S(1)} %get-tuple-element.122), channel_id=1, source_target_pairs={{0,4},{4,0},{1,5},{5,1},{2,6},{6,2},{3,7},{7,3},{8,12},{12,8},{9,1... | collective-permute-start | bytes 393224 | tf_op jit(solution)/shard_map/ppermute | solution.py:357
  273.9 5.0 %collective-permute-start.33 = (bf16[128,512]{1,0:T(8,128)(2,1)S(1)}, bf16[128,512]{1,0:T(8,128)(2,1)S(1)}, u32[]{:S(2)}, u32[]{:S(2)}) collective-permute-start(bf16[128,512]{1,0:T(8,128)(2,1)S(1)} %get-tuple-element.123), channel_id=1, source_target_pairs={{0,1},{1,0},{2,3},{3,2},{4,5},{5,4},{6,7},{7,6},{8,9},{9,8},{10,11... | collective-permute-start | bytes 393224 | tf_op jit(solution)/shard_map/ppermute | solution.py:358
  (19 other events, 414.4 us)

commit v3 on v2

--- a/solution.py
+++ b/solution.py
@@ -73,9 +73,9 @@
         functools.partial(pack_kernel, plan),
         out_shape=shapes,
         in_specs=[SMEM] + [HBM] * len(rest),
-        out_specs=[pl.BlockSpec(memory_space=pl.ANY)] * len(shapes),
+        out_specs=[VMEM] * len(shapes),
         scratch_shapes=[pltpu.SemaphoreType.DMA((starts.shape[0],))],
-        compiler_params=pltpu.CompilerParams(vmem_limit_bytes=4 * MIB),
+        compiler_params=pltpu.CompilerParams(vmem_limit_bytes=16 * MIB),
         cost_estimate=pl.CostEstimate(flops=0, bytes_accessed=moved, transcendentals=0),
     )(starts, *[in_hbm(item[1]) for item in rest])
     for n, *_, groups in rest:
@@ -209,7 +209,7 @@
     for n, part in enumerate(parts):
         width = part.shape[1]
         here = out.at[:, pl.ds(pl.multiple_of(starts[n], width), width)]
-        copies.append(pltpu.make_async_copy(part, here, done.at[n]))
+        copies.append(pltpu.make_async_copy(part.at[: out.shape[0], :], here, done.at[n]))
     for copy in copies:
         copy.start()
     for copy in copies:
@@ -217,14 +217,14 @@
 
 
 def join(parts, starts):
-    rows, width = parts[0].shape
+    rows, width = parts[-1].shape
     return pl.pallas_call(
         join_kernel,
         out_shape=jax.ShapeDtypeStruct((rows, width * len(parts)), parts[0].dtype),
-        in_specs=[SMEM] + [pl.BlockSpec(memory_space=pl.ANY)] * len(parts),
+        in_specs=[SMEM] + [VMEM] * len(parts),
         out_specs=HBM,
         scratch_shapes=[pltpu.SemaphoreType.DMA((len(parts),))],
-        compiler_params=pltpu.CompilerParams(vmem_limit_bytes=4 * MIB),
+        compiler_params=pltpu.CompilerParams(vmem_limit_bytes=16 * MIB),
         cost_estimate=pl.CostEstimate(flops=0, bytes_accessed=4 * rows * width * len(parts), transcendentals=0),
     )(jnp.stack(starts).astype(jnp.int32), *parts)
 
@@ -253,25 +253,35 @@
     cots = {(0, 0): cotangent}
     for s in range(1, fsdp):
         cots[0, s] = lax.ppermute(cotangent, "fsdp", ring(fsdp, s))
-    packed, after = [], []
-    for ms in stages:
-        columns = [[column(z ^ m, i, k, s) for m in ms for i in range(PAIR)] for k, s in shifts]
-        rows = [((z ^ m) * PAIR * CORES + i * CORES + 1 - c) * share for m in ms for i in range(PAIR)]
-        (mine, (weight,)), after = pack([(activations, 1, share, columns), (own_weight, 0, share, [rows])], after)
-        if packed:
-            packed[-1] = (after[:-1], after[-1])
-        packed.append((mine, weight))
-        after = [*mine, weight]
-    acts, other = [], []
-    for mine, weight in packed:
+    columns = [[column(z ^ m, i, k, s) for m in ms for i in range(PAIR)] for ms in stages for k, s in shifts]
+    rows = [[((z ^ m) * PAIR * CORES + i * CORES + 1 - c) * share for m in ms for i in range(PAIR)] for ms in stages]
+    (mine, weights), _ = pack([(activations, 1, share, columns), (own_weight, 0, share, rows)])
+    acts = []
+    for stage in range(len(stages)):
         came = []
-        for (k, s), part in zip(shifts, mine):
+        for (k, s), part in zip(shifts, mine[stage * len(shifts) :]):
             came.append(part if (k, s) == (0, 0) else lax.ppermute(part, ("core", "fsdp"), pair_ring(k, s)))
         acts.append(came)
-        other.append(lax.ppermute(weight, "core", swap))
+    other = [lax.ppermute(weight, "core", swap) for weight in weights]
     cots[1, 0] = lax.ppermute(cotangent, "core", swap)
     for s in range(1, fsdp):
         cots[1, s] = lax.ppermute(cots[0, s], "core", swap)
+
+    far = [(i, k, s) for k in range(CORES) for i in range(PAIR) for s in range(fsdp)]
+    index = lambda i, k, s: ((i % PAIR) * CORES + k % CORES) * fsdp + s % fsdp
+    every = [(i, k, s) for i in range(PAIR) for k in range(CORES) for s in range(fsdp)]
+    groups = [[column(z ^ m, (x + i) % PAIR, k, s) for m in range(nz)] for i, k, s in far]
+    (mine,), _ = pack([(next_activations, 1, share, groups)])
+    mine = dict(zip(far, mine))
+    nexts = {}
+
+    def send_next(i, k, s):
+        pairs = [(index(*e), index(e[0] + i, e[1] + k, e[2] + s)) for e in every]
+        nexts[i, k, s] = lax.ppermute(mine[i, k, s], ("x", "core", "fsdp"), pairs) if i or k or s else mine[i, k, s]
+
+    near, away = [e for e in far if e[0] == 0], [e for e in far if e[0]]
+    for e in near:
+        send_next(*e)
 
     total = {}
     given = None
@@ -280,6 +290,9 @@
             place = jnp.stack([((z ^ m) * PAIR + i) * CORES + c for i in range(PAIR)] + [x]).astype(jnp.int32)
             at = n * PAIR * share
             ordered = [cots[k, s] for k, s in shifts]
+            if m == 0:
+                place, *came = lax.optimization_barrier((place, *[nexts[e] for e in near]))
+                nexts.update(zip(near, came))
             if given is not None:
                 place, _ = lax.optimization_barrier((place, given))
             given, keep = inner_block(place, acts[stage], at, ordered, own_weight, other[stage], at, share)
@@ -291,36 +304,16 @@
                 total[m ^ low] = came if m ^ low not in total else total[m ^ low] + came
     summed = total[0]
 
+    given, *island_cots = lax.optimization_barrier((given, *[cots[0, s] for s in range(fsdp)]))
     grad_rows = lax.dot_general(
-        jnp.concatenate([cots[0, s] for s in range(fsdp)], axis=0),
-        own_weight,
-        (((1,), (1,)), ((), ())),
-        preferred_element_type=f32,
+        jnp.concatenate(island_cots, axis=0), own_weight, (((1,), (1,)), ((), ())), preferred_element_type=f32
     ).astype(bf16)
-    parts = [grad_rows[:tok]]
+    parts = [grad_rows]
     for s in range(1, fsdp):
         parts.append(lax.ppermute(grad_rows[s * tok : (s + 1) * tok], "fsdp", ring(fsdp, -s)))
 
-    far = [(i, k, s) for k in range(CORES) for i in range(PAIR) for s in range(fsdp)]
-    at = lambda i, k, s: ((i % PAIR) * CORES + k % CORES) * fsdp + s % fsdp
-    every = [(i, k, s) for i in range(PAIR) for k in range(CORES) for s in range(fsdp)]
-    groups = [[column(z ^ m, (x + i) % PAIR, k, s) for m in range(nz)] for i, k, s in far]
-    (mine,), _ = pack([(next_activations, 1, share, groups)])
-    mine = dict(zip(far, mine))
-    nexts = {}
-
-    def send_next(i, k, s):
-        pairs = [(at(*e), at(e[0] + i, e[1] + k, e[2] + s)) for e in every]
-        nexts[i, k, s] = lax.ppermute(mine[i, k, s], ("x", "core", "fsdp"), pairs) if i or k or s else mine[i, k, s]
-
-    near, away = [e for e in far if e[0] == 0], [e for e in far if e[0]]
-    for e in near:
-        send_next(*e)
-    held = [summed, *parts, *[nexts[e] for e in near], *[mine[e] for e in away]]
-    summed, *held = lax.optimization_barrier(held)
-    parts, held = held[: len(parts)], held[len(parts) :]
-    nexts.update(zip(near, held))
-    mine.update(zip(away, held[len(near) :]))
+    summed, *held = lax.optimization_barrier((summed, *[mine[e] for e in away]))
+    mine.update(zip(away, held))
 
     pseudo_grad = outer_weight - summed / (nz * PAIR * CORES)
     new_momentum = nesterov * outer_momentum + pseudo_grad
@@ -331,16 +324,20 @@
         low = m & -m
         source = rows[m ^ low]
         if m == nz - 1:
-            input_grad = join(parts, [((f + s) % fsdp) * width for s in range(fsdp)])
             for e in away:
                 send_next(*e)
-            source, input_grad, *came = lax.optimization_barrier((source, input_grad, *[nexts[e] for e in away]))
-            nexts.update(zip(away, came))
+            held = [source, *rows[1:], *[nexts[e] for e in away]]
+            source, *held = lax.optimization_barrier(held)
+            rows[1:], held = held[: m - 1], held[m - 1 :]
+            nexts.update(zip(away, held))
+            source, *parts = lax.optimization_barrier((source, *parts))
+            input_grad = join(parts, [((f + s) % fsdp) * width for s in range(fsdp)])
         rows.append(lax.ppermute(source, "z", [(i, i ^ low) for i in range(nz)]))
 
     half = len(far) // CORES
     near, away = [nexts[e] for e in far[:half]], [nexts[e] for e in far[half:]]
     give, keep = keys_part(away, rows[:-1], 0), keys_part(near, rows[:-1], 0)
+    give, keep, input_grad = lax.optimization_barrier((give, keep, input_grad))
     last = (nz - 1) * share
     give = keys_part(away, rows[-1:], last, [give])
     keep = keys_part(near, rows[-1:], last, [keep])

time: 280 us -> 184 us (0.66)
  Pallas kernels: 155 us -> 32.3 us
  local copies, waits for them, and re-layouts: 7.71 us -> 20 us
  waiting for transfers between devices: 77.8 us -> 86.3 us
  starting transfers between devices: 28.2 us -> 31 us
    pallas_call x3 -> x2, Pallas kernels: 105 us -> 9.16 us  [pack(): pl.pallas_call(functools.partial(pack_kernel, plan), out_shape=shapes, in...]
    pallas_call x1, Pallas kernels: 33.4 us -> 1.87 us  [join(): pl.pallas_call(join_kernel, out_shape=jax.ShapeDtypeStruct((rows, width *...]
    ppermute x7, waiting for transfers between devices: 4.54 us -> 18.4 us  [send_next(): lax.ppermute(mine[i, k, s], ('x', 'core', 'fsdp'), pairs)]
    unnamed x34 -> x80, local copies, waits for them, and re-layouts: 5.86 us -> 19.6 us
    ppermute x4, waiting for transfers between devices: 22.5 us -> 10.3 us  [local(): held = keep + lax.ppermute(given, 'x', ring(PAIR, 1)).astype(f32)]
    ppermute x6, waiting for transfers between devices: 9.74 us -> 14.3 us  [local(): lax.ppermute(part, ('core', 'fsdp'), pair_ring(k, s))]
    pallas_call x4, Pallas kernels: 2.84 us -> 6.84 us  [keys_part(): pl.pallas_call(functools.partial(keys_kernel, len(acts), at), out_shape=j...]
  transfers between devices with their start and end apart: 34 -> 34, of which waited for: 17 -> 21; matrix products, arithmetic and copies ran while one was open for 3% -> 7% of each run, Pallas kernels for 18% -> 13%
where the time goes in v3:
time: 184 us; the launch traced here: 183 us
  waiting for transfers between devices  86.3 us (47%)
  Pallas kernels  32.3 us (18%)
  starting transfers between devices  31 us (17%)
  local copies, waits for them, and re-layouts  20 us (11%)
  other arithmetic  6.14 us (3%)
  matrix products  5.85 us (3%)
    unnamed x80, local copies, waits for them, and re-layouts  19.6 us
    ppermute x7, waiting for transfers between devices, send_next(): lax.ppermute(mine[i, k, s], ('x', 'core', 'fsdp'), pairs)  18.4 us
    ppermute x3, waiting for transfers between devices, local(): lax.ppermute(total[m].astype(bf16), 'z', [(i, i ^ low) for i in range(nz)])  15.4 us
    ppermute x6, waiting for transfers between devices, local(): lax.ppermute(part, ('core', 'fsdp'), pair_ring(k, s))  14.3 us
    pallas_call x4, Pallas kernels, inner_block(): pl.pallas_call(functools.partial(inner_kernel, pieces, share, inner_rate...  13.4 us
    ppermute x4, waiting for transfers between devices, local(): held = keep + lax.ppermute(given, 'x', ring(PAIR, 1)).astype(f32)  10.3 us
    ppermute x3, waiting for transfers between devices, local(): rows.append(lax.ppermute(source, 'z', [(i, i ^ low) for i in range(nz)]))  10.3 us
    ppermute x2, waiting for transfers between devices, home(): from_x = lax.ppermute(to_x, 'x', ring(PAIR, 1))  9.17 us
  transfers between devices with their start and end apart: 34, of which 21 were waited for; matrix products, arithmetic and copies ran while one was open for 7% of the time, Pallas kernels for 13%

profile of v3, /device:TPU:0, one launch (start us, length us, event | category | flops | bytes accessed | tf_op | source)
XLA Modules:
  0.0 182.7 jit_solution(4748202918428970927)
XLA Ops:
  0.9 5.9 %shard_map.94 = (bf16[128,512]{1,0:T(8,128)(2,1)S(1)}, bf16[128,512]{1,0:T(8,128)(2,1)S(1)}, bf16[128,512]{1,0:T(8,128)(2,1)S(1)}, bf16[128,512]{1,0:T(8,128)(2,...) custom-call(s32[40]{0:T(128)S(1)} %stack.359.starts, ...), custom_call_target="tpu_custom_call" | custom-call | bytes 12582912 | tf_op jit(solution)/shard_map/pallas_call | solution.py:72
  10.3 3.0 %collective-permute-start.7 = (bf16[128,1024]{1,0:T(8,128)(2,1)S(1)}, bf16[128,1024]{1,0:T(8,128)(2,1)}, u32[]{:S(2)}, u32[]{:S(2)}) collective-permute-start(bf16[128,1024]{1,0:T(8,128)(2,1)S(1)} %copy-done), channel_id=1, source_target_pairs={{0,1},{1,0},{2,3},{3,2},{4,5},{5,4},{6,7},{7,6},{8,9},{9,8},{10,11... | collective-permute-start | bytes 786440 | tf_op jit(solution)/shard_map/ppermute | solution.py:255
  13.4 2.5 %collective-permute-done.3.refs_1_ = bf16[128,512]{1,0:T(8,128)(2,1)S(1)} collective-permute-done((bf16[128,512]{1,0:T(8,128)(2,1)S(1)}, bf16[128,512]{1,0:T(8,128)(2,1)S(1)}, u32[]{:S(2)}, u32[]{:S(2)}) %collective-permute-start.3) | collective-permute-done | bytes 131104 | tf_op jit(solution)/shard_map/ppermute | solution.py:263
  16.6 3.9 %collective-permute-done.7.refs_6_ = bf16[128,1024]{1,0:T(8,128)(2,1)} collective-permute-done((bf16[128,1024]{1,0:T(8,128)(2,1)S(1)}, bf16[128,1024]{1,0:T(8,128)(2,1)}, u32[]{:S(2)}, u32[]{:S(2)}) %collective-permute-start.7) | collective-permute-done | bytes 262176 | tf_op jit(solution)/shard_map/ppermute | solution.py:255
  20.5 2.1 %collective-permute-done.4.refs_2_ = bf16[128,512]{1,0:T(8,128)(2,1)S(1)} collective-permute-done((bf16[128,512]{1,0:T(8,128)(2,1)S(1)}, bf16[128,512]{1,0:T(8,128)(2,1)S(1)}, u32[]{:S(2)}, u32[]{:S(2)}) %collective-permute-start.4) | collective-permute-done | bytes 131104 | tf_op jit(solution)/shard_map/ppermute | solution.py:263
  23.8 5.2 %collective-permute-done.5.refs_3_ = bf16[128,512]{1,0:T(8,128)(2,1)} collective-permute-done((bf16[128,512]{1,0:T(8,128)(2,1)}, bf16[128,512]{1,0:T(8,128)(2,1)}, u32[]{:S(2)}, u32[]{:S(2)}) %collective-permute-start.5) | collective-permute-done | bytes 131104 | tf_op jit(solution)/shard_map/ppermute | solution.py:263
  30.9 3.4 %shard_map.95 = (bf16[256,1024]{1,0:T(8,128)(2,1)S(1)}, f32[256,1024]{1,0:T(8,128)S(1)}) custom-call(s32[3]{0:T(128)S(1)} %get-tuple-element.132.place, bf16[128,512]{1,0:T(8,128)(2,1)S(1)} %get-tuple-element.73.refs_0_, bf16[128,512]{1,0:T(8,128)(2,1)S(1)} %copy-done.21, bf16[128,512]{1,0:T(8,128)(2,1)S(1)} %copy-done.23, ...), custom_call_target="tpu_custom_call" | custom-call | flops 134217728 | bytes 262144 | tf_op jit(solution)/shard_map/pallas_call | solution.py:116
  34.3 2.0 %collective-permute-start.16 = (bf16[256,1024]{1,0:T(8,128)(2,1)S(1)}, bf16[256,1024]{1,0:T(8,128)(2,1)S(1)}, u32[]{:S(2)}, u32[]{:S(2)}) collective-permute-start(bf16[256,1024]{1,0:T(8,128)(2,1)S(1)} %get-tuple-element.78), channel_id=1, source_target_pairs={{0,4},{4,0},{1,5},{5,1},{2,6},{6,2},{3,7},{7,3},{8,12},{12,8},{9,1... | collective-permute-start | bytes 1572872 | tf_op jit(solution)/shard_map/ppermute | solution.py:299
  38.2 10.3 %collective-permute-done.16 = bf16[256,1024]{1,0:T(8,128)(2,1)S(1)} collective-permute-done((bf16[256,1024]{1,0:T(8,128)(2,1)S(1)}, bf16[256,1024]{1,0:T(8,128)(2,1)S(1)}, u32[]{:S(2)}, u32[]{:S(2)}) %collective-permute-start.16) | collective-permute-done | bytes 524320 | tf_op jit(solution)/shard_map/ppermute | solution.py:299
  51.3 4.5 %collective-permute-done.12.refs_3_ = bf16[128,1536]{1,0:T(8,128)(2,1)S(1)} collective-permute-done((bf16[128,1536]{1,0:T(8,128)(2,1)S(1)}, bf16[128,1536]{1,0:T(8,128)(2,1)S(1)}, u32[]{:S(2)}, u32[]{:S(2)}) %collective-permute-start.12) | collective-permute-done | bytes 393248 | tf_op jit(solution)/shard_map/ppermute | solution.py:263
  55.8 3.7 %shard_map.96 = (bf16[256,1024]{1,0:T(8,128)(2,1)}, f32[256,1024]{1,0:T(8,128)S(1)}) custom-call(s32[3]{0:T(128)S(1)} %get-tuple-element.79.place, bf16[128,1536]{1,0:T(8,128)(2,1)S(1)} %copy-done.2, bf16[128,1536]{1,0:T(8,128)(2,1)S(1)} %collective-permute-done.10.refs_1_, bf16[128,1536]{1,0:T(8,128)(2,1)S(1)} %collective-permute-done.11.refs_2_, ...), custom_call_target="tpu_custom_call" | custom-call | flops 134217728 | bytes 262144 | tf_op jit(solution)/shard_map/pallas_call | solution.py:116
  60.7 3.3 %shard_map.93 = (bf16[128,1024]{1,0:T(8,128)(2,1)S(1)}, bf16[128,1024]{1,0:T(8,128)(2,1)}, bf16[128,1024]{1,0:T(8,128)(2,1)S(1)}, bf16[128,1024]{1,0:T(8,128)(2,...) custom-call(s32[32]{0:T(128)S(1)} %stack.309.starts, ...), custom_call_target="tpu_custom_call" | custom-call | bytes 4194304 | tf_op jit(solution)/shard_map/pallas_call | solution.py:72
  73.8 3.4 %shard_map.97 = (bf16[256,1024]{1,0:T(8,128)(2,1)}, f32[256,1024]{1,0:T(8,128)S(1)}) custom-call(s32[3]{0:T(128)S(1)} %add_add_fusion.2.place, bf16[128,1536]{1,0:T(8,128)(2,1)S(1)} %copy-done.3, bf16[128,1536]{1,0:T(8,128)(2,1)S(1)} %copy-done.6, bf16[128,1536]{1,0:T(8,128)(2,1)S(1)} %copy-done.9, bf16[128,1536]{1,0:T(8,128)(2,1)S(1)} %copy-done.12, ...), custom_call_target="tpu_custom_call" | custom-call | flops 134217728 | bytes 262144 | tf_op jit(solution)/shard_map/pallas_call | solution.py:116
  78.2 2.0 %collective-permute-start.19 = (bf16[256,1024]{1,0:T(8,128)(2,1)}, bf16[256,1024]{1,0:T(8,128)(2,1)}, u32[]{:S(2)}, u32[]{:S(2)}) collective-permute-start(bf16[256,1024]{1,0:T(8,128)(2,1)} %get-tuple-element.87), channel_id=1, source_target_pairs={{0,4},{4,0},{1,5},{5,1},{2,6},{6,2},{3,7},{7,3},{8,12},{12,8},{9,1... | collective-permute-start | bytes 1572872 | tf_op jit(solution)/shard_map/ppermute | solution.py:299
  86.1 2.8 %shard_map.98 = (bf16[256,1024]{1,0:T(8,128)(2,1)S(1)}, f32[256,1024]{1,0:T(8,128)S(1)}) custom-call(s32[3]{0:T(128)S(1)} %add_add_fusion.1.place, bf16[128,1536]{1,0:T(8,128)(2,1)S(1)} %copy-done.4, bf16[128,1536]{1,0:T(8,128)(2,1)S(1)} %copy-done.7, bf16[128,1536]{1,0:T(8,128)(2,1)S(1)} %copy-done.10, bf16[128,1536]{1,0:T(8,128)(2,1)S(1)} %copy-done.13, ...), custom_call_target="tpu_custom_call" | custom-call | flops 134217728 | bytes 262144 | tf_op jit(solution)/shard_map/pallas_call | solution.py:116
  92.0 2.7 %collective-permute-start.18 = (bf16[256,1024]{1,0:T(8,128)(2,1)S(1)}, bf16[256,1024]{1,0:T(8,128)(2,1)S(1)}, u32[]{:S(2)}, u32[]{:S(2)}) collective-permute-start(bf16[256,1024]{1,0:T(8,128)(2,1)S(1)} %add_convert_fusion.1), channel_id=1, source_target_pairs={{0,16},{8,24},{16,0},{24,8},{1,17},{9,25},{17,1},{25,9},{2,18},{10... | collective-permute-start | bytes 1572872 | tf_op jit(solution)/shard_map/ppermute | solution.py:303
  97.5 5.8 %convolution_convert_fusion.refs_0_ = bf16[256,4096]{1,0:T(8,128)(2,1)S(1)} fusion(bf16[128,1024]{1,0:T(8,128)(2,1)} %collective-permute-done.7.refs_6_, bf16[128,1024]{1,0:T(8,128)(2,1)S(1)} %copy-done, bf16[1,4096,1024]{2,1,0:T(8,128)(2,1)} %param.8), kind=kOutput, calls=%fused_computation | convolution fusion | flops 2149580800 | bytes 11010048 | tf_op jit(solution)/shard_map/dot_general | solution.py:308
  104.5 14.0 %collective-permute-done.18 = bf16[256,1024]{1,0:T(8,128)(2,1)S(1)} collective-permute-done((bf16[256,1024]{1,0:T(8,128)(2,1)S(1)}, bf16[256,1024]{1,0:T(8,128)(2,1)S(1)}, u32[]{:S(2)}, u32[]{:S(2)}) %collective-permute-start.18) | collective-permute-done | bytes 524320 | tf_op jit(solution)/shard_map/ppermute | solution.py:303
  120.8 1.9 %collective-permute-start.24 = (bf16[128,1024]{1,0:T(8,128)(2,1)S(1)}, bf16[128,1024]{1,0:T(8,128)(2,1)S(1)}, u32[]{:S(2)}, u32[]{:S(2)}) collective-permute-start(bf16[128,1024]{1,0:T(8,128)(2,1)S(1)} %copy-done.35), channel_id=1, source_target_pairs={{0,5},{1,4},{2,7},{3,6},{4,1},{5,0},{6,3},{7,2},{8,13},{9,12},{10,... | collective-permute-start | bytes 786440 | tf_op jit(solution)/shard_map/ppermute | solution.py:280
  122.7 1.9 %fusion.5 = (bf16[256,1024]{1,0:T(8,128)(2,1)S(1)}, f32[256,1024]{1,0:T(8,128)}, f32[256,1024]{1,0:T(8,128)}) fusion(f32[256,1024]{1,0:T(8,128)S(1)} %copy-done.38, f32[256,1024]{1,0:T(8,128)S(1)} %add_add_fusion, f32[256,1024]{1,0:T(8,128)S(1)} %copy-done.39), kind=kLoop, calls=%fused_computation.18 | loop fusion | flops 2359296 | bytes 5767168 | tf_op jit(solution)/shard_map/convert_element_type | solution.py:322
  124.8 2.8 %collective-permute-start.21 = (bf16[256,1024]{1,0:T(8,128)(2,1)S(1)}, bf16[256,1024]{1,0:T(8,128)(2,1)S(1)}, u32[]{:S(2)}, u32[]{:S(2)}) collective-permute-start(bf16[256,1024]{1,0:T(8,128)(2,1)S(1)} %get-tuple-element.128.refs_4_), channel_id=1, source_target_pairs={{0,16},{8,24},{16,0},{24,8},{1,17},{9,25},{17,1},{25,9},{2,18},{10... | collective-permute-start | bytes 1572872 | tf_op jit(solution)/shard_map/ppermute | solution.py:335
  127.6 2.0 %collective-permute-done.23.refs_2_ = bf16[128,1024]{1,0:T(8,128)(2,1)S(1)} collective-permute-done((bf16[128,1024]{1,0:T(8,128)(2,1)S(1)}, bf16[128,1024]{1,0:T(8,128)(2,1)S(1)}, u32[]{:S(2)}, u32[]{:S(2)}) %collective-permute-start.23) | collective-permute-done | bytes 262176 | tf_op jit(solution)/shard_map/ppermute | solution.py:280
  129.6 4.9 %collective-permute-done.24.refs_3_ = bf16[128,1024]{1,0:T(8,128)(2,1)S(1)} collective-permute-done((bf16[128,1024]{1,0:T(8,128)(2,1)S(1)}, bf16[128,1024]{1,0:T(8,128)(2,1)S(1)}, u32[]{:S(2)}, u32[]{:S(2)}) %collective-permute-start.24) | collective-permute-done | bytes 262176 | tf_op jit(solution)/shard_map/ppermute | solution.py:280
  134.5 3.7 %collective-permute-done.25.refs_2_ = bf16[128,1024]{1,0:T(8,128)(2,1)S(1)} collective-permute-done((bf16[128,1024]{1,0:T(8,128)(2,1)S(1)}, bf16[128,1024]{1,0:T(8,128)(2,1)S(1)}, u32[]{:S(2)}, u32[]{:S(2)}) %collective-permute-start.25) | collective-permute-done | bytes 262176 | tf_op jit(solution)/shard_map/ppermute | solution.py:280
  138.3 6.0 %collective-permute-done.26.refs_3_ = bf16[128,1024]{1,0:T(8,128)(2,1)S(1)} collective-permute-done((bf16[128,1024]{1,0:T(8,128)(2,1)S(1)}, bf16[128,1024]{1,0:T(8,128)(2,1)S(1)}, u32[]{:S(2)}, u32[]{:S(2)}) %collective-permute-start.26) | collective-permute-done | bytes 262176 | tf_op jit(solution)/shard_map/ppermute | solution.py:280
  144.2 3.9 %collective-permute-done.22.refs_5_ = bf16[256,1024]{1,0:T(8,128)(2,1)S(1)} collective-permute-done((bf16[256,1024]{1,0:T(8,128)(2,1)S(1)}, bf16[256,1024]{1,0:T(8,128)(2,1)S(1)}, u32[]{:S(2)}, u32[]{:S(2)}) %collective-permute-start.22) | collective-permute-done | bytes 524320 | tf_op jit(solution)/shard_map/ppermute | solution.py:335
  152.1 2.1 %shard_map.99.refs_5_ = f32[512,1024]{1,0:T(8,128)S(1)} custom-call(bf16[128,1024]{1,0:T(8,128)(2,1)} %collective-permute-done.1.refs_0_, bf16[128,1024]{1,0:T(8,128)(2,1)} %collective-permute-done.2.refs_1_, bf16[128,1024]{1,0:T(8,128)(2,1)S(1)} %collective-permute-done.25.refs_2_, bf16[128,1024]{1,0:T(8,128)(2,1)S(1)} %collective-permute-done.26.refs_3_, ...), custom_call_target="tpu_custom_call" | custom-call | flops 805306368 | bytes 524288 | tf_op jit(solution)/shard_map/pallas_call | solution.py:147
  154.1 1.9 %shard_map.100.refs_5_ = f32[512,1024]{1,0:T(8,128)S(1)} custom-call(bf16[128,1024]{1,0:T(8,128)(2,1)S(1)} %copy-done.15, bf16[128,1024]{1,0:T(8,128)(2,1)} %collective-permute-done.refs_1_, bf16[128,1024]{1,0:T(8,128)(2,1)S(1)} %collective-permute-done.23.refs_2_, bf16[128,1024]{1,0:T(8,128)(2,1)S(1)} %collective-permute-done.24.refs_3_, ...), custom_call_target="tpu_custom_call" | custom-call | flops 805306368 | bytes 524288 | tf_op jit(solution)/shard_map/pallas_call | solution.py:147
  156.1 4.7 %collective-permute-done.28.refs_4_ = bf16[256,1024]{1,0:T(8,128)(2,1)S(1)} collective-permute-done((bf16[256,1024]{1,0:T(8,128)(2,1)S(1)}, bf16[256,1024]{1,0:T(8,128)(2,1)S(1)}, u32[]{:S(2)}, u32[]{:S(2)}) %collective-permute-start.28) | collective-permute-done | bytes 524320 | tf_op jit(solution)/shard_map/ppermute | solution.py:335
  163.7 2.7 %collective-permute-done.29.came = f32[512,1024]{1,0:T(8,128)S(1)} collective-permute-done((f32[512,1024]{1,0:T(8,128)S(1)}, f32[512,1024]{1,0:T(8,128)S(1)}, u32[]{:S(2)}, u32[]{:S(2)}) %collective-permute-start.29) | collective-permute-done | bytes 2097184 | tf_op jit(solution)/shard_map/ppermute | solution.py:344
  168.3 6.8 %collective-permute-done.30.refs_2_ = bf16[256,512]{1,0:T(8,128)(2,1)S(1)} collective-permute-done((bf16[256,512]{1,0:T(8,128)(2,1)S(1)}, bf16[256,512]{1,0:T(8,128)(2,1)S(1)}, u32[]{:S(2)}, u32[]{:S(2)}) %collective-permute-start.30) | collective-permute-done | bytes 262176 | tf_op jit(solution)/shard_map/ppermute | solution.py:354
  178.1 2.4 %collective-permute-done.32.from_x = bf16[128,512]{1,0:T(8,128)(2,1)S(1)} collective-permute-done((bf16[128,512]{1,0:T(8,128)(2,1)S(1)}, bf16[128,512]{1,0:T(8,128)(2,1)S(1)}, u32[]{:S(2)}, u32[]{:S(2)}) %collective-permute-start.32) | collective-permute-done | bytes 131104 | tf_op jit(solution)/shard_map/ppermute | solution.py:354
  (143 shorter events, 53.4 us)
Async XLA Ops:
  9.8 46.0 %collective-permute-start.13 = (bf16[1536,1024]{1,0:T(8,128)(2,1)}, bf16[1536,1024]{1,0:T(8,128)(2,1)S(1)}, u32[]{:S(2)}, u32[]{:S(2)}) collective-permute-start(bf16[1536,1024]{1,0:T(8,128)(2,1)} %get-tuple-element.84), channel_id=1, source_target_pairs={{0,2},{2,0},{1,3},{3,1},{4,6},{6,4},{5,7},{7,5},{8,10},{10,8},{9,1... | collective-permute-start | bytes 9437192 | tf_op jit(solution)/shard_map/ppermute | solution.py:265
  10.3 18.8 %collective-permute-start.9 = (bf16[512,1024]{1,0:T(8,128)(2,1)}, bf16[512,1024]{1,0:T(8,128)(2,1)}, u32[]{:S(2)}, u32[]{:S(2)}) collective-permute-start(bf16[512,1024]{1,0:T(8,128)(2,1)} %get-tuple-element.77), channel_id=1, source_target_pairs={{0,2},{2,0},{1,3},{3,1},{4,6},{6,4},{5,7},{7,5},{8,10},{10,8},{9,1... | collective-permute-start | bytes 3145736 | tf_op jit(solution)/shard_map/ppermute | solution.py:265
  10.3 10.2 %collective-permute-start.7 = (bf16[128,1024]{1,0:T(8,128)(2,1)S(1)}, bf16[128,1024]{1,0:T(8,128)(2,1)}, u32[]{:S(2)}, u32[]{:S(2)}) collective-permute-start(bf16[128,1024]{1,0:T(8,128)(2,1)S(1)} %copy-done), channel_id=1, source_target_pairs={{0,1},{1,0},{2,3},{3,2},{4,5},{5,4},{6,7},{7,6},{8,9},{9,8},{10,11... | collective-permute-start | bytes 786440 | tf_op jit(solution)/shard_map/ppermute | solution.py:255
  13.3 9.3 %collective-permute-start.4 = (bf16[128,512]{1,0:T(8,128)(2,1)S(1)}, bf16[128,512]{1,0:T(8,128)(2,1)S(1)}, u32[]{:S(2)}, u32[]{:S(2)}) collective-permute-start(bf16[128,512]{1,0:T(8,128)(2,1)S(1)} %get-tuple-element.75), channel_id=1, source_target_pairs={{0,1},{1,0},{2,3},{3,2},{4,5},{5,4},{6,7},{7,6},{8,9},{9,8},{10,11... | collective-permute-start | bytes 393224 | tf_op jit(solution)/shard_map/ppermute | solution.py:263
  16.5 12.5 %collective-permute-start.6 = (bf16[128,1024]{1,0:T(8,128)(2,1)S(1)}, bf16[128,1024]{1,0:T(8,128)(2,1)}, u32[]{:S(2)}, u32[]{:S(2)}) collective-permute-start(bf16[128,1024]{1,0:T(8,128)(2,1)S(1)} %copy-done), channel_id=1, source_target_pairs={{0,2},{2,0},{1,3},{3,1},{4,6},{6,4},{5,7},{7,5},{8,10},{10,8},{9,1... | collective-permute-start | bytes 786440 | tf_op jit(solution)/shard_map/ppermute | solution.py:266
  20.5 8.5 %collective-permute-start.8 = (bf16[128,1024]{1,0:T(8,128)(2,1)}, bf16[128,1024]{1,0:T(8,128)(2,1)}, u32[]{:S(2)}, u32[]{:S(2)}) collective-permute-start(bf16[128,1024]{1,0:T(8,128)(2,1)} %collective-permute-done.7.refs_6_), channel_id=1, source_target_pairs={{0,2},{2,0},{1,3},{3,1},{4,6},{6,4},{5,7},{7,5},{8,10},{10,8},{9,1... | collective-permute-start | bytes 786440 | tf_op jit(solution)/shard_map/ppermute | solution.py:268
  23.2 5.8 %collective-permute-start.5 = (bf16[128,512]{1,0:T(8,128)(2,1)}, bf16[128,512]{1,0:T(8,128)(2,1)}, u32[]{:S(2)}, u32[]{:S(2)}) collective-permute-start(bf16[128,512]{1,0:T(8,128)(2,1)} %get-tuple-element.76), channel_id=1, source_target_pairs={{0,3},{1,2},{2,1},{3,0},{4,7},{5,6},{6,5},{7,4},{8,11},{9,10},{10,... | collective-permute-start | bytes 393224 | tf_op jit(solution)/shard_map/ppermute | solution.py:263
  34.3 14.2 %collective-permute-start.16 = (bf16[256,1024]{1,0:T(8,128)(2,1)S(1)}, bf16[256,1024]{1,0:T(8,128)(2,1)S(1)}, u32[]{:S(2)}, u32[]{:S(2)}) collective-permute-start(bf16[256,1024]{1,0:T(8,128)(2,1)S(1)} %get-tuple-element.78), channel_id=1, source_target_pairs={{0,4},{4,0},{1,5},{5,1},{2,6},{6,2},{3,7},{7,3},{8,12},{12,8},{9,1... | collective-permute-start | bytes 1572872 | tf_op jit(solution)/shard_map/ppermute | solution.py:299
  36.3 15.0 %collective-permute-start.10 = (bf16[128,1536]{1,0:T(8,128)(2,1)S(1)}, bf16[128,1536]{1,0:T(8,128)(2,1)S(1)}, u32[]{:S(2)}, u32[]{:S(2)}) collective-permute-start(bf16[128,1536]{1,0:T(8,128)(2,1)S(1)} %copy-done.29), channel_id=1, source_target_pairs={{0,2},{1,3},{2,0},{3,1},{4,6},{5,7},{6,4},{7,5},{8,10},{9,11},{10,... | collective-permute-start | bytes 1179656 | tf_op jit(solution)/shard_map/ppermute | solution.py:263
  36.3 15.0 %collective-permute-start.11 = (bf16[128,1536]{1,0:T(8,128)(2,1)S(1)}, bf16[128,1536]{1,0:T(8,128)(2,1)S(1)}, u32[]{:S(2)}, u32[]{:S(2)}) collective-permute-start(bf16[128,1536]{1,0:T(8,128)(2,1)S(1)} %copy-done.27), channel_id=1, source_target_pairs={{0,1},{1,0},{2,3},{3,2},{4,5},{5,4},{6,7},{7,6},{8,9},{9,8},{10,11... | collective-permute-start | bytes 1179656 | tf_op jit(solution)/shard_map/ppermute | solution.py:263
  37.3 18.5 %collective-permute-start.12 = (bf16[128,1536]{1,0:T(8,128)(2,1)S(1)}, bf16[128,1536]{1,0:T(8,128)(2,1)S(1)}, u32[]{:S(2)}, u32[]{:S(2)}) collective-permute-start(bf16[128,1536]{1,0:T(8,128)(2,1)S(1)} %copy-done.25), channel_id=1, source_target_pairs={{0,3},{1,2},{2,1},{3,0},{4,7},{5,6},{6,5},{7,4},{8,11},{9,10},{10,... | collective-permute-start | bytes 1179656 | tf_op jit(solution)/shard_map/ppermute | solution.py:263
  49.5 41.1 %collective-permute-start.17 = (bf16[256,1024]{1,0:T(8,128)(2,1)}, bf16[256,1024]{1,0:T(8,128)(2,1)}, u32[]{:S(2)}, u32[]{:S(2)}) collective-permute-start(bf16[256,1024]{1,0:T(8,128)(2,1)} %add_convert_fusion.2), channel_id=1, source_target_pairs={{0,8},{8,0},{16,24},{24,16},{1,9},{9,1},{17,25},{25,17},{2,10},{10... | collective-permute-start | bytes 1572872 | tf_op jit(solution)/shard_map/ppermute | solution.py:303
  60.5 30.0 %collective-permute-start.15 = (bf16[256,1024]{1,0:T(8,128)(2,1)}, bf16[256,1024]{1,0:T(8,128)(2,1)}, u32[]{:S(2)}, u32[]{:S(2)}) collective-permute-start(bf16[256,1024]{1,0:T(8,128)(2,1)} %get-tuple-element.85), channel_id=1, source_target_pairs={{0,4},{4,0},{1,5},{5,1},{2,6},{6,2},{3,7},{7,3},{8,12},{12,8},{9,1... | collective-permute-start | bytes 1572872 | tf_op jit(solution)/shard_map/ppermute | solution.py:299
  67.5 10.6 %collective-permute-start = (bf16[128,1024]{1,0:T(8,128)(2,1)}, bf16[128,1024]{1,0:T(8,128)(2,1)}, u32[]{:S(2)}, u32[]{:S(2)}) collective-permute-start(bf16[128,1024]{1,0:T(8,128)(2,1)} %get-tuple-element.67), channel_id=1, source_target_pairs={{0,1},{1,0},{2,3},{3,2},{4,5},{5,4},{6,7},{7,6},{8,9},{9,8},{10,11... | collective-permute-start | bytes 786440 | tf_op jit(solution)/shard_map/ppermute | solution.py:280
  69.0 11.3 %collective-permute-start.1 = (bf16[128,1024]{1,0:T(8,128)(2,1)}, bf16[128,1024]{1,0:T(8,128)(2,1)}, u32[]{:S(2)}, u32[]{:S(2)}) collective-permute-start(bf16[128,1024]{1,0:T(8,128)(2,1)} %get-tuple-element.68), channel_id=1, source_target_pairs={{0,2},{1,3},{2,0},{3,1},{4,6},{5,7},{6,4},{7,5},{8,10},{9,11},{10,... | collective-permute-start | bytes 786440 | tf_op jit(solution)/shard_map/ppermute | solution.py:280
  69.1 12.9 %collective-permute-start.2 = (bf16[128,1024]{1,0:T(8,128)(2,1)}, bf16[128,1024]{1,0:T(8,128)(2,1)}, u32[]{:S(2)}, u32[]{:S(2)}) collective-permute-start(bf16[128,1024]{1,0:T(8,128)(2,1)} %get-tuple-element.69), channel_id=1, source_target_pairs={{0,3},{1,2},{2,1},{3,0},{4,7},{5,6},{6,5},{7,4},{8,11},{9,10},{10,... | collective-permute-start | bytes 786440 | tf_op jit(solution)/shard_map/ppermute | solution.py:280
  78.2 16.5 %collective-permute-start.19 = (bf16[256,1024]{1,0:T(8,128)(2,1)}, bf16[256,1024]{1,0:T(8,128)(2,1)}, u32[]{:S(2)}, u32[]{:S(2)}) collective-permute-start(bf16[256,1024]{1,0:T(8,128)(2,1)} %get-tuple-element.87), channel_id=1, source_target_pairs={{0,4},{4,0},{1,5},{5,1},{2,6},{6,2},{3,7},{7,3},{8,12},{12,8},{9,1... | collective-permute-start | bytes 1572872 | tf_op jit(solution)/shard_map/ppermute | solution.py:299
  88.9 15.6 %collective-permute-start.14 = (bf16[256,1024]{1,0:T(8,128)(2,1)S(1)}, bf16[256,1024]{1,0:T(8,128)(2,1)S(1)}, u32[]{:S(2)}, u32[]{:S(2)}) collective-permute-start(bf16[256,1024]{1,0:T(8,128)(2,1)S(1)} %get-tuple-element.90), channel_id=1, source_target_pairs={{0,4},{4,0},{1,5},{5,1},{2,6},{6,2},{3,7},{7,3},{8,12},{12,8},{9,1... | collective-permute-start | bytes 1572872 | tf_op jit(solution)/shard_map/ppermute | solution.py:299
  92.0 26.4 %collective-permute-start.18 = (bf16[256,1024]{1,0:T(8,128)(2,1)S(1)}, bf16[256,1024]{1,0:T(8,128)(2,1)S(1)}, u32[]{:S(2)}, u32[]{:S(2)}) collective-permute-start(bf16[256,1024]{1,0:T(8,128)(2,1)S(1)} %add_convert_fusion.1), channel_id=1, source_target_pairs={{0,16},{8,24},{16,0},{24,8},{1,17},{9,25},{17,1},{25,9},{2,18},{10... | collective-permute-start | bytes 1572872 | tf_op jit(solution)/shard_map/ppermute | solution.py:303
  95.9 24.0 %collective-permute-start.20 = (bf16[256,1024]{1,0:T(8,128)(2,1)S(1)}, bf16[256,1024]{1,0:T(8,128)(2,1)S(1)}, u32[]{:S(2)}, u32[]{:S(2)}) collective-permute-start(bf16[256,1024]{1,0:T(8,128)(2,1)S(1)} %add_convert_fusion), channel_id=1, source_target_pairs={{0,8},{8,0},{16,24},{24,16},{1,9},{9,1},{17,25},{25,17},{2,10},{10... | collective-permute-start | bytes 1572872 | tf_op jit(solution)/shard_map/ppermute | solution.py:303
  103.5 46.3 %collective-permute-start.27 = (bf16[128,4096]{1,0:T(8,128)(2,1)S(1)}, bf16[128,4096]{1,0:T(8,128)(2,1)S(1)}, u32[]{:S(2)}, u32[]{:S(2)}) collective-permute-start(bf16[128,4096]{1,0:T(8,128)(2,1)S(1)} %slice.4), channel_id=1, source_target_pairs={{0,1},{1,0},{2,3},{3,2},{4,5},{5,4},{6,7},{7,6},{8,9},{9,8},{10,11... | collective-permute-start | bytes 3145736 | tf_op jit(solution)/shard_map/ppermute | solution.py:313
  120.3 9.3 %collective-permute-start.23 = (bf16[128,1024]{1,0:T(8,128)(2,1)S(1)}, bf16[128,1024]{1,0:T(8,128)(2,1)S(1)}, u32[]{:S(2)}, u32[]{:S(2)}) collective-permute-start(bf16[128,1024]{1,0:T(8,128)(2,1)S(1)} %copy-done.37), channel_id=1, source_target_pairs={{0,4},{1,5},{2,6},{3,7},{4,0},{5,1},{6,2},{7,3},{8,12},{9,13},{10,... | collective-permute-start | bytes 786440 | tf_op jit(solution)/shard_map/ppermute | solution.py:280
  120.8 13.7 %collective-permute-start.24 = (bf16[128,1024]{1,0:T(8,128)(2,1)S(1)}, bf16[128,1024]{1,0:T(8,128)(2,1)S(1)}, u32[]{:S(2)}, u32[]{:S(2)}) collective-permute-start(bf16[128,1024]{1,0:T(8,128)(2,1)S(1)} %copy-done.35), channel_id=1, source_target_pairs={{0,5},{1,4},{2,7},{3,6},{4,1},{5,0},{6,3},{7,2},{8,13},{9,12},{10,... | collective-permute-start | bytes 786440 | tf_op jit(solution)/shard_map/ppermute | solution.py:280
  124.6 23.5 %collective-permute-start.22 = (bf16[256,1024]{1,0:T(8,128)(2,1)S(1)}, bf16[256,1024]{1,0:T(8,128)(2,1)S(1)}, u32[]{:S(2)}, u32[]{:S(2)}) collective-permute-start(bf16[256,1024]{1,0:T(8,128)(2,1)S(1)} %get-tuple-element.128.refs_4_), channel_id=1, source_target_pairs={{0,8},{8,0},{16,24},{24,16},{1,9},{9,1},{17,25},{25,17},{2,10},{10... | collective-permute-start | bytes 1572872 | tf_op jit(solution)/shard_map/ppermute | solution.py:335
  124.8 25.1 %collective-permute-start.21 = (bf16[256,1024]{1,0:T(8,128)(2,1)S(1)}, bf16[256,1024]{1,0:T(8,128)(2,1)S(1)}, u32[]{:S(2)}, u32[]{:S(2)}) collective-permute-start(bf16[256,1024]{1,0:T(8,128)(2,1)S(1)} %get-tuple-element.128.refs_4_), channel_id=1, source_target_pairs={{0,16},{8,24},{16,0},{24,8},{1,17},{9,25},{17,1},{25,9},{2,18},{10... | collective-permute-start | bytes 1572872 | tf_op jit(solution)/shard_map/ppermute | solution.py:335
  129.6 8.7 %collective-permute-start.25 = (bf16[128,1024]{1,0:T(8,128)(2,1)S(1)}, bf16[128,1024]{1,0:T(8,128)(2,1)S(1)}, u32[]{:S(2)}, u32[]{:S(2)}) collective-permute-start(bf16[128,1024]{1,0:T(8,128)(2,1)S(1)} %copy-done.33), channel_id=1, source_target_pairs={{0,6},{1,7},{2,4},{3,5},{4,2},{5,3},{6,0},{7,1},{8,14},{9,15},{10,... | collective-permute-start | bytes 786440 | tf_op jit(solution)/shard_map/ppermute | solution.py:280
  134.5 9.7 %collective-permute-start.26 = (bf16[128,1024]{1,0:T(8,128)(2,1)S(1)}, bf16[128,1024]{1,0:T(8,128)(2,1)S(1)}, u32[]{:S(2)}, u32[]{:S(2)}) collective-permute-start(bf16[128,1024]{1,0:T(8,128)(2,1)S(1)} %copy-done.31), channel_id=1, source_target_pairs={{0,7},{1,6},{2,5},{3,4},{4,3},{5,2},{6,1},{7,0},{8,15},{9,14},{10,... | collective-permute-start | bytes 786440 | tf_op jit(solution)/shard_map/ppermute | solution.py:280
  149.9 10.9 %collective-permute-start.28 = (bf16[256,1024]{1,0:T(8,128)(2,1)S(1)}, bf16[256,1024]{1,0:T(8,128)(2,1)S(1)}, u32[]{:S(2)}, u32[]{:S(2)}) collective-permute-start(bf16[256,1024]{1,0:T(8,128)(2,1)S(1)} %collective-permute-done.21.refs_6_), channel_id=1, source_target_pairs={{0,8},{8,0},{16,24},{24,16},{1,9},{9,1},{17,25},{25,17},{2,10},{10... | collective-permute-start | bytes 1572872 | tf_op jit(solution)/shard_map/ppermute | solution.py:335
  166.7 8.4 %collective-permute-start.30 = (bf16[256,512]{1,0:T(8,128)(2,1)S(1)}, bf16[256,512]{1,0:T(8,128)(2,1)S(1)}, u32[]{:S(2)}, u32[]{:S(2)}) collective-permute-start(bf16[256,512]{1,0:T(8,128)(2,1)S(1)} %get-tuple-element.122), channel_id=1, source_target_pairs={{0,4},{4,0},{1,5},{5,1},{2,6},{6,2},{3,7},{7,3},{8,12},{12,8},{9,1... | collective-permute-start | bytes 786440 | tf_op jit(solution)/shard_map/ppermute | solution.py:354
  167.3 8.1 %collective-permute-start.31 = (bf16[256,512]{1,0:T(8,128)(2,1)S(1)}, bf16[256,512]{1,0:T(8,128)(2,1)S(1)}, u32[]{:S(2)}, u32[]{:S(2)}) collective-permute-start(bf16[256,512]{1,0:T(8,128)(2,1)S(1)} %get-tuple-element.123), channel_id=1, source_target_pairs={{0,1},{1,0},{2,3},{3,2},{4,5},{5,4},{6,7},{7,6},{8,9},{9,8},{10,11... | collective-permute-start | bytes 786440 | tf_op jit(solution)/shard_map/ppermute | solution.py:355
  175.4 5.0 %collective-permute-start.32 = (bf16[128,512]{1,0:T(8,128)(2,1)S(1)}, bf16[128,512]{1,0:T(8,128)(2,1)S(1)}, u32[]{:S(2)}, u32[]{:S(2)}) collective-permute-start(bf16[128,512]{1,0:T(8,128)(2,1)S(1)} %get-tuple-element.126), channel_id=1, source_target_pairs={{0,4},{4,0},{1,5},{5,1},{2,6},{6,2},{3,7},{7,3},{8,12},{12,8},{9,1... | collective-permute-start | bytes 393224 | tf_op jit(solution)/shard_map/ppermute | solution.py:354
  177.0 5.0 %collective-permute-start.33 = (bf16[128,512]{1,0:T(8,128)(2,1)S(1)}, bf16[128,512]{1,0:T(8,128)(2,1)S(1)}, u32[]{:S(2)}, u32[]{:S(2)}) collective-permute-start(bf16[128,512]{1,0:T(8,128)(2,1)S(1)} %get-tuple-element.127), channel_id=1, source_target_pairs={{0,1},{1,0},{2,3},{3,2},{4,5},{5,4},{6,7},{7,6},{8,9},{9,8},{10,11... | collective-permute-start | bytes 393224 | tf_op jit(solution)/shard_map/ppermute | solution.py:355
  (42 other events, 203.4 us)

commit v4 on v3

--- a/solution.py
+++ b/solution.py
@@ -16,7 +16,7 @@
 
 bf16, f32 = jnp.bfloat16, jnp.float32
 VMEM, HBM = pl.BlockSpec(memory_space=pltpu.VMEM), pl.BlockSpec(memory_space=pltpu.HBM)
-SMEM = pl.BlockSpec(memory_space=pltpu.SMEM)
+SMEM, ANY = pl.BlockSpec(memory_space=pltpu.SMEM), pl.BlockSpec(memory_space=pl.ANY)
 MIB = 1024 * 1024
 
 
@@ -73,7 +73,7 @@
         functools.partial(pack_kernel, plan),
         out_shape=shapes,
         in_specs=[SMEM] + [HBM] * len(rest),
-        out_specs=[VMEM] * len(shapes),
+        out_specs=[pl.BlockSpec()] * len(shapes),
         scratch_shapes=[pltpu.SemaphoreType.DMA((starts.shape[0],))],
         compiler_params=pltpu.CompilerParams(vmem_limit_bytes=16 * MIB),
         cost_estimate=pl.CostEstimate(flops=0, bytes_accessed=moved, transcendentals=0),
@@ -83,20 +83,29 @@
     return [result[n] for n in range(len(items))], list(after)
 
 
-def inner_kernel(pieces, share, scale, act_at, other_at, place, *refs):
+def inner_kernel(pieces, share, scale, act_at, place, *refs):
     acts, cots = refs[:pieces], refs[pieces : 2 * pieces]
-    own, other, give, keep, rows, total, done = refs[2 * pieces :]
+    own, other, give, keep, left, right, rows, total, done = refs[2 * pieces :]
+    tok = cots[0].shape[0]
     copies = []
+
+    def fetch(source, target):
+        copies.append(pltpu.make_async_copy(source, target, done.at[len(copies)]))
+
+    for n, (act, cot) in enumerate(zip(acts, cots)):
+        here = pl.ds(n * tok, tok)
+        fetch(act.at[:, pl.ds(act_at, PAIR * share)], left.at[here, :])
+        fetch(cot, right.at[here, :])
     for i in range(PAIR):
-        for n, (weight, at) in enumerate(((own, place[i] * share), (other, other_at + i * share))):
-            source = weight.at[pl.ds(pl.multiple_of(at, share), share), :]
-            copies.append(pltpu.make_async_copy(source, rows.at[n, i], done.at[n, i]))
+        strip = pl.ds(pl.multiple_of(place[i] * share, share), share)
+        fetch(own.at[strip, :], rows.at[0, i])
+        fetch(other.at[strip, :], rows.at[1, i])
     for copy in copies:
         copy.start()
-    left = jnp.concatenate([a[:, act_at : act_at + PAIR * share] for a in acts], axis=0)
-    right = jnp.concatenate([g[...] for g in cots], axis=0)
-    total[...] = lax.dot_general(left, right, (((0,), (0,)), ((), ())), preferred_element_type=f32)
-    for copy in copies:
+    for copy in copies[: 2 * pieces]:
+        copy.wait()
+    total[...] = lax.dot_general(left[...], right[...], (((0,), (0,)), ((), ())), preferred_element_type=f32)
+    for copy in copies[2 * pieces :]:
         copy.wait()
     x = place[PAIR]
 
@@ -108,22 +117,24 @@
     keep[...] = inner_new(x)
 
 
-def inner_block(place, acts, act_at, cots, own, other, other_at, share):
+def inner_block(place, acts, act_at, cots, own, other, share):
     pieces = len(acts)
     tok, kv = cots[0].shape
     if act_at % LANES or PAIR * share % LANES:
         acts, act_at = [a[:, act_at : act_at + PAIR * share] for a in acts], 0
     return pl.pallas_call(
-        functools.partial(inner_kernel, pieces, share, inner_rate / (tok * pieces // CORES), act_at, other_at),
+        functools.partial(inner_kernel, pieces, share, inner_rate / (tok * pieces // CORES), act_at),
         out_shape=[jax.ShapeDtypeStruct((share, kv), bf16), jax.ShapeDtypeStruct((share, kv), f32)],
-        in_specs=[SMEM] + [VMEM] * (2 * pieces) + [HBM] * 2,
-        out_specs=[VMEM] * 2,
+        in_specs=[SMEM] + [ANY] * (2 * pieces) + [HBM, ANY],
+        out_specs=[pl.BlockSpec()] * 2,
         scratch_shapes=[
+            pltpu.VMEM((pieces * tok, PAIR * share), bf16),
+            pltpu.VMEM((pieces * tok, kv), bf16),
             pltpu.VMEM((CORES, PAIR, share, kv), bf16),
             pltpu.VMEM((PAIR * share, kv), f32),
-            pltpu.SemaphoreType.DMA((CORES, PAIR)),
+            pltpu.SemaphoreType.DMA((2 * pieces + CORES * PAIR,)),
         ],
-        compiler_params=pltpu.CompilerParams(vmem_limit_bytes=24 * MIB),
+        compiler_params=pltpu.CompilerParams(vmem_limit_bytes=32 * MIB),
         cost_estimate=pl.CostEstimate(flops=pieces * tok * share * kv, bytes_accessed=share * kv, transcendentals=0),
     )(place, *acts, *cots, in_hbm(own), other)
 
@@ -147,8 +158,8 @@
     return pl.pallas_call(
         functools.partial(keys_kernel, len(acts), at),
         out_shape=jax.ShapeDtypeStruct((rows, kv), f32),
-        in_specs=[VMEM] * (len(acts) + len(blocks) + len(before)),
-        out_specs=VMEM,
+        in_specs=[pl.BlockSpec()] * (len(acts) + len(blocks) + len(before)),
+        out_specs=pl.BlockSpec(),
         compiler_params=pltpu.CompilerParams(vmem_limit_bytes=24 * MIB),
         cost_estimate=pl.CostEstimate(flops=2 * rows * depth * kv, bytes_accessed=rows * kv, transcendentals=0),
     )(*acts, *blocks, *before)
@@ -248,21 +259,21 @@
         return [(at(i, j), at(i + k, j + s)) for i in range(CORES) for j in range(fsdp)]
 
     shifts = [(k, s) for s in range(fsdp) for k in range(CORES)]
-    stages = [[nz - 1], list(range(nz - 2, -1, -1))]
+    order = list(range(nz - 1, -1, -1))
+    stages = [order[: nz // 2], order[nz // 2 :]]
 
     cots = {(0, 0): cotangent}
     for s in range(1, fsdp):
         cots[0, s] = lax.ppermute(cotangent, "fsdp", ring(fsdp, s))
     columns = [[column(z ^ m, i, k, s) for m in ms for i in range(PAIR)] for ms in stages for k, s in shifts]
-    rows = [[((z ^ m) * PAIR * CORES + i * CORES + 1 - c) * share for m in ms for i in range(PAIR)] for ms in stages]
-    (mine, weights), _ = pack([(activations, 1, share, columns), (own_weight, 0, share, rows)])
+    (mine,), _ = pack([(activations, 1, share, columns)])
     acts = []
     for stage in range(len(stages)):
         came = []
         for (k, s), part in zip(shifts, mine[stage * len(shifts) :]):
             came.append(part if (k, s) == (0, 0) else lax.ppermute(part, ("core", "fsdp"), pair_ring(k, s)))
         acts.append(came)
-    other = [lax.ppermute(weight, "core", swap) for weight in weights]
+    other_weight = lax.ppermute(own_weight, "core", swap)
     cots[1, 0] = lax.ppermute(cotangent, "core", swap)
     for s in range(1, fsdp):
         cots[1, s] = lax.ppermute(cots[0, s], "core", swap)
@@ -271,46 +282,58 @@
     index = lambda i, k, s: ((i % PAIR) * CORES + k % CORES) * fsdp + s % fsdp
     every = [(i, k, s) for i in range(PAIR) for k in range(CORES) for s in range(fsdp)]
     groups = [[column(z ^ m, (x + i) % PAIR, k, s) for m in range(nz)] for i, k, s in far]
-    (mine,), _ = pack([(next_activations, 1, share, groups)])
-    mine = dict(zip(far, mine))
-    nexts = {}
+    mine, nexts = {}, {}
 
     def send_next(i, k, s):
         pairs = [(index(*e), index(e[0] + i, e[1] + k, e[2] + s)) for e in every]
         nexts[i, k, s] = lax.ppermute(mine[i, k, s], ("x", "core", "fsdp"), pairs) if i or k or s else mine[i, k, s]
 
     near, away = [e for e in far if e[0] == 0], [e for e in far if e[0]]
-    for e in near:
-        send_next(*e)
-
-    total = {}
-    given = None
+
+    gives, keeps = {}, {}
     for stage, ms in enumerate(stages):
         for n, m in enumerate(ms):
             place = jnp.stack([((z ^ m) * PAIR + i) * CORES + c for i in range(PAIR)] + [x]).astype(jnp.int32)
             at = n * PAIR * share
             ordered = [cots[k, s] for k, s in shifts]
+            if stage and n == 0:
+                (parts,), (gives[m + 1],) = pack([(next_activations, 1, share, groups)], [gives[m + 1]])
+                mine.update(zip(far, parts))
+                for e in near:
+                    send_next(*e)
             if m == 0:
                 place, *came = lax.optimization_barrier((place, *[nexts[e] for e in near]))
                 nexts.update(zip(near, came))
-            if given is not None:
-                place, _ = lax.optimization_barrier((place, given))
-            given, keep = inner_block(place, acts[stage], at, ordered, own_weight, other[stage], at, share)
-            held = keep + lax.ppermute(given, "x", ring(PAIR, 1)).astype(f32)
-            total[m] = held if m not in total else held + total[m]
-            if m:
-                low = m & -m
-                came = lax.ppermute(total[m].astype(bf16), "z", [(i, i ^ low) for i in range(nz)]).astype(f32)
-                total[m ^ low] = came if m ^ low not in total else total[m ^ low] + came
-    summed = total[0]
-
-    given, *island_cots = lax.optimization_barrier((given, *[cots[0, s] for s in range(fsdp)]))
+            if n:
+                place, gives[m + 1] = lax.optimization_barrier((place, gives[m + 1]))
+            gives[m], keeps[m] = inner_block(place, acts[stage], at, ordered, own_weight, other_weight, share)
+    keeps[0], *island_cots = lax.optimization_barrier((keeps[0], *[cots[0, s] for s in range(fsdp)]))
     grad_rows = lax.dot_general(
         jnp.concatenate(island_cots, axis=0), own_weight, (((1,), (1,)), ((), ())), preferred_element_type=f32
     ).astype(bf16)
     parts = [grad_rows]
     for s in range(1, fsdp):
         parts.append(lax.ppermute(grad_rows[s * tok : (s + 1) * tok], "fsdp", ring(fsdp, -s)))
+
+    total, over_x, over_z = {}, {}, {}
+    for m in order:
+        earlier = over_z if m % 2 else over_x
+        if m + 2 in earlier:
+            gives[m], earlier[m + 2] = lax.optimization_barrier((gives[m], earlier[m + 2]))
+        over_x[m] = lax.ppermute(gives[m], "x", ring(PAIR, 1))
+        if m % 2:
+            keeps[m], gives[m - 1] = lax.optimization_barrier((keeps[m], gives[m - 1]))
+            over_z[m] = lax.ppermute((keeps[m] + over_x[m].astype(f32)).astype(bf16), "z", [(i, i ^ 1) for i in range(nz)])
+    for m in order:
+        held = keeps[m] + over_x[m].astype(f32)
+        total[m] = held if m not in total else held + total[m]
+        if m:
+            low = m & -m
+            if m not in over_z:
+                over_z[m] = lax.ppermute(total[m].astype(bf16), "z", [(i, i ^ low) for i in range(nz)])
+            came = over_z[m].astype(f32)
+            total[m ^ low] = came if m ^ low not in total else total[m ^ low] + came
+    summed = total[0]
 
     summed, *held = lax.optimization_barrier((summed, *[mine[e] for e in away]))
     mine.update(zip(away, held))

time: 184 us -> 168 us (0.913)
  waiting for transfers between devices: 86.3 us -> 104 us
  local copies, waits for them, and re-layouts: 20 us -> 4.1 us
  Pallas kernels: 32.3 us -> 25.1 us
  starting transfers between devices: 31 us -> 25.7 us
  matrix products: 5.85 us -> 2.44 us
    ppermute x6 -> x7, waiting for transfers between devices: 10.3 us -> 27.7 us  [the longest x4 20.7 us: local(): over_x[m] = lax.ppermute(gives[m], 'x', ring(PAIR, 1))]
    unnamed x80 -> x34, local copies, waits for them, and re-layouts: 19.6 us -> 3.81 us
    ppermute x3 -> x1, waiting for transfers between devices: 15.4 us -> 6.8 us  [local(): lax.ppermute(total[m].astype(bf16), 'z', [(i, i ^ low) for i in range(nz)])]
    ppermute x7, waiting for transfers between devices: 18.4 us -> 26.4 us  [send_next(): lax.ppermute(mine[i, k, s], ('x', 'core', 'fsdp'), pairs)]
    ppermute x6, waiting for transfers between devices: 14.3 us -> 6.28 us  [local(): lax.ppermute(part, ('core', 'fsdp'), pair_ring(k, s))]
    pallas_call x4, Pallas kernels: 6.84 us -> 2.85 us  [keys_part(): pl.pallas_call(functools.partial(keys_kernel, len(acts), at), out_shape=j...]
    ppermute x3 -> x1, starting transfers between devices: 6.12 us -> 2.65 us  [local(): lax.ppermute(total[m].astype(bf16), 'z', [(i, i ^ low) for i in range(nz)])]
    dot_general x1, matrix products: 5.85 us -> 2.44 us  [local(): lax.dot_general(jnp.concatenate(island_cots, axis=0), own_weight, (((1,),...]
  transfers between devices with their start and end apart: 34 -> 33, of which waited for: 21 -> 23; matrix products, arithmetic and copies ran while one was open for 7% -> 5% of each run, Pallas kernels for 13% -> 12%
where the time goes in v4:
time: 168 us
  waiting for transfers between devices  104 us (62%)
  starting transfers between devices  25.7 us (15%)
  Pallas kernels  25.1 us (15%)
  other arithmetic  5.96 us (4%)
  local copies, waits for them, and re-layouts  4.1 us (2%)
  matrix products  2.44 us (1%)
    ppermute x7, waiting for transfers between devices, send_next(): lax.ppermute(mine[i, k, s], ('x', 'core', 'fsdp'), pairs)  26.4 us
    ppermute x4, waiting for transfers between devices, local(): over_x[m] = lax.ppermute(gives[m], 'x', ring(PAIR, 1))  20.7 us
    ppermute x3, waiting for transfers between devices, local(): rows.append(lax.ppermute(source, 'z', [(i, i ^ low) for i in range(nz)]))  13.7 us
    pallas_call x4, Pallas kernels, inner_block(): pl.pallas_call(functools.partial(inner_kernel, pieces, share, inner_rate...  12.8 us
    ppermute x2, waiting for transfers between devices, home(): from_x = lax.ppermute(to_x, 'x', ring(PAIR, 1))  11 us
    ppermute x2, waiting for transfers between devices, local(): lax.ppermute((keeps[m] + over_x[m].astype(f32)).astype(bf16), 'z', [(i, i...  7.02 us
    ppermute x1, waiting for transfers between devices, local(): lax.ppermute(total[m].astype(bf16), 'z', [(i, i ^ low) for i in range(nz)])  6.8 us
    pallas_call x2, Pallas kernels, pack(): pl.pallas_call(functools.partial(pack_kernel, plan), out_shape=shapes, in...  6.52 us
  transfers between devices with their start and end apart: 33, of which 23 were waited for; matrix products, arithmetic and copies ran while one was open for 5% of the time, Pallas kernels for 12%

profile of v4, /device:TPU:0, one launch (start us, length us, event | category | flops | bytes accessed | tf_op | source)
XLA Modules:
  0.0 168.0 jit_solution(515928797346130634)
XLA Ops:
  1.2 2.6 %collective-permute-start.4 = (bf16[128,1024]{1,0:T(8,128)(2,1)}, bf16[128,1024]{1,0:T(8,128)(2,1)S(1)}, u32[]{:S(2)}, u32[]{:S(2)}) collective-permute-start(bf16[128,1024]{1,0:T(8,128)(2,1)} %refs_4_.7), channel_id=1, source_target_pairs={{0,1},{1,0},{2,3},{3,2},{4,5},{5,4},{6,7},{7,6},{8,9},{9,8},{10,11... | collective-permute-start | bytes 786440 | tf_op jit(solution)/shard_map/ppermute | solution.py:267
  4.0 3.2 %shard_map.93 = (bf16[128,1024]{1,0:T(8,128)(2,1)S(1)}, bf16[128,1024]{1,0:T(8,128)(2,1)S(1)}, bf16[128,1024]{1,0:T(8,128)(2,1)S(1)}, bf16[128,1024]{1,0:T(8,128...) custom-call(s32[32]{0:T(128)S(1)} %stack.324.starts, ...), custom_call_target="tpu_custom_call" | custom-call | bytes 4194304 | tf_op jit(solution)/shard_map/pallas_call | solution.py:72
  7.8 3.4 %collective-permute-done.4.refs_6_ = bf16[128,1024]{1,0:T(8,128)(2,1)S(1)} collective-permute-done((bf16[128,1024]{1,0:T(8,128)(2,1)}, bf16[128,1024]{1,0:T(8,128)(2,1)S(1)}, u32[]{:S(2)}, u32[]{:S(2)}) %collective-permute-start.4) | collective-permute-done | bytes 262176 | tf_op jit(solution)/shard_map/ppermute | solution.py:267
  11.9 3.0 %collective-permute-done.3.refs_5_ = bf16[128,1024]{1,0:T(8,128)(2,1)S(1)} collective-permute-done((bf16[128,1024]{1,0:T(8,128)(2,1)}, bf16[128,1024]{1,0:T(8,128)(2,1)S(1)}, u32[]{:S(2)}, u32[]{:S(2)}) %collective-permute-start.3) | collective-permute-done | bytes 262176 | tf_op jit(solution)/shard_map/ppermute | solution.py:277
  16.9 4.7 %collective-permute-done.2.refs_3_ = bf16[128,1024]{1,0:T(8,128)(2,1)S(1)} collective-permute-done((bf16[128,1024]{1,0:T(8,128)(2,1)S(1)}, bf16[128,1024]{1,0:T(8,128)(2,1)S(1)}, u32[]{:S(2)}, u32[]{:S(2)}) %collective-permute-start.2) | collective-permute-done | bytes 262176 | tf_op jit(solution)/shard_map/ppermute | solution.py:274
  21.6 3.4 %shard_map.94 = (bf16[256,1024]{1,0:T(8,128)(2,1)}, f32[256,1024]{1,0:T(8,128)S(1)}) custom-call(s32[3]{0:T(128)S(1)} %get-tuple-element.152.place, bf16[128,1024]{1,0:T(8,128)(2,1)S(1)} %get-tuple-element.76.refs_0_, bf16[128,1024]{1,0:T(8,128)(2,1)S(1)} %collective-permute-done.refs_1_, bf16[128,1024]{1,0:T(8,128)(2,1)S(1)} %collective-permute-done.1.refs_2_, ...), custom_call_target="tpu_custom_call" | custom-call | flops 134217728 | bytes 262144 | tf_op jit(solution)/shard_map/pallas_call | solution.py:125
  29.7 3.4 %shard_map.95 = (bf16[256,1024]{1,0:T(8,128)(2,1)}, f32[256,1024]{1,0:T(8,128)S(1)}) custom-call(s32[3]{0:T(128)S(1)} %get-tuple-element.81.place, bf16[128,1024]{1,0:T(8,128)(2,1)S(1)} %get-tuple-element.76.refs_0_, bf16[128,1024]{1,0:T(8,128)(2,1)S(1)} %collective-permute-done.refs_1_, bf16[128,1024]{1,0:T(8,128)(2,1)S(1)} %collective-permute-done.1.refs_2_, ...), custom_call_target="tpu_custom_call" | custom-call | flops 134217728 | bytes 262144 | tf_op jit(solution)/shard_map/pallas_call | solution.py:125
  33.1 7.3 %collective-permute-done.15 = bf16[256,1024]{1,0:T(8,128)(2,1)} collective-permute-done((bf16[256,1024]{1,0:T(8,128)(2,1)}, bf16[256,1024]{1,0:T(8,128)(2,1)}, u32[]{:S(2)}, u32[]{:S(2)}) %collective-permute-start.15) | collective-permute-done | bytes 524320 | tf_op jit(solution)/shard_map/ppermute | solution.py:323
  40.5 2.0 %add_convert_fusion.2 = bf16[256,1024]{1,0:T(8,128)(2,1)} fusion(f32[256,1024]{1,0:T(8,128)S(1)} %copy-done.2, bf16[256,1024]{1,0:T(8,128)(2,1)} %collective-permute-done.15), kind=kLoop, calls=%fused_computation.7 | loop fusion | flops 786432 | bytes 2097152 | tf_op jit(solution)/shard_map/convert_element_type | solution.py:326
  45.7 3.3 %shard_map.96 = (bf16[128,1024]{1,0:T(8,128)(2,1)S(1)}, bf16[128,1024]{1,0:T(8,128)(2,1)}, bf16[128,1024]{1,0:T(8,128)(2,1)S(1)}, bf16[128,1024]{1,0:T(8,128)(2,...) custom-call(s32[32]{0:T(128)S(1)} %stack.285.starts, ...), custom_call_target="tpu_custom_call" | custom-call | bytes 4194304 | tf_op jit(solution)/shard_map/pallas_call | solution.py:72
  54.2 3.0 %shard_map.97 = (bf16[256,1024]{1,0:T(8,128)(2,1)S(1)}, f32[256,1024]{1,0:T(8,128)S(1)}) custom-call(s32[3]{0:T(128)S(1)} %add_add_fusion.4.place, bf16[128,1024]{1,0:T(8,128)(2,1)S(1)} %get-tuple-element.91.refs_0_, bf16[128,1024]{1,0:T(8,128)(2,1)S(1)} %collective-permute-done.10.refs_1_, bf16[128,1024]{1,0:T(8,128)(2,1)S(1)} %collective-permute-done.11.refs_2_, ...), custom_call_target="tpu_custom_call" | custom-call | flops 134217728 | bytes 262144 | tf_op jit(solution)/shard_map/pallas_call | solution.py:125
  57.2 4.1 %collective-permute-done.7.refs_1_ = bf16[128,1024]{1,0:T(8,128)(2,1)S(1)} collective-permute-done((bf16[128,1024]{1,0:T(8,128)(2,1)}, bf16[128,1024]{1,0:T(8,128)(2,1)S(1)}, u32[]{:S(2)}, u32[]{:S(2)}) %collective-permute-start.7) | collective-permute-done | bytes 262176 | tf_op jit(solution)/shard_map/ppermute | solution.py:289
  61.3 2.6 %collective-permute-done.9.refs_1_ = bf16[128,1024]{1,0:T(8,128)(2,1)S(1)} collective-permute-done((bf16[128,1024]{1,0:T(8,128)(2,1)}, bf16[128,1024]{1,0:T(8,128)(2,1)S(1)}, u32[]{:S(2)}, u32[]{:S(2)}) %collective-permute-start.9) | collective-permute-done | bytes 262176 | tf_op jit(solution)/shard_map/ppermute | solution.py:289
  64.5 3.0 %shard_map.98 = (bf16[256,1024]{1,0:T(8,128)(2,1)S(1)}, f32[256,1024]{1,0:T(8,128)S(1)}) custom-call(s32[3]{0:T(128)S(1)} %add_add_fusion.1.place, bf16[128,1024]{1,0:T(8,128)(2,1)S(1)} %get-tuple-element.91.refs_0_, bf16[128,1024]{1,0:T(8,128)(2,1)S(1)} %collective-permute-done.10.refs_1_, bf16[128,1024]{1,0:T(8,128)(2,1)S(1)} %collective-permute-done.11.refs_2_, ...), custom_call_target="tpu_custom_call" | custom-call | flops 134217728 | bytes 262144 | tf_op jit(solution)/shard_map/pallas_call | solution.py:125
  70.4 2.7 %collective-permute-start.17 = (bf16[256,1024]{1,0:T(8,128)(2,1)S(1)}, bf16[256,1024]{1,0:T(8,128)(2,1)S(1)}, u32[]{:S(2)}, u32[]{:S(2)}) collective-permute-start(bf16[256,1024]{1,0:T(8,128)(2,1)S(1)} %add_convert_fusion.1), channel_id=1, source_target_pairs={{0,16},{8,24},{16,0},{24,8},{1,17},{9,25},{17,1},{25,9},{2,18},{10... | collective-permute-start | bytes 1572872 | tf_op jit(solution)/shard_map/ppermute | solution.py:333
  73.0 5.7 %collective-permute-done.18 = bf16[256,1024]{1,0:T(8,128)(2,1)S(1)} collective-permute-done((bf16[256,1024]{1,0:T(8,128)(2,1)S(1)}, bf16[256,1024]{1,0:T(8,128)(2,1)S(1)}, u32[]{:S(2)}, u32[]{:S(2)}) %collective-permute-start.18) | collective-permute-done | bytes 524320 | tf_op jit(solution)/shard_map/ppermute | solution.py:323
  79.4 2.4 %convolution_convert_fusion.refs_0_ = bf16[256,4096]{1,0:T(8,128)(2,1)S(1)} fusion(bf16[128,1024]{1,0:T(8,128)(2,1)S(1)} %collective-permute-done.4.refs_6_, bf16[128,1024]{1,0:T(8,128)(2,1)S(1)} %copy-done, bf16[1,4096,1024]{2,1,0:T(8,128)(2,1)S(1)} %bitcast.84), kind=kOutput, calls=%fused_computation | convolution fusion | flops 2149580800 | bytes 11010048 | tf_op jit(solution)/shard_map/dot_general | solution.py:311
  82.1 7.7 %collective-permute-done.14 = bf16[256,1024]{1,0:T(8,128)(2,1)S(1)} collective-permute-done((bf16[256,1024]{1,0:T(8,128)(2,1)S(1)}, bf16[256,1024]{1,0:T(8,128)(2,1)S(1)}, u32[]{:S(2)}, u32[]{:S(2)}) %collective-permute-start.14) | collective-permute-done | bytes 524320 | tf_op jit(solution)/shard_map/ppermute | solution.py:323
  89.8 6.8 %collective-permute-done.17 = bf16[256,1024]{1,0:T(8,128)(2,1)S(1)} collective-permute-done((bf16[256,1024]{1,0:T(8,128)(2,1)S(1)}, bf16[256,1024]{1,0:T(8,128)(2,1)S(1)}, u32[]{:S(2)}, u32[]{:S(2)}) %collective-permute-start.17) | collective-permute-done | bytes 524320 | tf_op jit(solution)/shard_map/ppermute | solution.py:333
  96.6 7.0 %collective-permute-done.19 = bf16[256,1024]{1,0:T(8,128)(2,1)S(1)} collective-permute-done((bf16[256,1024]{1,0:T(8,128)(2,1)S(1)}, bf16[256,1024]{1,0:T(8,128)(2,1)S(1)}, u32[]{:S(2)}, u32[]{:S(2)}) %collective-permute-start.19) | collective-permute-done | bytes 524320 | tf_op jit(solution)/shard_map/ppermute | solution.py:326
  107.8 2.0 %collective-permute-start.20 = (bf16[256,1024]{1,0:T(8,128)(2,1)S(1)}, bf16[256,1024]{1,0:T(8,128)(2,1)S(1)}, u32[]{:S(2)}, u32[]{:S(2)}) collective-permute-start(bf16[256,1024]{1,0:T(8,128)(2,1)S(1)} %get-tuple-element.148.refs_4_), channel_id=1, source_target_pairs={{0,16},{8,24},{16,0},{24,8},{1,17},{9,25},{17,1},{25,9},{2,18},{10... | collective-permute-start | bytes 1572872 | tf_op jit(solution)/shard_map/ppermute | solution.py:358
  109.8 3.5 %collective-permute-done.22.refs_2_ = bf16[128,1024]{1,0:T(8,128)(2,1)S(1)} collective-permute-done((bf16[128,1024]{1,0:T(8,128)(2,1)S(1)}, bf16[128,1024]{1,0:T(8,128)(2,1)S(1)}, u32[]{:S(2)}, u32[]{:S(2)}) %collective-permute-start.22) | collective-permute-done | bytes 262176 | tf_op jit(solution)/shard_map/ppermute | solution.py:289
  113.3 5.5 %collective-permute-done.23.refs_3_ = bf16[128,1024]{1,0:T(8,128)(2,1)S(1)} collective-permute-done((bf16[128,1024]{1,0:T(8,128)(2,1)S(1)}, bf16[128,1024]{1,0:T(8,128)(2,1)S(1)}, u32[]{:S(2)}, u32[]{:S(2)}) %collective-permute-start.23) | collective-permute-done | bytes 262176 | tf_op jit(solution)/shard_map/ppermute | solution.py:289
  118.7 3.2 %collective-permute-done.24.refs_2_ = bf16[128,1024]{1,0:T(8,128)(2,1)S(1)} collective-permute-done((bf16[128,1024]{1,0:T(8,128)(2,1)S(1)}, bf16[128,1024]{1,0:T(8,128)(2,1)S(1)}, u32[]{:S(2)}, u32[]{:S(2)}) %collective-permute-start.24) | collective-permute-done | bytes 262176 | tf_op jit(solution)/shard_map/ppermute | solution.py:289
  121.9 7.5 %collective-permute-done.25.refs_3_ = bf16[128,1024]{1,0:T(8,128)(2,1)S(1)} collective-permute-done((bf16[128,1024]{1,0:T(8,128)(2,1)S(1)}, bf16[128,1024]{1,0:T(8,128)(2,1)S(1)}, u32[]{:S(2)}, u32[]{:S(2)}) %collective-permute-start.25) | collective-permute-done | bytes 262176 | tf_op jit(solution)/shard_map/ppermute | solution.py:289
  129.4 2.4 %collective-permute-done.21.refs_5_ = bf16[256,1024]{1,0:T(8,128)(2,1)S(1)} collective-permute-done((bf16[256,1024]{1,0:T(8,128)(2,1)S(1)}, bf16[256,1024]{1,0:T(8,128)(2,1)S(1)}, u32[]{:S(2)}, u32[]{:S(2)}) %collective-permute-start.21) | collective-permute-done | bytes 524320 | tf_op jit(solution)/shard_map/ppermute | solution.py:358
  131.8 2.1 %collective-permute-done.20.refs_6_ = bf16[256,1024]{1,0:T(8,128)(2,1)S(1)} collective-permute-done((bf16[256,1024]{1,0:T(8,128)(2,1)S(1)}, bf16[256,1024]{1,0:T(8,128)(2,1)S(1)}, u32[]{:S(2)}, u32[]{:S(2)}) %collective-permute-start.20) | collective-permute-done | bytes 524320 | tf_op jit(solution)/shard_map/ppermute | solution.py:358
  134.0 1.9 %shard_map.101 = bf16[128,8192]{1,0:T(8,128)(2,1)} custom-call(s32[2]{0:T(128)S(1)} %pad_add_fusion.starts, bf16[256,4096]{1,0:T(8,128)(2,1)S(1)} %convolution_convert_fusion.refs_0_, bf16[128,4096]{1,0:T(8,128)(2,1)S(1)} %collective-permute-done.26.refs_1_), custom_call_target="tpu_custom_call" | custom-call | bytes 4194304 | tf_op jit(solution)/shard_map/pallas_call | solution.py:232
  137.9 9.2 %collective-permute-done.27.refs_4_ = bf16[256,1024]{1,0:T(8,128)(2,1)S(1)} collective-permute-done((bf16[256,1024]{1,0:T(8,128)(2,1)S(1)}, bf16[256,1024]{1,0:T(8,128)(2,1)S(1)}, u32[]{:S(2)}, u32[]{:S(2)}) %collective-permute-start.27) | collective-permute-done | bytes 524320 | tf_op jit(solution)/shard_map/ppermute | solution.py:358
  148.1 3.7 %collective-permute-done.28.came = f32[512,1024]{1,0:T(8,128)S(1)} collective-permute-done((f32[512,1024]{1,0:T(8,128)S(1)}, f32[512,1024]{1,0:T(8,128)S(1)}, u32[]{:S(2)}, u32[]{:S(2)}) %collective-permute-start.28) | collective-permute-done | bytes 2097184 | tf_op jit(solution)/shard_map/ppermute | solution.py:367
  152.6 7.8 %collective-permute-done.29.refs_2_ = bf16[256,512]{1,0:T(8,128)(2,1)S(1)} collective-permute-done((bf16[256,512]{1,0:T(8,128)(2,1)S(1)}, bf16[256,512]{1,0:T(8,128)(2,1)S(1)}, u32[]{:S(2)}, u32[]{:S(2)}) %collective-permute-start.29) | collective-permute-done | bytes 262176 | tf_op jit(solution)/shard_map/ppermute | solution.py:377
  162.6 3.2 %collective-permute-done.31.from_x = bf16[128,512]{1,0:T(8,128)(2,1)S(1)} collective-permute-done((bf16[128,512]{1,0:T(8,128)(2,1)S(1)}, bf16[128,512]{1,0:T(8,128)(2,1)S(1)}, u32[]{:S(2)}, u32[]{:S(2)}) %collective-permute-start.31) | collective-permute-done | bytes 131104 | tf_op jit(solution)/shard_map/ppermute | solution.py:377
  (96 shorter events, 33.7 us)
Async XLA Ops:
  0.6 21.0 %collective-permute-start.6 = (bf16[4096,1024]{1,0:T(8,128)(2,1)}, bf16[4096,1024]{1,0:T(8,128)(2,1)}, u32[]{:S(2)}, u32[]{:S(2)}) collective-permute-start(bf16[4096,1024]{1,0:T(8,128)(2,1)} %bitcast.78), channel_id=1, source_target_pairs={{0,2},{2,0},{1,3},{3,1},{4,6},{6,4},{5,7},{7,5},{8,10},{10,8},{9,1... | collective-permute-start | bytes 25165832 | tf_op jit(solution)/shard_map/ppermute | solution.py:276
  1.2 10.0 %collective-permute-start.4 = (bf16[128,1024]{1,0:T(8,128)(2,1)}, bf16[128,1024]{1,0:T(8,128)(2,1)S(1)}, u32[]{:S(2)}, u32[]{:S(2)}) collective-permute-start(bf16[128,1024]{1,0:T(8,128)(2,1)} %refs_4_.7), channel_id=1, source_target_pairs={{0,1},{1,0},{2,3},{3,2},{4,5},{5,4},{6,7},{7,6},{8,9},{9,8},{10,11... | collective-permute-start | bytes 786440 | tf_op jit(solution)/shard_map/ppermute | solution.py:267
  3.8 11.1 %collective-permute-start.3 = (bf16[128,1024]{1,0:T(8,128)(2,1)}, bf16[128,1024]{1,0:T(8,128)(2,1)S(1)}, u32[]{:S(2)}, u32[]{:S(2)}) collective-permute-start(bf16[128,1024]{1,0:T(8,128)(2,1)} %refs_4_.7), channel_id=1, source_target_pairs={{0,2},{2,0},{1,3},{3,1},{4,6},{6,4},{5,7},{7,5},{8,10},{10,8},{9,1... | collective-permute-start | bytes 786440 | tf_op jit(solution)/shard_map/ppermute | solution.py:277
  7.3 8.1 %collective-permute-start = (bf16[128,1024]{1,0:T(8,128)(2,1)S(1)}, bf16[128,1024]{1,0:T(8,128)(2,1)S(1)}, u32[]{:S(2)}, u32[]{:S(2)}) collective-permute-start(bf16[128,1024]{1,0:T(8,128)(2,1)S(1)} %get-tuple-element.77), channel_id=1, source_target_pairs={{0,2},{1,3},{2,0},{3,1},{4,6},{5,7},{6,4},{7,5},{8,10},{9,11},{10,... | collective-permute-start | bytes 786440 | tf_op jit(solution)/shard_map/ppermute | solution.py:274
  7.7 9.2 %collective-permute-start.1 = (bf16[128,1024]{1,0:T(8,128)(2,1)S(1)}, bf16[128,1024]{1,0:T(8,128)(2,1)S(1)}, u32[]{:S(2)}, u32[]{:S(2)}) collective-permute-start(bf16[128,1024]{1,0:T(8,128)(2,1)S(1)} %get-tuple-element.78), channel_id=1, source_target_pairs={{0,1},{1,0},{2,3},{3,2},{4,5},{5,4},{6,7},{7,6},{8,9},{9,8},{10,11... | collective-permute-start | bytes 786440 | tf_op jit(solution)/shard_map/ppermute | solution.py:274
  11.1 10.5 %collective-permute-start.2 = (bf16[128,1024]{1,0:T(8,128)(2,1)S(1)}, bf16[128,1024]{1,0:T(8,128)(2,1)S(1)}, u32[]{:S(2)}, u32[]{:S(2)}) collective-permute-start(bf16[128,1024]{1,0:T(8,128)(2,1)S(1)} %get-tuple-element.79), channel_id=1, source_target_pairs={{0,3},{1,2},{2,1},{3,0},{4,7},{5,6},{6,5},{7,4},{8,11},{9,10},{10,... | collective-permute-start | bytes 786440 | tf_op jit(solution)/shard_map/ppermute | solution.py:274
  14.9 6.7 %collective-permute-start.5 = (bf16[128,1024]{1,0:T(8,128)(2,1)S(1)}, bf16[128,1024]{1,0:T(8,128)(2,1)S(1)}, u32[]{:S(2)}, u32[]{:S(2)}) collective-permute-start(bf16[128,1024]{1,0:T(8,128)(2,1)S(1)} %collective-permute-done.4.refs_6_), channel_id=1, source_target_pairs={{0,2},{2,0},{1,3},{3,1},{4,6},{6,4},{5,7},{7,5},{8,10},{10,8},{9,1... | collective-permute-start | bytes 786440 | tf_op jit(solution)/shard_map/ppermute | solution.py:279
  26.0 14.4 %collective-permute-start.15 = (bf16[256,1024]{1,0:T(8,128)(2,1)}, bf16[256,1024]{1,0:T(8,128)(2,1)}, u32[]{:S(2)}, u32[]{:S(2)}) collective-permute-start(bf16[256,1024]{1,0:T(8,128)(2,1)} %get-tuple-element.110), channel_id=1, source_target_pairs={{0,4},{4,0},{1,5},{5,1},{2,6},{6,2},{3,7},{7,3},{8,12},{12,8},{9,1... | collective-permute-start | bytes 1572872 | tf_op jit(solution)/shard_map/ppermute | solution.py:323
  27.8 24.1 %collective-permute-start.10 = (bf16[128,1024]{1,0:T(8,128)(2,1)}, bf16[128,1024]{1,0:T(8,128)(2,1)S(1)}, u32[]{:S(2)}, u32[]{:S(2)}) collective-permute-start(bf16[128,1024]{1,0:T(8,128)(2,1)} %get-tuple-element.92), channel_id=1, source_target_pairs={{0,2},{1,3},{2,0},{3,1},{4,6},{5,7},{6,4},{7,5},{8,10},{9,11},{10,... | collective-permute-start | bytes 786440 | tf_op jit(solution)/shard_map/ppermute | solution.py:274
  27.8 25.6 %collective-permute-start.11 = (bf16[128,1024]{1,0:T(8,128)(2,1)}, bf16[128,1024]{1,0:T(8,128)(2,1)S(1)}, u32[]{:S(2)}, u32[]{:S(2)}) collective-permute-start(bf16[128,1024]{1,0:T(8,128)(2,1)} %get-tuple-element.93), channel_id=1, source_target_pairs={{0,1},{1,0},{2,3},{3,2},{4,5},{5,4},{6,7},{7,6},{8,9},{9,8},{10,11... | collective-permute-start | bytes 786440 | tf_op jit(solution)/shard_map/ppermute | solution.py:274
  29.3 24.1 %collective-permute-start.12 = (bf16[128,1024]{1,0:T(8,128)(2,1)S(1)}, bf16[128,1024]{1,0:T(8,128)(2,1)S(1)}, u32[]{:S(2)}, u32[]{:S(2)}) collective-permute-start(bf16[128,1024]{1,0:T(8,128)(2,1)S(1)} %get-tuple-element.94), channel_id=1, source_target_pairs={{0,3},{1,2},{2,1},{3,0},{4,7},{5,6},{6,5},{7,4},{8,11},{9,10},{10,... | collective-permute-start | bytes 786440 | tf_op jit(solution)/shard_map/ppermute | solution.py:274
  42.4 21.5 %collective-permute-start.16 = (bf16[256,1024]{1,0:T(8,128)(2,1)}, bf16[256,1024]{1,0:T(8,128)(2,1)}, u32[]{:S(2)}, u32[]{:S(2)}) collective-permute-start(bf16[256,1024]{1,0:T(8,128)(2,1)} %add_convert_fusion.2), channel_id=1, source_target_pairs={{0,8},{8,0},{16,24},{24,16},{1,9},{9,1},{17,25},{25,17},{2,10},{10... | collective-permute-start | bytes 1572872 | tf_op jit(solution)/shard_map/ppermute | solution.py:326
  44.3 23.3 %collective-permute-start.13 = (bf16[256,1024]{1,0:T(8,128)(2,1)}, bf16[256,1024]{1,0:T(8,128)(2,1)}, u32[]{:S(2)}, u32[]{:S(2)}) collective-permute-start(bf16[256,1024]{1,0:T(8,128)(2,1)} %get-tuple-element.104), channel_id=1, source_target_pairs={{0,4},{4,0},{1,5},{5,1},{2,6},{6,2},{3,7},{7,3},{8,12},{12,8},{9,1... | collective-permute-start | bytes 1572872 | tf_op jit(solution)/shard_map/ppermute | solution.py:323
  51.9 9.5 %collective-permute-start.7 = (bf16[128,1024]{1,0:T(8,128)(2,1)}, bf16[128,1024]{1,0:T(8,128)(2,1)S(1)}, u32[]{:S(2)}, u32[]{:S(2)}) collective-permute-start(bf16[128,1024]{1,0:T(8,128)(2,1)} %get-tuple-element.85), channel_id=1, source_target_pairs={{0,1},{1,0},{2,3},{3,2},{4,5},{5,4},{6,7},{7,6},{8,9},{9,8},{10,11... | collective-permute-start | bytes 786440 | tf_op jit(solution)/shard_map/ppermute | solution.py:289
  53.4 7.9 %collective-permute-start.8 = (bf16[128,1024]{1,0:T(8,128)(2,1)}, bf16[128,1024]{1,0:T(8,128)(2,1)S(1)}, u32[]{:S(2)}, u32[]{:S(2)}) collective-permute-start(bf16[128,1024]{1,0:T(8,128)(2,1)} %get-tuple-element.86), channel_id=1, source_target_pairs={{0,2},{1,3},{2,0},{3,1},{4,6},{5,7},{6,4},{7,5},{8,10},{9,11},{10,... | collective-permute-start | bytes 786440 | tf_op jit(solution)/shard_map/ppermute | solution.py:289
  53.4 10.6 %collective-permute-start.9 = (bf16[128,1024]{1,0:T(8,128)(2,1)}, bf16[128,1024]{1,0:T(8,128)(2,1)S(1)}, u32[]{:S(2)}, u32[]{:S(2)}) collective-permute-start(bf16[128,1024]{1,0:T(8,128)(2,1)} %get-tuple-element.87), channel_id=1, source_target_pairs={{0,3},{1,2},{2,1},{3,0},{4,7},{5,6},{6,5},{7,4},{8,11},{9,10},{10,... | collective-permute-start | bytes 786440 | tf_op jit(solution)/shard_map/ppermute | solution.py:289
  64.0 14.8 %collective-permute-start.18 = (bf16[256,1024]{1,0:T(8,128)(2,1)S(1)}, bf16[256,1024]{1,0:T(8,128)(2,1)S(1)}, u32[]{:S(2)}, u32[]{:S(2)}) collective-permute-start(bf16[256,1024]{1,0:T(8,128)(2,1)S(1)} %get-tuple-element.113), channel_id=1, source_target_pairs={{0,4},{4,0},{1,5},{5,1},{2,6},{6,2},{3,7},{7,3},{8,12},{12,8},{9,1... | collective-permute-start | bytes 1572872 | tf_op jit(solution)/shard_map/ppermute | solution.py:323
  67.5 22.2 %collective-permute-start.14 = (bf16[256,1024]{1,0:T(8,128)(2,1)S(1)}, bf16[256,1024]{1,0:T(8,128)(2,1)S(1)}, u32[]{:S(2)}, u32[]{:S(2)}) collective-permute-start(bf16[256,1024]{1,0:T(8,128)(2,1)S(1)} %get-tuple-element.105), channel_id=1, source_target_pairs={{0,4},{4,0},{1,5},{5,1},{2,6},{6,2},{3,7},{7,3},{8,12},{12,8},{9,1... | collective-permute-start | bytes 1572872 | tf_op jit(solution)/shard_map/ppermute | solution.py:323
  70.4 26.2 %collective-permute-start.17 = (bf16[256,1024]{1,0:T(8,128)(2,1)S(1)}, bf16[256,1024]{1,0:T(8,128)(2,1)S(1)}, u32[]{:S(2)}, u32[]{:S(2)}) collective-permute-start(bf16[256,1024]{1,0:T(8,128)(2,1)S(1)} %add_convert_fusion.1), channel_id=1, source_target_pairs={{0,16},{8,24},{16,0},{24,8},{1,17},{9,25},{17,1},{25,9},{2,18},{10... | collective-permute-start | bytes 1572872 | tf_op jit(solution)/shard_map/ppermute | solution.py:333
  78.9 24.7 %collective-permute-start.19 = (bf16[256,1024]{1,0:T(8,128)(2,1)S(1)}, bf16[256,1024]{1,0:T(8,128)(2,1)S(1)}, u32[]{:S(2)}, u32[]{:S(2)}) collective-permute-start(bf16[256,1024]{1,0:T(8,128)(2,1)S(1)} %add_convert_fusion), channel_id=1, source_target_pairs={{0,8},{8,0},{16,24},{24,16},{1,9},{9,1},{17,25},{25,17},{2,10},{10... | collective-permute-start | bytes 1572872 | tf_op jit(solution)/shard_map/ppermute | solution.py:326
  82.0 51.9 %collective-permute-start.26 = (bf16[128,4096]{1,0:T(8,128)(2,1)S(1)}, bf16[128,4096]{1,0:T(8,128)(2,1)S(1)}, u32[]{:S(2)}, u32[]{:S(2)}) collective-permute-start(bf16[128,4096]{1,0:T(8,128)(2,1)S(1)} %slice.4), channel_id=1, source_target_pairs={{0,1},{1,0},{2,3},{3,2},{4,5},{5,4},{6,7},{7,6},{8,9},{9,8},{10,11... | collective-permute-start | bytes 3145736 | tf_op jit(solution)/shard_map/ppermute | solution.py:316
  103.9 9.3 %collective-permute-start.22 = (bf16[128,1024]{1,0:T(8,128)(2,1)S(1)}, bf16[128,1024]{1,0:T(8,128)(2,1)S(1)}, u32[]{:S(2)}, u32[]{:S(2)}) collective-permute-start(bf16[128,1024]{1,0:T(8,128)(2,1)S(1)} %copy-done.12), channel_id=1, source_target_pairs={{0,4},{1,5},{2,6},{3,7},{4,0},{5,1},{6,2},{7,3},{8,12},{9,13},{10,... | collective-permute-start | bytes 786440 | tf_op jit(solution)/shard_map/ppermute | solution.py:289
  104.5 14.2 %collective-permute-start.23 = (bf16[128,1024]{1,0:T(8,128)(2,1)S(1)}, bf16[128,1024]{1,0:T(8,128)(2,1)S(1)}, u32[]{:S(2)}, u32[]{:S(2)}) collective-permute-start(bf16[128,1024]{1,0:T(8,128)(2,1)S(1)} %copy-done.10), channel_id=1, source_target_pairs={{0,5},{1,4},{2,7},{3,6},{4,1},{5,0},{6,3},{7,2},{8,13},{9,12},{10,... | collective-permute-start | bytes 786440 | tf_op jit(solution)/shard_map/ppermute | solution.py:289
  107.8 24.1 %collective-permute-start.21 = (bf16[256,1024]{1,0:T(8,128)(2,1)S(1)}, bf16[256,1024]{1,0:T(8,128)(2,1)S(1)}, u32[]{:S(2)}, u32[]{:S(2)}) collective-permute-start(bf16[256,1024]{1,0:T(8,128)(2,1)S(1)} %get-tuple-element.148.refs_4_), channel_id=1, source_target_pairs={{0,8},{8,0},{16,24},{24,16},{1,9},{9,1},{17,25},{25,17},{2,10},{10... | collective-permute-start | bytes 1572872 | tf_op jit(solution)/shard_map/ppermute | solution.py:358
  107.8 26.2 %collective-permute-start.20 = (bf16[256,1024]{1,0:T(8,128)(2,1)S(1)}, bf16[256,1024]{1,0:T(8,128)(2,1)S(1)}, u32[]{:S(2)}, u32[]{:S(2)}) collective-permute-start(bf16[256,1024]{1,0:T(8,128)(2,1)S(1)} %get-tuple-element.148.refs_4_), channel_id=1, source_target_pairs={{0,16},{8,24},{16,0},{24,8},{1,17},{9,25},{17,1},{25,9},{2,18},{10... | collective-permute-start | bytes 1572872 | tf_op jit(solution)/shard_map/ppermute | solution.py:358
  113.3 8.7 %collective-permute-start.24 = (bf16[128,1024]{1,0:T(8,128)(2,1)S(1)}, bf16[128,1024]{1,0:T(8,128)(2,1)S(1)}, u32[]{:S(2)}, u32[]{:S(2)}) collective-permute-start(bf16[128,1024]{1,0:T(8,128)(2,1)S(1)} %copy-done.8), channel_id=1, source_target_pairs={{0,6},{1,7},{2,4},{3,5},{4,2},{5,3},{6,0},{7,1},{8,14},{9,15},{10,... | collective-permute-start | bytes 786440 | tf_op jit(solution)/shard_map/ppermute | solution.py:289
  118.7 10.7 %collective-permute-start.25 = (bf16[128,1024]{1,0:T(8,128)(2,1)S(1)}, bf16[128,1024]{1,0:T(8,128)(2,1)S(1)}, u32[]{:S(2)}, u32[]{:S(2)}) collective-permute-start(bf16[128,1024]{1,0:T(8,128)(2,1)S(1)} %copy-done.6), channel_id=1, source_target_pairs={{0,7},{1,6},{2,5},{3,4},{4,3},{5,2},{6,1},{7,0},{8,15},{9,14},{10,... | collective-permute-start | bytes 786440 | tf_op jit(solution)/shard_map/ppermute | solution.py:289
  133.9 13.2 %collective-permute-start.27 = (bf16[256,1024]{1,0:T(8,128)(2,1)S(1)}, bf16[256,1024]{1,0:T(8,128)(2,1)S(1)}, u32[]{:S(2)}, u32[]{:S(2)}) collective-permute-start(bf16[256,1024]{1,0:T(8,128)(2,1)S(1)} %collective-permute-done.20.refs_6_), channel_id=1, source_target_pairs={{0,8},{8,0},{16,24},{24,16},{1,9},{9,1},{17,25},{25,17},{2,10},{10... | collective-permute-start | bytes 1572872 | tf_op jit(solution)/shard_map/ppermute | solution.py:358
  152.0 8.4 %collective-permute-start.29 = (bf16[256,512]{1,0:T(8,128)(2,1)S(1)}, bf16[256,512]{1,0:T(8,128)(2,1)S(1)}, u32[]{:S(2)}, u32[]{:S(2)}) collective-permute-start(bf16[256,512]{1,0:T(8,128)(2,1)S(1)} %get-tuple-element.142), channel_id=1, source_target_pairs={{0,4},{4,0},{1,5},{5,1},{2,6},{6,2},{3,7},{7,3},{8,12},{12,8},{9,1... | collective-permute-start | bytes 786440 | tf_op jit(solution)/shard_map/ppermute | solution.py:377
  152.6 8.1 %collective-permute-start.30 = (bf16[256,512]{1,0:T(8,128)(2,1)S(1)}, bf16[256,512]{1,0:T(8,128)(2,1)S(1)}, u32[]{:S(2)}, u32[]{:S(2)}) collective-permute-start(bf16[256,512]{1,0:T(8,128)(2,1)S(1)} %get-tuple-element.143), channel_id=1, source_target_pairs={{0,1},{1,0},{2,3},{3,2},{4,5},{5,4},{6,7},{7,6},{8,9},{9,8},{10,11... | collective-permute-start | bytes 786440 | tf_op jit(solution)/shard_map/ppermute | solution.py:378
  160.7 5.0 %collective-permute-start.31 = (bf16[128,512]{1,0:T(8,128)(2,1)S(1)}, bf16[128,512]{1,0:T(8,128)(2,1)S(1)}, u32[]{:S(2)}, u32[]{:S(2)}) collective-permute-start(bf16[128,512]{1,0:T(8,128)(2,1)S(1)} %get-tuple-element.146), channel_id=1, source_target_pairs={{0,4},{4,0},{1,5},{5,1},{2,6},{6,2},{3,7},{7,3},{8,12},{12,8},{9,1... | collective-permute-start | bytes 393224 | tf_op jit(solution)/shard_map/ppermute | solution.py:377
  162.3 5.0 %collective-permute-start.32 = (bf16[128,512]{1,0:T(8,128)(2,1)S(1)}, bf16[128,512]{1,0:T(8,128)(2,1)S(1)}, u32[]{:S(2)}, u32[]{:S(2)}) collective-permute-start(bf16[128,512]{1,0:T(8,128)(2,1)S(1)} %get-tuple-element.147), channel_id=1, source_target_pairs={{0,1},{1,0},{2,3},{3,2},{4,5},{5,4},{6,7},{7,6},{8,9},{9,8},{10,11... | collective-permute-start | bytes 393224 | tf_op jit(solution)/shard_map/ppermute | solution.py:378
  (18 other events, 218.0 us)

commit v5 on v4

--- a/solution.py
+++ b/solution.py
@@ -48,7 +48,7 @@
         copy.wait()
 
 
-def pack(items, after=()):
+def pack(items, after=(), target=jax.ShapeDtypeStruct):
     result, rest = {}, []
     for n, (array, axis, size, groups) in enumerate(items):
         if axis == 1 and size % LANES:
@@ -67,8 +67,8 @@
         plan.append((axis, size, counts))
         for n in counts:
             shape = (n * size, array.shape[1]) if axis == 0 else (array.shape[0], n * size)
-            shapes.append(jax.ShapeDtypeStruct(shape, array.dtype))
-    moved = sum(4 * shape.size for shape in shapes)
+            shapes.append(target(shape, array.dtype))
+    moved = 4 * starts.shape[0] * 1024 * LANES
     outs = pl.pallas_call(
         functools.partial(pack_kernel, plan),
         out_shape=shapes,
@@ -85,8 +85,9 @@
 
 def inner_kernel(pieces, share, scale, act_at, place, *refs):
     acts, cots = refs[:pieces], refs[pieces : 2 * pieces]
-    own, other, give, keep, left, right, rows, total, done = refs[2 * pieces :]
-    tok = cots[0].shape[0]
+    own, other, to_x, stay_x, to_z, stay_z, left, right, rows, total, done = refs[2 * pieces :]
+    tok, kv = cots[0].shape
+    strips = 2 * PAIR
     copies = []
 
     def fetch(source, target):
@@ -94,12 +95,13 @@
 
     for n, (act, cot) in enumerate(zip(acts, cots)):
         here = pl.ds(n * tok, tok)
-        fetch(act.at[:, pl.ds(act_at, PAIR * share)], left.at[here, :])
+        fetch(act.at[:, pl.ds(act_at, strips * share)], left.at[here, :])
         fetch(cot, right.at[here, :])
-    for i in range(PAIR):
-        strip = pl.ds(pl.multiple_of(place[i] * share, share), share)
-        fetch(own.at[strip, :], rows.at[0, i])
-        fetch(other.at[strip, :], rows.at[1, i])
+    for i in range(strips):
+        strip_rows = pl.ds(pl.multiple_of(place[i] * share, share), share)
+        here = pl.ds(i * share, share)
+        fetch(own.at[strip_rows, :], rows.at[0, here, :])
+        fetch(other.at[strip_rows, :], rows.at[1, here, :])
     for copy in copies:
         copy.start()
     for copy in copies[: 2 * pieces]:
@@ -107,62 +109,118 @@
     total[...] = lax.dot_general(left[...], right[...], (((0,), (0,)), ((), ())), preferred_element_type=f32)
     for copy in copies[2 * pieces :]:
         copy.wait()
-    x = place[PAIR]
-
-    def inner_new(i):
-        grad = total[pl.ds(pl.multiple_of(i * share, share), share), :]
-        return (rows[0, i].astype(f32) + rows[1, i].astype(f32)) - scale * grad
-
-    give[...] = inner_new(1 - x).astype(bf16)
-    keep[...] = inner_new(x)
-
-
-def inner_block(place, acts, act_at, cots, own, other, share):
+
+    def inner_new(i, columns):
+        here = slice(i * share, (i + 1) * share)
+        return (rows[0, here, columns].astype(f32) + rows[1, here, columns].astype(f32)) - scale * total[here, columns]
+
+    first, second = slice(0, kv // 2), slice(kv // 2, kv)
+    for n in range(2):
+        here = slice(n * share, (n + 1) * share)
+        to_x[here, :] = inner_new(PAIR * n + 1, first).astype(bf16)
+        to_z[here, :] = inner_new(n, second).astype(bf16)
+    for n in range(2):
+        here = slice(n * share, (n + 1) * share)
+        stay_x[here, :] = inner_new(PAIR * n, first)
+        stay_z[here, :] = inner_new(PAIR + n, second)
+
+
+def inner_blocks(place, acts, act_at, cots, own, other, share):
     pieces = len(acts)
     tok, kv = cots[0].shape
-    if act_at % LANES or PAIR * share % LANES:
-        acts, act_at = [a[:, act_at : act_at + PAIR * share] for a in acts], 0
+    rows = 2 * PAIR * share
+    if act_at % LANES or rows % LANES:
+        acts, act_at = [a[:, act_at : act_at + rows] for a in acts], 0
+    sent, kept = (jax.ShapeDtypeStruct((2 * share, kv // 2), kind) for kind in (bf16, f32))
     return pl.pallas_call(
         functools.partial(inner_kernel, pieces, share, inner_rate / (tok * pieces // CORES), act_at),
-        out_shape=[jax.ShapeDtypeStruct((share, kv), bf16), jax.ShapeDtypeStruct((share, kv), f32)],
+        out_shape=[sent, kept, sent, kept],
         in_specs=[SMEM] + [ANY] * (2 * pieces) + [HBM, ANY],
-        out_specs=[pl.BlockSpec()] * 2,
+        out_specs=[pl.BlockSpec()] * 4,
         scratch_shapes=[
-            pltpu.VMEM((pieces * tok, PAIR * share), bf16),
+            pltpu.VMEM((pieces * tok, rows), bf16),
             pltpu.VMEM((pieces * tok, kv), bf16),
-            pltpu.VMEM((CORES, PAIR, share, kv), bf16),
-            pltpu.VMEM((PAIR * share, kv), f32),
-            pltpu.SemaphoreType.DMA((2 * pieces + CORES * PAIR,)),
+            pltpu.VMEM((CORES, rows, kv), bf16),
+            pltpu.VMEM((rows, kv), f32),
+            pltpu.SemaphoreType.DMA((2 * pieces + 2 * CORES * PAIR,)),
         ],
         compiler_params=pltpu.CompilerParams(vmem_limit_bytes=32 * MIB),
         cost_estimate=pl.CostEstimate(flops=pieces * tok * share * kv, bytes_accessed=share * kv, transcendentals=0),
     )(place, *acts, *cots, in_hbm(own), other)
 
 
-def keys_kernel(acts_count, at, *refs):
-    acts, (*blocks, out) = refs[:acts_count], refs[acts_count:]
+def middle_kernel(share, stay_x, from_x, stay_z, from_z, to_z, keep_left, to_x, keep_right):
+    over_x = stay_x[...] + from_x[...].astype(f32)
+    over_z = stay_z[...] + from_z[...].astype(f32)
+    to_z[...] = over_x[:share].astype(bf16)
+    to_x[...] = over_z[share:].astype(bf16)
+    keep_left[...] = over_x[share:]
+    keep_right[...] = over_z[:share]
+
+
+def block_sum(keep_left, from_z, keep_right, from_x, came):
+    left = keep_left[...] + from_z[...].astype(f32)
+    right = keep_right[...] + from_x[...].astype(f32)
+    total = jnp.concatenate([left, right], axis=1)
+    for other in came:
+        total = total + other[...].astype(f32)
+    return total
+
+
+def gather_kernel(keep_left, keep_right, *refs):
+    *came, left, right = refs
+    total = jnp.concatenate([keep_left[...], keep_right[...]], axis=1)
+    for other in came:
+        total = total + other[...].astype(f32)
+    left[...] = total[:, : left.shape[1]]
+    right[...] = total[:, left.shape[1] :]
+
+
+def block_kernel(*refs):
+    *inputs, out = refs
+    out[...] = block_sum(*inputs[:4], inputs[4:]).astype(bf16)
+
+
+def update_kernel(replicas, *refs):
+    *inputs, weight, momentum, share, new_outer, new_momentum = refs
+    summed = block_sum(*inputs[:4], inputs[4:])
+    pseudo_grad = weight[...] - summed / replicas
+    moment = nesterov * momentum[...] + pseudo_grad
+    outer = weight[...] - outer_rate * (pseudo_grad + nesterov * moment)
+    share[...] = outer.astype(bf16)
+    new_outer[...] = outer
+    new_momentum[...] = moment
+
+
+def keys_kernel(acts_count, counts, at, *refs):
+    acts, (*pieces, out) = refs[:acts_count], refs[acts_count:]
     if at:
-        *blocks, before = blocks
-    weight = jnp.concatenate([w[...] for w in blocks], axis=0)
+        *pieces, before = pieces
+    blocks = []
+    for count in counts:
+        blocks.append(jnp.concatenate([w[...] for w in pieces[:count]], axis=1))
+        pieces = pieces[count:]
+    weight = jnp.concatenate(blocks, axis=0)
     left = jnp.concatenate([a[:, at : at + weight.shape[0]] for a in acts], axis=0)
     product = jnp.dot(left, weight, preferred_element_type=f32)
     out[...] = before[...] + product if at else product
 
 
 def keys_part(acts, blocks, at, before=()):
-    rows, kv = len(acts) * acts[0].shape[0], blocks[0].shape[1]
-    depth = sum(w.shape[0] for w in blocks)
+    rows, kv = len(acts) * acts[0].shape[0], sum(w.shape[1] for w in blocks[0])
+    depth = sum(block[0].shape[0] for block in blocks)
     if at % LANES:
         acts = [a[:, at:] for a in acts]
         return before[0] + keys_part(acts, blocks, 0)
+    pieces = [w for block in blocks for w in block]
     return pl.pallas_call(
-        functools.partial(keys_kernel, len(acts), at),
+        functools.partial(keys_kernel, len(acts), [len(block) for block in blocks], at),
         out_shape=jax.ShapeDtypeStruct((rows, kv), f32),
-        in_specs=[pl.BlockSpec()] * (len(acts) + len(blocks) + len(before)),
+        in_specs=[pl.BlockSpec()] * (len(acts) + len(pieces) + len(before)),
         out_specs=pl.BlockSpec(),
         compiler_params=pltpu.CompilerParams(vmem_limit_bytes=24 * MIB),
         cost_estimate=pl.CostEstimate(flops=2 * rows * depth * kv, bytes_accessed=rows * kv, transcendentals=0),
-    )(*acts, *blocks, *before)
+    )(*acts, *pieces, *before)
 
 
 def core_sum_kernel(fsdp, tok, keep, came, to_x, stay_x, stay_f, *to_f):
@@ -202,15 +260,15 @@
     keys[:, half:] = (right[...] + from_x[...].astype(f32)).astype(bf16)
 
 
-def small_call(kernel, shapes, *args):
-    size = sum(shape.size for shape in shapes)
+def small_call(kernel, shapes, *args, spec=VMEM, weight=1):
+    size = weight * sum(shape.size for shape in shapes)
     return pl.pallas_call(
         kernel,
         out_shape=shapes,
-        in_specs=[VMEM] * len(args),
-        out_specs=[VMEM] * len(shapes),
+        in_specs=[spec] * len(args),
+        out_specs=[spec] * len(shapes),
         compiler_params=pltpu.CompilerParams(vmem_limit_bytes=24 * MIB),
-        cost_estimate=pl.CostEstimate(flops=size, bytes_accessed=8 * size, transcendentals=0),
+        cost_estimate=pl.CostEstimate(flops=size // 8, bytes_accessed=size // 8, transcendentals=0),
     )(*args)
 
 
@@ -259,13 +317,12 @@
         return [(at(i, j), at(i + k, j + s)) for i in range(CORES) for j in range(fsdp)]
 
     shifts = [(k, s) for s in range(fsdp) for k in range(CORES)]
-    order = list(range(nz - 1, -1, -1))
-    stages = [order[: nz // 2], order[nz // 2 :]]
+    stages = [(m + 1, m) for m in range(nz - 2, -1, -2)]
 
     cots = {(0, 0): cotangent}
     for s in range(1, fsdp):
         cots[0, s] = lax.ppermute(cotangent, "fsdp", ring(fsdp, s))
-    columns = [[column(z ^ m, i, k, s) for m in ms for i in range(PAIR)] for ms in stages for k, s in shifts]
+    columns = [[column(z ^ m, (x + i) % PAIR, k, s) for m in ms for i in range(PAIR)] for ms in stages for k, s in shifts]
     (mine,), _ = pack([(activations, 1, share, columns)])
     acts = []
     for stage in range(len(stages)):
@@ -279,83 +336,106 @@
         cots[1, s] = lax.ppermute(cots[0, s], "core", swap)
 
     far = [(i, k, s) for k in range(CORES) for i in range(PAIR) for s in range(fsdp)]
+    near, away = [e for e in far if e[0] == 0], [e for e in far if e[0]]
     index = lambda i, k, s: ((i % PAIR) * CORES + k % CORES) * fsdp + s % fsdp
     every = [(i, k, s) for i in range(PAIR) for k in range(CORES) for s in range(fsdp)]
     groups = [[column(z ^ m, (x + i) % PAIR, k, s) for m in range(nz)] for i, k, s in far]
-    mine, nexts = {}, {}
+    wanted = [cots[0, s] for s in range(1, fsdp)]
+    (parts,), wanted = pack([(next_activations, 1, share, groups)], wanted, pltpu.HBM)
+    cots.update({(0, s): got for s, got in enumerate(wanted, 1)})
+    mine, nexts = dict(zip(far, parts)), {}
 
     def send_next(i, k, s):
         pairs = [(index(*e), index(e[0] + i, e[1] + k, e[2] + s)) for e in every]
         nexts[i, k, s] = lax.ppermute(mine[i, k, s], ("x", "core", "fsdp"), pairs) if i or k or s else mine[i, k, s]
 
-    near, away = [e for e in far if e[0] == 0], [e for e in far if e[0]]
-
-    gives, keeps = {}, {}
+    ordered = [cots[k, s] for k, s in shifts]
+    across_x, across_z = ring(PAIR, 1), [(i, i ^ 1) for i in range(nz)]
+    over_z = {}
+
+    def finish(m, to_z, to_x, keep_left, keep_right):
+        from_z, from_x = lax.ppermute(to_z, "z", across_z), lax.ppermute(to_x, "x", across_x)
+        return [keep_left, from_z, keep_right, from_x] + over_z.get(m, [])
+
+    shape = lambda n, kind: jax.ShapeDtypeStruct((n * share, kv // 2), kind)
     for stage, ms in enumerate(stages):
-        for n, m in enumerate(ms):
-            place = jnp.stack([((z ^ m) * PAIR + i) * CORES + c for i in range(PAIR)] + [x]).astype(jnp.int32)
-            at = n * PAIR * share
-            ordered = [cots[k, s] for k, s in shifts]
-            if stage and n == 0:
-                (parts,), (gives[m + 1],) = pack([(next_activations, 1, share, groups)], [gives[m + 1]])
-                mine.update(zip(far, parts))
-                for e in near:
-                    send_next(*e)
-            if m == 0:
-                place, *came = lax.optimization_barrier((place, *[nexts[e] for e in near]))
-                nexts.update(zip(near, came))
-            if n:
-                place, gives[m + 1] = lax.optimization_barrier((place, gives[m + 1]))
-            gives[m], keeps[m] = inner_block(place, acts[stage], at, ordered, own_weight, other_weight, share)
-    keeps[0], *island_cots = lax.optimization_barrier((keeps[0], *[cots[0, s] for s in range(fsdp)]))
-    grad_rows = lax.dot_general(
-        jnp.concatenate(island_cots, axis=0), own_weight, (((1,), (1,)), ((), ())), preferred_element_type=f32
-    ).astype(bf16)
-    parts = [grad_rows]
-    for s in range(1, fsdp):
-        parts.append(lax.ppermute(grad_rows[s * tok : (s + 1) * tok], "fsdp", ring(fsdp, -s)))
-
-    total, over_x, over_z = {}, {}, {}
-    for m in order:
-        earlier = over_z if m % 2 else over_x
-        if m + 2 in earlier:
-            gives[m], earlier[m + 2] = lax.optimization_barrier((gives[m], earlier[m + 2]))
-        over_x[m] = lax.ppermute(gives[m], "x", ring(PAIR, 1))
-        if m % 2:
-            keeps[m], gives[m - 1] = lax.optimization_barrier((keeps[m], gives[m - 1]))
-            over_z[m] = lax.ppermute((keeps[m] + over_x[m].astype(f32)).astype(bf16), "z", [(i, i ^ 1) for i in range(nz)])
-    for m in order:
-        held = keeps[m] + over_x[m].astype(f32)
-        total[m] = held if m not in total else held + total[m]
-        if m:
+        blocks = [((z ^ m) * PAIR + (x + i) % PAIR) * CORES + c for m in ms for i in range(PAIR)]
+        place = jnp.stack(blocks).astype(jnp.int32)
+        if not stage:
+            place, *held = lax.optimization_barrier((place, *[mine[e] for e in far]))
+            mine.update(zip(far, held))
+            for e in near:
+                send_next(*e)
+        if stage:
+            place, to_z, to_x = lax.optimization_barrier((place, to_z, to_x))
+            m = stages[stage - 1][1]
+            inputs = finish(m, to_z, to_x, keep_left, keep_right)
+            (block_total,) = small_call(
+                block_kernel, [jax.ShapeDtypeStruct((share, kv), bf16)], *inputs, spec=pl.BlockSpec()
+            )
             low = m & -m
-            if m not in over_z:
-                over_z[m] = lax.ppermute(total[m].astype(bf16), "z", [(i, i ^ low) for i in range(nz)])
-            came = over_z[m].astype(f32)
-            total[m ^ low] = came if m ^ low not in total else total[m ^ low] + came
-    summed = total[0]
-
-    summed, *held = lax.optimization_barrier((summed, *[mine[e] for e in away]))
-    mine.update(zip(away, held))
-
-    pseudo_grad = outer_weight - summed / (nz * PAIR * CORES)
-    new_momentum = nesterov * outer_momentum + pseudo_grad
-    new_outer = outer_weight - outer_rate * (pseudo_grad + nesterov * new_momentum)
-
-    rows = [new_outer.astype(bf16)]
-    for m in range(1, nz):
+        to_x, stay_x, to_z, stay_z = inner_blocks(place, acts[stage], 0, ordered, own_weight, other_weight, share)
+        if stage:
+            to_x, to_z, block_total = lax.optimization_barrier((to_x, to_z, block_total))
+            over_z.setdefault(m ^ low, []).append(lax.ppermute(block_total, "z", [(i, i ^ low) for i in range(nz)]))
+        if not stage:
+            stay_x, *island_cots = lax.optimization_barrier((stay_x, *[cots[0, s] for s in range(fsdp)]))
+            grad_rows = lax.dot_general(
+                jnp.concatenate(island_cots, axis=0), own_weight, (((1,), (1,)), ((), ())), preferred_element_type=f32
+            ).astype(bf16)
+            parts = [grad_rows] + [grad_rows[s * tok : (s + 1) * tok] for s in range(1, fsdp)]
+            stay_x, *parts = lax.optimization_barrier((stay_x, *parts))
+            for s in range(1, fsdp):
+                parts[s] = lax.ppermute(parts[s], "fsdp", ring(fsdp, -s))
+        from_x, from_z = lax.ppermute(to_x, "x", across_x), lax.ppermute(to_z, "z", across_z)
+        to_z, keep_left, to_x, keep_right = small_call(
+            functools.partial(middle_kernel, share),
+            [shape(1, bf16), shape(1, f32)] * 2,
+            stay_x,
+            from_x,
+            stay_z,
+            from_z,
+            spec=pl.BlockSpec(),
+        )
+
+    straight, diagonal = [e for e in away if e[2] == 0], [e for e in away if e[2]]
+    held = (to_z, to_x, *[nexts[e] for e in near], *[mine[e] for e in straight])
+    to_z, to_x, *held = lax.optimization_barrier(held)
+    nexts.update(zip(near, held))
+    mine.update(zip(straight, held[len(near) :]))
+    inputs = finish(0, to_z, to_x, keep_left, keep_right)
+    for e in straight:
+        send_next(*e)
+    inputs[0], inputs[2] = small_call(
+        gather_kernel, [shape(1, f32)] * 2, keep_left, keep_right, *inputs[4:], spec=pl.BlockSpec(), weight=1 << 17
+    )
+    inputs[0], *held = lax.optimization_barrier((inputs[0], *[mine[e] for e in diagonal]))
+    mine.update(zip(diagonal, held))
+    for e in diagonal:
+        send_next(*e)
+
+    whole = jax.ShapeDtypeStruct((share, kv), f32)
+    share_rows, new_outer, new_momentum = small_call(
+        functools.partial(update_kernel, nz * PAIR * CORES),
+        [jax.ShapeDtypeStruct((share, kv), bf16), whole, whole],
+        *inputs[:4],
+        outer_weight,
+        outer_momentum,
+        spec=pl.BlockSpec(),
+    )
+
+    rows = {}
+    for m in sorted(range(1, nz), key=lambda m: (m & (m - 1)).bit_count() * nz - m):
         low = m & -m
-        source = rows[m ^ low]
+        pieces = [share_rows] if m == low else list(rows[m ^ low])
+        if m == 1:
+            pieces[0], *held = lax.optimization_barrier((pieces[0], *[nexts[e] for e in straight]))
+            nexts.update(zip(straight, held))
         if m == nz - 1:
-            for e in away:
-                send_next(*e)
-            held = [source, *rows[1:], *[nexts[e] for e in away]]
-            source, *held = lax.optimization_barrier(held)
-            rows[1:], held = held[: m - 1], held[m - 1 :]
-            nexts.update(zip(away, held))
-            source, *parts = lax.optimization_barrier((source, *parts))
-            input_grad = join(parts, [((f + s) % fsdp) * width for s in range(fsdp)])
-        rows.append(lax.ppermute(source, "z", [(i, i ^ low) for i in range(nz)]))
+            pieces[0], *parts = lax.optimization_barrier((pieces[0], *parts))
+        rows[m] = [lax.ppermute(piece, "z", [(i, i ^ low) for i in range(nz)]) for piece in pieces]
+    rows = [[share_rows]] + [rows[m] for m in range(1, nz)]
+    input_grad = join(parts, [((f + s) % fsdp) * width for s in range(fsdp)])
 
     half = len(far) // CORES
     near, away = [nexts[e] for e in far[:half]], [nexts[e] for e in far[half:]]

time: 168 us -> 153 us (0.911)
  waiting for transfers between devices: 104 us -> 90 us
  starting transfers between devices: 25.7 us -> 35.5 us
  other arithmetic: 5.96 us -> 0.23 us
  local copies, waits for them, and re-layouts: 4.1 us -> 0.37 us
  Pallas kernels: 25.1 us -> 22.9 us
    ppermute x7, waiting for transfers between devices: 26.4 us -> 16.3 us  [send_next(): lax.ppermute(mine[i, k, s], ('x', 'core', 'fsdp'), pairs)]
    convert_element_type x4 -> x0, other arithmetic: 5.35 us -> none  [the longest x2 2.12 us: local(): (keeps[m] + over_x[m].astype(f32)).astype(bf16)]
    ppermute x11 -> x13, waiting for transfers between devices: 48.3 us -> 53.3 us  [the longest x3 20.5 us: local(): lax.ppermute(piece, 'z', [(i, i ^ low) for i in range(nz)])]
    ppermute x6, starting transfers between devices: 3.1 us -> 7.52 us  [local(): lax.ppermute(part, ('core', 'fsdp'), pair_ring(k, s))]
    ppermute x11 -> x13, starting transfers between devices: 12.2 us -> 16.5 us  [the longest x1 4.08 us: local(): parts[s] = lax.ppermute(parts[s], 'fsdp', ring(fsdp, -s))]
    unnamed x34 -> x26, local copies, waits for them, and re-layouts: 3.81 us -> 0.06 us
    ppermute x1, waiting for transfers between devices: 3.03 us -> 0.01 us  [local(): cots[1, 0] = lax.ppermute(cotangent, 'core', swap)]
    pallas_call x11 -> x14, Pallas kernels: 16.7 us -> 13.9 us  [the longest x2 7.74 us: inner_blocks(): pl.pallas_call(functools.partial(inner_kernel, pieces, share, inner_rate...]
  transfers between devices with their start and end apart: 33 -> 35, of which waited for: 23 -> 23; matrix products, arithmetic and copies ran while one was open for 5% -> 2% of each run, Pallas kernels for 12% -> 14%
where the time goes in v5:
time: 153 us; the launch traced here: 152 us
  waiting for transfers between devices  90 us (59%)
  starting transfers between devices  35.5 us (23%)
  Pallas kernels  22.9 us (15%)
  matrix products  2.38 us (2%)
    ppermute x3, waiting for transfers between devices, local(): lax.ppermute(piece, 'z', [(i, i ^ low) for i in range(nz)])  20.5 us
    ppermute x7, waiting for transfers between devices, send_next(): lax.ppermute(mine[i, k, s], ('x', 'core', 'fsdp'), pairs)  16.3 us
    ppermute x2, waiting for transfers between devices, local(): lax.ppermute(to_x, 'x', across_x)  12.2 us
    ppermute x2, waiting for transfers between devices, local(): lax.ppermute(to_z, 'z', across_z)  11.9 us
    ppermute x2, waiting for transfers between devices, home(): from_x = lax.ppermute(to_x, 'x', ring(PAIR, 1))  10.2 us
    pallas_call x2, Pallas kernels, inner_blocks(): pl.pallas_call(functools.partial(inner_kernel, pieces, share, inner_rate...  7.74 us
    ppermute x6, starting transfers between devices, local(): lax.ppermute(part, ('core', 'fsdp'), pair_ring(k, s))  7.52 us
    pallas_call x2, Pallas kernels, pack(): pl.pallas_call(functools.partial(pack_kernel, plan), out_shape=shapes, in...  7.2 us
  transfers between devices with their start and end apart: 35, of which 23 were waited for; matrix products, arithmetic and copies ran while one was open for 2% of the time, Pallas kernels for 14%

profile of v5, /device:TPU:0, one launch (start us, length us, event | category | flops | bytes accessed | tf_op | source)
XLA Modules:
  0.0 152.4 jit_solution(17988609946167733387)
XLA Ops:
  1.2 2.9 %collective-permute-start = (bf16[128,1024]{1,0:T(8,128)(2,1)}, bf16[128,1024]{1,0:T(8,128)(2,1)S(1)}, u32[]{:S(2)}, u32[]{:S(2)}) collective-permute-start(bf16[128,1024]{1,0:T(8,128)(2,1)} %refs_4_.4), channel_id=1, source_target_pairs={{0,1},{1,0},{2,3},{3,2},{4,5},{5,4},{6,7},{7,6},{8,9},{9,8},{10,11... | collective-permute-start | bytes 786440 | tf_op jit(solution)/shard_map/ppermute | solution.py:324
  4.3 3.2 %shard_map.94 = (bf16[128,1024]{1,0:T(8,128)(2,1)S(1)}, bf16[128,1024]{1,0:T(8,128)(2,1)}, bf16[128,1024]{1,0:T(8,128)(2,1)}, bf16[128,1024]{1,0:T(8,128)(2,1)S(...) custom-call(s32[32]{0:T(128)S(1)} %stack.216.starts, ...), custom_call_target="tpu_custom_call" | custom-call | bytes 16777216 | tf_op jit(solution)/shard_map/pallas_call | solution.py:72
  7.7 2.7 %collective-permute-start.3 = (bf16[128,1024]{1,0:T(8,128)(2,1)S(1)}, bf16[128,1024]{1,0:T(8,128)(2,1)S(1)}, u32[]{:S(2)}, u32[]{:S(2)}) collective-permute-start(bf16[128,1024]{1,0:T(8,128)(2,1)S(1)} %get-tuple-element.105), channel_id=1, source_target_pairs={{0,3},{1,2},{2,1},{3,0},{4,7},{5,6},{6,5},{7,4},{8,11},{9,10},{10,... | collective-permute-start | bytes 786440 | tf_op jit(solution)/shard_map/ppermute | solution.py:331
  11.5 4.0 %shard_map.93 = (bf16[128,1024]{1,0:T(8,128)(2,1)}, bf16[128,1024]{1,0:T(8,128)(2,1)}, bf16[128,1024]{1,0:T(8,128)(2,1)}, bf16[128,1024]{1,0:T(8,128)(2,1)}, bf1...) custom-call(s32[32]{0:T(128)S(1)} %stack.215.starts, ...), custom_call_target="tpu_custom_call" | custom-call | bytes 16777216 | tf_op jit(solution)/shard_map/pallas_call | solution.py:72
  17.0 2.2 %collective-permute-start.10 = (bf16[128,1024]{1,0:T(8,128)(2,1)S(1)}, bf16[128,1024]{1,0:T(8,128)(2,1)S(1)}, u32[]{:S(2)}, u32[]{:S(2)}) collective-permute-start(bf16[128,1024]{1,0:T(8,128)(2,1)S(1)} %get-tuple-element.120), channel_id=1, source_target_pairs={{0,1},{1,0},{2,3},{3,2},{4,5},{5,4},{6,7},{7,6},{8,9},{9,8},{10,11... | collective-permute-start | bytes 786440 | tf_op jit(solution)/shard_map/ppermute | solution.py:331
  19.2 3.1 %collective-permute-done.3.refs_3_ = bf16[128,1024]{1,0:T(8,128)(2,1)S(1)} collective-permute-done((bf16[128,1024]{1,0:T(8,128)(2,1)S(1)}, bf16[128,1024]{1,0:T(8,128)(2,1)S(1)}, u32[]{:S(2)}, u32[]{:S(2)}) %collective-permute-start.3) | collective-permute-done | bytes 262176 | tf_op jit(solution)/shard_map/ppermute | solution.py:331
  22.3 1.9 %collective-permute-start.11 = (bf16[128,1024]{1,0:T(8,128)(2,1)S(1)}, bf16[128,1024]{1,0:T(8,128)(2,1)S(1)}, u32[]{:S(2)}, u32[]{:S(2)}) collective-permute-start(bf16[128,1024]{1,0:T(8,128)(2,1)S(1)} %get-tuple-element.121), channel_id=1, source_target_pairs={{0,3},{1,2},{2,1},{3,0},{4,7},{5,6},{6,5},{7,4},{8,11},{9,10},{10,... | collective-permute-start | bytes 786440 | tf_op jit(solution)/shard_map/ppermute | solution.py:331
  24.2 4.0 %shard_map.95 = (bf16[512,512]{1,0:T(8,128)(2,1)S(1)}, f32[512,512]{1,0:T(8,128)S(1)}, bf16[512,512]{1,0:T(8,128)(2,1)S(1)}, f32[512,512]{1,0:T(8,128)S(1)}) custom-call(s32[4]{0:T(128)S(1)} %pad_add_fusion.1.place, bf16[128,1024]{1,0:T(8,128)(2,1)S(1)} %get-tuple-element.102.refs_0_, bf16[128,1024]{1,0:T(8,128)(2,1)S(1)} %collective-permute-done.1.refs_1_, ...), custom_call_target="tpu_custom_call" | custom-call | flops 134217728 | bytes 262144 | tf_op jit(solution)/shard_map/pallas_call | solution.py:135
  28.3 1.6 %collective-permute-start.7 = (bf16[512,512]{1,0:T(8,128)(2,1)S(1)}, bf16[512,512]{1,0:T(8,128)(2,1)S(1)}, u32[]{:S(2)}, u32[]{:S(2)}) collective-permute-start(bf16[512,512]{1,0:T(8,128)(2,1)S(1)} %get-tuple-element.112), channel_id=1, source_target_pairs={{0,4},{4,0},{1,5},{5,1},{2,6},{6,2},{3,7},{7,3},{8,12},{12,8},{9,1... | collective-permute-start | bytes 1572872 | tf_op jit(solution)/shard_map/ppermute | solution.py:390
  29.8 1.6 %collective-permute-start.8 = (bf16[512,512]{1,0:T(8,128)(2,1)S(1)}, bf16[512,512]{1,0:T(8,128)(2,1)S(1)}, u32[]{:S(2)}, u32[]{:S(2)}) collective-permute-start(bf16[512,512]{1,0:T(8,128)(2,1)S(1)} %get-tuple-element.114), channel_id=1, source_target_pairs={{0,8},{8,0},{16,24},{24,16},{1,9},{9,1},{17,25},{25,17},{2,10},{10... | collective-permute-start | bytes 1572872 | tf_op jit(solution)/shard_map/ppermute | solution.py:390
  31.4 2.4 %convolution_convert_fusion.refs_0_ = bf16[256,4096]{1,0:T(8,128)(2,1)S(1)} fusion(bf16[128,1024]{1,0:T(8,128)(2,1)S(1)} %collective-permute-done.refs_6_, bf16[128,1024]{1,0:T(8,128)(2,1)S(1)} %copy-done, bf16[1,4096,1024]{2,1,0:T(8,128)(2,1)S(1)} %bitcast.49), kind=kOutput, calls=%fused_computation | convolution fusion | flops 2149580800 | bytes 11010048 | tf_op jit(solution)/shard_map/dot_general | solution.py:383
  33.9 7.2 %collective-permute-done.7.from_x = bf16[512,512]{1,0:T(8,128)(2,1)S(1)} collective-permute-done((bf16[512,512]{1,0:T(8,128)(2,1)S(1)}, bf16[512,512]{1,0:T(8,128)(2,1)S(1)}, u32[]{:S(2)}, u32[]{:S(2)}) %collective-permute-start.7) | collective-permute-done | bytes 524320 | tf_op jit(solution)/shard_map/ppermute | solution.py:390
  42.5 1.6 %collective-permute-start.12 = (bf16[256,512]{1,0:T(8,128)(2,1)S(1)}, bf16[256,512]{1,0:T(8,128)(2,1)S(1)}, u32[]{:S(2)}, u32[]{:S(2)}) collective-permute-start(bf16[256,512]{1,0:T(8,128)(2,1)S(1)} %get-tuple-element.126), channel_id=1, source_target_pairs={{0,8},{8,0},{16,24},{24,16},{1,9},{9,1},{17,25},{25,17},{2,10},{10... | collective-permute-start | bytes 786440 | tf_op jit(solution)/shard_map/ppermute | solution.py:357
  44.7 3.7 %shard_map.97 = (bf16[512,512]{1,0:T(8,128)(2,1)S(1)}, f32[512,512]{1,0:T(8,128)S(1)}, bf16[512,512]{1,0:T(8,128)(2,1)S(1)}, f32[512,512]{1,0:T(8,128)S(1)}) custom-call(s32[4]{0:T(128)S(1)} %pad_add_fusion.place, bf16[128,1024]{1,0:T(8,128)(2,1)S(1)} %get-tuple-element.118.refs_0_, bf16[128,1024]{1,0:T(8,128)(2,1)S(1)} %collective-permute-done.9.refs_1_, ...), custom_call_target="tpu_custom_call" | custom-call | flops 134217728 | bytes 262144 | tf_op jit(solution)/shard_map/pallas_call | solution.py:135
  49.0 2.1 %collective-permute-done.13.refs_3_ = bf16[256,512]{1,0:T(8,128)(2,1)S(1)} collective-permute-done((bf16[256,512]{1,0:T(8,128)(2,1)S(1)}, bf16[256,512]{1,0:T(8,128)(2,1)S(1)}, u32[]{:S(2)}, u32[]{:S(2)}) %collective-permute-start.13) | collective-permute-done | bytes 262176 | tf_op jit(solution)/shard_map/ppermute | solution.py:357
  52.5 2.6 %collective-permute-start.19 = (bf16[256,1024]{1,0:T(8,128)(2,1)S(1)}, bf16[256,1024]{1,0:T(8,128)(2,1)S(1)}, u32[]{:S(2)}, u32[]{:S(2)}) collective-permute-start(bf16[256,1024]{1,0:T(8,128)(2,1)S(1)} %shard_map.98), channel_id=1, source_target_pairs={{0,16},{8,24},{16,0},{24,8},{1,17},{9,25},{17,1},{25,9},{2,18},{10... | collective-permute-start | bytes 1572872 | tf_op jit(solution)/shard_map/ppermute | solution.py:380
  55.1 1.7 %collective-permute-start.16 = (bf16[128,1024]{1,0:T(8,128)(2,1)S(1)}, bf16[128,1024]{1,0:T(8,128)(2,1)S(1)}, u32[]{:S(2)}, u32[]{:S(2)}) collective-permute-start(bf16[128,1024]{1,0:T(8,128)(2,1)S(1)} %copy-done.10), channel_id=1, source_target_pairs={{0,1},{1,0},{2,3},{3,2},{4,5},{5,4},{6,7},{7,6},{8,9},{9,8},{10,11... | collective-permute-start | bytes 786440 | tf_op jit(solution)/shard_map/ppermute | solution.py:350
  56.8 5.0 %collective-permute-done.14.from_x = bf16[512,512]{1,0:T(8,128)(2,1)S(1)} collective-permute-done((bf16[512,512]{1,0:T(8,128)(2,1)S(1)}, bf16[512,512]{1,0:T(8,128)(2,1)S(1)}, u32[]{:S(2)}, u32[]{:S(2)}) %collective-permute-start.14) | collective-permute-done | bytes 524320 | tf_op jit(solution)/shard_map/ppermute | solution.py:390
  62.0 10.7 %collective-permute-done.15.from_z = bf16[512,512]{1,0:T(8,128)(2,1)S(1)} collective-permute-done((bf16[512,512]{1,0:T(8,128)(2,1)S(1)}, bf16[512,512]{1,0:T(8,128)(2,1)S(1)}, u32[]{:S(2)}, u32[]{:S(2)}) %collective-permute-start.15) | collective-permute-done | bytes 524320 | tf_op jit(solution)/shard_map/ppermute | solution.py:390
  72.7 4.1 %collective-permute-start.28 = (bf16[128,4096]{1,0:T(8,128)(2,1)S(1)}, bf16[128,4096]{1,0:T(8,128)(2,1)S(1)}, u32[]{:S(2)}, u32[]{:S(2)}) collective-permute-start(bf16[128,4096]{1,0:T(8,128)(2,1)S(1)} %slice.4), channel_id=1, source_target_pairs={{0,1},{1,0},{2,3},{3,2},{4,5},{5,4},{6,7},{7,6},{8,9},{9,8},{10,11... | collective-permute-start | bytes 3145736 | tf_op jit(solution)/shard_map/ppermute | solution.py:389
  77.1 1.4 collective-permute-start.21
  78.6 5.1 %collective-permute-done.20.refs_1_ = bf16[256,512]{1,0:T(8,128)(2,1)S(1)} collective-permute-done((bf16[256,512]{1,0:T(8,128)(2,1)S(1)}, bf16[256,512]{1,0:T(8,128)(2,1)S(1)}, u32[]{:S(2)}, u32[]{:S(2)}) %collective-permute-start.20) | collective-permute-done | bytes 262176 | tf_op jit(solution)/shard_map/ppermute | solution.py:357
  83.8 1.7 %shard_map.101 = (bf16[256,1024]{1,0:T(8,128)(2,1)S(1)}, f32[256,1024]{1,0:T(8,128)}, f32[256,1024]{1,0:T(8,128)}) custom-call(f32[256,512]{1,0:T(8,128)S(1)} %get-tuple-element.148.refs_0_, bf16[256,512]{1,0:T(8,128)(2,1)S(1)} %collective-permute-done.20.refs_1_, f32[256,512]{1,0:T(8,128)S(1)} %get-tuple-element.150.refs_2_, ...), custom_call_target="tpu_custom_call" | custom-call | flops 98304 | bytes 98304 | tf_op jit(solution)/shard_map/pallas_call | solution.py:265
  87.4 7.1 %collective-permute-done.22.refs_2_ = bf16[128,1024]{1,0:T(8,128)(2,1)S(1)} collective-permute-done((bf16[128,1024]{1,0:T(8,128)(2,1)S(1)}, bf16[128,1024]{1,0:T(8,128)(2,1)S(1)}, u32[]{:S(2)}, u32[]{:S(2)}) %collective-permute-start.22) | collective-permute-done | bytes 262176 | tf_op jit(solution)/shard_map/ppermute | solution.py:350
  94.4 2.4 %collective-permute-done.23.refs_2_ = bf16[128,1024]{1,0:T(8,128)(2,1)S(1)} collective-permute-done((bf16[128,1024]{1,0:T(8,128)(2,1)S(1)}, bf16[128,1024]{1,0:T(8,128)(2,1)S(1)}, u32[]{:S(2)}, u32[]{:S(2)}) %collective-permute-start.23) | collective-permute-done | bytes 262176 | tf_op jit(solution)/shard_map/ppermute | solution.py:350
  98.9 10.3 %collective-permute-done.26.refs_6_ = bf16[256,1024]{1,0:T(8,128)(2,1)S(1)} collective-permute-done((bf16[256,1024]{1,0:T(8,128)(2,1)S(1)}, bf16[256,1024]{1,0:T(8,128)(2,1)S(1)}, u32[]{:S(2)}, u32[]{:S(2)}) %collective-permute-start.26) | collective-permute-done | bytes 524320 | tf_op jit(solution)/shard_map/ppermute | solution.py:436
  110.6 1.9 %shard_map.104 = bf16[128,8192]{1,0:T(8,128)(2,1)} custom-call(s32[2]{0:T(128)S(1)} %pad_add_fusion.2.starts, bf16[256,4096]{1,0:T(8,128)(2,1)S(1)} %convolution_convert_fusion.refs_0_, bf16[128,4096]{1,0:T(8,128)(2,1)S(1)} %collective-permute-done.28.refs_1_), custom_call_target="tpu_custom_call" | custom-call | bytes 4194304 | tf_op jit(solution)/shard_map/pallas_call | solution.py:290
  112.5 6.8 %collective-permute-done.27.refs_3_ = bf16[128,1024]{1,0:T(8,128)(2,1)S(1)} collective-permute-done((bf16[128,1024]{1,0:T(8,128)(2,1)S(1)}, bf16[128,1024]{1,0:T(8,128)(2,1)S(1)}, u32[]{:S(2)}, u32[]{:S(2)}) %collective-permute-start.27) | collective-permute-done | bytes 262176 | tf_op jit(solution)/shard_map/ppermute | solution.py:350
  122.2 9.2 %collective-permute-done.29.refs_4_ = bf16[256,1024]{1,0:T(8,128)(2,1)S(1)} collective-permute-done((bf16[256,1024]{1,0:T(8,128)(2,1)S(1)}, bf16[256,1024]{1,0:T(8,128)(2,1)S(1)}, u32[]{:S(2)}, u32[]{:S(2)}) %collective-permute-start.29) | collective-permute-done | bytes 524320 | tf_op jit(solution)/shard_map/ppermute | solution.py:436
  132.6 3.6 %collective-permute-done.30.came = f32[512,1024]{1,0:T(8,128)S(1)} collective-permute-done((f32[512,1024]{1,0:T(8,128)S(1)}, f32[512,1024]{1,0:T(8,128)S(1)}, u32[]{:S(2)}, u32[]{:S(2)}) %collective-permute-start.30) | collective-permute-done | bytes 2097184 | tf_op jit(solution)/shard_map/ppermute | solution.py:447
  138.3 6.5 %collective-permute-done.31.refs_2_ = bf16[256,512]{1,0:T(8,128)(2,1)S(1)} collective-permute-done((bf16[256,512]{1,0:T(8,128)(2,1)S(1)}, bf16[256,512]{1,0:T(8,128)(2,1)S(1)}, u32[]{:S(2)}, u32[]{:S(2)}) %collective-permute-start.31) | collective-permute-done | bytes 262176 | tf_op jit(solution)/shard_map/ppermute | solution.py:457
  147.2 3.7 %collective-permute-done.33.from_x = bf16[128,512]{1,0:T(8,128)(2,1)S(1)} collective-permute-done((bf16[128,512]{1,0:T(8,128)(2,1)S(1)}, bf16[128,512]{1,0:T(8,128)(2,1)S(1)}, u32[]{:S(2)}, u32[]{:S(2)}) %collective-permute-start.33) | collective-permute-done | bytes 131104 | tf_op jit(solution)/shard_map/ppermute | solution.py:457
  (89 shorter events, 23.4 us)
Async XLA Ops:
  0.6 23.6 %collective-permute-start.6 = (bf16[4096,1024]{1,0:T(8,128)(2,1)}, bf16[4096,1024]{1,0:T(8,128)(2,1)}, u32[]{:S(2)}, u32[]{:S(2)}) collective-permute-start(bf16[4096,1024]{1,0:T(8,128)(2,1)} %bitcast.45), channel_id=1, source_target_pairs={{0,2},{2,0},{1,3},{3,1},{4,6},{6,4},{5,7},{7,5},{8,10},{10,8},{9,1... | collective-permute-start | bytes 25165832 | tf_op jit(solution)/shard_map/ppermute | solution.py:333
  1.1 6.5 %collective-permute-start.4 = (bf16[128,1024]{1,0:T(8,128)(2,1)}, bf16[128,1024]{1,0:T(8,128)(2,1)S(1)}, u32[]{:S(2)}, u32[]{:S(2)}) collective-permute-start(bf16[128,1024]{1,0:T(8,128)(2,1)} %refs_4_.4), channel_id=1, source_target_pairs={{0,2},{2,0},{1,3},{3,1},{4,6},{6,4},{5,7},{7,5},{8,10},{10,8},{9,1... | collective-permute-start | bytes 786440 | tf_op jit(solution)/shard_map/ppermute | solution.py:334
  1.2 9.9 %collective-permute-start = (bf16[128,1024]{1,0:T(8,128)(2,1)}, bf16[128,1024]{1,0:T(8,128)(2,1)S(1)}, u32[]{:S(2)}, u32[]{:S(2)}) collective-permute-start(bf16[128,1024]{1,0:T(8,128)(2,1)} %refs_4_.4), channel_id=1, source_target_pairs={{0,1},{1,0},{2,3},{3,2},{4,5},{5,4},{6,7},{7,6},{8,9},{9,8},{10,11... | collective-permute-start | bytes 786440 | tf_op jit(solution)/shard_map/ppermute | solution.py:324
  7.5 7.9 %collective-permute-start.1 = (bf16[128,1024]{1,0:T(8,128)(2,1)}, bf16[128,1024]{1,0:T(8,128)(2,1)S(1)}, u32[]{:S(2)}, u32[]{:S(2)}) collective-permute-start(bf16[128,1024]{1,0:T(8,128)(2,1)} %get-tuple-element.103), channel_id=1, source_target_pairs={{0,2},{1,3},{2,0},{3,1},{4,6},{5,7},{6,4},{7,5},{8,10},{9,11},{10,... | collective-permute-start | bytes 786440 | tf_op jit(solution)/shard_map/ppermute | solution.py:331
  7.6 9.4 %collective-permute-start.2 = (bf16[128,1024]{1,0:T(8,128)(2,1)}, bf16[128,1024]{1,0:T(8,128)(2,1)S(1)}, u32[]{:S(2)}, u32[]{:S(2)}) collective-permute-start(bf16[128,1024]{1,0:T(8,128)(2,1)} %get-tuple-element.104), channel_id=1, source_target_pairs={{0,1},{1,0},{2,3},{3,2},{4,5},{5,4},{6,7},{7,6},{8,9},{9,8},{10,11... | collective-permute-start | bytes 786440 | tf_op jit(solution)/shard_map/ppermute | solution.py:331
  7.7 14.6 %collective-permute-start.3 = (bf16[128,1024]{1,0:T(8,128)(2,1)S(1)}, bf16[128,1024]{1,0:T(8,128)(2,1)S(1)}, u32[]{:S(2)}, u32[]{:S(2)}) collective-permute-start(bf16[128,1024]{1,0:T(8,128)(2,1)S(1)} %get-tuple-element.105), channel_id=1, source_target_pairs={{0,3},{1,2},{2,1},{3,0},{4,7},{5,6},{6,5},{7,4},{8,11},{9,10},{10,... | collective-permute-start | bytes 786440 | tf_op jit(solution)/shard_map/ppermute | solution.py:331
  11.2 13.0 %collective-permute-start.5 = (bf16[128,1024]{1,0:T(8,128)(2,1)S(1)}, bf16[128,1024]{1,0:T(8,128)(2,1)S(1)}, u32[]{:S(2)}, u32[]{:S(2)}) collective-permute-start(bf16[128,1024]{1,0:T(8,128)(2,1)S(1)} %collective-permute-done.refs_6_), channel_id=1, source_target_pairs={{0,2},{2,0},{1,3},{3,1},{4,6},{6,4},{5,7},{7,5},{8,10},{10,8},{9,1... | collective-permute-start | bytes 786440 | tf_op jit(solution)/shard_map/ppermute | solution.py:336
  15.5 29.3 %collective-permute-start.9 = (bf16[128,1024]{1,0:T(8,128)(2,1)S(1)}, bf16[128,1024]{1,0:T(8,128)(2,1)S(1)}, u32[]{:S(2)}, u32[]{:S(2)}) collective-permute-start(bf16[128,1024]{1,0:T(8,128)(2,1)S(1)} %get-tuple-element.119), channel_id=1, source_target_pairs={{0,2},{1,3},{2,0},{3,1},{4,6},{5,7},{6,4},{7,5},{8,10},{9,11},{10,... | collective-permute-start | bytes 786440 | tf_op jit(solution)/shard_map/ppermute | solution.py:331
  17.0 27.7 %collective-permute-start.10 = (bf16[128,1024]{1,0:T(8,128)(2,1)S(1)}, bf16[128,1024]{1,0:T(8,128)(2,1)S(1)}, u32[]{:S(2)}, u32[]{:S(2)}) collective-permute-start(bf16[128,1024]{1,0:T(8,128)(2,1)S(1)} %get-tuple-element.120), channel_id=1, source_target_pairs={{0,1},{1,0},{2,3},{3,2},{4,5},{5,4},{6,7},{7,6},{8,9},{9,8},{10,11... | collective-permute-start | bytes 786440 | tf_op jit(solution)/shard_map/ppermute | solution.py:331
  22.3 22.4 %collective-permute-start.11 = (bf16[128,1024]{1,0:T(8,128)(2,1)S(1)}, bf16[128,1024]{1,0:T(8,128)(2,1)S(1)}, u32[]{:S(2)}, u32[]{:S(2)}) collective-permute-start(bf16[128,1024]{1,0:T(8,128)(2,1)S(1)} %get-tuple-element.121), channel_id=1, source_target_pairs={{0,3},{1,2},{2,1},{3,0},{4,7},{5,6},{6,5},{7,4},{8,11},{9,10},{10,... | collective-permute-start | bytes 786440 | tf_op jit(solution)/shard_map/ppermute | solution.py:331
  28.3 12.8 %collective-permute-start.7 = (bf16[512,512]{1,0:T(8,128)(2,1)S(1)}, bf16[512,512]{1,0:T(8,128)(2,1)S(1)}, u32[]{:S(2)}, u32[]{:S(2)}) collective-permute-start(bf16[512,512]{1,0:T(8,128)(2,1)S(1)} %get-tuple-element.112), channel_id=1, source_target_pairs={{0,4},{4,0},{1,5},{5,1},{2,6},{6,2},{3,7},{7,3},{8,12},{12,8},{9,1... | collective-permute-start | bytes 1572872 | tf_op jit(solution)/shard_map/ppermute | solution.py:390
  29.8 12.5 %collective-permute-start.8 = (bf16[512,512]{1,0:T(8,128)(2,1)S(1)}, bf16[512,512]{1,0:T(8,128)(2,1)S(1)}, u32[]{:S(2)}, u32[]{:S(2)}) collective-permute-start(bf16[512,512]{1,0:T(8,128)(2,1)S(1)} %get-tuple-element.114), channel_id=1, source_target_pairs={{0,8},{8,0},{16,24},{24,16},{1,9},{9,1},{17,25},{25,17},{2,10},{10... | collective-permute-start | bytes 1572872 | tf_op jit(solution)/shard_map/ppermute | solution.py:390
  42.5 6.4 %collective-permute-start.12 = (bf16[256,512]{1,0:T(8,128)(2,1)S(1)}, bf16[256,512]{1,0:T(8,128)(2,1)S(1)}, u32[]{:S(2)}, u32[]{:S(2)}) collective-permute-start(bf16[256,512]{1,0:T(8,128)(2,1)S(1)} %get-tuple-element.126), channel_id=1, source_target_pairs={{0,8},{8,0},{16,24},{24,16},{1,9},{9,1},{17,25},{25,17},{2,10},{10... | collective-permute-start | bytes 786440 | tf_op jit(solution)/shard_map/ppermute | solution.py:357
  44.2 6.9 %collective-permute-start.13 = (bf16[256,512]{1,0:T(8,128)(2,1)S(1)}, bf16[256,512]{1,0:T(8,128)(2,1)S(1)}, u32[]{:S(2)}, u32[]{:S(2)}) collective-permute-start(bf16[256,512]{1,0:T(8,128)(2,1)S(1)} %get-tuple-element.128), channel_id=1, source_target_pairs={{0,4},{4,0},{1,5},{5,1},{2,6},{6,2},{3,7},{7,3},{8,12},{12,8},{9,1... | collective-permute-start | bytes 786440 | tf_op jit(solution)/shard_map/ppermute | solution.py:357
  51.2 10.6 %collective-permute-start.14 = (bf16[512,512]{1,0:T(8,128)(2,1)S(1)}, bf16[512,512]{1,0:T(8,128)(2,1)S(1)}, u32[]{:S(2)}, u32[]{:S(2)}) collective-permute-start(bf16[512,512]{1,0:T(8,128)(2,1)S(1)} %get-tuple-element.129), channel_id=1, source_target_pairs={{0,4},{4,0},{1,5},{5,1},{2,6},{6,2},{3,7},{7,3},{8,12},{12,8},{9,1... | collective-permute-start | bytes 1572872 | tf_op jit(solution)/shard_map/ppermute | solution.py:390
  51.8 20.9 %collective-permute-start.15 = (bf16[512,512]{1,0:T(8,128)(2,1)S(1)}, bf16[512,512]{1,0:T(8,128)(2,1)S(1)}, u32[]{:S(2)}, u32[]{:S(2)}) collective-permute-start(bf16[512,512]{1,0:T(8,128)(2,1)S(1)} %get-tuple-element.131), channel_id=1, source_target_pairs={{0,8},{8,0},{16,24},{24,16},{1,9},{9,1},{17,25},{25,17},{2,10},{10... | collective-permute-start | bytes 1572872 | tf_op jit(solution)/shard_map/ppermute | solution.py:390
  52.5 26.0 %collective-permute-start.19 = (bf16[256,1024]{1,0:T(8,128)(2,1)S(1)}, bf16[256,1024]{1,0:T(8,128)(2,1)S(1)}, u32[]{:S(2)}, u32[]{:S(2)}) collective-permute-start(bf16[256,1024]{1,0:T(8,128)(2,1)S(1)} %shard_map.98), channel_id=1, source_target_pairs={{0,16},{8,24},{16,0},{24,8},{1,17},{9,25},{17,1},{25,9},{2,18},{10... | collective-permute-start | bytes 1572872 | tf_op jit(solution)/shard_map/ppermute | solution.py:380
  55.1 21.8 %collective-permute-start.16 = (bf16[128,1024]{1,0:T(8,128)(2,1)S(1)}, bf16[128,1024]{1,0:T(8,128)(2,1)S(1)}, u32[]{:S(2)}, u32[]{:S(2)}) collective-permute-start(bf16[128,1024]{1,0:T(8,128)(2,1)S(1)} %copy-done.10), channel_id=1, source_target_pairs={{0,1},{1,0},{2,3},{3,2},{4,5},{5,4},{6,7},{7,6},{8,9},{9,8},{10,11... | collective-permute-start | bytes 786440 | tf_op jit(solution)/shard_map/ppermute | solution.py:350
  56.8 20.2 %collective-permute-start.17 = (bf16[128,1024]{1,0:T(8,128)(2,1)S(1)}, bf16[128,1024]{1,0:T(8,128)(2,1)S(1)}, u32[]{:S(2)}, u32[]{:S(2)}) collective-permute-start(bf16[128,1024]{1,0:T(8,128)(2,1)S(1)} %copy-done.9), channel_id=1, source_target_pairs={{0,2},{1,3},{2,0},{3,1},{4,6},{5,7},{6,4},{7,5},{8,10},{9,11},{10,... | collective-permute-start | bytes 786440 | tf_op jit(solution)/shard_map/ppermute | solution.py:350
  61.8 15.2 %collective-permute-start.18 = (bf16[128,1024]{1,0:T(8,128)(2,1)S(1)}, bf16[128,1024]{1,0:T(8,128)(2,1)S(1)}, u32[]{:S(2)}, u32[]{:S(2)}) collective-permute-start(bf16[128,1024]{1,0:T(8,128)(2,1)S(1)} %copy-done.8), channel_id=1, source_target_pairs={{0,3},{1,2},{2,1},{3,0},{4,7},{5,6},{6,5},{7,4},{8,11},{9,10},{10,... | collective-permute-start | bytes 786440 | tf_op jit(solution)/shard_map/ppermute | solution.py:350
  72.7 26.2 %collective-permute-start.28 = (bf16[128,4096]{1,0:T(8,128)(2,1)S(1)}, bf16[128,4096]{1,0:T(8,128)(2,1)S(1)}, u32[]{:S(2)}, u32[]{:S(2)}) collective-permute-start(bf16[128,4096]{1,0:T(8,128)(2,1)S(1)} %slice.4), channel_id=1, source_target_pairs={{0,1},{1,0},{2,3},{3,2},{4,5},{5,4},{6,7},{7,6},{8,9},{9,8},{10,11... | collective-permute-start | bytes 3145736 | tf_op jit(solution)/shard_map/ppermute | solution.py:389
  77.0 6.8 %collective-permute-start.20 = (bf16[256,512]{1,0:T(8,128)(2,1)S(1)}, bf16[256,512]{1,0:T(8,128)(2,1)S(1)}, u32[]{:S(2)}, u32[]{:S(2)}) collective-permute-start(bf16[256,512]{1,0:T(8,128)(2,1)S(1)} %get-tuple-element.149), channel_id=1, source_target_pairs={{0,8},{8,0},{16,24},{24,16},{1,9},{9,1},{17,25},{25,17},{2,10},{10... | collective-permute-start | bytes 786440 | tf_op jit(solution)/shard_map/ppermute | solution.py:357
  77.1 6.8 %collective-permute-start.21 = (bf16[256,512]{1,0:T(8,128)(2,1)S(1)}, bf16[256,512]{1,0:T(8,128)(2,1)S(1)}, u32[]{:S(2)}, u32[]{:S(2)}) collective-permute-start(bf16[256,512]{1,0:T(8,128)(2,1)S(1)} %get-tuple-element.151), channel_id=1, source_target_pairs={{0,4},{4,0},{1,5},{5,1},{2,6},{6,2},{3,7},{7,3},{8,12},{12,8},{9,1... | collective-permute-start | bytes 786440 | tf_op jit(solution)/shard_map/ppermute | solution.py:357
  85.5 23.6 %collective-permute-start.26 = (bf16[256,1024]{1,0:T(8,128)(2,1)S(1)}, bf16[256,1024]{1,0:T(8,128)(2,1)S(1)}, u32[]{:S(2)}, u32[]{:S(2)}) collective-permute-start(bf16[256,1024]{1,0:T(8,128)(2,1)S(1)} %get-tuple-element.157.refs_4_), channel_id=1, source_target_pairs={{0,16},{8,24},{16,0},{24,8},{1,17},{9,25},{17,1},{25,9},{2,18},{10... | collective-permute-start | bytes 1572872 | tf_op jit(solution)/shard_map/ppermute | solution.py:436
  86.0 8.4 %collective-permute-start.22 = (bf16[128,1024]{1,0:T(8,128)(2,1)S(1)}, bf16[128,1024]{1,0:T(8,128)(2,1)S(1)}, u32[]{:S(2)}, u32[]{:S(2)}) collective-permute-start(bf16[128,1024]{1,0:T(8,128)(2,1)S(1)} %copy-done.7), channel_id=1, source_target_pairs={{0,4},{1,5},{2,6},{3,7},{4,0},{5,1},{6,2},{7,3},{8,12},{9,13},{10,... | collective-permute-start | bytes 786440 | tf_op jit(solution)/shard_map/ppermute | solution.py:350
  87.4 9.5 %collective-permute-start.23 = (bf16[128,1024]{1,0:T(8,128)(2,1)S(1)}, bf16[128,1024]{1,0:T(8,128)(2,1)S(1)}, u32[]{:S(2)}, u32[]{:S(2)}) collective-permute-start(bf16[128,1024]{1,0:T(8,128)(2,1)S(1)} %copy-done.6), channel_id=1, source_target_pairs={{0,6},{1,7},{2,4},{3,5},{4,2},{5,3},{6,0},{7,1},{8,14},{9,15},{10,... | collective-permute-start | bytes 786440 | tf_op jit(solution)/shard_map/ppermute | solution.py:350
  96.9 23.4 %collective-permute-start.25 = (bf16[256,1024]{1,0:T(8,128)(2,1)S(1)}, bf16[256,1024]{1,0:T(8,128)(2,1)S(1)}, u32[]{:S(2)}, u32[]{:S(2)}) collective-permute-start(bf16[256,1024]{1,0:T(8,128)(2,1)S(1)} %get-tuple-element.157.refs_4_), channel_id=1, source_target_pairs={{0,8},{8,0},{16,24},{24,16},{1,9},{9,1},{17,25},{25,17},{2,10},{10... | collective-permute-start | bytes 1572872 | tf_op jit(solution)/shard_map/ppermute | solution.py:436
  109.1 22.3 %collective-permute-start.29 = (bf16[256,1024]{1,0:T(8,128)(2,1)S(1)}, bf16[256,1024]{1,0:T(8,128)(2,1)S(1)}, u32[]{:S(2)}, u32[]{:S(2)}) collective-permute-start(bf16[256,1024]{1,0:T(8,128)(2,1)S(1)} %collective-permute-done.26.refs_6_), channel_id=1, source_target_pairs={{0,8},{8,0},{16,24},{24,16},{1,9},{9,1},{17,25},{25,17},{2,10},{10... | collective-permute-start | bytes 1572872 | tf_op jit(solution)/shard_map/ppermute | solution.py:436
  109.1 10.1 %collective-permute-start.27 = (bf16[128,1024]{1,0:T(8,128)(2,1)S(1)}, bf16[128,1024]{1,0:T(8,128)(2,1)S(1)}, u32[]{:S(2)}, u32[]{:S(2)}) collective-permute-start(bf16[128,1024]{1,0:T(8,128)(2,1)S(1)} %copy-done.5), channel_id=1, source_target_pairs={{0,5},{1,4},{2,7},{3,6},{4,1},{5,0},{6,3},{7,2},{8,13},{9,12},{10,... | collective-permute-start | bytes 786440 | tf_op jit(solution)/shard_map/ppermute | solution.py:350
  110.5 10.7 %collective-permute-start.24 = (bf16[128,1024]{1,0:T(8,128)(2,1)S(1)}, bf16[128,1024]{1,0:T(8,128)(2,1)S(1)}, u32[]{:S(2)}, u32[]{:S(2)}) collective-permute-start(bf16[128,1024]{1,0:T(8,128)(2,1)S(1)} %copy-done.4), channel_id=1, source_target_pairs={{0,7},{1,6},{2,5},{3,4},{4,3},{5,2},{6,1},{7,0},{8,15},{9,14},{10,... | collective-permute-start | bytes 786440 | tf_op jit(solution)/shard_map/ppermute | solution.py:350
  136.4 8.4 %collective-permute-start.31 = (bf16[256,512]{1,0:T(8,128)(2,1)S(1)}, bf16[256,512]{1,0:T(8,128)(2,1)S(1)}, u32[]{:S(2)}, u32[]{:S(2)}) collective-permute-start(bf16[256,512]{1,0:T(8,128)(2,1)S(1)} %get-tuple-element.172), channel_id=1, source_target_pairs={{0,4},{4,0},{1,5},{5,1},{2,6},{6,2},{3,7},{7,3},{8,12},{12,8},{9,1... | collective-permute-start | bytes 786440 | tf_op jit(solution)/shard_map/ppermute | solution.py:457
  137.7 8.1 %collective-permute-start.32 = (bf16[256,512]{1,0:T(8,128)(2,1)S(1)}, bf16[256,512]{1,0:T(8,128)(2,1)S(1)}, u32[]{:S(2)}, u32[]{:S(2)}) collective-permute-start(bf16[256,512]{1,0:T(8,128)(2,1)S(1)} %get-tuple-element.173), channel_id=1, source_target_pairs={{0,1},{1,0},{2,3},{3,2},{4,5},{5,4},{6,7},{7,6},{8,9},{9,8},{10,11... | collective-permute-start | bytes 786440 | tf_op jit(solution)/shard_map/ppermute | solution.py:458
  (16 other events, 188.7 us)

commit v6 on v5

--- a/solution.py
+++ b/solution.py
@@ -114,7 +114,7 @@
         here = slice(i * share, (i + 1) * share)
         return (rows[0, here, columns].astype(f32) + rows[1, here, columns].astype(f32)) - scale * total[here, columns]
 
-    first, second = slice(0, kv // 2), slice(kv // 2, kv)
+    first, second = slice(0, to_x.shape[1]), slice(to_x.shape[1], kv)
     for n in range(2):
         here = slice(n * share, (n + 1) * share)
         to_x[here, :] = inner_new(PAIR * n + 1, first).astype(bf16)
@@ -125,16 +125,16 @@
         stay_z[here, :] = inner_new(PAIR + n, second)
 
 
-def inner_blocks(place, acts, act_at, cots, own, other, share):
+def inner_blocks(place, acts, act_at, cots, own, other, share, cut):
     pieces = len(acts)
     tok, kv = cots[0].shape
     rows = 2 * PAIR * share
     if act_at % LANES or rows % LANES:
         acts, act_at = [a[:, act_at : act_at + rows] for a in acts], 0
-    sent, kept = (jax.ShapeDtypeStruct((2 * share, kv // 2), kind) for kind in (bf16, f32))
+    shapes = [jax.ShapeDtypeStruct((2 * share, wide), kind) for wide in (cut, kv - cut) for kind in (bf16, f32)]
     return pl.pallas_call(
         functools.partial(inner_kernel, pieces, share, inner_rate / (tok * pieces // CORES), act_at),
-        out_shape=[sent, kept, sent, kept],
+        out_shape=shapes,
         in_specs=[SMEM] + [ANY] * (2 * pieces) + [HBM, ANY],
         out_specs=[pl.BlockSpec()] * 4,
         scratch_shapes=[
@@ -294,7 +294,7 @@
         out_specs=HBM,
         scratch_shapes=[pltpu.SemaphoreType.DMA((len(parts),))],
         compiler_params=pltpu.CompilerParams(vmem_limit_bytes=16 * MIB),
-        cost_estimate=pl.CostEstimate(flops=0, bytes_accessed=4 * rows * width * len(parts), transcendentals=0),
+        cost_estimate=pl.CostEstimate(flops=1 << 34, bytes_accessed=4 * rows * width * len(parts), transcendentals=0),
     )(jnp.stack(starts).astype(jnp.int32), *parts)
 
 
@@ -357,8 +357,8 @@
         from_z, from_x = lax.ppermute(to_z, "z", across_z), lax.ppermute(to_x, "x", across_x)
         return [keep_left, from_z, keep_right, from_x] + over_z.get(m, [])
 
-    shape = lambda n, kind: jax.ShapeDtypeStruct((n * share, kv // 2), kind)
     for stage, ms in enumerate(stages):
+        cut = kv // 2 if ms[1] else 3 * kv // 4
         blocks = [((z ^ m) * PAIR + (x + i) % PAIR) * CORES + c for m in ms for i in range(PAIR)]
         place = jnp.stack(blocks).astype(jnp.int32)
         if not stage:
@@ -370,13 +370,13 @@
             place, to_z, to_x = lax.optimization_barrier((place, to_z, to_x))
             m = stages[stage - 1][1]
             inputs = finish(m, to_z, to_x, keep_left, keep_right)
+            low = m & -m
+        to_x, stay_x, to_z, stay_z = inner_blocks(place, acts[stage], 0, ordered, own_weight, other_weight, share, cut)
+        if stage:
+            to_x, to_z, inputs[1], inputs[3] = lax.optimization_barrier((to_x, to_z, inputs[1], inputs[3]))
             (block_total,) = small_call(
                 block_kernel, [jax.ShapeDtypeStruct((share, kv), bf16)], *inputs, spec=pl.BlockSpec()
             )
-            low = m & -m
-        to_x, stay_x, to_z, stay_z = inner_blocks(place, acts[stage], 0, ordered, own_weight, other_weight, share)
-        if stage:
-            to_x, to_z, block_total = lax.optimization_barrier((to_x, to_z, block_total))
             over_z.setdefault(m ^ low, []).append(lax.ppermute(block_total, "z", [(i, i ^ low) for i in range(nz)]))
         if not stage:
             stay_x, *island_cots = lax.optimization_barrier((stay_x, *[cots[0, s] for s in range(fsdp)]))
@@ -390,7 +390,7 @@
         from_x, from_z = lax.ppermute(to_x, "x", across_x), lax.ppermute(to_z, "z", across_z)
         to_z, keep_left, to_x, keep_right = small_call(
             functools.partial(middle_kernel, share),
-            [shape(1, bf16), shape(1, f32)] * 2,
+            [jax.ShapeDtypeStruct((share, wide), kind) for wide in (cut, kv - cut) for kind in (bf16, f32)],
             stay_x,
             from_x,
             stay_z,
@@ -399,15 +399,13 @@
         )
 
     straight, diagonal = [e for e in away if e[2] == 0], [e for e in away if e[2]]
-    held = (to_z, to_x, *[nexts[e] for e in near], *[mine[e] for e in straight])
-    to_z, to_x, *held = lax.optimization_barrier(held)
-    nexts.update(zip(near, held))
-    mine.update(zip(straight, held[len(near) :]))
+    to_z, to_x, *held = lax.optimization_barrier((to_z, to_x, *[mine[e] for e in straight]))
+    mine.update(zip(straight, held))
     inputs = finish(0, to_z, to_x, keep_left, keep_right)
     for e in straight:
         send_next(*e)
     inputs[0], inputs[2] = small_call(
-        gather_kernel, [shape(1, f32)] * 2, keep_left, keep_right, *inputs[4:], spec=pl.BlockSpec(), weight=1 << 17
+        gather_kernel, [jax.ShapeDtypeStruct(part.shape, f32) for part in (keep_left, keep_right)], keep_left, keep_right, *inputs[4:], spec=pl.BlockSpec(), weight=200
     )
     inputs[0], *held = lax.optimization_barrier((inputs[0], *[mine[e] for e in diagonal]))
     mine.update(zip(diagonal, held))
@@ -428,14 +426,15 @@
     for m in sorted(range(1, nz), key=lambda m: (m & (m - 1)).bit_count() * nz - m):
         low = m & -m
         pieces = [share_rows] if m == low else list(rows[m ^ low])
-        if m == 1:
-            pieces[0], *held = lax.optimization_barrier((pieces[0], *[nexts[e] for e in straight]))
-            nexts.update(zip(straight, held))
         if m == nz - 1:
-            pieces[0], *parts = lax.optimization_barrier((pieces[0], *parts))
+            held = (share_rows, *parts, *[nexts[e] for e in far])
+            share_rows, *held = lax.optimization_barrier(held)
+            parts, held = held[: len(parts)], held[len(parts) :]
+            nexts.update(zip(far, held))
+            input_grad = join(parts, [((f + s) % fsdp) * width for s in range(fsdp)])
+            pieces[0], input_grad = lax.optimization_barrier((pieces[0], input_grad))
         rows[m] = [lax.ppermute(piece, "z", [(i, i ^ low) for i in range(nz)]) for piece in pieces]
     rows = [[share_rows]] + [rows[m] for m in range(1, nz)]
-    input_grad = join(parts, [((f + s) % fsdp) * width for s in range(fsdp)])
 
     half = len(far) // CORES
     near, away = [nexts[e] for e in far[:half]], [nexts[e] for e in far[half:]]

time: 153 us -> 156 us (1.020)
  waiting for transfers between devices: 90 us -> 94.4 us
    ppermute x7, waiting for transfers between devices: 16.3 us -> 30.2 us  [send_next(): lax.ppermute(mine[i, k, s], ('x', 'core', 'fsdp'), pairs)]
    ppermute x2, waiting for transfers between devices: 5.64 us -> 0.53 us  [finish(): lax.ppermute(to_z, 'z', across_z)]
    ppermute x2, waiting for transfers between devices: 12.2 us -> 8.98 us  [local(): lax.ppermute(to_x, 'x', across_x)]
    ppermute x2, waiting for transfers between devices: 11.9 us -> 9.53 us  [local(): lax.ppermute(to_z, 'z', across_z)]
    ppermute x1, starting transfers between devices: 4.08 us -> 1.77 us  [local(): parts[s] = lax.ppermute(parts[s], 'fsdp', ring(fsdp, -s))]
  transfers between devices with their start and end apart: 35 -> 35, of which waited for: 23 -> 22; matrix products, arithmetic and copies ran while one was open for 2% -> 2% of each run, Pallas kernels for 14% -> 14%
where the time goes in v6:
time: 156 us
  waiting for transfers between devices  94.4 us (61%)
  starting transfers between devices  34.5 us (22%)
  Pallas kernels  23 us (15%)
  matrix products  2.38 us (2%)
    ppermute x7, waiting for transfers between devices, send_next(): lax.ppermute(mine[i, k, s], ('x', 'core', 'fsdp'), pairs)  30.2 us
    ppermute x3, waiting for transfers between devices, local(): lax.ppermute(piece, 'z', [(i, i ^ low) for i in range(nz)])  21.7 us
    ppermute x2, waiting for transfers between devices, home(): from_x = lax.ppermute(to_x, 'x', ring(PAIR, 1))  10.8 us
    ppermute x2, waiting for transfers between devices, local(): lax.ppermute(to_z, 'z', across_z)  9.53 us
    ppermute x2, waiting for transfers between devices, local(): lax.ppermute(to_x, 'x', across_x)  8.98 us
    pallas_call x2, Pallas kernels, inner_blocks(): pl.pallas_call(functools.partial(inner_kernel, pieces, share, inner_rate...  7.74 us
    ppermute x6, starting transfers between devices, local(): lax.ppermute(part, ('core', 'fsdp'), pair_ring(k, s))  7.52 us
    pallas_call x2, Pallas kernels, pack(): pl.pallas_call(functools.partial(pack_kernel, plan), out_shape=shapes, in...  7.2 us
  transfers between devices with their start and end apart: 35, of which 22 were waited for; matrix products, arithmetic and copies ran while one was open for 2% of the time, Pallas kernels for 14%

profile of v6, /device:TPU:0, one launch (start us, length us, event | category | flops | bytes accessed | tf_op | source)
XLA Modules:
  0.0 155.8 jit_solution(13007247506519891464)
XLA Ops:
  1.2 2.9 %collective-permute-start = (bf16[128,1024]{1,0:T(8,128)(2,1)}, bf16[128,1024]{1,0:T(8,128)(2,1)S(1)}, u32[]{:S(2)}, u32[]{:S(2)}) collective-permute-start(bf16[128,1024]{1,0:T(8,128)(2,1)} %refs_4_.4), channel_id=1, source_target_pairs={{0,1},{1,0},{2,3},{3,2},{4,5},{5,4},{6,7},{7,6},{8,9},{9,8},{10,11... | collective-permute-start | bytes 786440 | tf_op jit(solution)/shard_map/ppermute | solution.py:324
  4.3 3.2 %shard_map.94 = (bf16[128,1024]{1,0:T(8,128)(2,1)S(1)}, bf16[128,1024]{1,0:T(8,128)(2,1)}, bf16[128,1024]{1,0:T(8,128)(2,1)}, bf16[128,1024]{1,0:T(8,128)(2,1)S(...) custom-call(s32[32]{0:T(128)S(1)} %stack.216.starts, ...), custom_call_target="tpu_custom_call" | custom-call | bytes 16777216 | tf_op jit(solution)/shard_map/pallas_call | solution.py:72
  7.7 2.7 %collective-permute-start.3 = (bf16[128,1024]{1,0:T(8,128)(2,1)S(1)}, bf16[128,1024]{1,0:T(8,128)(2,1)S(1)}, u32[]{:S(2)}, u32[]{:S(2)}) collective-permute-start(bf16[128,1024]{1,0:T(8,128)(2,1)S(1)} %get-tuple-element.109), channel_id=1, source_target_pairs={{0,3},{1,2},{2,1},{3,0},{4,7},{5,6},{6,5},{7,4},{8,11},{9,10},{10,... | collective-permute-start | bytes 786440 | tf_op jit(solution)/shard_map/ppermute | solution.py:331
  11.5 4.0 %shard_map.93 = (bf16[128,1024]{1,0:T(8,128)(2,1)}, bf16[128,1024]{1,0:T(8,128)(2,1)}, bf16[128,1024]{1,0:T(8,128)(2,1)}, bf16[128,1024]{1,0:T(8,128)(2,1)}, bf1...) custom-call(s32[32]{0:T(128)S(1)} %stack.215.starts, ...), custom_call_target="tpu_custom_call" | custom-call | bytes 16777216 | tf_op jit(solution)/shard_map/pallas_call | solution.py:72
  17.0 2.2 %collective-permute-start.10 = (bf16[128,1024]{1,0:T(8,128)(2,1)S(1)}, bf16[128,1024]{1,0:T(8,128)(2,1)S(1)}, u32[]{:S(2)}, u32[]{:S(2)}) collective-permute-start(bf16[128,1024]{1,0:T(8,128)(2,1)S(1)} %get-tuple-element.124), channel_id=1, source_target_pairs={{0,1},{1,0},{2,3},{3,2},{4,5},{5,4},{6,7},{7,6},{8,9},{9,8},{10,11... | collective-permute-start | bytes 786440 | tf_op jit(solution)/shard_map/ppermute | solution.py:331
  19.2 3.1 %collective-permute-done.3.refs_3_ = bf16[128,1024]{1,0:T(8,128)(2,1)S(1)} collective-permute-done((bf16[128,1024]{1,0:T(8,128)(2,1)S(1)}, bf16[128,1024]{1,0:T(8,128)(2,1)S(1)}, u32[]{:S(2)}, u32[]{:S(2)}) %collective-permute-start.3) | collective-permute-done | bytes 262176 | tf_op jit(solution)/shard_map/ppermute | solution.py:331
  22.3 1.9 %collective-permute-start.11 = (bf16[128,1024]{1,0:T(8,128)(2,1)S(1)}, bf16[128,1024]{1,0:T(8,128)(2,1)S(1)}, u32[]{:S(2)}, u32[]{:S(2)}) collective-permute-start(bf16[128,1024]{1,0:T(8,128)(2,1)S(1)} %get-tuple-element.125), channel_id=1, source_target_pairs={{0,3},{1,2},{2,1},{3,0},{4,7},{5,6},{6,5},{7,4},{8,11},{9,10},{10,... | collective-permute-start | bytes 786440 | tf_op jit(solution)/shard_map/ppermute | solution.py:331
  24.2 4.0 %shard_map.95 = (bf16[512,512]{1,0:T(8,128)(2,1)S(1)}, f32[512,512]{1,0:T(8,128)S(1)}, bf16[512,512]{1,0:T(8,128)(2,1)S(1)}, f32[512,512]{1,0:T(8,128)S(1)}) custom-call(s32[4]{0:T(128)S(1)} %pad_add_fusion.1.place, bf16[128,1024]{1,0:T(8,128)(2,1)S(1)} %get-tuple-element.106.refs_0_, bf16[128,1024]{1,0:T(8,128)(2,1)S(1)} %collective-permute-done.1.refs_1_, ...), custom_call_target="tpu_custom_call" | custom-call | flops 134217728 | bytes 262144 | tf_op jit(solution)/shard_map/pallas_call | solution.py:135
  28.3 1.6 collective-permute-start.7
  29.8 1.6 %collective-permute-start.8 = (bf16[512,512]{1,0:T(8,128)(2,1)S(1)}, bf16[512,512]{1,0:T(8,128)(2,1)S(1)}, u32[]{:S(2)}, u32[]{:S(2)}) collective-permute-start(bf16[512,512]{1,0:T(8,128)(2,1)S(1)} %get-tuple-element.118), channel_id=1, source_target_pairs={{0,8},{8,0},{16,24},{24,16},{1,9},{9,1},{17,25},{25,17},{2,10},{10... | collective-permute-start | bytes 1572872 | tf_op jit(solution)/shard_map/ppermute | solution.py:390
  31.4 2.4 %convolution_convert_fusion.refs_0_ = bf16[256,4096]{1,0:T(8,128)(2,1)S(1)} fusion(bf16[128,1024]{1,0:T(8,128)(2,1)S(1)} %collective-permute-done.refs_6_, bf16[128,1024]{1,0:T(8,128)(2,1)S(1)} %copy-done, bf16[1,4096,1024]{2,1,0:T(8,128)(2,1)S(1)} %bitcast.49), kind=kOutput, calls=%fused_computation | convolution fusion | flops 2149580800 | bytes 11010048 | tf_op jit(solution)/shard_map/dot_general | solution.py:383
  33.9 7.2 %collective-permute-done.7.from_x = bf16[512,512]{1,0:T(8,128)(2,1)S(1)} collective-permute-done((bf16[512,512]{1,0:T(8,128)(2,1)S(1)}, bf16[512,512]{1,0:T(8,128)(2,1)S(1)}, u32[]{:S(2)}, u32[]{:S(2)}) %collective-permute-start.7) | collective-permute-done | bytes 524320 | tf_op jit(solution)/shard_map/ppermute | solution.py:390
  42.5 1.6 %collective-permute-start.12 = (bf16[256,512]{1,0:T(8,128)(2,1)S(1)}, bf16[256,512]{1,0:T(8,128)(2,1)S(1)}, u32[]{:S(2)}, u32[]{:S(2)}) collective-permute-start(bf16[256,512]{1,0:T(8,128)(2,1)S(1)} %get-tuple-element.129), channel_id=1, source_target_pairs={{0,8},{8,0},{16,24},{24,16},{1,9},{9,1},{17,25},{25,17},{2,10},{10... | collective-permute-start | bytes 786440 | tf_op jit(solution)/shard_map/ppermute | solution.py:357
  44.7 3.7 %shard_map.97 = (bf16[512,768]{1,0:T(8,128)(2,1)S(1)}, f32[512,768]{1,0:T(8,128)S(1)}, bf16[512,256]{1,0:T(8,128)(2,1)S(1)}, f32[512,256]{1,0:T(8,128)S(1)}) custom-call(s32[4]{0:T(128)S(1)} %pad_add_fusion.place, bf16[128,1024]{1,0:T(8,128)(2,1)S(1)} %get-tuple-element.122.refs_0_, bf16[128,1024]{1,0:T(8,128)(2,1)S(1)} %collective-permute-done.9.refs_1_, ...), custom_call_target="tpu_custom_call" | custom-call | flops 134217728 | bytes 262144 | tf_op jit(solution)/shard_map/pallas_call | solution.py:135
  49.0 2.3 %collective-permute-done.13.refs_3_ = bf16[256,512]{1,0:T(8,128)(2,1)S(1)} collective-permute-done((bf16[256,512]{1,0:T(8,128)(2,1)S(1)}, bf16[256,512]{1,0:T(8,128)(2,1)S(1)}, u32[]{:S(2)}, u32[]{:S(2)}) %collective-permute-start.13) | collective-permute-done | bytes 262176 | tf_op jit(solution)/shard_map/ppermute | solution.py:357
  51.8 1.8 %collective-permute-start.19 = (bf16[128,4096]{1,0:T(8,128)(2,1)S(1)}, bf16[128,4096]{1,0:T(8,128)(2,1)S(1)}, u32[]{:S(2)}, u32[]{:S(2)}) collective-permute-start(bf16[128,4096]{1,0:T(8,128)(2,1)S(1)} %slice.4), channel_id=1, source_target_pairs={{0,1},{1,0},{2,3},{3,2},{4,5},{5,4},{6,7},{7,6},{8,9},{9,8},{10,11... | collective-permute-start | bytes 3145736 | tf_op jit(solution)/shard_map/ppermute | solution.py:389
  54.1 2.6 %collective-permute-start.16 = (bf16[256,1024]{1,0:T(8,128)(2,1)S(1)}, bf16[256,1024]{1,0:T(8,128)(2,1)S(1)}, u32[]{:S(2)}, u32[]{:S(2)}) collective-permute-start(bf16[256,1024]{1,0:T(8,128)(2,1)S(1)} %shard_map.99), channel_id=1, source_target_pairs={{0,16},{8,24},{16,0},{24,8},{1,17},{9,25},{17,1},{25,9},{2,18},{10... | collective-permute-start | bytes 1572872 | tf_op jit(solution)/shard_map/ppermute | solution.py:380
  57.3 8.3 %collective-permute-done.15.from_z = bf16[512,256]{1,0:T(8,128)(2,1)S(1)} collective-permute-done((bf16[512,256]{1,0:T(8,128)(2,1)S(1)}, bf16[512,256]{1,0:T(8,128)(2,1)S(1)}, u32[]{:S(2)}, u32[]{:S(2)}) %collective-permute-start.15) | collective-permute-done | bytes 262176 | tf_op jit(solution)/shard_map/ppermute | solution.py:390
  65.7 1.7 %collective-permute-done.14.from_x = bf16[512,768]{1,0:T(8,128)(2,1)S(1)} collective-permute-done((bf16[512,768]{1,0:T(8,128)(2,1)S(1)}, bf16[512,768]{1,0:T(8,128)(2,1)S(1)}, u32[]{:S(2)}, u32[]{:S(2)}) %collective-permute-start.14) | collective-permute-done | bytes 786464 | tf_op jit(solution)/shard_map/ppermute | solution.py:390
  68.2 12.3 %collective-permute-done.20.refs_1_ = bf16[128,1024]{1,0:T(8,128)(2,1)S(1)} collective-permute-done((bf16[128,1024]{1,0:T(8,128)(2,1)S(1)}, bf16[128,1024]{1,0:T(8,128)(2,1)S(1)}, u32[]{:S(2)}, u32[]{:S(2)}) %collective-permute-start.20) | collective-permute-done | bytes 262176 | tf_op jit(solution)/shard_map/ppermute | solution.py:350
  82.7 6.0 %collective-permute-done.24.refs_1_ = bf16[128,1024]{1,0:T(8,128)(2,1)S(1)} collective-permute-done((bf16[128,1024]{1,0:T(8,128)(2,1)S(1)}, bf16[128,1024]{1,0:T(8,128)(2,1)S(1)}, u32[]{:S(2)}, u32[]{:S(2)}) %collective-permute-start.24) | collective-permute-done | bytes 262176 | tf_op jit(solution)/shard_map/ppermute | solution.py:350
  90.5 2.0 %collective-permute-start.26 = (bf16[128,1024]{1,0:T(8,128)(2,1)S(1)}, bf16[128,1024]{1,0:T(8,128)(2,1)S(1)}, u32[]{:S(2)}, u32[]{:S(2)}) collective-permute-start(bf16[128,1024]{1,0:T(8,128)(2,1)S(1)} %copy-done.4), channel_id=1, source_target_pairs={{0,7},{1,6},{2,5},{3,4},{4,3},{5,2},{6,1},{7,0},{8,15},{9,14},{10,... | collective-permute-start | bytes 786440 | tf_op jit(solution)/shard_map/ppermute | solution.py:350
  92.6 1.7 %shard_map.101 = (bf16[256,1024]{1,0:T(8,128)(2,1)S(1)}, f32[256,1024]{1,0:T(8,128)}, f32[256,1024]{1,0:T(8,128)}) custom-call(f32[256,768]{1,0:T(8,128)S(1)} %get-tuple-element.143.refs_0_, bf16[256,768]{1,0:T(8,128)(2,1)S(1)} %collective-permute-done.17.refs_1_, f32[256,256]{1,0:T(8,128)S(1)} %get-tuple-element.149.refs_2_, ...), custom_call_target="tpu_custom_call" | custom-call | flops 98304 | bytes 98304 | tf_op jit(solution)/shard_map/pallas_call | solution.py:265
  94.2 2.6 %collective-permute-start.28 = (bf16[256,1024]{1,0:T(8,128)(2,1)S(1)}, bf16[256,1024]{1,0:T(8,128)(2,1)S(1)}, u32[]{:S(2)}, u32[]{:S(2)}) collective-permute-start(bf16[256,1024]{1,0:T(8,128)(2,1)S(1)} %get-tuple-element.166.refs_4_), channel_id=1, source_target_pairs={{0,16},{8,24},{16,0},{24,8},{1,17},{9,25},{17,1},{25,9},{2,18},{10... | collective-permute-start | bytes 1572872 | tf_op jit(solution)/shard_map/ppermute | solution.py:436
  98.2 6.7 %collective-permute-done.22.refs_3_ = bf16[128,1024]{1,0:T(8,128)(2,1)S(1)} collective-permute-done((bf16[128,1024]{1,0:T(8,128)(2,1)S(1)}, bf16[128,1024]{1,0:T(8,128)(2,1)S(1)}, u32[]{:S(2)}, u32[]{:S(2)}) %collective-permute-start.22) | collective-permute-done | bytes 262176 | tf_op jit(solution)/shard_map/ppermute | solution.py:350
  104.9 4.4 %collective-permute-done.26.refs_3_ = bf16[128,1024]{1,0:T(8,128)(2,1)S(1)} collective-permute-done((bf16[128,1024]{1,0:T(8,128)(2,1)S(1)}, bf16[128,1024]{1,0:T(8,128)(2,1)S(1)}, u32[]{:S(2)}, u32[]{:S(2)}) %collective-permute-start.26) | collective-permute-done | bytes 262176 | tf_op jit(solution)/shard_map/ppermute | solution.py:350
  109.3 1.9 %shard_map.104 = bf16[128,8192]{1,0:T(8,128)(2,1)} custom-call(s32[2]{0:T(128)S(1)} %pad_add_fusion.2.starts, bf16[256,4096]{1,0:T(8,128)(2,1)S(1)} %convolution_convert_fusion.refs_0_, bf16[128,4096]{1,0:T(8,128)(2,1)S(1)} %collective-permute-done.19.refs_1_), custom_call_target="tpu_custom_call" | custom-call | flops 17179869184 | bytes 4194304 | tf_op jit(solution)/shard_map/pallas_call | solution.py:290
  111.2 9.8 %collective-permute-done.28.refs_6_ = bf16[256,1024]{1,0:T(8,128)(2,1)S(1)} collective-permute-done((bf16[256,1024]{1,0:T(8,128)(2,1)S(1)}, bf16[256,1024]{1,0:T(8,128)(2,1)S(1)}, u32[]{:S(2)}, u32[]{:S(2)}) %collective-permute-start.28) | collective-permute-done | bytes 524320 | tf_op jit(solution)/shard_map/ppermute | solution.py:436
  124.2 10.7 %collective-permute-done.29.refs_4_ = bf16[256,1024]{1,0:T(8,128)(2,1)S(1)} collective-permute-done((bf16[256,1024]{1,0:T(8,128)(2,1)S(1)}, bf16[256,1024]{1,0:T(8,128)(2,1)S(1)}, u32[]{:S(2)}, u32[]{:S(2)}) %collective-permute-start.29) | collective-permute-done | bytes 524320 | tf_op jit(solution)/shard_map/ppermute | solution.py:436
  135.9 3.7 %collective-permute-done.30.came = f32[512,1024]{1,0:T(8,128)S(1)} collective-permute-done((f32[512,1024]{1,0:T(8,128)S(1)}, f32[512,1024]{1,0:T(8,128)S(1)}, u32[]{:S(2)}, u32[]{:S(2)}) %collective-permute-start.30) | collective-permute-done | bytes 2097184 | tf_op jit(solution)/shard_map/ppermute | solution.py:446
  140.7 7.5 %collective-permute-done.31.refs_2_ = bf16[256,512]{1,0:T(8,128)(2,1)S(1)} collective-permute-done((bf16[256,512]{1,0:T(8,128)(2,1)S(1)}, bf16[256,512]{1,0:T(8,128)(2,1)S(1)}, u32[]{:S(2)}, u32[]{:S(2)}) %collective-permute-start.31) | collective-permute-done | bytes 262176 | tf_op jit(solution)/shard_map/ppermute | solution.py:456
  150.4 3.3 %collective-permute-done.33.from_x = bf16[128,512]{1,0:T(8,128)(2,1)S(1)} collective-permute-done((bf16[128,512]{1,0:T(8,128)(2,1)S(1)}, bf16[128,512]{1,0:T(8,128)(2,1)S(1)}, u32[]{:S(2)}, u32[]{:S(2)}) %collective-permute-start.33) | collective-permute-done | bytes 131104 | tf_op jit(solution)/shard_map/ppermute | solution.py:456
  (89 shorter events, 23.4 us)
Async XLA Ops:
  0.6 23.6 %collective-permute-start.6 = (bf16[4096,1024]{1,0:T(8,128)(2,1)}, bf16[4096,1024]{1,0:T(8,128)(2,1)}, u32[]{:S(2)}, u32[]{:S(2)}) collective-permute-start(bf16[4096,1024]{1,0:T(8,128)(2,1)} %bitcast.45), channel_id=1, source_target_pairs={{0,2},{2,0},{1,3},{3,1},{4,6},{6,4},{5,7},{7,5},{8,10},{10,8},{9,1... | collective-permute-start | bytes 25165832 | tf_op jit(solution)/shard_map/ppermute | solution.py:333
  1.1 6.5 %collective-permute-start.4 = (bf16[128,1024]{1,0:T(8,128)(2,1)}, bf16[128,1024]{1,0:T(8,128)(2,1)S(1)}, u32[]{:S(2)}, u32[]{:S(2)}) collective-permute-start(bf16[128,1024]{1,0:T(8,128)(2,1)} %refs_4_.4), channel_id=1, source_target_pairs={{0,2},{2,0},{1,3},{3,1},{4,6},{6,4},{5,7},{7,5},{8,10},{10,8},{9,1... | collective-permute-start | bytes 786440 | tf_op jit(solution)/shard_map/ppermute | solution.py:334
  1.2 9.9 %collective-permute-start = (bf16[128,1024]{1,0:T(8,128)(2,1)}, bf16[128,1024]{1,0:T(8,128)(2,1)S(1)}, u32[]{:S(2)}, u32[]{:S(2)}) collective-permute-start(bf16[128,1024]{1,0:T(8,128)(2,1)} %refs_4_.4), channel_id=1, source_target_pairs={{0,1},{1,0},{2,3},{3,2},{4,5},{5,4},{6,7},{7,6},{8,9},{9,8},{10,11... | collective-permute-start | bytes 786440 | tf_op jit(solution)/shard_map/ppermute | solution.py:324
  7.5 7.9 %collective-permute-start.1 = (bf16[128,1024]{1,0:T(8,128)(2,1)}, bf16[128,1024]{1,0:T(8,128)(2,1)S(1)}, u32[]{:S(2)}, u32[]{:S(2)}) collective-permute-start(bf16[128,1024]{1,0:T(8,128)(2,1)} %get-tuple-element.107), channel_id=1, source_target_pairs={{0,2},{1,3},{2,0},{3,1},{4,6},{5,7},{6,4},{7,5},{8,10},{9,11},{10,... | collective-permute-start | bytes 786440 | tf_op jit(solution)/shard_map/ppermute | solution.py:331
  7.6 9.4 %collective-permute-start.2 = (bf16[128,1024]{1,0:T(8,128)(2,1)}, bf16[128,1024]{1,0:T(8,128)(2,1)S(1)}, u32[]{:S(2)}, u32[]{:S(2)}) collective-permute-start(bf16[128,1024]{1,0:T(8,128)(2,1)} %get-tuple-element.108), channel_id=1, source_target_pairs={{0,1},{1,0},{2,3},{3,2},{4,5},{5,4},{6,7},{7,6},{8,9},{9,8},{10,11... | collective-permute-start | bytes 786440 | tf_op jit(solution)/shard_map/ppermute | solution.py:331
  7.7 14.6 %collective-permute-start.3 = (bf16[128,1024]{1,0:T(8,128)(2,1)S(1)}, bf16[128,1024]{1,0:T(8,128)(2,1)S(1)}, u32[]{:S(2)}, u32[]{:S(2)}) collective-permute-start(bf16[128,1024]{1,0:T(8,128)(2,1)S(1)} %get-tuple-element.109), channel_id=1, source_target_pairs={{0,3},{1,2},{2,1},{3,0},{4,7},{5,6},{6,5},{7,4},{8,11},{9,10},{10,... | collective-permute-start | bytes 786440 | tf_op jit(solution)/shard_map/ppermute | solution.py:331
  11.2 13.0 %collective-permute-start.5 = (bf16[128,1024]{1,0:T(8,128)(2,1)S(1)}, bf16[128,1024]{1,0:T(8,128)(2,1)S(1)}, u32[]{:S(2)}, u32[]{:S(2)}) collective-permute-start(bf16[128,1024]{1,0:T(8,128)(2,1)S(1)} %collective-permute-done.refs_6_), channel_id=1, source_target_pairs={{0,2},{2,0},{1,3},{3,1},{4,6},{6,4},{5,7},{7,5},{8,10},{10,8},{9,1... | collective-permute-start | bytes 786440 | tf_op jit(solution)/shard_map/ppermute | solution.py:336
  15.5 29.3 %collective-permute-start.9 = (bf16[128,1024]{1,0:T(8,128)(2,1)S(1)}, bf16[128,1024]{1,0:T(8,128)(2,1)S(1)}, u32[]{:S(2)}, u32[]{:S(2)}) collective-permute-start(bf16[128,1024]{1,0:T(8,128)(2,1)S(1)} %get-tuple-element.123), channel_id=1, source_target_pairs={{0,2},{1,3},{2,0},{3,1},{4,6},{5,7},{6,4},{7,5},{8,10},{9,11},{10,... | collective-permute-start | bytes 786440 | tf_op jit(solution)/shard_map/ppermute | solution.py:331
  17.0 27.7 %collective-permute-start.10 = (bf16[128,1024]{1,0:T(8,128)(2,1)S(1)}, bf16[128,1024]{1,0:T(8,128)(2,1)S(1)}, u32[]{:S(2)}, u32[]{:S(2)}) collective-permute-start(bf16[128,1024]{1,0:T(8,128)(2,1)S(1)} %get-tuple-element.124), channel_id=1, source_target_pairs={{0,1},{1,0},{2,3},{3,2},{4,5},{5,4},{6,7},{7,6},{8,9},{9,8},{10,11... | collective-permute-start | bytes 786440 | tf_op jit(solution)/shard_map/ppermute | solution.py:331
  22.3 22.4 %collective-permute-start.11 = (bf16[128,1024]{1,0:T(8,128)(2,1)S(1)}, bf16[128,1024]{1,0:T(8,128)(2,1)S(1)}, u32[]{:S(2)}, u32[]{:S(2)}) collective-permute-start(bf16[128,1024]{1,0:T(8,128)(2,1)S(1)} %get-tuple-element.125), channel_id=1, source_target_pairs={{0,3},{1,2},{2,1},{3,0},{4,7},{5,6},{6,5},{7,4},{8,11},{9,10},{10,... | collective-permute-start | bytes 786440 | tf_op jit(solution)/shard_map/ppermute | solution.py:331
  28.3 12.8 %collective-permute-start.7 = (bf16[512,512]{1,0:T(8,128)(2,1)S(1)}, bf16[512,512]{1,0:T(8,128)(2,1)S(1)}, u32[]{:S(2)}, u32[]{:S(2)}) collective-permute-start(bf16[512,512]{1,0:T(8,128)(2,1)S(1)} %get-tuple-element.116), channel_id=1, source_target_pairs={{0,4},{4,0},{1,5},{5,1},{2,6},{6,2},{3,7},{7,3},{8,12},{12,8},{9,1... | collective-permute-start | bytes 1572872 | tf_op jit(solution)/shard_map/ppermute | solution.py:390
  29.8 12.5 %collective-permute-start.8 = (bf16[512,512]{1,0:T(8,128)(2,1)S(1)}, bf16[512,512]{1,0:T(8,128)(2,1)S(1)}, u32[]{:S(2)}, u32[]{:S(2)}) collective-permute-start(bf16[512,512]{1,0:T(8,128)(2,1)S(1)} %get-tuple-element.118), channel_id=1, source_target_pairs={{0,8},{8,0},{16,24},{24,16},{1,9},{9,1},{17,25},{25,17},{2,10},{10... | collective-permute-start | bytes 1572872 | tf_op jit(solution)/shard_map/ppermute | solution.py:390
  42.5 6.4 %collective-permute-start.12 = (bf16[256,512]{1,0:T(8,128)(2,1)S(1)}, bf16[256,512]{1,0:T(8,128)(2,1)S(1)}, u32[]{:S(2)}, u32[]{:S(2)}) collective-permute-start(bf16[256,512]{1,0:T(8,128)(2,1)S(1)} %get-tuple-element.129), channel_id=1, source_target_pairs={{0,8},{8,0},{16,24},{24,16},{1,9},{9,1},{17,25},{25,17},{2,10},{10... | collective-permute-start | bytes 786440 | tf_op jit(solution)/shard_map/ppermute | solution.py:357
  44.2 7.1 %collective-permute-start.13 = (bf16[256,512]{1,0:T(8,128)(2,1)S(1)}, bf16[256,512]{1,0:T(8,128)(2,1)S(1)}, u32[]{:S(2)}, u32[]{:S(2)}) collective-permute-start(bf16[256,512]{1,0:T(8,128)(2,1)S(1)} %get-tuple-element.130), channel_id=1, source_target_pairs={{0,4},{4,0},{1,5},{5,1},{2,6},{6,2},{3,7},{7,3},{8,12},{12,8},{9,1... | collective-permute-start | bytes 786440 | tf_op jit(solution)/shard_map/ppermute | solution.py:357
  51.3 16.1 %collective-permute-start.14 = (bf16[512,768]{1,0:T(8,128)(2,1)S(1)}, bf16[512,768]{1,0:T(8,128)(2,1)S(1)}, u32[]{:S(2)}, u32[]{:S(2)}) collective-permute-start(bf16[512,768]{1,0:T(8,128)(2,1)S(1)} %get-tuple-element.131), channel_id=1, source_target_pairs={{0,4},{4,0},{1,5},{5,1},{2,6},{6,2},{3,7},{7,3},{8,12},{12,8},{9,1... | collective-permute-start | bytes 2359304 | tf_op jit(solution)/shard_map/ppermute | solution.py:390
  51.8 42.5 %collective-permute-start.19 = (bf16[128,4096]{1,0:T(8,128)(2,1)S(1)}, bf16[128,4096]{1,0:T(8,128)(2,1)S(1)}, u32[]{:S(2)}, u32[]{:S(2)}) collective-permute-start(bf16[128,4096]{1,0:T(8,128)(2,1)S(1)} %slice.4), channel_id=1, source_target_pairs={{0,1},{1,0},{2,3},{3,2},{4,5},{5,4},{6,7},{7,6},{8,9},{9,8},{10,11... | collective-permute-start | bytes 3145736 | tf_op jit(solution)/shard_map/ppermute | solution.py:389
  53.5 12.1 %collective-permute-start.15 = (bf16[512,256]{1,0:T(8,128)(2,1)S(1)}, bf16[512,256]{1,0:T(8,128)(2,1)S(1)}, u32[]{:S(2)}, u32[]{:S(2)}) collective-permute-start(bf16[512,256]{1,0:T(8,128)(2,1)S(1)} %get-tuple-element.133), channel_id=1, source_target_pairs={{0,8},{8,0},{16,24},{24,16},{1,9},{9,1},{17,25},{25,17},{2,10},{10... | collective-permute-start | bytes 786440 | tf_op jit(solution)/shard_map/ppermute | solution.py:390
  54.1 26.3 %collective-permute-start.16 = (bf16[256,1024]{1,0:T(8,128)(2,1)S(1)}, bf16[256,1024]{1,0:T(8,128)(2,1)S(1)}, u32[]{:S(2)}, u32[]{:S(2)}) collective-permute-start(bf16[256,1024]{1,0:T(8,128)(2,1)S(1)} %shard_map.99), channel_id=1, source_target_pairs={{0,16},{8,24},{16,0},{24,8},{1,17},{9,25},{17,1},{25,9},{2,18},{10... | collective-permute-start | bytes 1572872 | tf_op jit(solution)/shard_map/ppermute | solution.py:380
  56.8 23.7 %collective-permute-start.20 = (bf16[128,1024]{1,0:T(8,128)(2,1)S(1)}, bf16[128,1024]{1,0:T(8,128)(2,1)S(1)}, u32[]{:S(2)}, u32[]{:S(2)}) collective-permute-start(bf16[128,1024]{1,0:T(8,128)(2,1)S(1)} %copy-done.10), channel_id=1, source_target_pairs={{0,1},{1,0},{2,3},{3,2},{4,5},{5,4},{6,7},{7,6},{8,9},{9,8},{10,11... | collective-permute-start | bytes 786440 | tf_op jit(solution)/shard_map/ppermute | solution.py:350
  67.6 22.9 %collective-permute-start.17 = (bf16[256,768]{1,0:T(8,128)(2,1)S(1)}, bf16[256,768]{1,0:T(8,128)(2,1)S(1)}, u32[]{:S(2)}, u32[]{:S(2)}) collective-permute-start(bf16[256,768]{1,0:T(8,128)(2,1)S(1)} %get-tuple-element.148), channel_id=1, source_target_pairs={{0,8},{8,0},{16,24},{24,16},{1,9},{9,1},{17,25},{25,17},{2,10},{10... | collective-permute-start | bytes 1179656 | tf_op jit(solution)/shard_map/ppermute | solution.py:357
  68.2 13.8 %collective-permute-start.23 = (bf16[128,1024]{1,0:T(8,128)(2,1)S(1)}, bf16[128,1024]{1,0:T(8,128)(2,1)S(1)}, u32[]{:S(2)}, u32[]{:S(2)}) collective-permute-start(bf16[128,1024]{1,0:T(8,128)(2,1)S(1)} %copy-done.9), channel_id=1, source_target_pairs={{0,2},{1,3},{2,0},{3,1},{4,6},{5,7},{6,4},{7,5},{8,10},{9,11},{10,... | collective-permute-start | bytes 786440 | tf_op jit(solution)/shard_map/ppermute | solution.py:350
  80.5 8.3 %collective-permute-start.24 = (bf16[128,1024]{1,0:T(8,128)(2,1)S(1)}, bf16[128,1024]{1,0:T(8,128)(2,1)S(1)}, u32[]{:S(2)}, u32[]{:S(2)}) collective-permute-start(bf16[128,1024]{1,0:T(8,128)(2,1)S(1)} %copy-done.8), channel_id=1, source_target_pairs={{0,3},{1,2},{2,1},{3,0},{4,7},{5,6},{6,5},{7,4},{8,11},{9,10},{10,... | collective-permute-start | bytes 786440 | tf_op jit(solution)/shard_map/ppermute | solution.py:350
  80.5 9.7 %collective-permute-start.18 = (bf16[256,256]{1,0:T(8,128)(2,1)S(1)}, bf16[256,256]{1,0:T(8,128)(2,1)S(1)}, u32[]{:S(2)}, u32[]{:S(2)}) collective-permute-start(bf16[256,256]{1,0:T(8,128)(2,1)S(1)} %get-tuple-element.150), channel_id=1, source_target_pairs={{0,4},{4,0},{1,5},{5,1},{2,6},{6,2},{3,7},{7,3},{8,12},{12,8},{9,1... | collective-permute-start | bytes 393224 | tf_op jit(solution)/shard_map/ppermute | solution.py:357
  82.0 14.8 %collective-permute-start.21 = (bf16[128,1024]{1,0:T(8,128)(2,1)S(1)}, bf16[128,1024]{1,0:T(8,128)(2,1)S(1)}, u32[]{:S(2)}, u32[]{:S(2)}) collective-permute-start(bf16[128,1024]{1,0:T(8,128)(2,1)S(1)} %copy-done.7), channel_id=1, source_target_pairs={{0,4},{1,5},{2,6},{3,7},{4,0},{5,1},{6,2},{7,3},{8,12},{9,13},{10,... | collective-permute-start | bytes 786440 | tf_op jit(solution)/shard_map/ppermute | solution.py:350
  88.8 9.5 %collective-permute-start.25 = (bf16[128,1024]{1,0:T(8,128)(2,1)S(1)}, bf16[128,1024]{1,0:T(8,128)(2,1)S(1)}, u32[]{:S(2)}, u32[]{:S(2)}) collective-permute-start(bf16[128,1024]{1,0:T(8,128)(2,1)S(1)} %copy-done.6), channel_id=1, source_target_pairs={{0,6},{1,7},{2,4},{3,5},{4,2},{5,3},{6,0},{7,1},{8,14},{9,15},{10,... | collective-permute-start | bytes 786440 | tf_op jit(solution)/shard_map/ppermute | solution.py:350
  90.2 14.7 %collective-permute-start.22 = (bf16[128,1024]{1,0:T(8,128)(2,1)S(1)}, bf16[128,1024]{1,0:T(8,128)(2,1)S(1)}, u32[]{:S(2)}, u32[]{:S(2)}) collective-permute-start(bf16[128,1024]{1,0:T(8,128)(2,1)S(1)} %copy-done.5), channel_id=1, source_target_pairs={{0,5},{1,4},{2,7},{3,6},{4,1},{5,0},{6,3},{7,2},{8,13},{9,12},{10,... | collective-permute-start | bytes 786440 | tf_op jit(solution)/shard_map/ppermute | solution.py:350
  90.5 18.8 %collective-permute-start.26 = (bf16[128,1024]{1,0:T(8,128)(2,1)S(1)}, bf16[128,1024]{1,0:T(8,128)(2,1)S(1)}, u32[]{:S(2)}, u32[]{:S(2)}) collective-permute-start(bf16[128,1024]{1,0:T(8,128)(2,1)S(1)} %copy-done.4), channel_id=1, source_target_pairs={{0,7},{1,6},{2,5},{3,4},{4,3},{5,2},{6,1},{7,0},{8,15},{9,14},{10,... | collective-permute-start | bytes 786440 | tf_op jit(solution)/shard_map/ppermute | solution.py:350
  94.2 26.8 %collective-permute-start.28 = (bf16[256,1024]{1,0:T(8,128)(2,1)S(1)}, bf16[256,1024]{1,0:T(8,128)(2,1)S(1)}, u32[]{:S(2)}, u32[]{:S(2)}) collective-permute-start(bf16[256,1024]{1,0:T(8,128)(2,1)S(1)} %get-tuple-element.166.refs_4_), channel_id=1, source_target_pairs={{0,16},{8,24},{16,0},{24,8},{1,17},{9,25},{17,1},{25,9},{2,18},{10... | collective-permute-start | bytes 1572872 | tf_op jit(solution)/shard_map/ppermute | solution.py:436
  96.8 25.4 %collective-permute-start.27 = (bf16[256,1024]{1,0:T(8,128)(2,1)S(1)}, bf16[256,1024]{1,0:T(8,128)(2,1)S(1)}, u32[]{:S(2)}, u32[]{:S(2)}) collective-permute-start(bf16[256,1024]{1,0:T(8,128)(2,1)S(1)} %get-tuple-element.166.refs_4_), channel_id=1, source_target_pairs={{0,8},{8,0},{16,24},{24,16},{1,9},{9,1},{17,25},{25,17},{2,10},{10... | collective-permute-start | bytes 1572872 | tf_op jit(solution)/shard_map/ppermute | solution.py:436
  121.0 13.9 %collective-permute-start.29 = (bf16[256,1024]{1,0:T(8,128)(2,1)S(1)}, bf16[256,1024]{1,0:T(8,128)(2,1)S(1)}, u32[]{:S(2)}, u32[]{:S(2)}) collective-permute-start(bf16[256,1024]{1,0:T(8,128)(2,1)S(1)} %collective-permute-done.28.refs_6_), channel_id=1, source_target_pairs={{0,8},{8,0},{16,24},{24,16},{1,9},{9,1},{17,25},{25,17},{2,10},{10... | collective-permute-start | bytes 1572872 | tf_op jit(solution)/shard_map/ppermute | solution.py:436
  139.8 8.4 %collective-permute-start.31 = (bf16[256,512]{1,0:T(8,128)(2,1)S(1)}, bf16[256,512]{1,0:T(8,128)(2,1)S(1)}, u32[]{:S(2)}, u32[]{:S(2)}) collective-permute-start(bf16[256,512]{1,0:T(8,128)(2,1)S(1)} %get-tuple-element.180), channel_id=1, source_target_pairs={{0,4},{4,0},{1,5},{5,1},{2,6},{6,2},{3,7},{7,3},{8,12},{12,8},{9,1... | collective-permute-start | bytes 786440 | tf_op jit(solution)/shard_map/ppermute | solution.py:456
  140.5 8.1 %collective-permute-start.32 = (bf16[256,512]{1,0:T(8,128)(2,1)S(1)}, bf16[256,512]{1,0:T(8,128)(2,1)S(1)}, u32[]{:S(2)}, u32[]{:S(2)}) collective-permute-start(bf16[256,512]{1,0:T(8,128)(2,1)S(1)} %get-tuple-element.181), channel_id=1, source_target_pairs={{0,1},{1,0},{2,3},{3,2},{4,5},{5,4},{6,7},{7,6},{8,9},{9,8},{10,11... | collective-permute-start | bytes 786440 | tf_op jit(solution)/shard_map/ppermute | solution.py:457
  (16 other events, 254.2 us)

commit v7 on v6

--- a/solution.py
+++ b/solution.py
@@ -193,33 +193,34 @@
 
 
 def keys_kernel(acts_count, counts, at, *refs):
-    acts, (*pieces, out) = refs[:acts_count], refs[acts_count:]
-    if at:
-        *pieces, before = pieces
+    acts, refs = refs[:acts_count], refs[acts_count:]
     blocks = []
     for count in counts:
-        blocks.append(jnp.concatenate([w[...] for w in pieces[:count]], axis=1))
-        pieces = pieces[count:]
+        blocks.append(jnp.concatenate([w[...] for w in refs[:count]], axis=1))
+        refs = refs[count:]
     weight = jnp.concatenate(blocks, axis=0)
-    left = jnp.concatenate([a[:, at : at + weight.shape[0]] for a in acts], axis=0)
-    product = jnp.dot(left, weight, preferred_element_type=f32)
-    out[...] = before[...] + product if at else product
-
-
-def keys_part(acts, blocks, at, before=()):
-    rows, kv = len(acts) * acts[0].shape[0], sum(w.shape[1] for w in blocks[0])
+    before, outs = (refs[:1], refs[1:]) if at else ([], refs)
+    each = acts_count // len(outs)
+    for n, out in enumerate(outs):
+        left = jnp.concatenate([a[:, at : at + weight.shape[0]] for a in acts[n * each : (n + 1) * each]], axis=0)
+        product = jnp.dot(left, weight, preferred_element_type=f32)
+        out[...] = before[0][...] + product if at else product
+
+
+def keys_part(acts, blocks, at, before=(), outs=1):
+    rows, kv = len(acts) * acts[0].shape[0] // outs, sum(w.shape[1] for w in blocks[0])
     depth = sum(block[0].shape[0] for block in blocks)
     if at % LANES:
-        acts = [a[:, at:] for a in acts]
-        return before[0] + keys_part(acts, blocks, 0)
+        return [before[0] + keys_part([a[:, at:] for a in acts], blocks, 0)[0]]
     pieces = [w for block in blocks for w in block]
+    flops = rows * depth * kv if at else 1 << 34
     return pl.pallas_call(
         functools.partial(keys_kernel, len(acts), [len(block) for block in blocks], at),
-        out_shape=jax.ShapeDtypeStruct((rows, kv), f32),
+        out_shape=[jax.ShapeDtypeStruct((rows, kv), f32)] * outs,
         in_specs=[pl.BlockSpec()] * (len(acts) + len(pieces) + len(before)),
-        out_specs=pl.BlockSpec(),
-        compiler_params=pltpu.CompilerParams(vmem_limit_bytes=24 * MIB),
-        cost_estimate=pl.CostEstimate(flops=2 * rows * depth * kv, bytes_accessed=rows * kv, transcendentals=0),
+        out_specs=[pl.BlockSpec()] * outs,
+        compiler_params=pltpu.CompilerParams(vmem_limit_bytes=32 * MIB),
+        cost_estimate=pl.CostEstimate(flops=flops, bytes_accessed=rows * kv, transcendentals=0),
     )(*acts, *pieces, *before)
 
 
@@ -336,7 +337,6 @@
         cots[1, s] = lax.ppermute(cots[0, s], "core", swap)
 
     far = [(i, k, s) for k in range(CORES) for i in range(PAIR) for s in range(fsdp)]
-    near, away = [e for e in far if e[0] == 0], [e for e in far if e[0]]
     index = lambda i, k, s: ((i % PAIR) * CORES + k % CORES) * fsdp + s % fsdp
     every = [(i, k, s) for i in range(PAIR) for k in range(CORES) for s in range(fsdp)]
     groups = [[column(z ^ m, (x + i) % PAIR, k, s) for m in range(nz)] for i, k, s in far]
@@ -364,8 +364,6 @@
         if not stage:
             place, *held = lax.optimization_barrier((place, *[mine[e] for e in far]))
             mine.update(zip(far, held))
-            for e in near:
-                send_next(*e)
         if stage:
             place, to_z, to_x = lax.optimization_barrier((place, to_z, to_x))
             m = stages[stage - 1][1]
@@ -398,20 +396,10 @@
             spec=pl.BlockSpec(),
         )
 
-    straight, diagonal = [e for e in away if e[2] == 0], [e for e in away if e[2]]
-    to_z, to_x, *held = lax.optimization_barrier((to_z, to_x, *[mine[e] for e in straight]))
-    mine.update(zip(straight, held))
     inputs = finish(0, to_z, to_x, keep_left, keep_right)
-    for e in straight:
-        send_next(*e)
     inputs[0], inputs[2] = small_call(
         gather_kernel, [jax.ShapeDtypeStruct(part.shape, f32) for part in (keep_left, keep_right)], keep_left, keep_right, *inputs[4:], spec=pl.BlockSpec(), weight=200
     )
-    inputs[0], *held = lax.optimization_barrier((inputs[0], *[mine[e] for e in diagonal]))
-    mine.update(zip(diagonal, held))
-    for e in diagonal:
-        send_next(*e)
-
     whole = jax.ShapeDtypeStruct((share, kv), f32)
     share_rows, new_outer, new_momentum = small_call(
         functools.partial(update_kernel, nz * PAIR * CORES),
@@ -422,15 +410,17 @@
         spec=pl.BlockSpec(),
     )
 
+    share_rows, *held = lax.optimization_barrier((share_rows, *[mine[e] for e in far]))
+    mine.update(zip(far, held))
+    for e in far:
+        send_next(*e)
+
     rows = {}
     for m in sorted(range(1, nz), key=lambda m: (m & (m - 1)).bit_count() * nz - m):
         low = m & -m
         pieces = [share_rows] if m == low else list(rows[m ^ low])
         if m == nz - 1:
-            held = (share_rows, *parts, *[nexts[e] for e in far])
-            share_rows, *held = lax.optimization_barrier(held)
-            parts, held = held[: len(parts)], held[len(parts) :]
-            nexts.update(zip(far, held))
+            share_rows, *parts = lax.optimization_barrier((share_rows, *parts))
             input_grad = join(parts, [((f + s) % fsdp) * width for s in range(fsdp)])
             pieces[0], input_grad = lax.optimization_barrier((pieces[0], input_grad))
         rows[m] = [lax.ppermute(piece, "z", [(i, i ^ low) for i in range(nz)]) for piece in pieces]
@@ -438,11 +428,11 @@
 
     half = len(far) // CORES
     near, away = [nexts[e] for e in far[:half]], [nexts[e] for e in far[half:]]
-    give, keep = keys_part(away, rows[:-1], 0), keys_part(near, rows[:-1], 0)
+    give, keep = keys_part(away + near, rows[:-1], 0, outs=2)
     give, keep, input_grad = lax.optimization_barrier((give, keep, input_grad))
     last = (nz - 1) * share
-    give = keys_part(away, rows[-1:], last, [give])
-    keep = keys_part(near, rows[-1:], last, [keep])
+    (give,) = keys_part(away, rows[-1:], last, [give])
+    (keep,) = keys_part(near, rows[-1:], last, [keep])
     came = lax.ppermute(give, "core", swap)
     shape = lambda n, kind: jax.ShapeDtypeStruct((n, kv // 2), kind)
     to_x, stay_x, stay_f, *to_f = small_call(

time: 156 us -> 149 us (0.955)
  waiting for transfers between devices: 94.4 us -> 75.2 us
  starting transfers between devices: 34.5 us -> 46.8 us
    ppermute x7, waiting for transfers between devices: 30.2 us -> 5.94 us  [send_next(): lax.ppermute(mine[i, k, s], ('x', 'core', 'fsdp'), pairs)]
    ppermute x7, starting transfers between devices: 5.02 us -> 13.9 us  [send_next(): lax.ppermute(mine[i, k, s], ('x', 'core', 'fsdp'), pairs)]
    ppermute x3, waiting for transfers between devices: 21.7 us -> 15.6 us  [local(): lax.ppermute(piece, 'z', [(i, i ^ low) for i in range(nz)])]
    ppermute x2, waiting for transfers between devices: 8.98 us -> 14.5 us  [local(): lax.ppermute(to_x, 'x', across_x)]
    ppermute x2, waiting for transfers between devices: 0.53 us -> 5.72 us  [finish(): lax.ppermute(to_z, 'z', across_z)]
    ppermute x1, waiting for transfers between devices: 0.01 us -> 4.26 us  [local(): lax.ppermute(block_total, 'z', [(i, i ^ low) for i in range(nz)])]
    ppermute x3, starting transfers between devices: 3.16 us -> 6.97 us  [local(): lax.ppermute(piece, 'z', [(i, i ^ low) for i in range(nz)])]
    ppermute x2, waiting for transfers between devices: 9.53 us -> 5.8 us  [local(): lax.ppermute(to_z, 'z', across_z)]
  transfers between devices with their start and end apart: 35 -> 35, of which waited for: 22 -> 21; matrix products, arithmetic and copies ran while one was open for 2% -> 2% of each run, Pallas kernels for 14% -> 14%
where the time goes in v7:
time: 149 us
  waiting for transfers between devices  75.2 us (50%)
  starting transfers between devices  46.8 us (31%)
  Pallas kernels  22.8 us (15%)
  matrix products  2.38 us (2%)
    ppermute x3, waiting for transfers between devices, local(): lax.ppermute(piece, 'z', [(i, i ^ low) for i in range(nz)])  15.6 us
    ppermute x2, waiting for transfers between devices, local(): lax.ppermute(to_x, 'x', across_x)  14.5 us
    ppermute x7, starting transfers between devices, send_next(): lax.ppermute(mine[i, k, s], ('x', 'core', 'fsdp'), pairs)  13.9 us
    ppermute x2, waiting for transfers between devices, home(): from_x = lax.ppermute(to_x, 'x', ring(PAIR, 1))  10.7 us
    pallas_call x2, Pallas kernels, inner_blocks(): pl.pallas_call(functools.partial(inner_kernel, pieces, share, inner_rate...  7.74 us
    ppermute x6, starting transfers between devices, local(): lax.ppermute(part, ('core', 'fsdp'), pair_ring(k, s))  7.54 us
    pallas_call x2, Pallas kernels, pack(): pl.pallas_call(functools.partial(pack_kernel, plan), out_shape=shapes, in...  7.2 us
    ppermute x3, starting transfers between devices, local(): lax.ppermute(piece, 'z', [(i, i ^ low) for i in range(nz)])  6.97 us
  transfers between devices with their start and end apart: 35, of which 21 were waited for; matrix products, arithmetic and copies ran while one was open for 2% of the time, Pallas kernels for 14%

profile of v7, /device:TPU:0, one launch (start us, length us, event | category | flops | bytes accessed | tf_op | source)
XLA Modules:
  0.0 148.7 jit_solution(4671103850948513565)
XLA Ops:
  1.2 2.9 %collective-permute-start = (bf16[128,1024]{1,0:T(8,128)(2,1)}, bf16[128,1024]{1,0:T(8,128)(2,1)S(1)}, u32[]{:S(2)}, u32[]{:S(2)}) collective-permute-start(bf16[128,1024]{1,0:T(8,128)(2,1)} %refs_4_.4), channel_id=1, source_target_pairs={{0,1},{1,0},{2,3},{3,2},{4,5},{5,4},{6,7},{7,6},{8,9},{9,8},{10,11... | collective-permute-start | bytes 786440 | tf_op jit(solution)/shard_map/ppermute | solution.py:325
  4.3 3.2 %shard_map.94 = (bf16[128,1024]{1,0:T(8,128)(2,1)S(1)}, bf16[128,1024]{1,0:T(8,128)(2,1)}, bf16[128,1024]{1,0:T(8,128)(2,1)}, bf16[128,1024]{1,0:T(8,128)(2,1)S(...) custom-call(s32[32]{0:T(128)S(1)} %stack.216.starts, ...), custom_call_target="tpu_custom_call" | custom-call | bytes 16777216 | tf_op jit(solution)/shard_map/pallas_call | solution.py:72
  7.7 2.7 %collective-permute-start.3 = (bf16[128,1024]{1,0:T(8,128)(2,1)S(1)}, bf16[128,1024]{1,0:T(8,128)(2,1)S(1)}, u32[]{:S(2)}, u32[]{:S(2)}) collective-permute-start(bf16[128,1024]{1,0:T(8,128)(2,1)S(1)} %get-tuple-element.105), channel_id=1, source_target_pairs={{0,3},{1,2},{2,1},{3,0},{4,7},{5,6},{6,5},{7,4},{8,11},{9,10},{10,... | collective-permute-start | bytes 786440 | tf_op jit(solution)/shard_map/ppermute | solution.py:332
  11.5 4.0 %shard_map.93 = (bf16[128,1024]{1,0:T(8,128)(2,1)}, bf16[128,1024]{1,0:T(8,128)(2,1)}, bf16[128,1024]{1,0:T(8,128)(2,1)}, bf16[128,1024]{1,0:T(8,128)(2,1)}, bf1...) custom-call(s32[32]{0:T(128)S(1)} %stack.215.starts, ...), custom_call_target="tpu_custom_call" | custom-call | bytes 16777216 | tf_op jit(solution)/shard_map/pallas_call | solution.py:72
  17.0 2.2 %collective-permute-start.10 = (bf16[128,1024]{1,0:T(8,128)(2,1)S(1)}, bf16[128,1024]{1,0:T(8,128)(2,1)S(1)}, u32[]{:S(2)}, u32[]{:S(2)}) collective-permute-start(bf16[128,1024]{1,0:T(8,128)(2,1)S(1)} %get-tuple-element.120), channel_id=1, source_target_pairs={{0,1},{1,0},{2,3},{3,2},{4,5},{5,4},{6,7},{7,6},{8,9},{9,8},{10,11... | collective-permute-start | bytes 786440 | tf_op jit(solution)/shard_map/ppermute | solution.py:332
  19.2 3.1 %collective-permute-done.3.refs_3_ = bf16[128,1024]{1,0:T(8,128)(2,1)S(1)} collective-permute-done((bf16[128,1024]{1,0:T(8,128)(2,1)S(1)}, bf16[128,1024]{1,0:T(8,128)(2,1)S(1)}, u32[]{:S(2)}, u32[]{:S(2)}) %collective-permute-start.3) | collective-permute-done | bytes 262176 | tf_op jit(solution)/shard_map/ppermute | solution.py:332
  22.3 1.9 %collective-permute-start.11 = (bf16[128,1024]{1,0:T(8,128)(2,1)S(1)}, bf16[128,1024]{1,0:T(8,128)(2,1)S(1)}, u32[]{:S(2)}, u32[]{:S(2)}) collective-permute-start(bf16[128,1024]{1,0:T(8,128)(2,1)S(1)} %get-tuple-element.121), channel_id=1, source_target_pairs={{0,3},{1,2},{2,1},{3,0},{4,7},{5,6},{6,5},{7,4},{8,11},{9,10},{10,... | collective-permute-start | bytes 786440 | tf_op jit(solution)/shard_map/ppermute | solution.py:332
  24.2 4.0 %shard_map.95 = (bf16[512,512]{1,0:T(8,128)(2,1)S(1)}, f32[512,512]{1,0:T(8,128)S(1)}, bf16[512,512]{1,0:T(8,128)(2,1)S(1)}, f32[512,512]{1,0:T(8,128)S(1)}) custom-call(s32[4]{0:T(128)S(1)} %pad_add_fusion.1.place, bf16[128,1024]{1,0:T(8,128)(2,1)S(1)} %get-tuple-element.102.refs_0_, bf16[128,1024]{1,0:T(8,128)(2,1)S(1)} %collective-permute-done.1.refs_1_, ...), custom_call_target="tpu_custom_call" | custom-call | flops 134217728 | bytes 262144 | tf_op jit(solution)/shard_map/pallas_call | solution.py:135
  31.4 2.4 %convolution_convert_fusion.refs_0_ = bf16[256,4096]{1,0:T(8,128)(2,1)S(1)} fusion(bf16[128,1024]{1,0:T(8,128)(2,1)S(1)} %collective-permute-done.refs_6_, bf16[128,1024]{1,0:T(8,128)(2,1)S(1)} %copy-done, bf16[1,4096,1024]{2,1,0:T(8,128)(2,1)S(1)} %bitcast.49), kind=kOutput, calls=%fused_computation | convolution fusion | flops 2149580800 | bytes 11010048 | tf_op jit(solution)/shard_map/dot_general | solution.py:381
  33.9 7.2 %collective-permute-done.7.from_x = bf16[512,512]{1,0:T(8,128)(2,1)S(1)} collective-permute-done((bf16[512,512]{1,0:T(8,128)(2,1)S(1)}, bf16[512,512]{1,0:T(8,128)(2,1)S(1)}, u32[]{:S(2)}, u32[]{:S(2)}) %collective-permute-start.7) | collective-permute-done | bytes 524320 | tf_op jit(solution)/shard_map/ppermute | solution.py:388
  44.7 3.7 %shard_map.97 = (bf16[512,768]{1,0:T(8,128)(2,1)S(1)}, f32[512,768]{1,0:T(8,128)S(1)}, bf16[512,256]{1,0:T(8,128)(2,1)S(1)}, f32[512,256]{1,0:T(8,128)S(1)}) custom-call(s32[4]{0:T(128)S(1)} %pad_add_fusion.place, bf16[128,1024]{1,0:T(8,128)(2,1)S(1)} %get-tuple-element.118.refs_0_, bf16[128,1024]{1,0:T(8,128)(2,1)S(1)} %collective-permute-done.9.refs_1_, ...), custom_call_target="tpu_custom_call" | custom-call | flops 134217728 | bytes 262144 | tf_op jit(solution)/shard_map/pallas_call | solution.py:135
  49.0 2.3 %collective-permute-done.13.refs_3_ = bf16[256,512]{1,0:T(8,128)(2,1)S(1)} collective-permute-done((bf16[256,512]{1,0:T(8,128)(2,1)S(1)}, bf16[256,512]{1,0:T(8,128)(2,1)S(1)}, u32[]{:S(2)}, u32[]{:S(2)}) %collective-permute-start.13) | collective-permute-done | bytes 262176 | tf_op jit(solution)/shard_map/ppermute | solution.py:357
  52.6 2.7 %collective-permute-start.16 = (bf16[256,1024]{1,0:T(8,128)(2,1)S(1)}, bf16[256,1024]{1,0:T(8,128)(2,1)S(1)}, u32[]{:S(2)}, u32[]{:S(2)}) collective-permute-start(bf16[256,1024]{1,0:T(8,128)(2,1)S(1)} %shard_map.99), channel_id=1, source_target_pairs={{0,16},{8,24},{16,0},{24,8},{1,17},{9,25},{17,1},{25,9},{2,18},{10... | collective-permute-start | bytes 1572872 | tf_op jit(solution)/shard_map/ppermute | solution.py:378
  56.8 4.6 %collective-permute-done.15.from_z = bf16[512,256]{1,0:T(8,128)(2,1)S(1)} collective-permute-done((bf16[512,256]{1,0:T(8,128)(2,1)S(1)}, bf16[512,256]{1,0:T(8,128)(2,1)S(1)}, u32[]{:S(2)}, u32[]{:S(2)}) %collective-permute-start.15) | collective-permute-done | bytes 262176 | tf_op jit(solution)/shard_map/ppermute | solution.py:388
  61.4 7.2 %collective-permute-done.14.from_x = bf16[512,768]{1,0:T(8,128)(2,1)S(1)} collective-permute-done((bf16[512,768]{1,0:T(8,128)(2,1)S(1)}, bf16[512,768]{1,0:T(8,128)(2,1)S(1)}, u32[]{:S(2)}, u32[]{:S(2)}) %collective-permute-start.14) | collective-permute-done | bytes 786464 | tf_op jit(solution)/shard_map/ppermute | solution.py:388
  69.5 4.3 %collective-permute-done.16.refs_0_ = bf16[256,1024]{1,0:T(8,128)(2,1)S(1)} collective-permute-done((bf16[256,1024]{1,0:T(8,128)(2,1)S(1)}, bf16[256,1024]{1,0:T(8,128)(2,1)S(1)}, u32[]{:S(2)}, u32[]{:S(2)}) %collective-permute-start.16) | collective-permute-done | bytes 524320 | tf_op jit(solution)/shard_map/ppermute | solution.py:378
  74.0 5.2 %collective-permute-done.17.refs_1_ = bf16[256,768]{1,0:T(8,128)(2,1)S(1)} collective-permute-done((bf16[256,768]{1,0:T(8,128)(2,1)S(1)}, bf16[256,768]{1,0:T(8,128)(2,1)S(1)}, u32[]{:S(2)}, u32[]{:S(2)}) %collective-permute-start.17) | collective-permute-done | bytes 393248 | tf_op jit(solution)/shard_map/ppermute | solution.py:357
  79.1 1.7 %shard_map.101 = (bf16[256,1024]{1,0:T(8,128)(2,1)S(1)}, f32[256,1024]{1,0:T(8,128)}, f32[256,1024]{1,0:T(8,128)}) custom-call(f32[256,768]{1,0:T(8,128)S(1)} %get-tuple-element.136.refs_0_, bf16[256,768]{1,0:T(8,128)(2,1)S(1)} %collective-permute-done.17.refs_1_, f32[256,256]{1,0:T(8,128)S(1)} %get-tuple-element.138.refs_2_, ...), custom_call_target="tpu_custom_call" | custom-call | flops 98304 | bytes 98304 | tf_op jit(solution)/shard_map/pallas_call | solution.py:266
  80.8 3.8 %collective-permute-start.28 = (bf16[256,1024]{1,0:T(8,128)(2,1)S(1)}, bf16[256,1024]{1,0:T(8,128)(2,1)S(1)}, u32[]{:S(2)}, u32[]{:S(2)}) collective-permute-start(bf16[256,1024]{1,0:T(8,128)(2,1)S(1)} %get-tuple-element.160.refs_8_), channel_id=1, source_target_pairs={{0,16},{8,24},{16,0},{24,8},{1,17},{9,25},{17,1},{25,9},{2,18},{10... | collective-permute-start | bytes 1572872 | tf_op jit(solution)/shard_map/ppermute | solution.py:426
  84.6 5.2 %collective-permute-start.20 = (bf16[128,1024]{1,0:T(8,128)(2,1)S(1)}, bf16[128,1024]{1,0:T(8,128)(2,1)S(1)}, u32[]{:S(2)}, u32[]{:S(2)}) collective-permute-start(bf16[128,1024]{1,0:T(8,128)(2,1)S(1)} %copy-done.9), channel_id=1, source_target_pairs={{0,3},{1,2},{2,1},{3,0},{4,7},{5,6},{6,5},{7,4},{8,11},{9,10},{10,... | collective-permute-start | bytes 786440 | tf_op jit(solution)/shard_map/ppermute | solution.py:350
  90.3 2.5 %collective-permute-start.27 = (bf16[256,1024]{1,0:T(8,128)(2,1)S(1)}, bf16[256,1024]{1,0:T(8,128)(2,1)S(1)}, u32[]{:S(2)}, u32[]{:S(2)}) collective-permute-start(bf16[256,1024]{1,0:T(8,128)(2,1)S(1)} %get-tuple-element.160.refs_8_), channel_id=1, source_target_pairs={{0,8},{8,0},{16,24},{24,16},{1,9},{9,1},{17,25},{25,17},{2,10},{10... | collective-permute-start | bytes 1572872 | tf_op jit(solution)/shard_map/ppermute | solution.py:426
  93.3 3.1 %collective-permute-done.20.refs_1_ = bf16[128,1024]{1,0:T(8,128)(2,1)S(1)} collective-permute-done((bf16[128,1024]{1,0:T(8,128)(2,1)S(1)}, bf16[128,1024]{1,0:T(8,128)(2,1)S(1)}, u32[]{:S(2)}, u32[]{:S(2)}) %collective-permute-start.20) | collective-permute-done | bytes 262176 | tf_op jit(solution)/shard_map/ppermute | solution.py:350
  98.9 8.1 %collective-permute-done.28.refs_10_ = bf16[256,1024]{1,0:T(8,128)(2,1)S(1)} collective-permute-done((bf16[256,1024]{1,0:T(8,128)(2,1)S(1)}, bf16[256,1024]{1,0:T(8,128)(2,1)S(1)}, u32[]{:S(2)}, u32[]{:S(2)}) %collective-permute-start.28) | collective-permute-done | bytes 524320 | tf_op jit(solution)/shard_map/ppermute | solution.py:426
  106.9 5.6 %collective-permute-start.25 = (bf16[128,1024]{1,0:T(8,128)(2,1)S(1)}, bf16[128,1024]{1,0:T(8,128)(2,1)S(1)}, u32[]{:S(2)}, u32[]{:S(2)}) collective-permute-start(bf16[128,1024]{1,0:T(8,128)(2,1)S(1)} %copy-done.4), channel_id=1, source_target_pairs={{0,5},{1,4},{2,7},{3,6},{4,1},{5,0},{6,3},{7,2},{8,13},{9,12},{10,... | collective-permute-start | bytes 786440 | tf_op jit(solution)/shard_map/ppermute | solution.py:350
  112.6 1.9 %shard_map.103 = bf16[128,8192]{1,0:T(8,128)(2,1)} custom-call(s32[2]{0:T(128)S(1)} %pad_add_fusion.2.starts, bf16[256,4096]{1,0:T(8,128)(2,1)S(1)} %convolution_convert_fusion.refs_0_, bf16[128,4096]{1,0:T(8,128)(2,1)S(1)} %collective-permute-done.26.refs_1_), custom_call_target="tpu_custom_call" | custom-call | flops 17179869184 | bytes 4194304 | tf_op jit(solution)/shard_map/pallas_call | solution.py:291
  115.2 2.5 %collective-permute-done.25.refs_7_.refs_3_ = bf16[128,1024]{1,0:T(8,128)(2,1)S(1)} collective-permute-done((bf16[128,1024]{1,0:T(8,128)(2,1)S(1)}, bf16[128,1024]{1,0:T(8,128)(2,1)S(1)}, u32[]{:S(2)}, u32[]{:S(2)}) %collective-permute-start.25) | collective-permute-done | bytes 262176 | tf_op jit(solution)/shard_map/ppermute | solution.py:350
  117.7 1.8 %shard_map.102 = (f32[512,1024]{1,0:T(8,128)S(1)}, f32[512,1024]{1,0:T(8,128)S(1)}) custom-call(bf16[128,1024]{1,0:T(8,128)(2,1)S(1)} %collective-permute-done.19.refs_0_, bf16[128,1024]{1,0:T(8,128)(2,1)S(1)} %collective-permute-done.20.refs_1_, bf16[128,1024]{1,0:T(8,128)(2,1)S(1)} %collective-permute-done.21.refs_2_, ...), custom_call_target="tpu_custom_call" | custom-call | flops 17179869184 | bytes 524288 | tf_op jit(solution)/shard_map/pallas_call | solution.py:217
  119.5 7.5 %collective-permute-done.29.refs_4_ = bf16[256,1024]{1,0:T(8,128)(2,1)S(1)} collective-permute-done((bf16[256,1024]{1,0:T(8,128)(2,1)S(1)}, bf16[256,1024]{1,0:T(8,128)(2,1)S(1)}, u32[]{:S(2)}, u32[]{:S(2)}) %collective-permute-start.29) | collective-permute-done | bytes 524320 | tf_op jit(solution)/shard_map/ppermute | solution.py:426
  128.0 3.7 %collective-permute-done.30.came = f32[512,1024]{1,0:T(8,128)S(1)} collective-permute-done((f32[512,1024]{1,0:T(8,128)S(1)}, f32[512,1024]{1,0:T(8,128)S(1)}, u32[]{:S(2)}, u32[]{:S(2)}) %collective-permute-start.30) | collective-permute-done | bytes 2097184 | tf_op jit(solution)/shard_map/ppermute | solution.py:436
  131.9 2.5 %collective-permute-start.31 = (bf16[256,512]{1,0:T(8,128)(2,1)S(1)}, bf16[256,512]{1,0:T(8,128)(2,1)S(1)}, u32[]{:S(2)}, u32[]{:S(2)}) collective-permute-start(bf16[256,512]{1,0:T(8,128)(2,1)S(1)} %get-tuple-element.172), channel_id=1, source_target_pairs={{0,4},{4,0},{1,5},{5,1},{2,6},{6,2},{3,7},{7,3},{8,12},{12,8},{9,1... | collective-permute-start | bytes 786440 | tf_op jit(solution)/shard_map/ppermute | solution.py:446
  134.4 6.6 %collective-permute-done.31.refs_2_ = bf16[256,512]{1,0:T(8,128)(2,1)S(1)} collective-permute-done((bf16[256,512]{1,0:T(8,128)(2,1)S(1)}, bf16[256,512]{1,0:T(8,128)(2,1)S(1)}, u32[]{:S(2)}, u32[]{:S(2)}) %collective-permute-start.31) | collective-permute-done | bytes 262176 | tf_op jit(solution)/shard_map/ppermute | solution.py:446
  143.5 4.1 %collective-permute-done.33.from_x = bf16[128,512]{1,0:T(8,128)(2,1)S(1)} collective-permute-done((bf16[128,512]{1,0:T(8,128)(2,1)S(1)}, bf16[128,512]{1,0:T(8,128)(2,1)S(1)}, u32[]{:S(2)}, u32[]{:S(2)}) %collective-permute-start.33) | collective-permute-done | bytes 131104 | tf_op jit(solution)/shard_map/ppermute | solution.py:446
  (88 shorter events, 23.6 us)
Async XLA Ops:
  0.6 23.6 %collective-permute-start.6 = (bf16[4096,1024]{1,0:T(8,128)(2,1)}, bf16[4096,1024]{1,0:T(8,128)(2,1)}, u32[]{:S(2)}, u32[]{:S(2)}) collective-permute-start(bf16[4096,1024]{1,0:T(8,128)(2,1)} %bitcast.45), channel_id=1, source_target_pairs={{0,2},{2,0},{1,3},{3,1},{4,6},{6,4},{5,7},{7,5},{8,10},{10,8},{9,1... | collective-permute-start | bytes 25165832 | tf_op jit(solution)/shard_map/ppermute | solution.py:334
  1.1 6.5 %collective-permute-start.4 = (bf16[128,1024]{1,0:T(8,128)(2,1)}, bf16[128,1024]{1,0:T(8,128)(2,1)S(1)}, u32[]{:S(2)}, u32[]{:S(2)}) collective-permute-start(bf16[128,1024]{1,0:T(8,128)(2,1)} %refs_4_.4), channel_id=1, source_target_pairs={{0,2},{2,0},{1,3},{3,1},{4,6},{6,4},{5,7},{7,5},{8,10},{10,8},{9,1... | collective-permute-start | bytes 786440 | tf_op jit(solution)/shard_map/ppermute | solution.py:335
  1.2 9.9 %collective-permute-start = (bf16[128,1024]{1,0:T(8,128)(2,1)}, bf16[128,1024]{1,0:T(8,128)(2,1)S(1)}, u32[]{:S(2)}, u32[]{:S(2)}) collective-permute-start(bf16[128,1024]{1,0:T(8,128)(2,1)} %refs_4_.4), channel_id=1, source_target_pairs={{0,1},{1,0},{2,3},{3,2},{4,5},{5,4},{6,7},{7,6},{8,9},{9,8},{10,11... | collective-permute-start | bytes 786440 | tf_op jit(solution)/shard_map/ppermute | solution.py:325
  7.5 7.9 %collective-permute-start.1 = (bf16[128,1024]{1,0:T(8,128)(2,1)}, bf16[128,1024]{1,0:T(8,128)(2,1)S(1)}, u32[]{:S(2)}, u32[]{:S(2)}) collective-permute-start(bf16[128,1024]{1,0:T(8,128)(2,1)} %get-tuple-element.103), channel_id=1, source_target_pairs={{0,2},{1,3},{2,0},{3,1},{4,6},{5,7},{6,4},{7,5},{8,10},{9,11},{10,... | collective-permute-start | bytes 786440 | tf_op jit(solution)/shard_map/ppermute | solution.py:332
  7.6 9.4 %collective-permute-start.2 = (bf16[128,1024]{1,0:T(8,128)(2,1)}, bf16[128,1024]{1,0:T(8,128)(2,1)S(1)}, u32[]{:S(2)}, u32[]{:S(2)}) collective-permute-start(bf16[128,1024]{1,0:T(8,128)(2,1)} %get-tuple-element.104), channel_id=1, source_target_pairs={{0,1},{1,0},{2,3},{3,2},{4,5},{5,4},{6,7},{7,6},{8,9},{9,8},{10,11... | collective-permute-start | bytes 786440 | tf_op jit(solution)/shard_map/ppermute | solution.py:332
  7.7 14.6 %collective-permute-start.3 = (bf16[128,1024]{1,0:T(8,128)(2,1)S(1)}, bf16[128,1024]{1,0:T(8,128)(2,1)S(1)}, u32[]{:S(2)}, u32[]{:S(2)}) collective-permute-start(bf16[128,1024]{1,0:T(8,128)(2,1)S(1)} %get-tuple-element.105), channel_id=1, source_target_pairs={{0,3},{1,2},{2,1},{3,0},{4,7},{5,6},{6,5},{7,4},{8,11},{9,10},{10,... | collective-permute-start | bytes 786440 | tf_op jit(solution)/shard_map/ppermute | solution.py:332
  11.2 13.0 %collective-permute-start.5 = (bf16[128,1024]{1,0:T(8,128)(2,1)S(1)}, bf16[128,1024]{1,0:T(8,128)(2,1)S(1)}, u32[]{:S(2)}, u32[]{:S(2)}) collective-permute-start(bf16[128,1024]{1,0:T(8,128)(2,1)S(1)} %collective-permute-done.refs_6_), channel_id=1, source_target_pairs={{0,2},{2,0},{1,3},{3,1},{4,6},{6,4},{5,7},{7,5},{8,10},{10,8},{9,1... | collective-permute-start | bytes 786440 | tf_op jit(solution)/shard_map/ppermute | solution.py:337
  15.5 29.2 %collective-permute-start.9 = (bf16[128,1024]{1,0:T(8,128)(2,1)S(1)}, bf16[128,1024]{1,0:T(8,128)(2,1)S(1)}, u32[]{:S(2)}, u32[]{:S(2)}) collective-permute-start(bf16[128,1024]{1,0:T(8,128)(2,1)S(1)} %get-tuple-element.119), channel_id=1, source_target_pairs={{0,2},{1,3},{2,0},{3,1},{4,6},{5,7},{6,4},{7,5},{8,10},{9,11},{10,... | collective-permute-start | bytes 786440 | tf_op jit(solution)/shard_map/ppermute | solution.py:332
  17.0 27.7 %collective-permute-start.10 = (bf16[128,1024]{1,0:T(8,128)(2,1)S(1)}, bf16[128,1024]{1,0:T(8,128)(2,1)S(1)}, u32[]{:S(2)}, u32[]{:S(2)}) collective-permute-start(bf16[128,1024]{1,0:T(8,128)(2,1)S(1)} %get-tuple-element.120), channel_id=1, source_target_pairs={{0,1},{1,0},{2,3},{3,2},{4,5},{5,4},{6,7},{7,6},{8,9},{9,8},{10,11... | collective-permute-start | bytes 786440 | tf_op jit(solution)/shard_map/ppermute | solution.py:332
  22.3 22.4 %collective-permute-start.11 = (bf16[128,1024]{1,0:T(8,128)(2,1)S(1)}, bf16[128,1024]{1,0:T(8,128)(2,1)S(1)}, u32[]{:S(2)}, u32[]{:S(2)}) collective-permute-start(bf16[128,1024]{1,0:T(8,128)(2,1)S(1)} %get-tuple-element.121), channel_id=1, source_target_pairs={{0,3},{1,2},{2,1},{3,0},{4,7},{5,6},{6,5},{7,4},{8,11},{9,10},{10,... | collective-permute-start | bytes 786440 | tf_op jit(solution)/shard_map/ppermute | solution.py:332
  28.3 12.8 %collective-permute-start.7 = (bf16[512,512]{1,0:T(8,128)(2,1)S(1)}, bf16[512,512]{1,0:T(8,128)(2,1)S(1)}, u32[]{:S(2)}, u32[]{:S(2)}) collective-permute-start(bf16[512,512]{1,0:T(8,128)(2,1)S(1)} %get-tuple-element.112), channel_id=1, source_target_pairs={{0,4},{4,0},{1,5},{5,1},{2,6},{6,2},{3,7},{7,3},{8,12},{12,8},{9,1... | collective-permute-start | bytes 1572872 | tf_op jit(solution)/shard_map/ppermute | solution.py:388
  29.8 12.5 %collective-permute-start.8 = (bf16[512,512]{1,0:T(8,128)(2,1)S(1)}, bf16[512,512]{1,0:T(8,128)(2,1)S(1)}, u32[]{:S(2)}, u32[]{:S(2)}) collective-permute-start(bf16[512,512]{1,0:T(8,128)(2,1)S(1)} %get-tuple-element.114), channel_id=1, source_target_pairs={{0,8},{8,0},{16,24},{24,16},{1,9},{9,1},{17,25},{25,17},{2,10},{10... | collective-permute-start | bytes 1572872 | tf_op jit(solution)/shard_map/ppermute | solution.py:388
  42.5 6.4 %collective-permute-start.12 = (bf16[256,512]{1,0:T(8,128)(2,1)S(1)}, bf16[256,512]{1,0:T(8,128)(2,1)S(1)}, u32[]{:S(2)}, u32[]{:S(2)}) collective-permute-start(bf16[256,512]{1,0:T(8,128)(2,1)S(1)} %get-tuple-element.125), channel_id=1, source_target_pairs={{0,8},{8,0},{16,24},{24,16},{1,9},{9,1},{17,25},{25,17},{2,10},{10... | collective-permute-start | bytes 786440 | tf_op jit(solution)/shard_map/ppermute | solution.py:357
  44.2 7.1 %collective-permute-start.13 = (bf16[256,512]{1,0:T(8,128)(2,1)S(1)}, bf16[256,512]{1,0:T(8,128)(2,1)S(1)}, u32[]{:S(2)}, u32[]{:S(2)}) collective-permute-start(bf16[256,512]{1,0:T(8,128)(2,1)S(1)} %get-tuple-element.126), channel_id=1, source_target_pairs={{0,4},{4,0},{1,5},{5,1},{2,6},{6,2},{3,7},{7,3},{8,12},{12,8},{9,1... | collective-permute-start | bytes 786440 | tf_op jit(solution)/shard_map/ppermute | solution.py:357
  51.3 17.3 %collective-permute-start.14 = (bf16[512,768]{1,0:T(8,128)(2,1)S(1)}, bf16[512,768]{1,0:T(8,128)(2,1)S(1)}, u32[]{:S(2)}, u32[]{:S(2)}) collective-permute-start(bf16[512,768]{1,0:T(8,128)(2,1)S(1)} %get-tuple-element.127), channel_id=1, source_target_pairs={{0,4},{4,0},{1,5},{5,1},{2,6},{6,2},{3,7},{7,3},{8,12},{12,8},{9,1... | collective-permute-start | bytes 2359304 | tf_op jit(solution)/shard_map/ppermute | solution.py:388
  51.8 9.6 %collective-permute-start.15 = (bf16[512,256]{1,0:T(8,128)(2,1)S(1)}, bf16[512,256]{1,0:T(8,128)(2,1)S(1)}, u32[]{:S(2)}, u32[]{:S(2)}) collective-permute-start(bf16[512,256]{1,0:T(8,128)(2,1)S(1)} %get-tuple-element.129), channel_id=1, source_target_pairs={{0,8},{8,0},{16,24},{24,16},{1,9},{9,1},{17,25},{25,17},{2,10},{10... | collective-permute-start | bytes 786440 | tf_op jit(solution)/shard_map/ppermute | solution.py:388
  52.6 21.1 %collective-permute-start.16 = (bf16[256,1024]{1,0:T(8,128)(2,1)S(1)}, bf16[256,1024]{1,0:T(8,128)(2,1)S(1)}, u32[]{:S(2)}, u32[]{:S(2)}) collective-permute-start(bf16[256,1024]{1,0:T(8,128)(2,1)S(1)} %shard_map.99), channel_id=1, source_target_pairs={{0,16},{8,24},{16,0},{24,8},{1,17},{9,25},{17,1},{25,9},{2,18},{10... | collective-permute-start | bytes 1572872 | tf_op jit(solution)/shard_map/ppermute | solution.py:378
  55.3 35.0 %collective-permute-start.26 = (bf16[128,4096]{1,0:T(8,128)(2,1)S(1)}, bf16[128,4096]{1,0:T(8,128)(2,1)S(1)}, u32[]{:S(2)}, u32[]{:S(2)}) collective-permute-start(bf16[128,4096]{1,0:T(8,128)(2,1)S(1)} %slice.4), channel_id=1, source_target_pairs={{0,1},{1,0},{2,3},{3,2},{4,5},{5,4},{6,7},{7,6},{8,9},{9,8},{10,11... | collective-permute-start | bytes 3145736 | tf_op jit(solution)/shard_map/ppermute | solution.py:387
  68.8 10.3 %collective-permute-start.17 = (bf16[256,768]{1,0:T(8,128)(2,1)S(1)}, bf16[256,768]{1,0:T(8,128)(2,1)S(1)}, u32[]{:S(2)}, u32[]{:S(2)}) collective-permute-start(bf16[256,768]{1,0:T(8,128)(2,1)S(1)} %get-tuple-element.137), channel_id=1, source_target_pairs={{0,8},{8,0},{16,24},{24,16},{1,9},{9,1},{17,25},{25,17},{2,10},{10... | collective-permute-start | bytes 1179656 | tf_op jit(solution)/shard_map/ppermute | solution.py:357
  68.9 5.0 %collective-permute-start.18 = (bf16[256,256]{1,0:T(8,128)(2,1)S(1)}, bf16[256,256]{1,0:T(8,128)(2,1)S(1)}, u32[]{:S(2)}, u32[]{:S(2)}) collective-permute-start(bf16[256,256]{1,0:T(8,128)(2,1)S(1)} %get-tuple-element.139), channel_id=1, source_target_pairs={{0,4},{4,0},{1,5},{5,1},{2,6},{6,2},{3,7},{7,3},{8,12},{12,8},{9,1... | collective-permute-start | bytes 393224 | tf_op jit(solution)/shard_map/ppermute | solution.py:357
  80.8 26.1 %collective-permute-start.28 = (bf16[256,1024]{1,0:T(8,128)(2,1)S(1)}, bf16[256,1024]{1,0:T(8,128)(2,1)S(1)}, u32[]{:S(2)}, u32[]{:S(2)}) collective-permute-start(bf16[256,1024]{1,0:T(8,128)(2,1)S(1)} %get-tuple-element.160.refs_8_), channel_id=1, source_target_pairs={{0,16},{8,24},{16,0},{24,8},{1,17},{9,25},{17,1},{25,9},{2,18},{10... | collective-permute-start | bytes 1572872 | tf_op jit(solution)/shard_map/ppermute | solution.py:426
  84.5 8.2 %collective-permute-start.19 = (bf16[128,1024]{1,0:T(8,128)(2,1)S(1)}, bf16[128,1024]{1,0:T(8,128)(2,1)S(1)}, u32[]{:S(2)}, u32[]{:S(2)}) collective-permute-start(bf16[128,1024]{1,0:T(8,128)(2,1)S(1)} %copy-done.10), channel_id=1, source_target_pairs={{0,2},{1,3},{2,0},{3,1},{4,6},{5,7},{6,4},{7,5},{8,10},{9,11},{10,... | collective-permute-start | bytes 786440 | tf_op jit(solution)/shard_map/ppermute | solution.py:350
  84.6 11.8 %collective-permute-start.20 = (bf16[128,1024]{1,0:T(8,128)(2,1)S(1)}, bf16[128,1024]{1,0:T(8,128)(2,1)S(1)}, u32[]{:S(2)}, u32[]{:S(2)}) collective-permute-start(bf16[128,1024]{1,0:T(8,128)(2,1)S(1)} %copy-done.9), channel_id=1, source_target_pairs={{0,3},{1,2},{2,1},{3,0},{4,7},{5,6},{6,5},{7,4},{8,11},{9,10},{10,... | collective-permute-start | bytes 786440 | tf_op jit(solution)/shard_map/ppermute | solution.py:350
  89.8 8.4 %collective-permute-start.21 = (bf16[128,1024]{1,0:T(8,128)(2,1)S(1)}, bf16[128,1024]{1,0:T(8,128)(2,1)S(1)}, u32[]{:S(2)}, u32[]{:S(2)}) collective-permute-start(bf16[128,1024]{1,0:T(8,128)(2,1)S(1)} %copy-done.8), channel_id=1, source_target_pairs={{0,6},{1,7},{2,4},{3,5},{4,2},{5,3},{6,0},{7,1},{8,14},{9,15},{10,... | collective-permute-start | bytes 786440 | tf_op jit(solution)/shard_map/ppermute | solution.py:350
  90.3 27.4 %collective-permute-start.27 = (bf16[256,1024]{1,0:T(8,128)(2,1)S(1)}, bf16[256,1024]{1,0:T(8,128)(2,1)S(1)}, u32[]{:S(2)}, u32[]{:S(2)}) collective-permute-start(bf16[256,1024]{1,0:T(8,128)(2,1)S(1)} %get-tuple-element.160.refs_8_), channel_id=1, source_target_pairs={{0,8},{8,0},{16,24},{24,16},{1,9},{9,1},{17,25},{25,17},{2,10},{10... | collective-permute-start | bytes 1572872 | tf_op jit(solution)/shard_map/ppermute | solution.py:426
  92.8 21.7 %collective-permute-start.22 = (bf16[128,1024]{1,0:T(8,128)(2,1)S(1)}, bf16[128,1024]{1,0:T(8,128)(2,1)S(1)}, u32[]{:S(2)}, u32[]{:S(2)}) collective-permute-start(bf16[128,1024]{1,0:T(8,128)(2,1)S(1)} %copy-done.7), channel_id=1, source_target_pairs={{0,7},{1,6},{2,5},{3,4},{4,3},{5,2},{6,1},{7,0},{8,15},{9,14},{10,... | collective-permute-start | bytes 786440 | tf_op jit(solution)/shard_map/ppermute | solution.py:350
  96.4 18.8 %collective-permute-start.23 = (bf16[128,1024]{1,0:T(8,128)(2,1)S(1)}, bf16[128,1024]{1,0:T(8,128)(2,1)S(1)}, u32[]{:S(2)}, u32[]{:S(2)}) collective-permute-start(bf16[128,1024]{1,0:T(8,128)(2,1)S(1)} %copy-done.6), channel_id=1, source_target_pairs={{0,1},{1,0},{2,3},{3,2},{4,5},{5,4},{6,7},{7,6},{8,9},{9,8},{10,11... | collective-permute-start | bytes 786440 | tf_op jit(solution)/shard_map/ppermute | solution.py:350
  98.1 17.1 %collective-permute-start.24 = (bf16[128,1024]{1,0:T(8,128)(2,1)S(1)}, bf16[128,1024]{1,0:T(8,128)(2,1)S(1)}, u32[]{:S(2)}, u32[]{:S(2)}) collective-permute-start(bf16[128,1024]{1,0:T(8,128)(2,1)S(1)} %copy-done.5), channel_id=1, source_target_pairs={{0,4},{1,5},{2,6},{3,7},{4,0},{5,1},{6,2},{7,3},{8,12},{9,13},{10,... | collective-permute-start | bytes 786440 | tf_op jit(solution)/shard_map/ppermute | solution.py:350
  106.9 10.8 %collective-permute-start.25 = (bf16[128,1024]{1,0:T(8,128)(2,1)S(1)}, bf16[128,1024]{1,0:T(8,128)(2,1)S(1)}, u32[]{:S(2)}, u32[]{:S(2)}) collective-permute-start(bf16[128,1024]{1,0:T(8,128)(2,1)S(1)} %copy-done.4), channel_id=1, source_target_pairs={{0,5},{1,4},{2,7},{3,6},{4,1},{5,0},{6,3},{7,2},{8,13},{9,12},{10,... | collective-permute-start | bytes 786440 | tf_op jit(solution)/shard_map/ppermute | solution.py:350
  114.5 12.6 %collective-permute-start.29 = (bf16[256,1024]{1,0:T(8,128)(2,1)S(1)}, bf16[256,1024]{1,0:T(8,128)(2,1)S(1)}, u32[]{:S(2)}, u32[]{:S(2)}) collective-permute-start(bf16[256,1024]{1,0:T(8,128)(2,1)S(1)} %collective-permute-done.28.refs_10_), channel_id=1, source_target_pairs={{0,8},{8,0},{16,24},{24,16},{1,9},{9,1},{17,25},{25,17},{2,10},{10... | collective-permute-start | bytes 1572872 | tf_op jit(solution)/shard_map/ppermute | solution.py:426
  131.9 9.1 %collective-permute-start.31 = (bf16[256,512]{1,0:T(8,128)(2,1)S(1)}, bf16[256,512]{1,0:T(8,128)(2,1)S(1)}, u32[]{:S(2)}, u32[]{:S(2)}) collective-permute-start(bf16[256,512]{1,0:T(8,128)(2,1)S(1)} %get-tuple-element.172), channel_id=1, source_target_pairs={{0,4},{4,0},{1,5},{5,1},{2,6},{6,2},{3,7},{7,3},{8,12},{12,8},{9,1... | collective-permute-start | bytes 786440 | tf_op jit(solution)/shard_map/ppermute | solution.py:446
  134.4 8.1 %collective-permute-start.32 = (bf16[256,512]{1,0:T(8,128)(2,1)S(1)}, bf16[256,512]{1,0:T(8,128)(2,1)S(1)}, u32[]{:S(2)}, u32[]{:S(2)}) collective-permute-start(bf16[256,512]{1,0:T(8,128)(2,1)S(1)} %get-tuple-element.173), channel_id=1, source_target_pairs={{0,1},{1,0},{2,3},{3,2},{4,5},{5,4},{6,7},{7,6},{8,9},{9,8},{10,11... | collective-permute-start | bytes 786440 | tf_op jit(solution)/shard_map/ppermute | solution.py:447
  (16 other events, 245.8 us)

commit v8 on v7

--- a/solution.py
+++ b/solution.py
@@ -181,15 +181,20 @@
     out[...] = block_sum(*inputs[:4], inputs[4:]).astype(bf16)
 
 
-def update_kernel(replicas, *refs):
-    *inputs, weight, momentum, share, new_outer, new_momentum = refs
-    summed = block_sum(*inputs[:4], inputs[4:])
-    pseudo_grad = weight[...] - summed / replicas
+def outer_step(replicas, inputs, weight, momentum):
+    pseudo_grad = weight[...] - block_sum(*inputs[:4], inputs[4:]) / replicas
     moment = nesterov * momentum[...] + pseudo_grad
-    outer = weight[...] - outer_rate * (pseudo_grad + nesterov * moment)
-    share[...] = outer.astype(bf16)
-    new_outer[...] = outer
-    new_momentum[...] = moment
+    return weight[...] - outer_rate * (pseudo_grad + nesterov * moment), moment
+
+
+def share_kernel(replicas, *refs):
+    *inputs, weight, momentum, share = refs
+    share[...] = outer_step(replicas, inputs, weight, momentum)[0].astype(bf16)
+
+
+def state_kernel(replicas, *refs):
+    *inputs, weight, momentum, new_outer, new_momentum = refs
+    new_outer[...], new_momentum[...] = outer_step(replicas, inputs, weight, momentum)
 
 
 def keys_kernel(acts_count, counts, at, *refs):
@@ -295,7 +300,7 @@
         out_specs=HBM,
         scratch_shapes=[pltpu.SemaphoreType.DMA((len(parts),))],
         compiler_params=pltpu.CompilerParams(vmem_limit_bytes=16 * MIB),
-        cost_estimate=pl.CostEstimate(flops=1 << 34, bytes_accessed=4 * rows * width * len(parts), transcendentals=0),
+        cost_estimate=pl.CostEstimate(flops=0, bytes_accessed=4 * rows * width * len(parts), transcendentals=0),
     )(jnp.stack(starts).astype(jnp.int32), *parts)
 
 
@@ -320,15 +325,33 @@
     shifts = [(k, s) for s in range(fsdp) for k in range(CORES)]
     stages = [(m + 1, m) for m in range(nz - 2, -1, -2)]
 
+    far = [(i, k, s) for k in range(CORES) for i in range(PAIR) for s in range(fsdp)]
+    early = [(0, 1, 0), (1, 0, 0)]
+    late = [e for e in far if e not in early]
+    index = lambda i, k, s: ((i % PAIR) * CORES + k % CORES) * fsdp + s % fsdp
+    every = [(i, k, s) for i in range(PAIR) for k in range(CORES) for s in range(fsdp)]
+    mine, nexts = {}, {}
+
+    def next_groups(places):
+        return [[column(z ^ m, (x + i) % PAIR, k, s) for m in range(nz)] for i, k, s in places]
+
+    def send_next(i, k, s):
+        pairs = [(index(*e), index(e[0] + i, e[1] + k, e[2] + s)) for e in every]
+        nexts[i, k, s] = lax.ppermute(mine[i, k, s], ("x", "core", "fsdp"), pairs) if i or k or s else mine[i, k, s]
+
     cots = {(0, 0): cotangent}
     for s in range(1, fsdp):
         cots[0, s] = lax.ppermute(cotangent, "fsdp", ring(fsdp, s))
     columns = [[column(z ^ m, (x + i) % PAIR, k, s) for m in ms for i in range(PAIR)] for ms in stages for k, s in shifts]
-    (mine,), _ = pack([(activations, 1, share, columns)])
+    items = [(activations, 1, share, columns), (next_activations, 1, share, next_groups(early))]
+    (packed, parts), _ = pack(items)
+    mine.update(zip(early, parts))
+    for e in early:
+        send_next(*e)
     acts = []
     for stage in range(len(stages)):
         came = []
-        for (k, s), part in zip(shifts, mine[stage * len(shifts) :]):
+        for (k, s), part in zip(shifts, packed[stage * len(shifts) :]):
             came.append(part if (k, s) == (0, 0) else lax.ppermute(part, ("core", "fsdp"), pair_ring(k, s)))
         acts.append(came)
     other_weight = lax.ppermute(own_weight, "core", swap)
@@ -336,18 +359,10 @@
     for s in range(1, fsdp):
         cots[1, s] = lax.ppermute(cots[0, s], "core", swap)
 
-    far = [(i, k, s) for k in range(CORES) for i in range(PAIR) for s in range(fsdp)]
-    index = lambda i, k, s: ((i % PAIR) * CORES + k % CORES) * fsdp + s % fsdp
-    every = [(i, k, s) for i in range(PAIR) for k in range(CORES) for s in range(fsdp)]
-    groups = [[column(z ^ m, (x + i) % PAIR, k, s) for m in range(nz)] for i, k, s in far]
     wanted = [cots[0, s] for s in range(1, fsdp)]
-    (parts,), wanted = pack([(next_activations, 1, share, groups)], wanted, pltpu.HBM)
+    (parts,), wanted = pack([(next_activations, 1, share, next_groups(late))], wanted, pltpu.HBM)
     cots.update({(0, s): got for s, got in enumerate(wanted, 1)})
-    mine, nexts = dict(zip(far, parts)), {}
-
-    def send_next(i, k, s):
-        pairs = [(index(*e), index(e[0] + i, e[1] + k, e[2] + s)) for e in every]
-        nexts[i, k, s] = lax.ppermute(mine[i, k, s], ("x", "core", "fsdp"), pairs) if i or k or s else mine[i, k, s]
+    mine.update(zip(late, parts))
 
     ordered = [cots[k, s] for k, s in shifts]
     across_x, across_z = ring(PAIR, 1), [(i, i ^ 1) for i in range(nz)]
@@ -362,8 +377,10 @@
         blocks = [((z ^ m) * PAIR + (x + i) % PAIR) * CORES + c for m in ms for i in range(PAIR)]
         place = jnp.stack(blocks).astype(jnp.int32)
         if not stage:
-            place, *held = lax.optimization_barrier((place, *[mine[e] for e in far]))
-            mine.update(zip(far, held))
+            held = (place, *[mine[e] for e in late], *[nexts[e] for e in early])
+            place, *held = lax.optimization_barrier(held)
+            mine.update(zip(late, held))
+            nexts.update(zip(early, held[len(late) :]))
         if stage:
             place, to_z, to_x = lax.optimization_barrier((place, to_z, to_x))
             m = stages[stage - 1][1]
@@ -400,19 +417,25 @@
     inputs[0], inputs[2] = small_call(
         gather_kernel, [jax.ShapeDtypeStruct(part.shape, f32) for part in (keep_left, keep_right)], keep_left, keep_right, *inputs[4:], spec=pl.BlockSpec(), weight=200
     )
-    whole = jax.ShapeDtypeStruct((share, kv), f32)
-    share_rows, new_outer, new_momentum = small_call(
-        functools.partial(update_kernel, nz * PAIR * CORES),
-        [jax.ShapeDtypeStruct((share, kv), bf16), whole, whole],
-        *inputs[:4],
-        outer_weight,
-        outer_momentum,
+    replicas = nz * PAIR * CORES
+    inputs = [*inputs[:4], outer_weight, outer_momentum]
+    (share_rows,) = small_call(
+        functools.partial(share_kernel, replicas),
+        [jax.ShapeDtypeStruct((share, kv), bf16)],
+        *inputs,
         spec=pl.BlockSpec(),
     )
-
-    share_rows, *held = lax.optimization_barrier((share_rows, *[mine[e] for e in far]))
-    mine.update(zip(far, held))
-    for e in far:
+    share_rows, *inputs = lax.optimization_barrier((share_rows, *inputs))
+    new_outer, new_momentum = small_call(
+        functools.partial(state_kernel, replicas),
+        [jax.ShapeDtypeStruct((share, kv), f32)] * 2,
+        *inputs,
+        spec=pl.BlockSpec(),
+        weight=1 << 17,
+    )
+    share_rows, *held = lax.optimization_barrier((share_rows, *[mine[e] for e in late]))
+    mine.update(zip(late, held))
+    for e in late:
         send_next(*e)
 
     rows = {}
@@ -420,11 +443,10 @@
         low = m & -m
         pieces = [share_rows] if m == low else list(rows[m ^ low])
         if m == nz - 1:
-            share_rows, *parts = lax.optimization_barrier((share_rows, *parts))
-            input_grad = join(parts, [((f + s) % fsdp) * width for s in range(fsdp)])
-            pieces[0], input_grad = lax.optimization_barrier((pieces[0], input_grad))
+            pieces[0], new_outer = lax.optimization_barrier((pieces[0], new_outer))
         rows[m] = [lax.ppermute(piece, "z", [(i, i ^ low) for i in range(nz)]) for piece in pieces]
     rows = [[share_rows]] + [rows[m] for m in range(1, nz)]
+    input_grad = join(parts, [((f + s) % fsdp) * width for s in range(fsdp)])
 
     half = len(far) // CORES
     near, away = [nexts[e] for e in far[:half]], [nexts[e] for e in far[half:]]

time: 149 us -> 149 us (level)
  starting transfers between devices: 46.8 us -> 38.9 us
  waiting for transfers between devices: 75.2 us -> 82.1 us
    ppermute x7, starting transfers between devices: 13.9 us -> 6.76 us  [send_next(): lax.ppermute(mine[i, k, s], ('x', 'core', 'fsdp'), pairs)]
    ppermute x3, waiting for transfers between devices: 15.6 us -> 19 us  [local(): lax.ppermute(piece, 'z', [(i, i ^ low) for i in range(nz)])]
    ppermute x2, waiting for transfers between devices: 5.8 us -> 9.09 us  [local(): lax.ppermute(to_z, 'z', across_z)]
    ppermute x7, waiting for transfers between devices: 5.94 us -> 7.92 us  [send_next(): lax.ppermute(mine[i, k, s], ('x', 'core', 'fsdp'), pairs)]
    ppermute x6, waiting for transfers between devices: 4.08 us -> 2.25 us  [local(): lax.ppermute(part, ('core', 'fsdp'), pair_ring(k, s))]
    ppermute x1, waiting for transfers between devices: 4.26 us -> 6.01 us  [local(): lax.ppermute(block_total, 'z', [(i, i ^ low) for i in range(nz)])]
    ppermute x2, waiting for transfers between devices: 14.5 us -> 12.9 us  [local(): lax.ppermute(to_x, 'x', across_x)]
    pallas_call x8 -> x9, Pallas kernels: 3.3 us -> 3.68 us  [small_call(): pl.pallas_call(kernel, out_shape=shapes, in_specs=[spec] * len(args), out...]
  transfers between devices with their start and end apart: 35 -> 35, of which waited for: 21 -> 20; matrix products, arithmetic and copies ran while one was open for 2% -> 2% of each run, Pallas kernels for 14% -> 15%
where the time goes in v8:
time: 149 us
  waiting for transfers between devices  82.1 us (55%)
  starting transfers between devices  38.9 us (26%)
  Pallas kernels  23.1 us (16%)
  matrix products  2.38 us (2%)
    ppermute x3, waiting for transfers between devices, local(): lax.ppermute(piece, 'z', [(i, i ^ low) for i in range(nz)])  19 us
    ppermute x2, waiting for transfers between devices, local(): lax.ppermute(to_x, 'x', across_x)  12.9 us
    ppermute x2, waiting for transfers between devices, home(): from_x = lax.ppermute(to_x, 'x', ring(PAIR, 1))  10.7 us
    ppermute x2, waiting for transfers between devices, local(): lax.ppermute(to_z, 'z', across_z)  9.09 us
    ppermute x7, waiting for transfers between devices, send_next(): lax.ppermute(mine[i, k, s], ('x', 'core', 'fsdp'), pairs)  7.92 us
    pallas_call x2, Pallas kernels, inner_blocks(): pl.pallas_call(functools.partial(inner_kernel, pieces, share, inner_rate...  7.74 us
    pallas_call x2, Pallas kernels, pack(): pl.pallas_call(functools.partial(pack_kernel, plan), out_shape=shapes, in...  7.15 us
    ppermute x3, starting transfers between devices, local(): lax.ppermute(piece, 'z', [(i, i ^ low) for i in range(nz)])  7.08 us
  transfers between devices with their start and end apart: 35, of which 20 were waited for; matrix products, arithmetic and copies ran while one was open for 2% of the time, Pallas kernels for 15%

profile of v8, /device:TPU:0, one launch (start us, length us, event | category | flops | bytes accessed | tf_op | source)
XLA Modules:
  0.0 148.7 jit_solution(8906597114765423944)
XLA Ops:
  1.2 2.9 %collective-permute-start = (bf16[128,1024]{1,0:T(8,128)(2,1)}, bf16[128,1024]{1,0:T(8,128)(2,1)S(1)}, u32[]{:S(2)}, u32[]{:S(2)}) collective-permute-start(bf16[128,1024]{1,0:T(8,128)(2,1)} %refs_4_.4), channel_id=1, source_target_pairs={{0,1},{1,0},{2,3},{3,2},{4,5},{5,4},{6,7},{7,6},{8,9},{9,8},{10,11... | collective-permute-start | bytes 786440 | tf_op jit(solution)/shard_map/ppermute | solution.py:344
  4.3 3.6 %shard_map.94 = (bf16[128,1024]{1,0:T(8,128)(2,1)S(1)}, bf16[128,1024]{1,0:T(8,128)(2,1)}, bf16[128,1024]{1,0:T(8,128)(2,1)}, bf16[128,1024]{1,0:T(8,128)(2,1)},...) custom-call(s32[40]{0:T(128)S(1)} %stack.211.starts, ...), custom_call_target="tpu_custom_call" | custom-call | bytes 20971520 | tf_op jit(solution)/shard_map/pallas_call | solution.py:72
  10.9 1.7 %collective-permute-start.4 = (bf16[128,1024]{1,0:T(8,128)(2,1)}, bf16[128,1024]{1,0:T(8,128)(2,1)S(1)}, u32[]{:S(2)}, u32[]{:S(2)}) collective-permute-start(bf16[128,1024]{1,0:T(8,128)(2,1)} %get-tuple-element.106), channel_id=1, source_target_pairs={{0,1},{1,0},{2,3},{3,2},{4,5},{5,4},{6,7},{7,6},{8,9},{9,8},{10,11... | collective-permute-start | bytes 786440 | tf_op jit(solution)/shard_map/ppermute | solution.py:355
  12.7 2.4 %collective-permute-done.1.refs_0_ = bf16[128,1024]{1,0:T(8,128)(2,1)S(1)} collective-permute-done((bf16[128,1024]{1,0:T(8,128)(2,1)S(1)}, bf16[128,1024]{1,0:T(8,128)(2,1)S(1)}, u32[]{:S(2)}, u32[]{:S(2)}) %collective-permute-start.1) | collective-permute-done | bytes 262176 | tf_op jit(solution)/shard_map/ppermute | solution.py:340
  15.1 2.6 %collective-permute-start.5 = (bf16[128,1024]{1,0:T(8,128)(2,1)}, bf16[128,1024]{1,0:T(8,128)(2,1)S(1)}, u32[]{:S(2)}, u32[]{:S(2)}) collective-permute-start(bf16[128,1024]{1,0:T(8,128)(2,1)} %get-tuple-element.107), channel_id=1, source_target_pairs={{0,3},{1,2},{2,1},{3,0},{4,7},{5,6},{6,5},{7,4},{8,11},{9,10},{10,... | collective-permute-start | bytes 786440 | tf_op jit(solution)/shard_map/ppermute | solution.py:355
  18.4 3.6 %shard_map.93 = (bf16[128,1024]{1,0:T(8,128)(2,1)}, bf16[128,1024]{1,0:T(8,128)(2,1)}, bf16[128,1024]{1,0:T(8,128)(2,1)}, bf16[128,1024]{1,0:T(8,128)(2,1)}, bf1...) custom-call(s32[24]{0:T(128)S(1)} %stack.202.starts, bf16[128,8192]{1,0:T(8,128)(2,1)} %refs_1_.1), custom_call_target="tpu_custom_call" | custom-call | bytes 12582912 | tf_op jit(solution)/shard_map/pallas_call | solution.py:72
  22.5 2.2 %collective-permute-done.5.refs_3_ = bf16[128,1024]{1,0:T(8,128)(2,1)S(1)} collective-permute-done((bf16[128,1024]{1,0:T(8,128)(2,1)}, bf16[128,1024]{1,0:T(8,128)(2,1)S(1)}, u32[]{:S(2)}, u32[]{:S(2)}) %collective-permute-start.5) | collective-permute-done | bytes 262176 | tf_op jit(solution)/shard_map/ppermute | solution.py:355
  24.7 1.8 %collective-permute-start.13 = (bf16[128,1024]{1,0:T(8,128)(2,1)S(1)}, bf16[128,1024]{1,0:T(8,128)(2,1)S(1)}, u32[]{:S(2)}, u32[]{:S(2)}) collective-permute-start(bf16[128,1024]{1,0:T(8,128)(2,1)S(1)} %get-tuple-element.123), channel_id=1, source_target_pairs={{0,3},{1,2},{2,1},{3,0},{4,7},{5,6},{6,5},{7,4},{8,11},{9,10},{10,... | collective-permute-start | bytes 786440 | tf_op jit(solution)/shard_map/ppermute | solution.py:355
  26.5 4.0 %shard_map.95 = (bf16[512,512]{1,0:T(8,128)(2,1)S(1)}, f32[512,512]{1,0:T(8,128)S(1)}, bf16[512,512]{1,0:T(8,128)(2,1)S(1)}, f32[512,512]{1,0:T(8,128)S(1)}) custom-call(s32[4]{0:T(128)S(1)} %pad_add_fusion.place, bf16[128,1024]{1,0:T(8,128)(2,1)S(1)} %get-tuple-element.104.refs_0_, bf16[128,1024]{1,0:T(8,128)(2,1)S(1)} %collective-permute-done.3.refs_1_, ...), custom_call_target="tpu_custom_call" | custom-call | flops 134217728 | bytes 262144 | tf_op jit(solution)/shard_map/pallas_call | solution.py:135
  30.6 1.6 %collective-permute-start.9 = (bf16[512,512]{1,0:T(8,128)(2,1)S(1)}, bf16[512,512]{1,0:T(8,128)(2,1)S(1)}, u32[]{:S(2)}, u32[]{:S(2)}) collective-permute-start(bf16[512,512]{1,0:T(8,128)(2,1)S(1)} %get-tuple-element.114), channel_id=1, source_target_pairs={{0,4},{4,0},{1,5},{5,1},{2,6},{6,2},{3,7},{7,3},{8,12},{12,8},{9,1... | collective-permute-start | bytes 1572872 | tf_op jit(solution)/shard_map/ppermute | solution.py:405
  32.1 1.6 %collective-permute-start.10 = (bf16[512,512]{1,0:T(8,128)(2,1)S(1)}, bf16[512,512]{1,0:T(8,128)(2,1)S(1)}, u32[]{:S(2)}, u32[]{:S(2)}) collective-permute-start(bf16[512,512]{1,0:T(8,128)(2,1)S(1)} %get-tuple-element.116), channel_id=1, source_target_pairs={{0,8},{8,0},{16,24},{24,16},{1,9},{9,1},{17,25},{25,17},{2,10},{10... | collective-permute-start | bytes 1572872 | tf_op jit(solution)/shard_map/ppermute | solution.py:405
  33.7 2.4 %convolution_convert_fusion.refs_0_ = bf16[256,4096]{1,0:T(8,128)(2,1)S(1)} fusion(bf16[128,1024]{1,0:T(8,128)(2,1)S(1)} %collective-permute-done.refs_6_, bf16[128,1024]{1,0:T(8,128)(2,1)S(1)} %copy-done, bf16[1,4096,1024]{2,1,0:T(8,128)(2,1)S(1)} %bitcast.49), kind=kOutput, calls=%fused_computation | convolution fusion | flops 2149580800 | bytes 11010048 | tf_op jit(solution)/shard_map/dot_general | solution.py:398
  36.2 8.3 %collective-permute-done.9.from_x = bf16[512,512]{1,0:T(8,128)(2,1)S(1)} collective-permute-done((bf16[512,512]{1,0:T(8,128)(2,1)S(1)}, bf16[512,512]{1,0:T(8,128)(2,1)S(1)}, u32[]{:S(2)}, u32[]{:S(2)}) %collective-permute-start.9) | collective-permute-done | bytes 524320 | tf_op jit(solution)/shard_map/ppermute | solution.py:405
  45.9 1.6 %collective-permute-start.14 = (bf16[256,512]{1,0:T(8,128)(2,1)S(1)}, bf16[256,512]{1,0:T(8,128)(2,1)S(1)}, u32[]{:S(2)}, u32[]{:S(2)}) collective-permute-start(bf16[256,512]{1,0:T(8,128)(2,1)S(1)} %get-tuple-element.127), channel_id=1, source_target_pairs={{0,8},{8,0},{16,24},{24,16},{1,9},{9,1},{17,25},{25,17},{2,10},{10... | collective-permute-start | bytes 786440 | tf_op jit(solution)/shard_map/ppermute | solution.py:372
  48.1 3.7 %shard_map.97 = (bf16[512,768]{1,0:T(8,128)(2,1)S(1)}, f32[512,768]{1,0:T(8,128)S(1)}, bf16[512,256]{1,0:T(8,128)(2,1)S(1)}, f32[512,256]{1,0:T(8,128)S(1)}) custom-call(s32[4]{0:T(128)S(1)} %pad_add_fusion.1.place, bf16[128,1024]{1,0:T(8,128)(2,1)S(1)} %get-tuple-element.120.refs_0_, bf16[128,1024]{1,0:T(8,128)(2,1)S(1)} %collective-permute-done.11.refs_1_, ...), custom_call_target="tpu_custom_call" | custom-call | flops 134217728 | bytes 262144 | tf_op jit(solution)/shard_map/pallas_call | solution.py:135
  55.6 2.7 %collective-permute-start.18 = (bf16[256,1024]{1,0:T(8,128)(2,1)S(1)}, bf16[256,1024]{1,0:T(8,128)(2,1)S(1)}, u32[]{:S(2)}, u32[]{:S(2)}) collective-permute-start(bf16[256,1024]{1,0:T(8,128)(2,1)S(1)} %shard_map.99), channel_id=1, source_target_pairs={{0,16},{8,24},{16,0},{24,8},{1,17},{9,25},{17,1},{25,9},{2,18},{10... | collective-permute-start | bytes 1572872 | tf_op jit(solution)/shard_map/ppermute | solution.py:395
  59.1 7.9 %collective-permute-done.17.from_z = bf16[512,256]{1,0:T(8,128)(2,1)S(1)} collective-permute-done((bf16[512,256]{1,0:T(8,128)(2,1)S(1)}, bf16[512,256]{1,0:T(8,128)(2,1)S(1)}, u32[]{:S(2)}, u32[]{:S(2)}) %collective-permute-start.17) | collective-permute-done | bytes 262176 | tf_op jit(solution)/shard_map/ppermute | solution.py:405
  67.0 4.6 %collective-permute-done.16.from_x = bf16[512,768]{1,0:T(8,128)(2,1)S(1)} collective-permute-done((bf16[512,768]{1,0:T(8,128)(2,1)S(1)}, bf16[512,768]{1,0:T(8,128)(2,1)S(1)}, u32[]{:S(2)}, u32[]{:S(2)}) %collective-permute-start.16) | collective-permute-done | bytes 786464 | tf_op jit(solution)/shard_map/ppermute | solution.py:405
  73.1 6.0 %collective-permute-done.18.refs_0_ = bf16[256,1024]{1,0:T(8,128)(2,1)S(1)} collective-permute-done((bf16[256,1024]{1,0:T(8,128)(2,1)S(1)}, bf16[256,1024]{1,0:T(8,128)(2,1)S(1)}, u32[]{:S(2)}, u32[]{:S(2)}) %collective-permute-start.18) | collective-permute-done | bytes 524320 | tf_op jit(solution)/shard_map/ppermute | solution.py:395
  79.2 5.4 %collective-permute-done.19.refs_1_ = bf16[256,768]{1,0:T(8,128)(2,1)S(1)} collective-permute-done((bf16[256,768]{1,0:T(8,128)(2,1)S(1)}, bf16[256,768]{1,0:T(8,128)(2,1)S(1)}, u32[]{:S(2)}, u32[]{:S(2)}) %collective-permute-start.19) | collective-permute-done | bytes 393248 | tf_op jit(solution)/shard_map/ppermute | solution.py:372
  85.0 3.9 %collective-permute-start.27 = (bf16[256,1024]{1,0:T(8,128)(2,1)S(1)}, bf16[256,1024]{1,0:T(8,128)(2,1)S(1)}, u32[]{:S(2)}, u32[]{:S(2)}) collective-permute-start(bf16[256,1024]{1,0:T(8,128)(2,1)S(1)} %shard_map.101.refs_8_), channel_id=1, source_target_pairs={{0,16},{8,24},{16,0},{24,8},{1,17},{9,25},{17,1},{25,9},{2,18},{10... | collective-permute-start | bytes 1572872 | tf_op jit(solution)/shard_map/ppermute | solution.py:447
  89.6 1.9 %shard_map.103 = bf16[128,8192]{1,0:T(8,128)(2,1)} custom-call(s32[2]{0:T(128)S(1)} %pad_add_fusion.2.starts, bf16[256,4096]{1,0:T(8,128)(2,1)S(1)} %convolution_convert_fusion.refs_0_, bf16[128,4096]{1,0:T(8,128)(2,1)S(1)} %collective-permute-done.28.refs_1_), custom_call_target="tpu_custom_call" | custom-call | bytes 4194304 | tf_op jit(solution)/shard_map/pallas_call | solution.py:296
  91.5 2.5 %collective-permute-start.26 = (bf16[256,1024]{1,0:T(8,128)(2,1)S(1)}, bf16[256,1024]{1,0:T(8,128)(2,1)S(1)}, u32[]{:S(2)}, u32[]{:S(2)}) collective-permute-start(bf16[256,1024]{1,0:T(8,128)(2,1)S(1)} %shard_map.101.refs_8_), channel_id=1, source_target_pairs={{0,8},{8,0},{16,24},{24,16},{1,9},{9,1},{17,25},{25,17},{2,10},{10... | collective-permute-start | bytes 1572872 | tf_op jit(solution)/shard_map/ppermute | solution.py:447
  98.6 13.1 %collective-permute-done.27.refs_10_ = bf16[256,1024]{1,0:T(8,128)(2,1)S(1)} collective-permute-done((bf16[256,1024]{1,0:T(8,128)(2,1)S(1)}, bf16[256,1024]{1,0:T(8,128)(2,1)S(1)}, u32[]{:S(2)}, u32[]{:S(2)}) %collective-permute-start.27) | collective-permute-done | bytes 524320 | tf_op jit(solution)/shard_map/ppermute | solution.py:447
  113.2 1.7 %shard_map.104 = (f32[256,1024]{1,0:T(8,128)}, f32[256,1024]{1,0:T(8,128)}) custom-call(f32[256,768]{1,0:T(8,128)S(1)} %get-tuple-element.162.refs_0_, bf16[256,768]{1,0:T(8,128)(2,1)S(1)} %collective-permute-done.19.refs_1_, f32[256,256]{1,0:T(8,128)S(1)} %get-tuple-element.164.refs_2_, bf16[256,256]{1,0:T(8,128)(2,1)S(1)} %collective-permute-done.20.refs_3_, ...), custom_call_target="tpu_custom_call" | custom-call | flops 8589934592 | bytes 8589934592 | tf_op jit(solution)/shard_map/pallas_call | solution.py:271
  115.6 4.1 %collective-permute-done.25.refs_7_.refs_3_ = bf16[128,1024]{1,0:T(8,128)(2,1)S(1)} collective-permute-done((bf16[128,1024]{1,0:T(8,128)(2,1)S(1)}, bf16[128,1024]{1,0:T(8,128)(2,1)S(1)}, u32[]{:S(2)}, u32[]{:S(2)}) %collective-permute-start.25) | collective-permute-done | bytes 262176 | tf_op jit(solution)/shard_map/ppermute | solution.py:340
  119.7 1.8 %shard_map.102 = (f32[512,1024]{1,0:T(8,128)S(1)}, f32[512,1024]{1,0:T(8,128)S(1)}) custom-call(bf16[128,1024]{1,0:T(8,128)(2,1)S(1)} %collective-permute-done.1.refs_0_, bf16[128,1024]{1,0:T(8,128)(2,1)S(1)} %collective-permute-done.21.refs_1_, bf16[128,1024]{1,0:T(8,128)(2,1)S(1)} %collective-permute-done.22.refs_2_, ...), custom_call_target="tpu_custom_call" | custom-call | flops 17179869184 | bytes 524288 | tf_op jit(solution)/shard_map/pallas_call | solution.py:222
  121.5 5.9 %collective-permute-done.29.refs_4_ = bf16[256,1024]{1,0:T(8,128)(2,1)S(1)} collective-permute-done((bf16[256,1024]{1,0:T(8,128)(2,1)S(1)}, bf16[256,1024]{1,0:T(8,128)(2,1)S(1)}, u32[]{:S(2)}, u32[]{:S(2)}) %collective-permute-start.29) | collective-permute-done | bytes 524320 | tf_op jit(solution)/shard_map/ppermute | solution.py:447
  128.3 3.7 %collective-permute-done.30.came = f32[512,1024]{1,0:T(8,128)S(1)} collective-permute-done((f32[512,1024]{1,0:T(8,128)S(1)}, f32[512,1024]{1,0:T(8,128)S(1)}, u32[]{:S(2)}, u32[]{:S(2)}) %collective-permute-start.30) | collective-permute-done | bytes 2097184 | tf_op jit(solution)/shard_map/ppermute | solution.py:458
  132.2 2.1 %collective-permute-start.31 = (bf16[256,512]{1,0:T(8,128)(2,1)S(1)}, bf16[256,512]{1,0:T(8,128)(2,1)S(1)}, u32[]{:S(2)}, u32[]{:S(2)}) collective-permute-start(bf16[256,512]{1,0:T(8,128)(2,1)S(1)} %get-tuple-element.174), channel_id=1, source_target_pairs={{0,4},{4,0},{1,5},{5,1},{2,6},{6,2},{3,7},{7,3},{8,12},{12,8},{9,1... | collective-permute-start | bytes 786440 | tf_op jit(solution)/shard_map/ppermute | solution.py:468
  134.4 6.6 %collective-permute-done.31.refs_2_ = bf16[256,512]{1,0:T(8,128)(2,1)S(1)} collective-permute-done((bf16[256,512]{1,0:T(8,128)(2,1)S(1)}, bf16[256,512]{1,0:T(8,128)(2,1)S(1)}, u32[]{:S(2)}, u32[]{:S(2)}) %collective-permute-start.31) | collective-permute-done | bytes 262176 | tf_op jit(solution)/shard_map/ppermute | solution.py:468
  143.4 4.1 %collective-permute-done.33.from_x = bf16[128,512]{1,0:T(8,128)(2,1)S(1)} collective-permute-done((bf16[128,512]{1,0:T(8,128)(2,1)S(1)}, bf16[128,512]{1,0:T(8,128)(2,1)S(1)}, u32[]{:S(2)}, u32[]{:S(2)}) %collective-permute-start.33) | collective-permute-done | bytes 131104 | tf_op jit(solution)/shard_map/ppermute | solution.py:468
  (89 shorter events, 25.7 us)
Async XLA Ops:
  0.6 25.9 %collective-permute-start.8 = (bf16[4096,1024]{1,0:T(8,128)(2,1)}, bf16[4096,1024]{1,0:T(8,128)(2,1)}, u32[]{:S(2)}, u32[]{:S(2)}) collective-permute-start(bf16[4096,1024]{1,0:T(8,128)(2,1)} %bitcast.45), channel_id=1, source_target_pairs={{0,2},{2,0},{1,3},{3,1},{4,6},{6,4},{5,7},{7,5},{8,10},{10,8},{9,1... | collective-permute-start | bytes 25165832 | tf_op jit(solution)/shard_map/ppermute | solution.py:357
  1.1 8.9 %collective-permute-start.6 = (bf16[128,1024]{1,0:T(8,128)(2,1)}, bf16[128,1024]{1,0:T(8,128)(2,1)S(1)}, u32[]{:S(2)}, u32[]{:S(2)}) collective-permute-start(bf16[128,1024]{1,0:T(8,128)(2,1)} %refs_4_.4), channel_id=1, source_target_pairs={{0,2},{2,0},{1,3},{3,1},{4,6},{6,4},{5,7},{7,5},{8,10},{10,8},{9,1... | collective-permute-start | bytes 786440 | tf_op jit(solution)/shard_map/ppermute | solution.py:358
  1.2 9.7 %collective-permute-start = (bf16[128,1024]{1,0:T(8,128)(2,1)}, bf16[128,1024]{1,0:T(8,128)(2,1)S(1)}, u32[]{:S(2)}, u32[]{:S(2)}) collective-permute-start(bf16[128,1024]{1,0:T(8,128)(2,1)} %refs_4_.4), channel_id=1, source_target_pairs={{0,1},{1,0},{2,3},{3,2},{4,5},{5,4},{6,7},{7,6},{8,9},{9,8},{10,11... | collective-permute-start | bytes 786440 | tf_op jit(solution)/shard_map/ppermute | solution.py:344
  8.6 6.5 %collective-permute-start.1 = (bf16[128,1024]{1,0:T(8,128)(2,1)S(1)}, bf16[128,1024]{1,0:T(8,128)(2,1)S(1)}, u32[]{:S(2)}, u32[]{:S(2)}) collective-permute-start(bf16[128,1024]{1,0:T(8,128)(2,1)S(1)} %get-tuple-element.100), channel_id=1, source_target_pairs={{0,2},{1,3},{2,0},{3,1},{4,6},{5,7},{6,4},{7,5},{8,10},{9,11},{10,... | collective-permute-start | bytes 786440 | tf_op jit(solution)/shard_map/ppermute | solution.py:340
  8.6 9.1 %collective-permute-start.2 = (bf16[128,1024]{1,0:T(8,128)(2,1)S(1)}, bf16[128,1024]{1,0:T(8,128)(2,1)S(1)}, u32[]{:S(2)}, u32[]{:S(2)}) collective-permute-start(bf16[128,1024]{1,0:T(8,128)(2,1)S(1)} %get-tuple-element.101), channel_id=1, source_target_pairs={{0,4},{1,5},{2,6},{3,7},{4,0},{5,1},{6,2},{7,3},{8,12},{9,13},{10,... | collective-permute-start | bytes 786440 | tf_op jit(solution)/shard_map/ppermute | solution.py:340
  10.1 11.9 %collective-permute-start.3 = (bf16[128,1024]{1,0:T(8,128)(2,1)}, bf16[128,1024]{1,0:T(8,128)(2,1)S(1)}, u32[]{:S(2)}, u32[]{:S(2)}) collective-permute-start(bf16[128,1024]{1,0:T(8,128)(2,1)} %get-tuple-element.105), channel_id=1, source_target_pairs={{0,2},{1,3},{2,0},{3,1},{4,6},{5,7},{6,4},{7,5},{8,10},{9,11},{10,... | collective-permute-start | bytes 786440 | tf_op jit(solution)/shard_map/ppermute | solution.py:355
  10.9 11.3 %collective-permute-start.4 = (bf16[128,1024]{1,0:T(8,128)(2,1)}, bf16[128,1024]{1,0:T(8,128)(2,1)S(1)}, u32[]{:S(2)}, u32[]{:S(2)}) collective-permute-start(bf16[128,1024]{1,0:T(8,128)(2,1)} %get-tuple-element.106), channel_id=1, source_target_pairs={{0,1},{1,0},{2,3},{3,2},{4,5},{5,4},{6,7},{7,6},{8,9},{9,8},{10,11... | collective-permute-start | bytes 786440 | tf_op jit(solution)/shard_map/ppermute | solution.py:355
  15.1 9.6 %collective-permute-start.5 = (bf16[128,1024]{1,0:T(8,128)(2,1)}, bf16[128,1024]{1,0:T(8,128)(2,1)S(1)}, u32[]{:S(2)}, u32[]{:S(2)}) collective-permute-start(bf16[128,1024]{1,0:T(8,128)(2,1)} %get-tuple-element.107), channel_id=1, source_target_pairs={{0,3},{1,2},{2,1},{3,0},{4,7},{5,6},{6,5},{7,4},{8,11},{9,10},{10,... | collective-permute-start | bytes 786440 | tf_op jit(solution)/shard_map/ppermute | solution.py:355
  17.7 8.8 %collective-permute-start.7 = (bf16[128,1024]{1,0:T(8,128)(2,1)S(1)}, bf16[128,1024]{1,0:T(8,128)(2,1)S(1)}, u32[]{:S(2)}, u32[]{:S(2)}) collective-permute-start(bf16[128,1024]{1,0:T(8,128)(2,1)S(1)} %collective-permute-done.refs_6_), channel_id=1, source_target_pairs={{0,2},{2,0},{1,3},{3,1},{4,6},{6,4},{5,7},{7,5},{8,10},{10,8},{9,1... | collective-permute-start | bytes 786440 | tf_op jit(solution)/shard_map/ppermute | solution.py:360
  22.0 26.1 %collective-permute-start.11 = (bf16[128,1024]{1,0:T(8,128)(2,1)S(1)}, bf16[128,1024]{1,0:T(8,128)(2,1)S(1)}, u32[]{:S(2)}, u32[]{:S(2)}) collective-permute-start(bf16[128,1024]{1,0:T(8,128)(2,1)S(1)} %copy-done.5), channel_id=1, source_target_pairs={{0,2},{1,3},{2,0},{3,1},{4,6},{5,7},{6,4},{7,5},{8,10},{9,11},{10,... | collective-permute-start | bytes 786440 | tf_op jit(solution)/shard_map/ppermute | solution.py:355
  22.2 25.9 %collective-permute-start.12 = (bf16[128,1024]{1,0:T(8,128)(2,1)S(1)}, bf16[128,1024]{1,0:T(8,128)(2,1)S(1)}, u32[]{:S(2)}, u32[]{:S(2)}) collective-permute-start(bf16[128,1024]{1,0:T(8,128)(2,1)S(1)} %get-tuple-element.122), channel_id=1, source_target_pairs={{0,1},{1,0},{2,3},{3,2},{4,5},{5,4},{6,7},{7,6},{8,9},{9,8},{10,11... | collective-permute-start | bytes 786440 | tf_op jit(solution)/shard_map/ppermute | solution.py:355
  24.7 23.4 %collective-permute-start.13 = (bf16[128,1024]{1,0:T(8,128)(2,1)S(1)}, bf16[128,1024]{1,0:T(8,128)(2,1)S(1)}, u32[]{:S(2)}, u32[]{:S(2)}) collective-permute-start(bf16[128,1024]{1,0:T(8,128)(2,1)S(1)} %get-tuple-element.123), channel_id=1, source_target_pairs={{0,3},{1,2},{2,1},{3,0},{4,7},{5,6},{6,5},{7,4},{8,11},{9,10},{10,... | collective-permute-start | bytes 786440 | tf_op jit(solution)/shard_map/ppermute | solution.py:355
  30.6 14.0 %collective-permute-start.9 = (bf16[512,512]{1,0:T(8,128)(2,1)S(1)}, bf16[512,512]{1,0:T(8,128)(2,1)S(1)}, u32[]{:S(2)}, u32[]{:S(2)}) collective-permute-start(bf16[512,512]{1,0:T(8,128)(2,1)S(1)} %get-tuple-element.114), channel_id=1, source_target_pairs={{0,4},{4,0},{1,5},{5,1},{2,6},{6,2},{3,7},{7,3},{8,12},{12,8},{9,1... | collective-permute-start | bytes 1572872 | tf_op jit(solution)/shard_map/ppermute | solution.py:405
  32.1 13.6 %collective-permute-start.10 = (bf16[512,512]{1,0:T(8,128)(2,1)S(1)}, bf16[512,512]{1,0:T(8,128)(2,1)S(1)}, u32[]{:S(2)}, u32[]{:S(2)}) collective-permute-start(bf16[512,512]{1,0:T(8,128)(2,1)S(1)} %get-tuple-element.116), channel_id=1, source_target_pairs={{0,8},{8,0},{16,24},{24,16},{1,9},{9,1},{17,25},{25,17},{2,10},{10... | collective-permute-start | bytes 1572872 | tf_op jit(solution)/shard_map/ppermute | solution.py:405
  45.9 7.2 %collective-permute-start.14 = (bf16[256,512]{1,0:T(8,128)(2,1)S(1)}, bf16[256,512]{1,0:T(8,128)(2,1)S(1)}, u32[]{:S(2)}, u32[]{:S(2)}) collective-permute-start(bf16[256,512]{1,0:T(8,128)(2,1)S(1)} %get-tuple-element.127), channel_id=1, source_target_pairs={{0,8},{8,0},{16,24},{24,16},{1,9},{9,1},{17,25},{25,17},{2,10},{10... | collective-permute-start | bytes 786440 | tf_op jit(solution)/shard_map/ppermute | solution.py:372
  47.6 6.8 %collective-permute-start.15 = (bf16[256,512]{1,0:T(8,128)(2,1)S(1)}, bf16[256,512]{1,0:T(8,128)(2,1)S(1)}, u32[]{:S(2)}, u32[]{:S(2)}) collective-permute-start(bf16[256,512]{1,0:T(8,128)(2,1)S(1)} %get-tuple-element.128), channel_id=1, source_target_pairs={{0,4},{4,0},{1,5},{5,1},{2,6},{6,2},{3,7},{7,3},{8,12},{12,8},{9,1... | collective-permute-start | bytes 786440 | tf_op jit(solution)/shard_map/ppermute | solution.py:372
  54.4 17.1 %collective-permute-start.16 = (bf16[512,768]{1,0:T(8,128)(2,1)S(1)}, bf16[512,768]{1,0:T(8,128)(2,1)S(1)}, u32[]{:S(2)}, u32[]{:S(2)}) collective-permute-start(bf16[512,768]{1,0:T(8,128)(2,1)S(1)} %get-tuple-element.129), channel_id=1, source_target_pairs={{0,4},{4,0},{1,5},{5,1},{2,6},{6,2},{3,7},{7,3},{8,12},{12,8},{9,1... | collective-permute-start | bytes 2359304 | tf_op jit(solution)/shard_map/ppermute | solution.py:405
  55.0 11.9 %collective-permute-start.17 = (bf16[512,256]{1,0:T(8,128)(2,1)S(1)}, bf16[512,256]{1,0:T(8,128)(2,1)S(1)}, u32[]{:S(2)}, u32[]{:S(2)}) collective-permute-start(bf16[512,256]{1,0:T(8,128)(2,1)S(1)} %get-tuple-element.131), channel_id=1, source_target_pairs={{0,8},{8,0},{16,24},{24,16},{1,9},{9,1},{17,25},{25,17},{2,10},{10... | collective-permute-start | bytes 786440 | tf_op jit(solution)/shard_map/ppermute | solution.py:405
  55.6 23.5 %collective-permute-start.18 = (bf16[256,1024]{1,0:T(8,128)(2,1)S(1)}, bf16[256,1024]{1,0:T(8,128)(2,1)S(1)}, u32[]{:S(2)}, u32[]{:S(2)}) collective-permute-start(bf16[256,1024]{1,0:T(8,128)(2,1)S(1)} %shard_map.99), channel_id=1, source_target_pairs={{0,16},{8,24},{16,0},{24,8},{1,17},{9,25},{17,1},{25,9},{2,18},{10... | collective-permute-start | bytes 1572872 | tf_op jit(solution)/shard_map/ppermute | solution.py:395
  58.2 31.3 %collective-permute-start.28 = (bf16[128,4096]{1,0:T(8,128)(2,1)S(1)}, bf16[128,4096]{1,0:T(8,128)(2,1)S(1)}, u32[]{:S(2)}, u32[]{:S(2)}) collective-permute-start(bf16[128,4096]{1,0:T(8,128)(2,1)S(1)} %slice.4), channel_id=1, source_target_pairs={{0,1},{1,0},{2,3},{3,2},{4,5},{5,4},{6,7},{7,6},{8,9},{9,8},{10,11... | collective-permute-start | bytes 3145736 | tf_op jit(solution)/shard_map/ppermute | solution.py:404
  71.8 12.9 %collective-permute-start.19 = (bf16[256,768]{1,0:T(8,128)(2,1)S(1)}, bf16[256,768]{1,0:T(8,128)(2,1)S(1)}, u32[]{:S(2)}, u32[]{:S(2)}) collective-permute-start(bf16[256,768]{1,0:T(8,128)(2,1)S(1)} %get-tuple-element.139), channel_id=1, source_target_pairs={{0,8},{8,0},{16,24},{24,16},{1,9},{9,1},{17,25},{25,17},{2,10},{10... | collective-permute-start | bytes 1179656 | tf_op jit(solution)/shard_map/ppermute | solution.py:372
  72.4 6.8 %collective-permute-start.20 = (bf16[256,256]{1,0:T(8,128)(2,1)S(1)}, bf16[256,256]{1,0:T(8,128)(2,1)S(1)}, u32[]{:S(2)}, u32[]{:S(2)}) collective-permute-start(bf16[256,256]{1,0:T(8,128)(2,1)S(1)} %get-tuple-element.141), channel_id=1, source_target_pairs={{0,4},{4,0},{1,5},{5,1},{2,6},{6,2},{3,7},{7,3},{8,12},{12,8},{9,1... | collective-permute-start | bytes 393224 | tf_op jit(solution)/shard_map/ppermute | solution.py:372
  85.0 26.8 %collective-permute-start.27 = (bf16[256,1024]{1,0:T(8,128)(2,1)S(1)}, bf16[256,1024]{1,0:T(8,128)(2,1)S(1)}, u32[]{:S(2)}, u32[]{:S(2)}) collective-permute-start(bf16[256,1024]{1,0:T(8,128)(2,1)S(1)} %shard_map.101.refs_8_), channel_id=1, source_target_pairs={{0,16},{8,24},{16,0},{24,8},{1,17},{9,25},{17,1},{25,9},{2,18},{10... | collective-permute-start | bytes 1572872 | tf_op jit(solution)/shard_map/ppermute | solution.py:447
  88.9 8.6 %collective-permute-start.21 = (bf16[128,1024]{1,0:T(8,128)(2,1)S(1)}, bf16[128,1024]{1,0:T(8,128)(2,1)S(1)}, u32[]{:S(2)}, u32[]{:S(2)}) collective-permute-start(bf16[128,1024]{1,0:T(8,128)(2,1)S(1)} %copy-done.10), channel_id=1, source_target_pairs={{0,3},{1,2},{2,1},{3,0},{4,7},{5,6},{6,5},{7,4},{8,11},{9,10},{10,... | collective-permute-start | bytes 786440 | tf_op jit(solution)/shard_map/ppermute | solution.py:340
  91.5 28.2 %collective-permute-start.26 = (bf16[256,1024]{1,0:T(8,128)(2,1)S(1)}, bf16[256,1024]{1,0:T(8,128)(2,1)S(1)}, u32[]{:S(2)}, u32[]{:S(2)}) collective-permute-start(bf16[256,1024]{1,0:T(8,128)(2,1)S(1)} %shard_map.101.refs_8_), channel_id=1, source_target_pairs={{0,8},{8,0},{16,24},{24,16},{1,9},{9,1},{17,25},{25,17},{2,10},{10... | collective-permute-start | bytes 1572872 | tf_op jit(solution)/shard_map/ppermute | solution.py:447
  94.0 20.9 %collective-permute-start.22 = (bf16[128,1024]{1,0:T(8,128)(2,1)S(1)}, bf16[128,1024]{1,0:T(8,128)(2,1)S(1)}, u32[]{:S(2)}, u32[]{:S(2)}) collective-permute-start(bf16[128,1024]{1,0:T(8,128)(2,1)S(1)} %copy-done.9), channel_id=1, source_target_pairs={{0,6},{1,7},{2,4},{3,5},{4,2},{5,3},{6,0},{7,1},{8,14},{9,15},{10,... | collective-permute-start | bytes 786440 | tf_op jit(solution)/shard_map/ppermute | solution.py:340
  95.1 20.4 %collective-permute-start.23 = (bf16[128,1024]{1,0:T(8,128)(2,1)S(1)}, bf16[128,1024]{1,0:T(8,128)(2,1)S(1)}, u32[]{:S(2)}, u32[]{:S(2)}) collective-permute-start(bf16[128,1024]{1,0:T(8,128)(2,1)S(1)} %copy-done.8), channel_id=1, source_target_pairs={{0,7},{1,6},{2,5},{3,4},{4,3},{5,2},{6,1},{7,0},{8,15},{9,14},{10,... | collective-permute-start | bytes 786440 | tf_op jit(solution)/shard_map/ppermute | solution.py:340
  97.5 18.1 %collective-permute-start.24 = (bf16[128,1024]{1,0:T(8,128)(2,1)S(1)}, bf16[128,1024]{1,0:T(8,128)(2,1)S(1)}, u32[]{:S(2)}, u32[]{:S(2)}) collective-permute-start(bf16[128,1024]{1,0:T(8,128)(2,1)S(1)} %copy-done.7), channel_id=1, source_target_pairs={{0,1},{1,0},{2,3},{3,2},{4,5},{5,4},{6,7},{7,6},{8,9},{9,8},{10,11... | collective-permute-start | bytes 786440 | tf_op jit(solution)/shard_map/ppermute | solution.py:340
  111.8 7.9 %collective-permute-start.25 = (bf16[128,1024]{1,0:T(8,128)(2,1)S(1)}, bf16[128,1024]{1,0:T(8,128)(2,1)S(1)}, u32[]{:S(2)}, u32[]{:S(2)}) collective-permute-start(bf16[128,1024]{1,0:T(8,128)(2,1)S(1)} %copy-done.6), channel_id=1, source_target_pairs={{0,5},{1,4},{2,7},{3,6},{4,1},{5,0},{6,3},{7,2},{8,13},{9,12},{10,... | collective-permute-start | bytes 786440 | tf_op jit(solution)/shard_map/ppermute | solution.py:340
  114.9 12.5 %collective-permute-start.29 = (bf16[256,1024]{1,0:T(8,128)(2,1)S(1)}, bf16[256,1024]{1,0:T(8,128)(2,1)S(1)}, u32[]{:S(2)}, u32[]{:S(2)}) collective-permute-start(bf16[256,1024]{1,0:T(8,128)(2,1)S(1)} %collective-permute-done.27.refs_10_), channel_id=1, source_target_pairs={{0,8},{8,0},{16,24},{24,16},{1,9},{9,1},{17,25},{25,17},{2,10},{10... | collective-permute-start | bytes 1572872 | tf_op jit(solution)/shard_map/ppermute | solution.py:447
  132.2 8.7 %collective-permute-start.31 = (bf16[256,512]{1,0:T(8,128)(2,1)S(1)}, bf16[256,512]{1,0:T(8,128)(2,1)S(1)}, u32[]{:S(2)}, u32[]{:S(2)}) collective-permute-start(bf16[256,512]{1,0:T(8,128)(2,1)S(1)} %get-tuple-element.174), channel_id=1, source_target_pairs={{0,4},{4,0},{1,5},{5,1},{2,6},{6,2},{3,7},{7,3},{8,12},{12,8},{9,1... | collective-permute-start | bytes 786440 | tf_op jit(solution)/shard_map/ppermute | solution.py:468
  134.4 8.1 %collective-permute-start.32 = (bf16[256,512]{1,0:T(8,128)(2,1)S(1)}, bf16[256,512]{1,0:T(8,128)(2,1)S(1)}, u32[]{:S(2)}, u32[]{:S(2)}) collective-permute-start(bf16[256,512]{1,0:T(8,128)(2,1)S(1)} %get-tuple-element.175), channel_id=1, source_target_pairs={{0,1},{1,0},{2,3},{3,2},{4,5},{5,4},{6,7},{7,6},{8,9},{9,8},{10,11... | collective-permute-start | bytes 786440 | tf_op jit(solution)/shard_map/ppermute | solution.py:469
  (16 other events, 158.0 us)

commit v9 on v8

--- a/solution.py
+++ b/solution.py
@@ -209,19 +209,19 @@
     for n, out in enumerate(outs):
         left = jnp.concatenate([a[:, at : at + weight.shape[0]] for a in acts[n * each : (n + 1) * each]], axis=0)
         product = jnp.dot(left, weight, preferred_element_type=f32)
-        out[...] = before[0][...] + product if at else product
-
-
-def keys_part(acts, blocks, at, before=(), outs=1):
+        out[...] = (before[0][...] + product if at else product).astype(out.dtype)
+
+
+def keys_part(acts, blocks, at, before=(), outs=1, kind=f32):
     rows, kv = len(acts) * acts[0].shape[0] // outs, sum(w.shape[1] for w in blocks[0])
     depth = sum(block[0].shape[0] for block in blocks)
     if at % LANES:
-        return [before[0] + keys_part([a[:, at:] for a in acts], blocks, 0)[0]]
+        return [(before[0] + keys_part([a[:, at:] for a in acts], blocks, 0)[0]).astype(kind)]
     pieces = [w for block in blocks for w in block]
     flops = rows * depth * kv if at else 1 << 34
     return pl.pallas_call(
         functools.partial(keys_kernel, len(acts), [len(block) for block in blocks], at),
-        out_shape=[jax.ShapeDtypeStruct((rows, kv), f32)] * outs,
+        out_shape=[jax.ShapeDtypeStruct((rows, kv), kind)] * outs,
         in_specs=[pl.BlockSpec()] * (len(acts) + len(pieces) + len(before)),
         out_specs=[pl.BlockSpec()] * outs,
         compiler_params=pltpu.CompilerParams(vmem_limit_bytes=32 * MIB),
@@ -231,7 +231,7 @@
 
 def core_sum_kernel(fsdp, tok, keep, came, to_x, stay_x, stay_f, *to_f):
     half = keep.shape[1] // 2
-    total = keep[...] + came[...]
+    total = keep[...] + came[...].astype(f32)
     rows = fsdp * tok
     stay_x[...] = total[:rows, :half]
     to_x[...] = total[rows:, :half].astype(bf16)
@@ -326,7 +326,7 @@
     stages = [(m + 1, m) for m in range(nz - 2, -1, -2)]
 
     far = [(i, k, s) for k in range(CORES) for i in range(PAIR) for s in range(fsdp)]
-    early = [(0, 1, 0), (1, 0, 0)]
+    early = [(0, 1, 0)]
     late = [e for e in far if e not in early]
     index = lambda i, k, s: ((i % PAIR) * CORES + k % CORES) * fsdp + s % fsdp
     every = [(i, k, s) for i in range(PAIR) for k in range(CORES) for s in range(fsdp)]
@@ -343,11 +343,7 @@
     for s in range(1, fsdp):
         cots[0, s] = lax.ppermute(cotangent, "fsdp", ring(fsdp, s))
     columns = [[column(z ^ m, (x + i) % PAIR, k, s) for m in ms for i in range(PAIR)] for ms in stages for k, s in shifts]
-    items = [(activations, 1, share, columns), (next_activations, 1, share, next_groups(early))]
-    (packed, parts), _ = pack(items)
-    mine.update(zip(early, parts))
-    for e in early:
-        send_next(*e)
+    (packed,), _ = pack([(activations, 1, share, columns)])
     acts = []
     for stage in range(len(stages)):
         came = []
@@ -360,9 +356,9 @@
         cots[1, s] = lax.ppermute(cots[0, s], "core", swap)
 
     wanted = [cots[0, s] for s in range(1, fsdp)]
-    (parts,), wanted = pack([(next_activations, 1, share, next_groups(late))], wanted, pltpu.HBM)
+    (parts,), wanted = pack([(next_activations, 1, share, next_groups(far))], wanted, pltpu.HBM)
     cots.update({(0, s): got for s, got in enumerate(wanted, 1)})
-    mine.update(zip(late, parts))
+    mine.update(zip(far, parts))
 
     ordered = [cots[k, s] for k, s in shifts]
     across_x, across_z = ring(PAIR, 1), [(i, i ^ 1) for i in range(nz)]
@@ -377,10 +373,10 @@
         blocks = [((z ^ m) * PAIR + (x + i) % PAIR) * CORES + c for m in ms for i in range(PAIR)]
         place = jnp.stack(blocks).astype(jnp.int32)
         if not stage:
-            held = (place, *[mine[e] for e in late], *[nexts[e] for e in early])
-            place, *held = lax.optimization_barrier(held)
-            mine.update(zip(late, held))
-            nexts.update(zip(early, held[len(late) :]))
+            place, *held = lax.optimization_barrier((place, *[mine[e] for e in far]))
+            mine.update(zip(far, held))
+            for e in early:
+                send_next(*e)
         if stage:
             place, to_z, to_x = lax.optimization_barrier((place, to_z, to_x))
             m = stages[stage - 1][1]
@@ -417,6 +413,8 @@
     inputs[0], inputs[2] = small_call(
         gather_kernel, [jax.ShapeDtypeStruct(part.shape, f32) for part in (keep_left, keep_right)], keep_left, keep_right, *inputs[4:], spec=pl.BlockSpec(), weight=200
     )
+    inputs[0], *held = lax.optimization_barrier((inputs[0], *[nexts[e] for e in early]))
+    nexts.update(zip(early, held))
     replicas = nz * PAIR * CORES
     inputs = [*inputs[:4], outer_weight, outer_momentum]
     (share_rows,) = small_call(
@@ -453,7 +451,7 @@
     give, keep = keys_part(away + near, rows[:-1], 0, outs=2)
     give, keep, input_grad = lax.optimization_barrier((give, keep, input_grad))
     last = (nz - 1) * share
-    (give,) = keys_part(away, rows[-1:], last, [give])
+    (give,) = keys_part(away, rows[-1:], last, [give], kind=bf16)
     (keep,) = keys_part(near, rows[-1:], last, [keep])
     came = lax.ppermute(give, "core", swap)
     shape = lambda n, kind: jax.ShapeDtypeStruct((n, kv // 2), kind)

time: 149 us -> 146 us (0.980)
  waiting for transfers between devices: 82.1 us -> 71.2 us
  starting transfers between devices: 38.9 us -> 47.5 us
    ppermute x7, starting transfers between devices: 6.76 us -> 14.3 us  [send_next(): lax.ppermute(mine[i, k, s], ('x', 'core', 'fsdp'), pairs)]
    ppermute x7, waiting for transfers between devices: 7.92 us -> 3.23 us  [send_next(): lax.ppermute(mine[i, k, s], ('x', 'core', 'fsdp'), pairs)]
    ppermute x2, waiting for transfers between devices: 9.09 us -> 5.76 us  [local(): lax.ppermute(to_z, 'z', across_z)]
    ppermute x3, waiting for transfers between devices: 19 us -> 16.1 us  [local(): lax.ppermute(piece, 'z', [(i, i ^ low) for i in range(nz)])]
    ppermute x6, waiting for transfers between devices: 2.25 us -> 4.09 us  [local(): lax.ppermute(part, ('core', 'fsdp'), pair_ring(k, s))]
    ppermute x1, waiting for transfers between devices: 3.7 us -> 2.2 us  [local(): came = lax.ppermute(give, 'core', swap)]
  transfers between devices with their start and end apart: 35 -> 35, of which waited for: 20 -> 21; matrix products, arithmetic and copies ran while one was open for 2% -> 2% of each run, Pallas kernels for 15% -> 15%
where the time goes in v9:
time: 146 us
  waiting for transfers between devices  71.2 us (49%)
  starting transfers between devices  47.5 us (33%)
  Pallas kernels  23.2 us (16%)
  matrix products  2.38 us (2%)
    ppermute x3, waiting for transfers between devices, local(): lax.ppermute(piece, 'z', [(i, i ^ low) for i in range(nz)])  16.1 us
    ppermute x7, starting transfers between devices, send_next(): lax.ppermute(mine[i, k, s], ('x', 'core', 'fsdp'), pairs)  14.3 us
    ppermute x2, waiting for transfers between devices, local(): lax.ppermute(to_x, 'x', across_x)  13.3 us
    ppermute x2, waiting for transfers between devices, home(): from_x = lax.ppermute(to_x, 'x', ring(PAIR, 1))  10.7 us
    pallas_call x2, Pallas kernels, inner_blocks(): pl.pallas_call(functools.partial(inner_kernel, pieces, share, inner_rate...  7.74 us
    ppermute x6, starting transfers between devices, local(): lax.ppermute(part, ('core', 'fsdp'), pair_ring(k, s))  7.53 us
    pallas_call x2, Pallas kernels, pack(): pl.pallas_call(functools.partial(pack_kernel, plan), out_shape=shapes, in...  7.2 us
    ppermute x3, starting transfers between devices, local(): lax.ppermute(piece, 'z', [(i, i ^ low) for i in range(nz)])  7.02 us
  transfers between devices with their start and end apart: 35, of which 21 were waited for; matrix products, arithmetic and copies ran while one was open for 2% of the time, Pallas kernels for 15%

profile of v9, /device:TPU:0, one launch (start us, length us, event | category | flops | bytes accessed | tf_op | source)
XLA Modules:
  0.0 145.7 jit_solution(2027703583314650972)
XLA Ops:
  1.2 2.9 %collective-permute-start = (bf16[128,1024]{1,0:T(8,128)(2,1)}, bf16[128,1024]{1,0:T(8,128)(2,1)S(1)}, u32[]{:S(2)}, u32[]{:S(2)}) collective-permute-start(bf16[128,1024]{1,0:T(8,128)(2,1)} %refs_4_.4), channel_id=1, source_target_pairs={{0,1},{1,0},{2,3},{3,2},{4,5},{5,4},{6,7},{7,6},{8,9},{9,8},{10,11... | collective-permute-start | bytes 786440 | tf_op jit(solution)/shard_map/ppermute | solution.py:344
  4.3 3.2 %shard_map.94 = (bf16[128,1024]{1,0:T(8,128)(2,1)S(1)}, bf16[128,1024]{1,0:T(8,128)(2,1)}, bf16[128,1024]{1,0:T(8,128)(2,1)}, bf16[128,1024]{1,0:T(8,128)(2,1)S(...) custom-call(s32[32]{0:T(128)S(1)} %stack.216.starts, ...), custom_call_target="tpu_custom_call" | custom-call | bytes 16777216 | tf_op jit(solution)/shard_map/pallas_call | solution.py:72
  7.7 2.7 %collective-permute-start.3 = (bf16[128,1024]{1,0:T(8,128)(2,1)S(1)}, bf16[128,1024]{1,0:T(8,128)(2,1)S(1)}, u32[]{:S(2)}, u32[]{:S(2)}) collective-permute-start(bf16[128,1024]{1,0:T(8,128)(2,1)S(1)} %get-tuple-element.109), channel_id=1, source_target_pairs={{0,3},{1,2},{2,1},{3,0},{4,7},{5,6},{6,5},{7,4},{8,11},{9,10},{10,... | collective-permute-start | bytes 786440 | tf_op jit(solution)/shard_map/ppermute | solution.py:351
  11.5 4.0 %shard_map.93 = (bf16[128,1024]{1,0:T(8,128)(2,1)}, bf16[128,1024]{1,0:T(8,128)(2,1)}, bf16[128,1024]{1,0:T(8,128)(2,1)}, bf16[128,1024]{1,0:T(8,128)(2,1)}, bf1...) custom-call(s32[32]{0:T(128)S(1)} %stack.215.starts, ...), custom_call_target="tpu_custom_call" | custom-call | bytes 16777216 | tf_op jit(solution)/shard_map/pallas_call | solution.py:72
  17.0 2.2 %collective-permute-start.10 = (bf16[128,1024]{1,0:T(8,128)(2,1)S(1)}, bf16[128,1024]{1,0:T(8,128)(2,1)S(1)}, u32[]{:S(2)}, u32[]{:S(2)}) collective-permute-start(bf16[128,1024]{1,0:T(8,128)(2,1)S(1)} %get-tuple-element.124), channel_id=1, source_target_pairs={{0,1},{1,0},{2,3},{3,2},{4,5},{5,4},{6,7},{7,6},{8,9},{9,8},{10,11... | collective-permute-start | bytes 786440 | tf_op jit(solution)/shard_map/ppermute | solution.py:351
  19.2 3.1 %collective-permute-done.3.refs_3_ = bf16[128,1024]{1,0:T(8,128)(2,1)S(1)} collective-permute-done((bf16[128,1024]{1,0:T(8,128)(2,1)S(1)}, bf16[128,1024]{1,0:T(8,128)(2,1)S(1)}, u32[]{:S(2)}, u32[]{:S(2)}) %collective-permute-start.3) | collective-permute-done | bytes 262176 | tf_op jit(solution)/shard_map/ppermute | solution.py:351
  22.3 1.9 %collective-permute-start.11 = (bf16[128,1024]{1,0:T(8,128)(2,1)S(1)}, bf16[128,1024]{1,0:T(8,128)(2,1)S(1)}, u32[]{:S(2)}, u32[]{:S(2)}) collective-permute-start(bf16[128,1024]{1,0:T(8,128)(2,1)S(1)} %get-tuple-element.125), channel_id=1, source_target_pairs={{0,3},{1,2},{2,1},{3,0},{4,7},{5,6},{6,5},{7,4},{8,11},{9,10},{10,... | collective-permute-start | bytes 786440 | tf_op jit(solution)/shard_map/ppermute | solution.py:351
  24.2 4.0 %shard_map.95 = (bf16[512,512]{1,0:T(8,128)(2,1)S(1)}, f32[512,512]{1,0:T(8,128)S(1)}, bf16[512,512]{1,0:T(8,128)(2,1)S(1)}, f32[512,512]{1,0:T(8,128)S(1)}) custom-call(s32[4]{0:T(128)S(1)} %pad_add_fusion.1.place, bf16[128,1024]{1,0:T(8,128)(2,1)S(1)} %get-tuple-element.106.refs_0_, bf16[128,1024]{1,0:T(8,128)(2,1)S(1)} %collective-permute-done.1.refs_1_, ...), custom_call_target="tpu_custom_call" | custom-call | flops 134217728 | bytes 262144 | tf_op jit(solution)/shard_map/pallas_call | solution.py:135
  31.4 2.4 %convolution_convert_fusion.refs_0_ = bf16[256,4096]{1,0:T(8,128)(2,1)S(1)} fusion(bf16[128,1024]{1,0:T(8,128)(2,1)S(1)} %collective-permute-done.refs_6_, bf16[128,1024]{1,0:T(8,128)(2,1)S(1)} %copy-done, bf16[1,4096,1024]{2,1,0:T(8,128)(2,1)S(1)} %bitcast.49), kind=kOutput, calls=%fused_computation | convolution fusion | flops 2149580800 | bytes 11010048 | tf_op jit(solution)/shard_map/dot_general | solution.py:394
  33.9 7.2 %collective-permute-done.7.from_x = bf16[512,512]{1,0:T(8,128)(2,1)S(1)} collective-permute-done((bf16[512,512]{1,0:T(8,128)(2,1)S(1)}, bf16[512,512]{1,0:T(8,128)(2,1)S(1)}, u32[]{:S(2)}, u32[]{:S(2)}) %collective-permute-start.7) | collective-permute-done | bytes 524320 | tf_op jit(solution)/shard_map/ppermute | solution.py:401
  44.7 3.7 %shard_map.97 = (bf16[512,768]{1,0:T(8,128)(2,1)S(1)}, f32[512,768]{1,0:T(8,128)S(1)}, bf16[512,256]{1,0:T(8,128)(2,1)S(1)}, f32[512,256]{1,0:T(8,128)S(1)}) custom-call(s32[4]{0:T(128)S(1)} %pad_add_fusion.place, bf16[128,1024]{1,0:T(8,128)(2,1)S(1)} %get-tuple-element.122.refs_0_, bf16[128,1024]{1,0:T(8,128)(2,1)S(1)} %collective-permute-done.9.refs_1_, ...), custom_call_target="tpu_custom_call" | custom-call | flops 134217728 | bytes 262144 | tf_op jit(solution)/shard_map/pallas_call | solution.py:135
  49.0 2.3 %collective-permute-done.13.refs_3_ = bf16[256,512]{1,0:T(8,128)(2,1)S(1)} collective-permute-done((bf16[256,512]{1,0:T(8,128)(2,1)S(1)}, bf16[256,512]{1,0:T(8,128)(2,1)S(1)}, u32[]{:S(2)}, u32[]{:S(2)}) %collective-permute-start.13) | collective-permute-done | bytes 262176 | tf_op jit(solution)/shard_map/ppermute | solution.py:368
  52.7 2.7 %collective-permute-start.16 = (bf16[256,1024]{1,0:T(8,128)(2,1)S(1)}, bf16[256,1024]{1,0:T(8,128)(2,1)S(1)}, u32[]{:S(2)}, u32[]{:S(2)}) collective-permute-start(bf16[256,1024]{1,0:T(8,128)(2,1)S(1)} %shard_map.99), channel_id=1, source_target_pairs={{0,16},{8,24},{16,0},{24,8},{1,17},{9,25},{17,1},{25,9},{2,18},{10... | collective-permute-start | bytes 1572872 | tf_op jit(solution)/shard_map/ppermute | solution.py:391
  56.8 4.6 %collective-permute-done.15.from_z = bf16[512,256]{1,0:T(8,128)(2,1)S(1)} collective-permute-done((bf16[512,256]{1,0:T(8,128)(2,1)S(1)}, bf16[512,256]{1,0:T(8,128)(2,1)S(1)}, u32[]{:S(2)}, u32[]{:S(2)}) %collective-permute-start.15) | collective-permute-done | bytes 262176 | tf_op jit(solution)/shard_map/ppermute | solution.py:401
  61.3 6.1 %collective-permute-done.14.from_x = bf16[512,768]{1,0:T(8,128)(2,1)S(1)} collective-permute-done((bf16[512,768]{1,0:T(8,128)(2,1)S(1)}, bf16[512,768]{1,0:T(8,128)(2,1)S(1)}, u32[]{:S(2)}, u32[]{:S(2)}) %collective-permute-start.14) | collective-permute-done | bytes 786464 | tf_op jit(solution)/shard_map/ppermute | solution.py:401
  68.7 5.1 %collective-permute-done.16.refs_0_ = bf16[256,1024]{1,0:T(8,128)(2,1)S(1)} collective-permute-done((bf16[256,1024]{1,0:T(8,128)(2,1)S(1)}, bf16[256,1024]{1,0:T(8,128)(2,1)S(1)}, u32[]{:S(2)}, u32[]{:S(2)}) %collective-permute-start.16) | collective-permute-done | bytes 524320 | tf_op jit(solution)/shard_map/ppermute | solution.py:391
  74.0 5.1 %collective-permute-done.18.refs_1_ = bf16[256,768]{1,0:T(8,128)(2,1)S(1)} collective-permute-done((bf16[256,768]{1,0:T(8,128)(2,1)S(1)}, bf16[256,768]{1,0:T(8,128)(2,1)S(1)}, u32[]{:S(2)}, u32[]{:S(2)}) %collective-permute-start.18) | collective-permute-done | bytes 393248 | tf_op jit(solution)/shard_map/ppermute | solution.py:368
  79.5 3.8 %collective-permute-start.27 = (bf16[256,1024]{1,0:T(8,128)(2,1)S(1)}, bf16[256,1024]{1,0:T(8,128)(2,1)S(1)}, u32[]{:S(2)}, u32[]{:S(2)}) collective-permute-start(bf16[256,1024]{1,0:T(8,128)(2,1)S(1)} %shard_map.101.refs_8_), channel_id=1, source_target_pairs={{0,16},{8,24},{16,0},{24,8},{1,17},{9,25},{17,1},{25,9},{2,18},{10... | collective-permute-start | bytes 1572872 | tf_op jit(solution)/shard_map/ppermute | solution.py:445
  83.3 4.4 %collective-permute-start.20 = (bf16[128,1024]{1,0:T(8,128)(2,1)S(1)}, bf16[128,1024]{1,0:T(8,128)(2,1)S(1)}, u32[]{:S(2)}, u32[]{:S(2)}) collective-permute-start(bf16[128,1024]{1,0:T(8,128)(2,1)S(1)} %copy-done.9), channel_id=1, source_target_pairs={{0,3},{1,2},{2,1},{3,0},{4,7},{5,6},{6,5},{7,4},{8,11},{9,10},{10,... | collective-permute-start | bytes 786440 | tf_op jit(solution)/shard_map/ppermute | solution.py:340
  89.0 1.9 %shard_map.103 = bf16[128,8192]{1,0:T(8,128)(2,1)} custom-call(s32[2]{0:T(128)S(1)} %pad_add_fusion.2.starts, bf16[256,4096]{1,0:T(8,128)(2,1)S(1)} %convolution_convert_fusion.refs_0_, bf16[128,4096]{1,0:T(8,128)(2,1)S(1)} %collective-permute-done.28.refs_1_), custom_call_target="tpu_custom_call" | custom-call | bytes 4194304 | tf_op jit(solution)/shard_map/pallas_call | solution.py:296
  90.9 2.5 %collective-permute-start.26 = (bf16[256,1024]{1,0:T(8,128)(2,1)S(1)}, bf16[256,1024]{1,0:T(8,128)(2,1)S(1)}, u32[]{:S(2)}, u32[]{:S(2)}) collective-permute-start(bf16[256,1024]{1,0:T(8,128)(2,1)S(1)} %shard_map.101.refs_8_), channel_id=1, source_target_pairs={{0,8},{8,0},{16,24},{24,16},{1,9},{9,1},{17,25},{25,17},{2,10},{10... | collective-permute-start | bytes 1572872 | tf_op jit(solution)/shard_map/ppermute | solution.py:445
  94.4 2.6 %collective-permute-start.23 = (bf16[128,1024]{1,0:T(8,128)(2,1)S(1)}, bf16[128,1024]{1,0:T(8,128)(2,1)S(1)}, u32[]{:S(2)}, u32[]{:S(2)}) collective-permute-start(bf16[128,1024]{1,0:T(8,128)(2,1)S(1)} %copy-done.6), channel_id=1, source_target_pairs={{0,1},{1,0},{2,3},{3,2},{4,5},{5,4},{6,7},{7,6},{8,9},{9,8},{10,11... | collective-permute-start | bytes 786440 | tf_op jit(solution)/shard_map/ppermute | solution.py:340
  97.0 8.7 %collective-permute-done.27.refs_10_ = bf16[256,1024]{1,0:T(8,128)(2,1)S(1)} collective-permute-done((bf16[256,1024]{1,0:T(8,128)(2,1)S(1)}, bf16[256,1024]{1,0:T(8,128)(2,1)S(1)}, u32[]{:S(2)}, u32[]{:S(2)}) %collective-permute-start.27) | collective-permute-done | bytes 524320 | tf_op jit(solution)/shard_map/ppermute | solution.py:445
  105.7 5.6 %collective-permute-start.25 = (bf16[128,1024]{1,0:T(8,128)(2,1)S(1)}, bf16[128,1024]{1,0:T(8,128)(2,1)S(1)}, u32[]{:S(2)}, u32[]{:S(2)}) collective-permute-start(bf16[128,1024]{1,0:T(8,128)(2,1)S(1)} %copy-done.4), channel_id=1, source_target_pairs={{0,5},{1,4},{2,7},{3,6},{4,1},{5,0},{6,3},{7,2},{8,13},{9,12},{10,... | collective-permute-start | bytes 786440 | tf_op jit(solution)/shard_map/ppermute | solution.py:340
  111.4 1.7 %shard_map.104 = (f32[256,1024]{1,0:T(8,128)}, f32[256,1024]{1,0:T(8,128)}) custom-call(f32[256,768]{1,0:T(8,128)S(1)} %get-tuple-element.168.refs_0_, bf16[256,768]{1,0:T(8,128)(2,1)S(1)} %collective-permute-done.18.refs_1_, f32[256,256]{1,0:T(8,128)S(1)} %get-tuple-element.170.refs_2_, bf16[256,256]{1,0:T(8,128)(2,1)S(1)} %collective-permute-done.19.refs_3_, ...), custom_call_target="tpu_custom_call" | custom-call | flops 8589934592 | bytes 8589934592 | tf_op jit(solution)/shard_map/pallas_call | solution.py:271
  113.7 2.8 %collective-permute-done.25.refs_7_.refs_3_ = bf16[128,1024]{1,0:T(8,128)(2,1)S(1)} collective-permute-done((bf16[128,1024]{1,0:T(8,128)(2,1)S(1)}, bf16[128,1024]{1,0:T(8,128)(2,1)S(1)}, u32[]{:S(2)}, u32[]{:S(2)}) %collective-permute-start.25) | collective-permute-done | bytes 262176 | tf_op jit(solution)/shard_map/ppermute | solution.py:340
  116.5 1.8 %shard_map.102 = (f32[512,1024]{1,0:T(8,128)S(1)}, f32[512,1024]{1,0:T(8,128)S(1)}) custom-call(bf16[128,1024]{1,0:T(8,128)(2,1)S(1)} %collective-permute-done.17.refs_0_, bf16[128,1024]{1,0:T(8,128)(2,1)S(1)} %collective-permute-done.20.refs_1_, bf16[128,1024]{1,0:T(8,128)(2,1)S(1)} %collective-permute-done.21.refs_2_, ...), custom_call_target="tpu_custom_call" | custom-call | flops 17179869184 | bytes 524288 | tf_op jit(solution)/shard_map/pallas_call | solution.py:222
  118.3 7.3 %collective-permute-done.29.refs_4_ = bf16[256,1024]{1,0:T(8,128)(2,1)S(1)} collective-permute-done((bf16[256,1024]{1,0:T(8,128)(2,1)S(1)}, bf16[256,1024]{1,0:T(8,128)(2,1)S(1)}, u32[]{:S(2)}, u32[]{:S(2)}) %collective-permute-start.29) | collective-permute-done | bytes 524320 | tf_op jit(solution)/shard_map/ppermute | solution.py:445
  126.6 2.2 %collective-permute-done.30.came = bf16[512,1024]{1,0:T(8,128)(2,1)S(1)} collective-permute-done((bf16[512,1024]{1,0:T(8,128)(2,1)S(1)}, bf16[512,1024]{1,0:T(8,128)(2,1)S(1)}, u32[]{:S(2)}, u32[]{:S(2)}) %collective-permute-start.30) | collective-permute-done | bytes 1048608 | tf_op jit(solution)/shard_map/ppermute | solution.py:456
  129.0 2.4 %collective-permute-start.31 = (bf16[256,512]{1,0:T(8,128)(2,1)S(1)}, bf16[256,512]{1,0:T(8,128)(2,1)S(1)}, u32[]{:S(2)}, u32[]{:S(2)}) collective-permute-start(bf16[256,512]{1,0:T(8,128)(2,1)S(1)} %get-tuple-element.180), channel_id=1, source_target_pairs={{0,4},{4,0},{1,5},{5,1},{2,6},{6,2},{3,7},{7,3},{8,12},{12,8},{9,1... | collective-permute-start | bytes 786440 | tf_op jit(solution)/shard_map/ppermute | solution.py:466
  131.4 6.6 %collective-permute-done.31.refs_2_ = bf16[256,512]{1,0:T(8,128)(2,1)S(1)} collective-permute-done((bf16[256,512]{1,0:T(8,128)(2,1)S(1)}, bf16[256,512]{1,0:T(8,128)(2,1)S(1)}, u32[]{:S(2)}, u32[]{:S(2)}) %collective-permute-start.31) | collective-permute-done | bytes 262176 | tf_op jit(solution)/shard_map/ppermute | solution.py:466
  140.4 4.1 %collective-permute-done.33.from_x = bf16[128,512]{1,0:T(8,128)(2,1)S(1)} collective-permute-done((bf16[128,512]{1,0:T(8,128)(2,1)S(1)}, bf16[128,512]{1,0:T(8,128)(2,1)S(1)}, u32[]{:S(2)}, u32[]{:S(2)}) %collective-permute-start.33) | collective-permute-done | bytes 131104 | tf_op jit(solution)/shard_map/ppermute | solution.py:466
  (89 shorter events, 23.1 us)
Async XLA Ops:
  0.6 23.6 %collective-permute-start.6 = (bf16[4096,1024]{1,0:T(8,128)(2,1)}, bf16[4096,1024]{1,0:T(8,128)(2,1)}, u32[]{:S(2)}, u32[]{:S(2)}) collective-permute-start(bf16[4096,1024]{1,0:T(8,128)(2,1)} %bitcast.45), channel_id=1, source_target_pairs={{0,2},{2,0},{1,3},{3,1},{4,6},{6,4},{5,7},{7,5},{8,10},{10,8},{9,1... | collective-permute-start | bytes 25165832 | tf_op jit(solution)/shard_map/ppermute | solution.py:353
  1.1 6.5 %collective-permute-start.4 = (bf16[128,1024]{1,0:T(8,128)(2,1)}, bf16[128,1024]{1,0:T(8,128)(2,1)S(1)}, u32[]{:S(2)}, u32[]{:S(2)}) collective-permute-start(bf16[128,1024]{1,0:T(8,128)(2,1)} %refs_4_.4), channel_id=1, source_target_pairs={{0,2},{2,0},{1,3},{3,1},{4,6},{6,4},{5,7},{7,5},{8,10},{10,8},{9,1... | collective-permute-start | bytes 786440 | tf_op jit(solution)/shard_map/ppermute | solution.py:354
  1.2 9.9 %collective-permute-start = (bf16[128,1024]{1,0:T(8,128)(2,1)}, bf16[128,1024]{1,0:T(8,128)(2,1)S(1)}, u32[]{:S(2)}, u32[]{:S(2)}) collective-permute-start(bf16[128,1024]{1,0:T(8,128)(2,1)} %refs_4_.4), channel_id=1, source_target_pairs={{0,1},{1,0},{2,3},{3,2},{4,5},{5,4},{6,7},{7,6},{8,9},{9,8},{10,11... | collective-permute-start | bytes 786440 | tf_op jit(solution)/shard_map/ppermute | solution.py:344
  7.5 7.9 %collective-permute-start.1 = (bf16[128,1024]{1,0:T(8,128)(2,1)}, bf16[128,1024]{1,0:T(8,128)(2,1)S(1)}, u32[]{:S(2)}, u32[]{:S(2)}) collective-permute-start(bf16[128,1024]{1,0:T(8,128)(2,1)} %get-tuple-element.107), channel_id=1, source_target_pairs={{0,2},{1,3},{2,0},{3,1},{4,6},{5,7},{6,4},{7,5},{8,10},{9,11},{10,... | collective-permute-start | bytes 786440 | tf_op jit(solution)/shard_map/ppermute | solution.py:351
  7.6 9.4 %collective-permute-start.2 = (bf16[128,1024]{1,0:T(8,128)(2,1)}, bf16[128,1024]{1,0:T(8,128)(2,1)S(1)}, u32[]{:S(2)}, u32[]{:S(2)}) collective-permute-start(bf16[128,1024]{1,0:T(8,128)(2,1)} %get-tuple-element.108), channel_id=1, source_target_pairs={{0,1},{1,0},{2,3},{3,2},{4,5},{5,4},{6,7},{7,6},{8,9},{9,8},{10,11... | collective-permute-start | bytes 786440 | tf_op jit(solution)/shard_map/ppermute | solution.py:351
  7.7 14.6 %collective-permute-start.3 = (bf16[128,1024]{1,0:T(8,128)(2,1)S(1)}, bf16[128,1024]{1,0:T(8,128)(2,1)S(1)}, u32[]{:S(2)}, u32[]{:S(2)}) collective-permute-start(bf16[128,1024]{1,0:T(8,128)(2,1)S(1)} %get-tuple-element.109), channel_id=1, source_target_pairs={{0,3},{1,2},{2,1},{3,0},{4,7},{5,6},{6,5},{7,4},{8,11},{9,10},{10,... | collective-permute-start | bytes 786440 | tf_op jit(solution)/shard_map/ppermute | solution.py:351
  11.2 13.0 %collective-permute-start.5 = (bf16[128,1024]{1,0:T(8,128)(2,1)S(1)}, bf16[128,1024]{1,0:T(8,128)(2,1)S(1)}, u32[]{:S(2)}, u32[]{:S(2)}) collective-permute-start(bf16[128,1024]{1,0:T(8,128)(2,1)S(1)} %collective-permute-done.refs_6_), channel_id=1, source_target_pairs={{0,2},{2,0},{1,3},{3,1},{4,6},{6,4},{5,7},{7,5},{8,10},{10,8},{9,1... | collective-permute-start | bytes 786440 | tf_op jit(solution)/shard_map/ppermute | solution.py:356
  15.5 29.2 %collective-permute-start.9 = (bf16[128,1024]{1,0:T(8,128)(2,1)S(1)}, bf16[128,1024]{1,0:T(8,128)(2,1)S(1)}, u32[]{:S(2)}, u32[]{:S(2)}) collective-permute-start(bf16[128,1024]{1,0:T(8,128)(2,1)S(1)} %get-tuple-element.123), channel_id=1, source_target_pairs={{0,2},{1,3},{2,0},{3,1},{4,6},{5,7},{6,4},{7,5},{8,10},{9,11},{10,... | collective-permute-start | bytes 786440 | tf_op jit(solution)/shard_map/ppermute | solution.py:351
  17.0 27.7 %collective-permute-start.10 = (bf16[128,1024]{1,0:T(8,128)(2,1)S(1)}, bf16[128,1024]{1,0:T(8,128)(2,1)S(1)}, u32[]{:S(2)}, u32[]{:S(2)}) collective-permute-start(bf16[128,1024]{1,0:T(8,128)(2,1)S(1)} %get-tuple-element.124), channel_id=1, source_target_pairs={{0,1},{1,0},{2,3},{3,2},{4,5},{5,4},{6,7},{7,6},{8,9},{9,8},{10,11... | collective-permute-start | bytes 786440 | tf_op jit(solution)/shard_map/ppermute | solution.py:351
  22.3 22.4 %collective-permute-start.11 = (bf16[128,1024]{1,0:T(8,128)(2,1)S(1)}, bf16[128,1024]{1,0:T(8,128)(2,1)S(1)}, u32[]{:S(2)}, u32[]{:S(2)}) collective-permute-start(bf16[128,1024]{1,0:T(8,128)(2,1)S(1)} %get-tuple-element.125), channel_id=1, source_target_pairs={{0,3},{1,2},{2,1},{3,0},{4,7},{5,6},{6,5},{7,4},{8,11},{9,10},{10,... | collective-permute-start | bytes 786440 | tf_op jit(solution)/shard_map/ppermute | solution.py:351
  28.3 12.8 %collective-permute-start.7 = (bf16[512,512]{1,0:T(8,128)(2,1)S(1)}, bf16[512,512]{1,0:T(8,128)(2,1)S(1)}, u32[]{:S(2)}, u32[]{:S(2)}) collective-permute-start(bf16[512,512]{1,0:T(8,128)(2,1)S(1)} %get-tuple-element.116), channel_id=1, source_target_pairs={{0,4},{4,0},{1,5},{5,1},{2,6},{6,2},{3,7},{7,3},{8,12},{12,8},{9,1... | collective-permute-start | bytes 1572872 | tf_op jit(solution)/shard_map/ppermute | solution.py:401
  29.8 12.5 %collective-permute-start.8 = (bf16[512,512]{1,0:T(8,128)(2,1)S(1)}, bf16[512,512]{1,0:T(8,128)(2,1)S(1)}, u32[]{:S(2)}, u32[]{:S(2)}) collective-permute-start(bf16[512,512]{1,0:T(8,128)(2,1)S(1)} %get-tuple-element.118), channel_id=1, source_target_pairs={{0,8},{8,0},{16,24},{24,16},{1,9},{9,1},{17,25},{25,17},{2,10},{10... | collective-permute-start | bytes 1572872 | tf_op jit(solution)/shard_map/ppermute | solution.py:401
  42.5 6.4 %collective-permute-start.12 = (bf16[256,512]{1,0:T(8,128)(2,1)S(1)}, bf16[256,512]{1,0:T(8,128)(2,1)S(1)}, u32[]{:S(2)}, u32[]{:S(2)}) collective-permute-start(bf16[256,512]{1,0:T(8,128)(2,1)S(1)} %get-tuple-element.129), channel_id=1, source_target_pairs={{0,8},{8,0},{16,24},{24,16},{1,9},{9,1},{17,25},{25,17},{2,10},{10... | collective-permute-start | bytes 786440 | tf_op jit(solution)/shard_map/ppermute | solution.py:368
  44.2 7.1 %collective-permute-start.13 = (bf16[256,512]{1,0:T(8,128)(2,1)S(1)}, bf16[256,512]{1,0:T(8,128)(2,1)S(1)}, u32[]{:S(2)}, u32[]{:S(2)}) collective-permute-start(bf16[256,512]{1,0:T(8,128)(2,1)S(1)} %get-tuple-element.130), channel_id=1, source_target_pairs={{0,4},{4,0},{1,5},{5,1},{2,6},{6,2},{3,7},{7,3},{8,12},{12,8},{9,1... | collective-permute-start | bytes 786440 | tf_op jit(solution)/shard_map/ppermute | solution.py:368
  51.3 16.1 %collective-permute-start.14 = (bf16[512,768]{1,0:T(8,128)(2,1)S(1)}, bf16[512,768]{1,0:T(8,128)(2,1)S(1)}, u32[]{:S(2)}, u32[]{:S(2)}) collective-permute-start(bf16[512,768]{1,0:T(8,128)(2,1)S(1)} %get-tuple-element.131), channel_id=1, source_target_pairs={{0,4},{4,0},{1,5},{5,1},{2,6},{6,2},{3,7},{7,3},{8,12},{12,8},{9,1... | collective-permute-start | bytes 2359304 | tf_op jit(solution)/shard_map/ppermute | solution.py:401
  51.8 9.6 %collective-permute-start.15 = (bf16[512,256]{1,0:T(8,128)(2,1)S(1)}, bf16[512,256]{1,0:T(8,128)(2,1)S(1)}, u32[]{:S(2)}, u32[]{:S(2)}) collective-permute-start(bf16[512,256]{1,0:T(8,128)(2,1)S(1)} %get-tuple-element.133), channel_id=1, source_target_pairs={{0,8},{8,0},{16,24},{24,16},{1,9},{9,1},{17,25},{25,17},{2,10},{10... | collective-permute-start | bytes 786440 | tf_op jit(solution)/shard_map/ppermute | solution.py:401
  52.7 21.1 %collective-permute-start.16 = (bf16[256,1024]{1,0:T(8,128)(2,1)S(1)}, bf16[256,1024]{1,0:T(8,128)(2,1)S(1)}, u32[]{:S(2)}, u32[]{:S(2)}) collective-permute-start(bf16[256,1024]{1,0:T(8,128)(2,1)S(1)} %shard_map.99), channel_id=1, source_target_pairs={{0,16},{8,24},{16,0},{24,8},{1,17},{9,25},{17,1},{25,9},{2,18},{10... | collective-permute-start | bytes 1572872 | tf_op jit(solution)/shard_map/ppermute | solution.py:391
  55.3 33.7 %collective-permute-start.28 = (bf16[128,4096]{1,0:T(8,128)(2,1)S(1)}, bf16[128,4096]{1,0:T(8,128)(2,1)S(1)}, u32[]{:S(2)}, u32[]{:S(2)}) collective-permute-start(bf16[128,4096]{1,0:T(8,128)(2,1)S(1)} %slice.4), channel_id=1, source_target_pairs={{0,1},{1,0},{2,3},{3,2},{4,5},{5,4},{6,7},{7,6},{8,9},{9,8},{10,11... | collective-permute-start | bytes 3145736 | tf_op jit(solution)/shard_map/ppermute | solution.py:400
  67.6 11.5 %collective-permute-start.18 = (bf16[256,768]{1,0:T(8,128)(2,1)S(1)}, bf16[256,768]{1,0:T(8,128)(2,1)S(1)}, u32[]{:S(2)}, u32[]{:S(2)}) collective-permute-start(bf16[256,768]{1,0:T(8,128)(2,1)S(1)} %get-tuple-element.144), channel_id=1, source_target_pairs={{0,8},{8,0},{16,24},{24,16},{1,9},{9,1},{17,25},{25,17},{2,10},{10... | collective-permute-start | bytes 1179656 | tf_op jit(solution)/shard_map/ppermute | solution.py:368
  68.1 5.8 %collective-permute-start.17 = (bf16[128,1024]{1,0:T(8,128)(2,1)S(1)}, bf16[128,1024]{1,0:T(8,128)(2,1)S(1)}, u32[]{:S(2)}, u32[]{:S(2)}) collective-permute-start(bf16[128,1024]{1,0:T(8,128)(2,1)S(1)} %copy-done.10), channel_id=1, source_target_pairs={{0,2},{1,3},{2,0},{3,1},{4,6},{5,7},{6,4},{7,5},{8,10},{9,11},{10,... | collective-permute-start | bytes 786440 | tf_op jit(solution)/shard_map/ppermute | solution.py:340
  68.1 5.9 %collective-permute-start.19 = (bf16[256,256]{1,0:T(8,128)(2,1)S(1)}, bf16[256,256]{1,0:T(8,128)(2,1)S(1)}, u32[]{:S(2)}, u32[]{:S(2)}) collective-permute-start(bf16[256,256]{1,0:T(8,128)(2,1)S(1)} %get-tuple-element.146), channel_id=1, source_target_pairs={{0,4},{4,0},{1,5},{5,1},{2,6},{6,2},{3,7},{7,3},{8,12},{12,8},{9,1... | collective-permute-start | bytes 393224 | tf_op jit(solution)/shard_map/ppermute | solution.py:368
  79.5 26.2 %collective-permute-start.27 = (bf16[256,1024]{1,0:T(8,128)(2,1)S(1)}, bf16[256,1024]{1,0:T(8,128)(2,1)S(1)}, u32[]{:S(2)}, u32[]{:S(2)}) collective-permute-start(bf16[256,1024]{1,0:T(8,128)(2,1)S(1)} %shard_map.101.refs_8_), channel_id=1, source_target_pairs={{0,16},{8,24},{16,0},{24,8},{1,17},{9,25},{17,1},{25,9},{2,18},{10... | collective-permute-start | bytes 1572872 | tf_op jit(solution)/shard_map/ppermute | solution.py:445
  83.3 11.0 %collective-permute-start.20 = (bf16[128,1024]{1,0:T(8,128)(2,1)S(1)}, bf16[128,1024]{1,0:T(8,128)(2,1)S(1)}, u32[]{:S(2)}, u32[]{:S(2)}) collective-permute-start(bf16[128,1024]{1,0:T(8,128)(2,1)S(1)} %copy-done.9), channel_id=1, source_target_pairs={{0,3},{1,2},{2,1},{3,0},{4,7},{5,6},{6,5},{7,4},{8,11},{9,10},{10,... | collective-permute-start | bytes 786440 | tf_op jit(solution)/shard_map/ppermute | solution.py:340
  87.8 9.2 %collective-permute-start.21 = (bf16[128,1024]{1,0:T(8,128)(2,1)S(1)}, bf16[128,1024]{1,0:T(8,128)(2,1)S(1)}, u32[]{:S(2)}, u32[]{:S(2)}) collective-permute-start(bf16[128,1024]{1,0:T(8,128)(2,1)S(1)} %copy-done.8), channel_id=1, source_target_pairs={{0,6},{1,7},{2,4},{3,5},{4,2},{5,3},{6,0},{7,1},{8,14},{9,15},{10,... | collective-permute-start | bytes 786440 | tf_op jit(solution)/shard_map/ppermute | solution.py:340
  90.9 25.6 %collective-permute-start.26 = (bf16[256,1024]{1,0:T(8,128)(2,1)S(1)}, bf16[256,1024]{1,0:T(8,128)(2,1)S(1)}, u32[]{:S(2)}, u32[]{:S(2)}) collective-permute-start(bf16[256,1024]{1,0:T(8,128)(2,1)S(1)} %shard_map.101.refs_8_), channel_id=1, source_target_pairs={{0,8},{8,0},{16,24},{24,16},{1,9},{9,1},{17,25},{25,17},{2,10},{10... | collective-permute-start | bytes 1572872 | tf_op jit(solution)/shard_map/ppermute | solution.py:445
  93.4 19.6 %collective-permute-start.22 = (bf16[128,1024]{1,0:T(8,128)(2,1)S(1)}, bf16[128,1024]{1,0:T(8,128)(2,1)S(1)}, u32[]{:S(2)}, u32[]{:S(2)}) collective-permute-start(bf16[128,1024]{1,0:T(8,128)(2,1)S(1)} %copy-done.7), channel_id=1, source_target_pairs={{0,7},{1,6},{2,5},{3,4},{4,3},{5,2},{6,1},{7,0},{8,15},{9,14},{10,... | collective-permute-start | bytes 786440 | tf_op jit(solution)/shard_map/ppermute | solution.py:340
  94.4 19.3 %collective-permute-start.23 = (bf16[128,1024]{1,0:T(8,128)(2,1)S(1)}, bf16[128,1024]{1,0:T(8,128)(2,1)S(1)}, u32[]{:S(2)}, u32[]{:S(2)}) collective-permute-start(bf16[128,1024]{1,0:T(8,128)(2,1)S(1)} %copy-done.6), channel_id=1, source_target_pairs={{0,1},{1,0},{2,3},{3,2},{4,5},{5,4},{6,7},{7,6},{8,9},{9,8},{10,11... | collective-permute-start | bytes 786440 | tf_op jit(solution)/shard_map/ppermute | solution.py:340
  97.0 16.7 %collective-permute-start.24 = (bf16[128,1024]{1,0:T(8,128)(2,1)S(1)}, bf16[128,1024]{1,0:T(8,128)(2,1)S(1)}, u32[]{:S(2)}, u32[]{:S(2)}) collective-permute-start(bf16[128,1024]{1,0:T(8,128)(2,1)S(1)} %copy-done.5), channel_id=1, source_target_pairs={{0,4},{1,5},{2,6},{3,7},{4,0},{5,1},{6,2},{7,3},{8,12},{9,13},{10,... | collective-permute-start | bytes 786440 | tf_op jit(solution)/shard_map/ppermute | solution.py:340
  105.7 10.7 %collective-permute-start.25 = (bf16[128,1024]{1,0:T(8,128)(2,1)S(1)}, bf16[128,1024]{1,0:T(8,128)(2,1)S(1)}, u32[]{:S(2)}, u32[]{:S(2)}) collective-permute-start(bf16[128,1024]{1,0:T(8,128)(2,1)S(1)} %copy-done.4), channel_id=1, source_target_pairs={{0,5},{1,4},{2,7},{3,6},{4,1},{5,0},{6,3},{7,2},{8,13},{9,12},{10,... | collective-permute-start | bytes 786440 | tf_op jit(solution)/shard_map/ppermute | solution.py:340
  113.0 12.6 %collective-permute-start.29 = (bf16[256,1024]{1,0:T(8,128)(2,1)S(1)}, bf16[256,1024]{1,0:T(8,128)(2,1)S(1)}, u32[]{:S(2)}, u32[]{:S(2)}) collective-permute-start(bf16[256,1024]{1,0:T(8,128)(2,1)S(1)} %collective-permute-done.27.refs_10_), channel_id=1, source_target_pairs={{0,8},{8,0},{16,24},{24,16},{1,9},{9,1},{17,25},{25,17},{2,10},{10... | collective-permute-start | bytes 1572872 | tf_op jit(solution)/shard_map/ppermute | solution.py:445
  129.0 9.0 %collective-permute-start.31 = (bf16[256,512]{1,0:T(8,128)(2,1)S(1)}, bf16[256,512]{1,0:T(8,128)(2,1)S(1)}, u32[]{:S(2)}, u32[]{:S(2)}) collective-permute-start(bf16[256,512]{1,0:T(8,128)(2,1)S(1)} %get-tuple-element.180), channel_id=1, source_target_pairs={{0,4},{4,0},{1,5},{5,1},{2,6},{6,2},{3,7},{7,3},{8,12},{12,8},{9,1... | collective-permute-start | bytes 786440 | tf_op jit(solution)/shard_map/ppermute | solution.py:466
  131.4 8.1 %collective-permute-start.32 = (bf16[256,512]{1,0:T(8,128)(2,1)S(1)}, bf16[256,512]{1,0:T(8,128)(2,1)S(1)}, u32[]{:S(2)}, u32[]{:S(2)}) collective-permute-start(bf16[256,512]{1,0:T(8,128)(2,1)S(1)} %get-tuple-element.181), channel_id=1, source_target_pairs={{0,1},{1,0},{2,3},{3,2},{4,5},{5,4},{6,7},{7,6},{8,9},{9,8},{10,11... | collective-permute-start | bytes 786440 | tf_op jit(solution)/shard_map/ppermute | solution.py:467
  (16 other events, 171.9 us)

commit v10 on v9

--- a/solution.py
+++ b/solution.py
@@ -197,7 +197,8 @@
     new_outer[...], new_momentum[...] = outer_step(replicas, inputs, weight, momentum)
 
 
-def keys_kernel(acts_count, counts, at, *refs):
+def keys_kernel(orders, counts, at, *refs):
+    acts_count = sum(len(order) for order in orders)
     acts, refs = refs[:acts_count], refs[acts_count:]
     blocks = []
     for count in counts:
@@ -205,14 +206,15 @@
         refs = refs[count:]
     weight = jnp.concatenate(blocks, axis=0)
     before, outs = (refs[:1], refs[1:]) if at else ([], refs)
-    each = acts_count // len(outs)
-    for n, out in enumerate(outs):
-        left = jnp.concatenate([a[:, at : at + weight.shape[0]] for a in acts[n * each : (n + 1) * each]], axis=0)
+    for order, out in zip(orders, outs):
+        left = jnp.concatenate([acts[n][:, at : at + weight.shape[0]] for n in order], axis=0)
         product = jnp.dot(left, weight, preferred_element_type=f32)
         out[...] = (before[0][...] + product if at else product).astype(out.dtype)
 
 
-def keys_part(acts, blocks, at, before=(), outs=1, kind=f32):
+def keys_part(acts, blocks, at, before=(), orders=None, kind=f32):
+    orders = orders or [list(range(len(acts)))]
+    outs = len(orders)
     rows, kv = len(acts) * acts[0].shape[0] // outs, sum(w.shape[1] for w in blocks[0])
     depth = sum(block[0].shape[0] for block in blocks)
     if at % LANES:
@@ -220,7 +222,7 @@
     pieces = [w for block in blocks for w in block]
     flops = rows * depth * kv if at else 1 << 34
     return pl.pallas_call(
-        functools.partial(keys_kernel, len(acts), [len(block) for block in blocks], at),
+        functools.partial(keys_kernel, orders, [len(block) for block in blocks], at),
         out_shape=[jax.ShapeDtypeStruct((rows, kv), kind)] * outs,
         in_specs=[pl.BlockSpec()] * (len(acts) + len(pieces) + len(before)),
         out_specs=[pl.BlockSpec()] * outs,
@@ -326,8 +328,6 @@
     stages = [(m + 1, m) for m in range(nz - 2, -1, -2)]
 
     far = [(i, k, s) for k in range(CORES) for i in range(PAIR) for s in range(fsdp)]
-    early = [(0, 1, 0)]
-    late = [e for e in far if e not in early]
     index = lambda i, k, s: ((i % PAIR) * CORES + k % CORES) * fsdp + s % fsdp
     every = [(i, k, s) for i in range(PAIR) for k in range(CORES) for s in range(fsdp)]
     mine, nexts = {}, {}
@@ -375,8 +375,6 @@
         if not stage:
             place, *held = lax.optimization_barrier((place, *[mine[e] for e in far]))
             mine.update(zip(far, held))
-            for e in early:
-                send_next(*e)
         if stage:
             place, to_z, to_x = lax.optimization_barrier((place, to_z, to_x))
             m = stages[stage - 1][1]
@@ -413,8 +411,6 @@
     inputs[0], inputs[2] = small_call(
         gather_kernel, [jax.ShapeDtypeStruct(part.shape, f32) for part in (keep_left, keep_right)], keep_left, keep_right, *inputs[4:], spec=pl.BlockSpec(), weight=200
     )
-    inputs[0], *held = lax.optimization_barrier((inputs[0], *[nexts[e] for e in early]))
-    nexts.update(zip(early, held))
     replicas = nz * PAIR * CORES
     inputs = [*inputs[:4], outer_weight, outer_momentum]
     (share_rows,) = small_call(
@@ -431,9 +427,9 @@
         spec=pl.BlockSpec(),
         weight=1 << 17,
     )
-    share_rows, *held = lax.optimization_barrier((share_rows, *[mine[e] for e in late]))
-    mine.update(zip(late, held))
-    for e in late:
+    share_rows, *held = lax.optimization_barrier((share_rows, *[mine[e] for e in far]))
+    mine.update(zip(far, held))
+    for e in far:
         send_next(*e)
 
     rows = {}
@@ -448,7 +444,8 @@
 
     half = len(far) // CORES
     near, away = [nexts[e] for e in far[:half]], [nexts[e] for e in far[half:]]
-    give, keep = keys_part(away + near, rows[:-1], 0, outs=2)
+    orders = [list(range(half)), [2 * half - 1] + list(range(half, 2 * half - 1))]
+    keep, give = keys_part(near + away[1:] + away[:1], rows[:-1], 0, orders=orders)
     give, keep, input_grad = lax.optimization_barrier((give, keep, input_grad))
     last = (nz - 1) * share
     (give,) = keys_part(away, rows[-1:], last, [give], kind=bf16)

time: 146 us -> 146 us (level)
  starting transfers between devices: 47.5 us -> 43.4 us
  waiting for transfers between devices: 71.2 us -> 75.2 us
    ppermute x7, starting transfers between devices: 14.3 us -> 6.81 us  [send_next(): lax.ppermute(mine[i, k, s], ('x', 'core', 'fsdp'), pairs)]
    ppermute x7, waiting for transfers between devices: 3.23 us -> 10.7 us  [send_next(): lax.ppermute(mine[i, k, s], ('x', 'core', 'fsdp'), pairs)]
    ppermute x2, starting transfers between devices: 0.49 us -> 3.2 us  [home(): lax.ppermute(part, 'fsdp', ring(fsdp, -s - 1))]
    ppermute x2, waiting for transfers between devices: 10.7 us -> 8.08 us  [home(): from_x = lax.ppermute(to_x, 'x', ring(PAIR, 1))]
    ppermute x3, starting transfers between devices: 7.02 us -> 8.78 us  [local(): lax.ppermute(piece, 'z', [(i, i ^ low) for i in range(nz)])]
  transfers between devices with their start and end apart: 35 -> 35, of which waited for: 21 -> 24; matrix products, arithmetic and copies ran while one was open for 2% -> 2% of each run, Pallas kernels for 15% -> 15%
where the time goes in v10:
time: 146 us
  waiting for transfers between devices  75.2 us (52%)
  starting transfers between devices  43.4 us (30%)
  Pallas kernels  23.2 us (16%)
  matrix products  2.38 us (2%)
    ppermute x3, waiting for transfers between devices, local(): lax.ppermute(piece, 'z', [(i, i ^ low) for i in range(nz)])  15 us
    ppermute x2, waiting for transfers between devices, local(): lax.ppermute(to_x, 'x', across_x)  14.5 us
    ppermute x7, waiting for transfers between devices, send_next(): lax.ppermute(mine[i, k, s], ('x', 'core', 'fsdp'), pairs)  10.7 us
    ppermute x3, starting transfers between devices, local(): lax.ppermute(piece, 'z', [(i, i ^ low) for i in range(nz)])  8.78 us
    ppermute x2, waiting for transfers between devices, home(): from_x = lax.ppermute(to_x, 'x', ring(PAIR, 1))  8.08 us
    pallas_call x2, Pallas kernels, inner_blocks(): pl.pallas_call(functools.partial(inner_kernel, pieces, share, inner_rate...  7.74 us
    ppermute x6, starting transfers between devices, local(): lax.ppermute(part, ('core', 'fsdp'), pair_ring(k, s))  7.53 us
    pallas_call x2, Pallas kernels, pack(): pl.pallas_call(functools.partial(pack_kernel, plan), out_shape=shapes, in...  7.21 us
  transfers between devices with their start and end apart: 35, of which 24 were waited for; matrix products, arithmetic and copies ran while one was open for 2% of the time, Pallas kernels for 15%

profile of v10, /device:TPU:0, one launch (start us, length us, event | category | flops | bytes accessed | tf_op | source)
XLA Modules:
  0.0 145.6 jit_solution(17132379624601433790)
XLA Ops:
  1.2 2.9 %collective-permute-start = (bf16[128,1024]{1,0:T(8,128)(2,1)}, bf16[128,1024]{1,0:T(8,128)(2,1)S(1)}, u32[]{:S(2)}, u32[]{:S(2)}) collective-permute-start(bf16[128,1024]{1,0:T(8,128)(2,1)} %refs_4_.4), channel_id=1, source_target_pairs={{0,1},{1,0},{2,3},{3,2},{4,5},{5,4},{6,7},{7,6},{8,9},{9,8},{10,11... | collective-permute-start | bytes 786440 | tf_op jit(solution)/shard_map/ppermute | solution.py:344
  4.3 3.2 %shard_map.94 = (bf16[128,1024]{1,0:T(8,128)(2,1)S(1)}, bf16[128,1024]{1,0:T(8,128)(2,1)}, bf16[128,1024]{1,0:T(8,128)(2,1)}, bf16[128,1024]{1,0:T(8,128)(2,1)S(...) custom-call(s32[32]{0:T(128)S(1)} %stack.216.starts, ...), custom_call_target="tpu_custom_call" | custom-call | bytes 16777216 | tf_op jit(solution)/shard_map/pallas_call | solution.py:72
  7.7 2.7 %collective-permute-start.3 = (bf16[128,1024]{1,0:T(8,128)(2,1)S(1)}, bf16[128,1024]{1,0:T(8,128)(2,1)S(1)}, u32[]{:S(2)}, u32[]{:S(2)}) collective-permute-start(bf16[128,1024]{1,0:T(8,128)(2,1)S(1)} %get-tuple-element.108), channel_id=1, source_target_pairs={{0,3},{1,2},{2,1},{3,0},{4,7},{5,6},{6,5},{7,4},{8,11},{9,10},{10,... | collective-permute-start | bytes 786440 | tf_op jit(solution)/shard_map/ppermute | solution.py:351
  11.5 4.0 %shard_map.93 = (bf16[128,1024]{1,0:T(8,128)(2,1)}, bf16[128,1024]{1,0:T(8,128)(2,1)}, bf16[128,1024]{1,0:T(8,128)(2,1)}, bf16[128,1024]{1,0:T(8,128)(2,1)}, bf1...) custom-call(s32[32]{0:T(128)S(1)} %stack.215.starts, ...), custom_call_target="tpu_custom_call" | custom-call | bytes 16777216 | tf_op jit(solution)/shard_map/pallas_call | solution.py:72
  17.0 2.2 %collective-permute-start.10 = (bf16[128,1024]{1,0:T(8,128)(2,1)S(1)}, bf16[128,1024]{1,0:T(8,128)(2,1)S(1)}, u32[]{:S(2)}, u32[]{:S(2)}) collective-permute-start(bf16[128,1024]{1,0:T(8,128)(2,1)S(1)} %get-tuple-element.123), channel_id=1, source_target_pairs={{0,1},{1,0},{2,3},{3,2},{4,5},{5,4},{6,7},{7,6},{8,9},{9,8},{10,11... | collective-permute-start | bytes 786440 | tf_op jit(solution)/shard_map/ppermute | solution.py:351
  19.2 3.1 %collective-permute-done.3.refs_3_ = bf16[128,1024]{1,0:T(8,128)(2,1)S(1)} collective-permute-done((bf16[128,1024]{1,0:T(8,128)(2,1)S(1)}, bf16[128,1024]{1,0:T(8,128)(2,1)S(1)}, u32[]{:S(2)}, u32[]{:S(2)}) %collective-permute-start.3) | collective-permute-done | bytes 262176 | tf_op jit(solution)/shard_map/ppermute | solution.py:351
  22.3 1.9 %collective-permute-start.11 = (bf16[128,1024]{1,0:T(8,128)(2,1)S(1)}, bf16[128,1024]{1,0:T(8,128)(2,1)S(1)}, u32[]{:S(2)}, u32[]{:S(2)}) collective-permute-start(bf16[128,1024]{1,0:T(8,128)(2,1)S(1)} %get-tuple-element.124), channel_id=1, source_target_pairs={{0,3},{1,2},{2,1},{3,0},{4,7},{5,6},{6,5},{7,4},{8,11},{9,10},{10,... | collective-permute-start | bytes 786440 | tf_op jit(solution)/shard_map/ppermute | solution.py:351
  24.2 4.0 %shard_map.95 = (bf16[512,512]{1,0:T(8,128)(2,1)S(1)}, f32[512,512]{1,0:T(8,128)S(1)}, bf16[512,512]{1,0:T(8,128)(2,1)S(1)}, f32[512,512]{1,0:T(8,128)S(1)}) custom-call(s32[4]{0:T(128)S(1)} %pad_add_fusion.1.place, bf16[128,1024]{1,0:T(8,128)(2,1)S(1)} %get-tuple-element.105.refs_0_, bf16[128,1024]{1,0:T(8,128)(2,1)S(1)} %collective-permute-done.1.refs_1_, ...), custom_call_target="tpu_custom_call" | custom-call | flops 134217728 | bytes 262144 | tf_op jit(solution)/shard_map/pallas_call | solution.py:135
  31.4 2.4 %convolution_convert_fusion.refs_0_ = bf16[256,4096]{1,0:T(8,128)(2,1)S(1)} fusion(bf16[128,1024]{1,0:T(8,128)(2,1)S(1)} %collective-permute-done.refs_6_, bf16[128,1024]{1,0:T(8,128)(2,1)S(1)} %copy-done, bf16[1,4096,1024]{2,1,0:T(8,128)(2,1)S(1)} %bitcast.49), kind=kOutput, calls=%fused_computation | convolution fusion | flops 2149580800 | bytes 11010048 | tf_op jit(solution)/shard_map/dot_general | solution.py:392
  33.9 7.2 %collective-permute-done.7.from_x = bf16[512,512]{1,0:T(8,128)(2,1)S(1)} collective-permute-done((bf16[512,512]{1,0:T(8,128)(2,1)S(1)}, bf16[512,512]{1,0:T(8,128)(2,1)S(1)}, u32[]{:S(2)}, u32[]{:S(2)}) %collective-permute-start.7) | collective-permute-done | bytes 524320 | tf_op jit(solution)/shard_map/ppermute | solution.py:399
  44.7 3.7 %shard_map.97 = (bf16[512,768]{1,0:T(8,128)(2,1)S(1)}, f32[512,768]{1,0:T(8,128)S(1)}, bf16[512,256]{1,0:T(8,128)(2,1)S(1)}, f32[512,256]{1,0:T(8,128)S(1)}) custom-call(s32[4]{0:T(128)S(1)} %pad_add_fusion.place, bf16[128,1024]{1,0:T(8,128)(2,1)S(1)} %get-tuple-element.121.refs_0_, bf16[128,1024]{1,0:T(8,128)(2,1)S(1)} %collective-permute-done.9.refs_1_, ...), custom_call_target="tpu_custom_call" | custom-call | flops 134217728 | bytes 262144 | tf_op jit(solution)/shard_map/pallas_call | solution.py:135
  49.0 2.3 %collective-permute-done.13.refs_3_ = bf16[256,512]{1,0:T(8,128)(2,1)S(1)} collective-permute-done((bf16[256,512]{1,0:T(8,128)(2,1)S(1)}, bf16[256,512]{1,0:T(8,128)(2,1)S(1)}, u32[]{:S(2)}, u32[]{:S(2)}) %collective-permute-start.13) | collective-permute-done | bytes 262176 | tf_op jit(solution)/shard_map/ppermute | solution.py:368
  52.6 2.7 %collective-permute-start.16 = (bf16[256,1024]{1,0:T(8,128)(2,1)S(1)}, bf16[256,1024]{1,0:T(8,128)(2,1)S(1)}, u32[]{:S(2)}, u32[]{:S(2)}) collective-permute-start(bf16[256,1024]{1,0:T(8,128)(2,1)S(1)} %shard_map.99), channel_id=1, source_target_pairs={{0,16},{8,24},{16,0},{24,8},{1,17},{9,25},{17,1},{25,9},{2,18},{10... | collective-permute-start | bytes 1572872 | tf_op jit(solution)/shard_map/ppermute | solution.py:389
  56.8 4.6 %collective-permute-done.15.from_z = bf16[512,256]{1,0:T(8,128)(2,1)S(1)} collective-permute-done((bf16[512,256]{1,0:T(8,128)(2,1)S(1)}, bf16[512,256]{1,0:T(8,128)(2,1)S(1)}, u32[]{:S(2)}, u32[]{:S(2)}) %collective-permute-start.15) | collective-permute-done | bytes 262176 | tf_op jit(solution)/shard_map/ppermute | solution.py:399
  61.4 7.2 %collective-permute-done.14.from_x = bf16[512,768]{1,0:T(8,128)(2,1)S(1)} collective-permute-done((bf16[512,768]{1,0:T(8,128)(2,1)S(1)}, bf16[512,768]{1,0:T(8,128)(2,1)S(1)}, u32[]{:S(2)}, u32[]{:S(2)}) %collective-permute-start.14) | collective-permute-done | bytes 786464 | tf_op jit(solution)/shard_map/ppermute | solution.py:399
  69.5 4.3 %collective-permute-done.16.refs_0_ = bf16[256,1024]{1,0:T(8,128)(2,1)S(1)} collective-permute-done((bf16[256,1024]{1,0:T(8,128)(2,1)S(1)}, bf16[256,1024]{1,0:T(8,128)(2,1)S(1)}, u32[]{:S(2)}, u32[]{:S(2)}) %collective-permute-start.16) | collective-permute-done | bytes 524320 | tf_op jit(solution)/shard_map/ppermute | solution.py:389
  74.0 5.2 %collective-permute-done.17.refs_1_ = bf16[256,768]{1,0:T(8,128)(2,1)S(1)} collective-permute-done((bf16[256,768]{1,0:T(8,128)(2,1)S(1)}, bf16[256,768]{1,0:T(8,128)(2,1)S(1)}, u32[]{:S(2)}, u32[]{:S(2)}) %collective-permute-start.17) | collective-permute-done | bytes 393248 | tf_op jit(solution)/shard_map/ppermute | solution.py:368
  79.5 3.8 %collective-permute-start.27 = (bf16[256,1024]{1,0:T(8,128)(2,1)S(1)}, bf16[256,1024]{1,0:T(8,128)(2,1)S(1)}, u32[]{:S(2)}, u32[]{:S(2)}) collective-permute-start(bf16[256,1024]{1,0:T(8,128)(2,1)S(1)} %shard_map.101.refs_8_), channel_id=1, source_target_pairs={{0,16},{8,24},{16,0},{24,8},{1,17},{9,25},{17,1},{25,9},{2,18},{10... | collective-permute-start | bytes 1572872 | tf_op jit(solution)/shard_map/ppermute | solution.py:441
  83.3 5.1 %collective-permute-start.19 = (bf16[128,1024]{1,0:T(8,128)(2,1)S(1)}, bf16[128,1024]{1,0:T(8,128)(2,1)S(1)}, u32[]{:S(2)}, u32[]{:S(2)}) collective-permute-start(bf16[128,1024]{1,0:T(8,128)(2,1)S(1)} %copy-done.10), channel_id=1, source_target_pairs={{0,1},{1,0},{2,3},{3,2},{4,5},{5,4},{6,7},{7,6},{8,9},{9,8},{10,11... | collective-permute-start | bytes 786440 | tf_op jit(solution)/shard_map/ppermute | solution.py:340
  90.1 1.9 %shard_map.103 = bf16[128,8192]{1,0:T(8,128)(2,1)} custom-call(s32[2]{0:T(128)S(1)} %pad_add_fusion.2.starts, bf16[256,4096]{1,0:T(8,128)(2,1)S(1)} %convolution_convert_fusion.refs_0_, bf16[128,4096]{1,0:T(8,128)(2,1)S(1)} %collective-permute-done.28.refs_1_), custom_call_target="tpu_custom_call" | custom-call | bytes 4194304 | tf_op jit(solution)/shard_map/pallas_call | solution.py:298
  92.0 2.5 %collective-permute-start.26 = (bf16[256,1024]{1,0:T(8,128)(2,1)S(1)}, bf16[256,1024]{1,0:T(8,128)(2,1)S(1)}, u32[]{:S(2)}, u32[]{:S(2)}) collective-permute-start(bf16[256,1024]{1,0:T(8,128)(2,1)S(1)} %shard_map.101.refs_8_), channel_id=1, source_target_pairs={{0,8},{8,0},{16,24},{24,16},{1,9},{9,1},{17,25},{25,17},{2,10},{10... | collective-permute-start | bytes 1572872 | tf_op jit(solution)/shard_map/ppermute | solution.py:441
  94.8 2.8 %collective-permute-done.20.refs_2_ = bf16[128,1024]{1,0:T(8,128)(2,1)S(1)} collective-permute-done((bf16[128,1024]{1,0:T(8,128)(2,1)S(1)}, bf16[128,1024]{1,0:T(8,128)(2,1)S(1)}, u32[]{:S(2)}, u32[]{:S(2)}) %collective-permute-start.20) | collective-permute-done | bytes 262176 | tf_op jit(solution)/shard_map/ppermute | solution.py:340
  97.7 5.1 %collective-permute-done.21.refs_3_ = bf16[128,1024]{1,0:T(8,128)(2,1)S(1)} collective-permute-done((bf16[128,1024]{1,0:T(8,128)(2,1)S(1)}, bf16[128,1024]{1,0:T(8,128)(2,1)S(1)}, u32[]{:S(2)}, u32[]{:S(2)}) %collective-permute-start.21) | collective-permute-done | bytes 262176 | tf_op jit(solution)/shard_map/ppermute | solution.py:340
  102.8 2.9 %collective-permute-done.27.refs_10_ = bf16[256,1024]{1,0:T(8,128)(2,1)S(1)} collective-permute-done((bf16[256,1024]{1,0:T(8,128)(2,1)S(1)}, bf16[256,1024]{1,0:T(8,128)(2,1)S(1)}, u32[]{:S(2)}, u32[]{:S(2)}) %collective-permute-start.27) | collective-permute-done | bytes 524320 | tf_op jit(solution)/shard_map/ppermute | solution.py:441
  107.4 2.4 %collective-permute-start.29 = (bf16[256,1024]{1,0:T(8,128)(2,1)S(1)}, bf16[256,1024]{1,0:T(8,128)(2,1)S(1)}, u32[]{:S(2)}, u32[]{:S(2)}) collective-permute-start(bf16[256,1024]{1,0:T(8,128)(2,1)S(1)} %collective-permute-done.27.refs_10_), channel_id=1, source_target_pairs={{0,8},{8,0},{16,24},{24,16},{1,9},{9,1},{17,25},{25,17},{2,10},{10... | collective-permute-start | bytes 1572872 | tf_op jit(solution)/shard_map/ppermute | solution.py:441
  109.8 2.6 %collective-permute-done.24.refs_6_.refs_3_ = bf16[128,1024]{1,0:T(8,128)(2,1)S(1)} collective-permute-done((bf16[128,1024]{1,0:T(8,128)(2,1)S(1)}, bf16[128,1024]{1,0:T(8,128)(2,1)S(1)}, u32[]{:S(2)}, u32[]{:S(2)}) %collective-permute-start.24) | collective-permute-done | bytes 262176 | tf_op jit(solution)/shard_map/ppermute | solution.py:340
  112.4 3.6 %collective-permute-done.26.refs_9_ = bf16[256,1024]{1,0:T(8,128)(2,1)S(1)} collective-permute-done((bf16[256,1024]{1,0:T(8,128)(2,1)S(1)}, bf16[256,1024]{1,0:T(8,128)(2,1)S(1)}, u32[]{:S(2)}, u32[]{:S(2)}) %collective-permute-start.26) | collective-permute-done | bytes 524320 | tf_op jit(solution)/shard_map/ppermute | solution.py:441
  116.0 1.8 %shard_map.102 = (f32[512,1024]{1,0:T(8,128)S(1)}, f32[512,1024]{1,0:T(8,128)S(1)}) custom-call(bf16[128,1024]{1,0:T(8,128)(2,1)S(1)} %copy-done.3, bf16[128,1024]{1,0:T(8,128)(2,1)S(1)} %collective-permute-done.19.refs_1_, bf16[128,1024]{1,0:T(8,128)(2,1)S(1)} %collective-permute-done.20.refs_2_, bf16[128,1024]{1,0:T(8,128)(2,1)S(1)} %collective-permute-done.21.refs_3_, ...), custom_call_target="tpu_custom_call" | custom-call | flops 17179869184 | bytes 524288 | tf_op jit(solution)/shard_map/pallas_call | solution.py:224
  117.8 8.4 %collective-permute-done.29.refs_4_ = bf16[256,1024]{1,0:T(8,128)(2,1)S(1)} collective-permute-done((bf16[256,1024]{1,0:T(8,128)(2,1)S(1)}, bf16[256,1024]{1,0:T(8,128)(2,1)S(1)}, u32[]{:S(2)}, u32[]{:S(2)}) %collective-permute-start.29) | collective-permute-done | bytes 524320 | tf_op jit(solution)/shard_map/ppermute | solution.py:441
  127.2 2.2 %collective-permute-done.30.came = bf16[512,1024]{1,0:T(8,128)(2,1)S(1)} collective-permute-done((bf16[512,1024]{1,0:T(8,128)(2,1)S(1)}, bf16[512,1024]{1,0:T(8,128)(2,1)S(1)}, u32[]{:S(2)}, u32[]{:S(2)}) %collective-permute-start.30) | collective-permute-done | bytes 1048608 | tf_op jit(solution)/shard_map/ppermute | solution.py:453
  131.7 6.3 %collective-permute-done.31.refs_2_ = bf16[256,512]{1,0:T(8,128)(2,1)S(1)} collective-permute-done((bf16[256,512]{1,0:T(8,128)(2,1)S(1)}, bf16[256,512]{1,0:T(8,128)(2,1)S(1)}, u32[]{:S(2)}, u32[]{:S(2)}) %collective-permute-start.31) | collective-permute-done | bytes 262176 | tf_op jit(solution)/shard_map/ppermute | solution.py:463
  141.5 1.8 %collective-permute-done.33.from_x = bf16[128,512]{1,0:T(8,128)(2,1)S(1)} collective-permute-done((bf16[128,512]{1,0:T(8,128)(2,1)S(1)}, bf16[128,512]{1,0:T(8,128)(2,1)S(1)}, u32[]{:S(2)}, u32[]{:S(2)}) %collective-permute-start.33) | collective-permute-done | bytes 131104 | tf_op jit(solution)/shard_map/ppermute | solution.py:463
  (89 shorter events, 27.7 us)
Async XLA Ops:
  0.6 23.6 %collective-permute-start.6 = (bf16[4096,1024]{1,0:T(8,128)(2,1)}, bf16[4096,1024]{1,0:T(8,128)(2,1)}, u32[]{:S(2)}, u32[]{:S(2)}) collective-permute-start(bf16[4096,1024]{1,0:T(8,128)(2,1)} %bitcast.45), channel_id=1, source_target_pairs={{0,2},{2,0},{1,3},{3,1},{4,6},{6,4},{5,7},{7,5},{8,10},{10,8},{9,1... | collective-permute-start | bytes 25165832 | tf_op jit(solution)/shard_map/ppermute | solution.py:353
  1.1 6.5 %collective-permute-start.4 = (bf16[128,1024]{1,0:T(8,128)(2,1)}, bf16[128,1024]{1,0:T(8,128)(2,1)S(1)}, u32[]{:S(2)}, u32[]{:S(2)}) collective-permute-start(bf16[128,1024]{1,0:T(8,128)(2,1)} %refs_4_.4), channel_id=1, source_target_pairs={{0,2},{2,0},{1,3},{3,1},{4,6},{6,4},{5,7},{7,5},{8,10},{10,8},{9,1... | collective-permute-start | bytes 786440 | tf_op jit(solution)/shard_map/ppermute | solution.py:354
  1.2 9.9 %collective-permute-start = (bf16[128,1024]{1,0:T(8,128)(2,1)}, bf16[128,1024]{1,0:T(8,128)(2,1)S(1)}, u32[]{:S(2)}, u32[]{:S(2)}) collective-permute-start(bf16[128,1024]{1,0:T(8,128)(2,1)} %refs_4_.4), channel_id=1, source_target_pairs={{0,1},{1,0},{2,3},{3,2},{4,5},{5,4},{6,7},{7,6},{8,9},{9,8},{10,11... | collective-permute-start | bytes 786440 | tf_op jit(solution)/shard_map/ppermute | solution.py:344
  7.5 7.9 %collective-permute-start.1 = (bf16[128,1024]{1,0:T(8,128)(2,1)}, bf16[128,1024]{1,0:T(8,128)(2,1)S(1)}, u32[]{:S(2)}, u32[]{:S(2)}) collective-permute-start(bf16[128,1024]{1,0:T(8,128)(2,1)} %get-tuple-element.106), channel_id=1, source_target_pairs={{0,2},{1,3},{2,0},{3,1},{4,6},{5,7},{6,4},{7,5},{8,10},{9,11},{10,... | collective-permute-start | bytes 786440 | tf_op jit(solution)/shard_map/ppermute | solution.py:351
  7.6 9.4 %collective-permute-start.2 = (bf16[128,1024]{1,0:T(8,128)(2,1)}, bf16[128,1024]{1,0:T(8,128)(2,1)S(1)}, u32[]{:S(2)}, u32[]{:S(2)}) collective-permute-start(bf16[128,1024]{1,0:T(8,128)(2,1)} %get-tuple-element.107), channel_id=1, source_target_pairs={{0,1},{1,0},{2,3},{3,2},{4,5},{5,4},{6,7},{7,6},{8,9},{9,8},{10,11... | collective-permute-start | bytes 786440 | tf_op jit(solution)/shard_map/ppermute | solution.py:351
  7.7 14.6 %collective-permute-start.3 = (bf16[128,1024]{1,0:T(8,128)(2,1)S(1)}, bf16[128,1024]{1,0:T(8,128)(2,1)S(1)}, u32[]{:S(2)}, u32[]{:S(2)}) collective-permute-start(bf16[128,1024]{1,0:T(8,128)(2,1)S(1)} %get-tuple-element.108), channel_id=1, source_target_pairs={{0,3},{1,2},{2,1},{3,0},{4,7},{5,6},{6,5},{7,4},{8,11},{9,10},{10,... | collective-permute-start | bytes 786440 | tf_op jit(solution)/shard_map/ppermute | solution.py:351
  11.2 13.0 %collective-permute-start.5 = (bf16[128,1024]{1,0:T(8,128)(2,1)S(1)}, bf16[128,1024]{1,0:T(8,128)(2,1)S(1)}, u32[]{:S(2)}, u32[]{:S(2)}) collective-permute-start(bf16[128,1024]{1,0:T(8,128)(2,1)S(1)} %collective-permute-done.refs_6_), channel_id=1, source_target_pairs={{0,2},{2,0},{1,3},{3,1},{4,6},{6,4},{5,7},{7,5},{8,10},{10,8},{9,1... | collective-permute-start | bytes 786440 | tf_op jit(solution)/shard_map/ppermute | solution.py:356
  15.5 29.2 %collective-permute-start.9 = (bf16[128,1024]{1,0:T(8,128)(2,1)S(1)}, bf16[128,1024]{1,0:T(8,128)(2,1)S(1)}, u32[]{:S(2)}, u32[]{:S(2)}) collective-permute-start(bf16[128,1024]{1,0:T(8,128)(2,1)S(1)} %get-tuple-element.122), channel_id=1, source_target_pairs={{0,2},{1,3},{2,0},{3,1},{4,6},{5,7},{6,4},{7,5},{8,10},{9,11},{10,... | collective-permute-start | bytes 786440 | tf_op jit(solution)/shard_map/ppermute | solution.py:351
  17.0 27.7 %collective-permute-start.10 = (bf16[128,1024]{1,0:T(8,128)(2,1)S(1)}, bf16[128,1024]{1,0:T(8,128)(2,1)S(1)}, u32[]{:S(2)}, u32[]{:S(2)}) collective-permute-start(bf16[128,1024]{1,0:T(8,128)(2,1)S(1)} %get-tuple-element.123), channel_id=1, source_target_pairs={{0,1},{1,0},{2,3},{3,2},{4,5},{5,4},{6,7},{7,6},{8,9},{9,8},{10,11... | collective-permute-start | bytes 786440 | tf_op jit(solution)/shard_map/ppermute | solution.py:351
  22.3 22.4 %collective-permute-start.11 = (bf16[128,1024]{1,0:T(8,128)(2,1)S(1)}, bf16[128,1024]{1,0:T(8,128)(2,1)S(1)}, u32[]{:S(2)}, u32[]{:S(2)}) collective-permute-start(bf16[128,1024]{1,0:T(8,128)(2,1)S(1)} %get-tuple-element.124), channel_id=1, source_target_pairs={{0,3},{1,2},{2,1},{3,0},{4,7},{5,6},{6,5},{7,4},{8,11},{9,10},{10,... | collective-permute-start | bytes 786440 | tf_op jit(solution)/shard_map/ppermute | solution.py:351
  28.3 12.8 %collective-permute-start.7 = (bf16[512,512]{1,0:T(8,128)(2,1)S(1)}, bf16[512,512]{1,0:T(8,128)(2,1)S(1)}, u32[]{:S(2)}, u32[]{:S(2)}) collective-permute-start(bf16[512,512]{1,0:T(8,128)(2,1)S(1)} %get-tuple-element.115), channel_id=1, source_target_pairs={{0,4},{4,0},{1,5},{5,1},{2,6},{6,2},{3,7},{7,3},{8,12},{12,8},{9,1... | collective-permute-start | bytes 1572872 | tf_op jit(solution)/shard_map/ppermute | solution.py:399
  29.8 12.5 %collective-permute-start.8 = (bf16[512,512]{1,0:T(8,128)(2,1)S(1)}, bf16[512,512]{1,0:T(8,128)(2,1)S(1)}, u32[]{:S(2)}, u32[]{:S(2)}) collective-permute-start(bf16[512,512]{1,0:T(8,128)(2,1)S(1)} %get-tuple-element.117), channel_id=1, source_target_pairs={{0,8},{8,0},{16,24},{24,16},{1,9},{9,1},{17,25},{25,17},{2,10},{10... | collective-permute-start | bytes 1572872 | tf_op jit(solution)/shard_map/ppermute | solution.py:399
  42.5 6.4 %collective-permute-start.12 = (bf16[256,512]{1,0:T(8,128)(2,1)S(1)}, bf16[256,512]{1,0:T(8,128)(2,1)S(1)}, u32[]{:S(2)}, u32[]{:S(2)}) collective-permute-start(bf16[256,512]{1,0:T(8,128)(2,1)S(1)} %get-tuple-element.128), channel_id=1, source_target_pairs={{0,8},{8,0},{16,24},{24,16},{1,9},{9,1},{17,25},{25,17},{2,10},{10... | collective-permute-start | bytes 786440 | tf_op jit(solution)/shard_map/ppermute | solution.py:368
  44.2 7.1 %collective-permute-start.13 = (bf16[256,512]{1,0:T(8,128)(2,1)S(1)}, bf16[256,512]{1,0:T(8,128)(2,1)S(1)}, u32[]{:S(2)}, u32[]{:S(2)}) collective-permute-start(bf16[256,512]{1,0:T(8,128)(2,1)S(1)} %get-tuple-element.129), channel_id=1, source_target_pairs={{0,4},{4,0},{1,5},{5,1},{2,6},{6,2},{3,7},{7,3},{8,12},{12,8},{9,1... | collective-permute-start | bytes 786440 | tf_op jit(solution)/shard_map/ppermute | solution.py:368
  51.3 17.3 %collective-permute-start.14 = (bf16[512,768]{1,0:T(8,128)(2,1)S(1)}, bf16[512,768]{1,0:T(8,128)(2,1)S(1)}, u32[]{:S(2)}, u32[]{:S(2)}) collective-permute-start(bf16[512,768]{1,0:T(8,128)(2,1)S(1)} %get-tuple-element.130), channel_id=1, source_target_pairs={{0,4},{4,0},{1,5},{5,1},{2,6},{6,2},{3,7},{7,3},{8,12},{12,8},{9,1... | collective-permute-start | bytes 2359304 | tf_op jit(solution)/shard_map/ppermute | solution.py:399
  51.8 9.6 %collective-permute-start.15 = (bf16[512,256]{1,0:T(8,128)(2,1)S(1)}, bf16[512,256]{1,0:T(8,128)(2,1)S(1)}, u32[]{:S(2)}, u32[]{:S(2)}) collective-permute-start(bf16[512,256]{1,0:T(8,128)(2,1)S(1)} %get-tuple-element.132), channel_id=1, source_target_pairs={{0,8},{8,0},{16,24},{24,16},{1,9},{9,1},{17,25},{25,17},{2,10},{10... | collective-permute-start | bytes 786440 | tf_op jit(solution)/shard_map/ppermute | solution.py:399
  52.6 21.1 %collective-permute-start.16 = (bf16[256,1024]{1,0:T(8,128)(2,1)S(1)}, bf16[256,1024]{1,0:T(8,128)(2,1)S(1)}, u32[]{:S(2)}, u32[]{:S(2)}) collective-permute-start(bf16[256,1024]{1,0:T(8,128)(2,1)S(1)} %shard_map.99), channel_id=1, source_target_pairs={{0,16},{8,24},{16,0},{24,8},{1,17},{9,25},{17,1},{25,9},{2,18},{10... | collective-permute-start | bytes 1572872 | tf_op jit(solution)/shard_map/ppermute | solution.py:389
  55.3 34.8 %collective-permute-start.28 = (bf16[128,4096]{1,0:T(8,128)(2,1)S(1)}, bf16[128,4096]{1,0:T(8,128)(2,1)S(1)}, u32[]{:S(2)}, u32[]{:S(2)}) collective-permute-start(bf16[128,4096]{1,0:T(8,128)(2,1)S(1)} %slice.4), channel_id=1, source_target_pairs={{0,1},{1,0},{2,3},{3,2},{4,5},{5,4},{6,7},{7,6},{8,9},{9,8},{10,11... | collective-permute-start | bytes 3145736 | tf_op jit(solution)/shard_map/ppermute | solution.py:398
  68.8 10.3 %collective-permute-start.17 = (bf16[256,768]{1,0:T(8,128)(2,1)S(1)}, bf16[256,768]{1,0:T(8,128)(2,1)S(1)}, u32[]{:S(2)}, u32[]{:S(2)}) collective-permute-start(bf16[256,768]{1,0:T(8,128)(2,1)S(1)} %get-tuple-element.140), channel_id=1, source_target_pairs={{0,8},{8,0},{16,24},{24,16},{1,9},{9,1},{17,25},{25,17},{2,10},{10... | collective-permute-start | bytes 1179656 | tf_op jit(solution)/shard_map/ppermute | solution.py:368
  68.9 5.0 %collective-permute-start.18 = (bf16[256,256]{1,0:T(8,128)(2,1)S(1)}, bf16[256,256]{1,0:T(8,128)(2,1)S(1)}, u32[]{:S(2)}, u32[]{:S(2)}) collective-permute-start(bf16[256,256]{1,0:T(8,128)(2,1)S(1)} %get-tuple-element.142), channel_id=1, source_target_pairs={{0,4},{4,0},{1,5},{5,1},{2,6},{6,2},{3,7},{7,3},{8,12},{12,8},{9,1... | collective-permute-start | bytes 393224 | tf_op jit(solution)/shard_map/ppermute | solution.py:368
  79.5 26.2 %collective-permute-start.27 = (bf16[256,1024]{1,0:T(8,128)(2,1)S(1)}, bf16[256,1024]{1,0:T(8,128)(2,1)S(1)}, u32[]{:S(2)}, u32[]{:S(2)}) collective-permute-start(bf16[256,1024]{1,0:T(8,128)(2,1)S(1)} %shard_map.101.refs_8_), channel_id=1, source_target_pairs={{0,16},{8,24},{16,0},{24,8},{1,17},{9,25},{17,1},{25,9},{2,18},{10... | collective-permute-start | bytes 1572872 | tf_op jit(solution)/shard_map/ppermute | solution.py:441
  83.3 11.3 %collective-permute-start.19 = (bf16[128,1024]{1,0:T(8,128)(2,1)S(1)}, bf16[128,1024]{1,0:T(8,128)(2,1)S(1)}, u32[]{:S(2)}, u32[]{:S(2)}) collective-permute-start(bf16[128,1024]{1,0:T(8,128)(2,1)S(1)} %copy-done.10), channel_id=1, source_target_pairs={{0,1},{1,0},{2,3},{3,2},{4,5},{5,4},{6,7},{7,6},{8,9},{9,8},{10,11... | collective-permute-start | bytes 786440 | tf_op jit(solution)/shard_map/ppermute | solution.py:340
  88.4 9.2 %collective-permute-start.20 = (bf16[128,1024]{1,0:T(8,128)(2,1)S(1)}, bf16[128,1024]{1,0:T(8,128)(2,1)S(1)}, u32[]{:S(2)}, u32[]{:S(2)}) collective-permute-start(bf16[128,1024]{1,0:T(8,128)(2,1)S(1)} %copy-done.9), channel_id=1, source_target_pairs={{0,4},{1,5},{2,6},{3,7},{4,0},{5,1},{6,2},{7,3},{8,12},{9,13},{10,... | collective-permute-start | bytes 786440 | tf_op jit(solution)/shard_map/ppermute | solution.py:340
  89.2 13.6 %collective-permute-start.21 = (bf16[128,1024]{1,0:T(8,128)(2,1)S(1)}, bf16[128,1024]{1,0:T(8,128)(2,1)S(1)}, u32[]{:S(2)}, u32[]{:S(2)}) collective-permute-start(bf16[128,1024]{1,0:T(8,128)(2,1)S(1)} %copy-done.8), channel_id=1, source_target_pairs={{0,5},{1,4},{2,7},{3,6},{4,1},{5,0},{6,3},{7,2},{8,13},{9,12},{10,... | collective-permute-start | bytes 786440 | tf_op jit(solution)/shard_map/ppermute | solution.py:340
  92.0 24.0 %collective-permute-start.26 = (bf16[256,1024]{1,0:T(8,128)(2,1)S(1)}, bf16[256,1024]{1,0:T(8,128)(2,1)S(1)}, u32[]{:S(2)}, u32[]{:S(2)}) collective-permute-start(bf16[256,1024]{1,0:T(8,128)(2,1)S(1)} %shard_map.101.refs_8_), channel_id=1, source_target_pairs={{0,8},{8,0},{16,24},{24,16},{1,9},{9,1},{17,25},{25,17},{2,10},{10... | collective-permute-start | bytes 1572872 | tf_op jit(solution)/shard_map/ppermute | solution.py:441
  94.6 12.8 %collective-permute-start.22 = (bf16[128,1024]{1,0:T(8,128)(2,1)S(1)}, bf16[128,1024]{1,0:T(8,128)(2,1)S(1)}, u32[]{:S(2)}, u32[]{:S(2)}) collective-permute-start(bf16[128,1024]{1,0:T(8,128)(2,1)S(1)} %copy-done.7), channel_id=1, source_target_pairs={{0,3},{1,2},{2,1},{3,0},{4,7},{5,6},{6,5},{7,4},{8,11},{9,10},{10,... | collective-permute-start | bytes 786440 | tf_op jit(solution)/shard_map/ppermute | solution.py:340
  97.7 12.2 %collective-permute-start.23 = (bf16[128,1024]{1,0:T(8,128)(2,1)S(1)}, bf16[128,1024]{1,0:T(8,128)(2,1)S(1)}, u32[]{:S(2)}, u32[]{:S(2)}) collective-permute-start(bf16[128,1024]{1,0:T(8,128)(2,1)S(1)} %copy-done.6), channel_id=1, source_target_pairs={{0,6},{1,7},{2,4},{3,5},{4,2},{5,3},{6,0},{7,1},{8,14},{9,15},{10,... | collective-permute-start | bytes 786440 | tf_op jit(solution)/shard_map/ppermute | solution.py:340
  102.8 9.6 %collective-permute-start.24 = (bf16[128,1024]{1,0:T(8,128)(2,1)S(1)}, bf16[128,1024]{1,0:T(8,128)(2,1)S(1)}, u32[]{:S(2)}, u32[]{:S(2)}) collective-permute-start(bf16[128,1024]{1,0:T(8,128)(2,1)S(1)} %copy-done.5), channel_id=1, source_target_pairs={{0,7},{1,6},{2,5},{3,4},{4,3},{5,2},{6,1},{7,0},{8,15},{9,14},{10,... | collective-permute-start | bytes 786440 | tf_op jit(solution)/shard_map/ppermute | solution.py:340
  105.7 6.6 %collective-permute-start.25 = (bf16[128,1024]{1,0:T(8,128)(2,1)S(1)}, bf16[128,1024]{1,0:T(8,128)(2,1)S(1)}, u32[]{:S(2)}, u32[]{:S(2)}) collective-permute-start(bf16[128,1024]{1,0:T(8,128)(2,1)S(1)} %copy-done.4), channel_id=1, source_target_pairs={{0,2},{1,3},{2,0},{3,1},{4,6},{5,7},{6,4},{7,5},{8,10},{9,11},{10,... | collective-permute-start | bytes 786440 | tf_op jit(solution)/shard_map/ppermute | solution.py:340
  107.4 18.8 %collective-permute-start.29 = (bf16[256,1024]{1,0:T(8,128)(2,1)S(1)}, bf16[256,1024]{1,0:T(8,128)(2,1)S(1)}, u32[]{:S(2)}, u32[]{:S(2)}) collective-permute-start(bf16[256,1024]{1,0:T(8,128)(2,1)S(1)} %collective-permute-done.27.refs_10_), channel_id=1, source_target_pairs={{0,8},{8,0},{16,24},{24,16},{1,9},{9,1},{17,25},{25,17},{2,10},{10... | collective-permute-start | bytes 1572872 | tf_op jit(solution)/shard_map/ppermute | solution.py:441
  129.6 8.4 %collective-permute-start.31 = (bf16[256,512]{1,0:T(8,128)(2,1)S(1)}, bf16[256,512]{1,0:T(8,128)(2,1)S(1)}, u32[]{:S(2)}, u32[]{:S(2)}) collective-permute-start(bf16[256,512]{1,0:T(8,128)(2,1)S(1)} %get-tuple-element.178), channel_id=1, source_target_pairs={{0,4},{4,0},{1,5},{5,1},{2,6},{6,2},{3,7},{7,3},{8,12},{12,8},{9,1... | collective-permute-start | bytes 786440 | tf_op jit(solution)/shard_map/ppermute | solution.py:463
  130.1 8.1 %collective-permute-start.32 = (bf16[256,512]{1,0:T(8,128)(2,1)S(1)}, bf16[256,512]{1,0:T(8,128)(2,1)S(1)}, u32[]{:S(2)}, u32[]{:S(2)}) collective-permute-start(bf16[256,512]{1,0:T(8,128)(2,1)S(1)} %get-tuple-element.179), channel_id=1, source_target_pairs={{0,1},{1,0},{2,3},{3,2},{4,5},{5,4},{6,7},{7,6},{8,9},{9,8},{10,11... | collective-permute-start | bytes 786440 | tf_op jit(solution)/shard_map/ppermute | solution.py:464
  (16 other events, 169.1 us)

commit v11 on v10

--- a/solution.py
+++ b/solution.py
@@ -419,14 +419,6 @@
         *inputs,
         spec=pl.BlockSpec(),
     )
-    share_rows, *inputs = lax.optimization_barrier((share_rows, *inputs))
-    new_outer, new_momentum = small_call(
-        functools.partial(state_kernel, replicas),
-        [jax.ShapeDtypeStruct((share, kv), f32)] * 2,
-        *inputs,
-        spec=pl.BlockSpec(),
-        weight=1 << 17,
-    )
     share_rows, *held = lax.optimization_barrier((share_rows, *[mine[e] for e in far]))
     mine.update(zip(far, held))
     for e in far:
@@ -437,6 +429,17 @@
         low = m & -m
         pieces = [share_rows] if m == low else list(rows[m ^ low])
         if m == nz - 1:
+            ready = rows[1] if m > 1 else [share_rows]
+            inputs[0], *ready = lax.optimization_barrier((inputs[0], *ready))
+            if m > 1:
+                rows[1] = ready
+            new_outer, new_momentum = small_call(
+                functools.partial(state_kernel, replicas),
+                [jax.ShapeDtypeStruct((share, kv), f32)] * 2,
+                *inputs,
+                spec=pl.BlockSpec(),
+                weight=1 << 17,
+            )
             pieces[0], new_outer = lax.optimization_barrier((pieces[0], new_outer))
         rows[m] = [lax.ppermute(piece, "z", [(i, i ^ low) for i in range(nz)]) for piece in pieces]
     rows = [[share_rows]] + [rows[m] for m in range(1, nz)]

time: 146 us -> 148 us (1.014)
  starting transfers between devices: 43.4 us -> 51.4 us
  waiting for transfers between devices: 75.2 us -> 69.1 us
    ppermute x7, starting transfers between devices: 6.81 us -> 13.5 us  [send_next(): lax.ppermute(mine[i, k, s], ('x', 'core', 'fsdp'), pairs)]
    ppermute x3, waiting for transfers between devices: 15 us -> 9.92 us  [local(): lax.ppermute(piece, 'z', [(i, i ^ low) for i in range(nz)])]
    ppermute x2, waiting for transfers between devices: 1.75 us -> 5.54 us  [home(): lax.ppermute(part, 'fsdp', ring(fsdp, -s - 1))]
    ppermute x2, waiting for transfers between devices: 8.08 us -> 4.29 us  [home(): from_x = lax.ppermute(to_x, 'x', ring(PAIR, 1))]
    ppermute x2, starting transfers between devices: 3.2 us -> 6.85 us  [home(): lax.ppermute(part, 'fsdp', ring(fsdp, -s - 1))]
    ppermute x3, starting transfers between devices: 8.78 us -> 6.29 us  [local(): lax.ppermute(piece, 'z', [(i, i ^ low) for i in range(nz)])]
  transfers between devices with their start and end apart: 35 -> 35, of which waited for: 24 -> 21; matrix products, arithmetic and copies ran while one was open for 2% -> 2% of each run, Pallas kernels for 15% -> 15%
where the time goes in v11:
time: 148 us
  waiting for transfers between devices  69.1 us (47%)
  starting transfers between devices  51.4 us (35%)
  Pallas kernels  23.2 us (16%)
  matrix products  2.38 us (2%)
    ppermute x2, waiting for transfers between devices, local(): lax.ppermute(to_x, 'x', across_x)  14.5 us
    ppermute x7, starting transfers between devices, send_next(): lax.ppermute(mine[i, k, s], ('x', 'core', 'fsdp'), pairs)  13.5 us
    ppermute x3, waiting for transfers between devices, local(): lax.ppermute(piece, 'z', [(i, i ^ low) for i in range(nz)])  9.92 us
    ppermute x7, waiting for transfers between devices, send_next(): lax.ppermute(mine[i, k, s], ('x', 'core', 'fsdp'), pairs)  9.61 us
    pallas_call x2, Pallas kernels, inner_blocks(): pl.pallas_call(functools.partial(inner_kernel, pieces, share, inner_rate...  7.74 us
    ppermute x6, starting transfers between devices, local(): lax.ppermute(part, ('core', 'fsdp'), pair_ring(k, s))  7.51 us
    pallas_call x2, Pallas kernels, pack(): pl.pallas_call(functools.partial(pack_kernel, plan), out_shape=shapes, in...  7.22 us
    ppermute x2, starting transfers between devices, home(): lax.ppermute(part, 'fsdp', ring(fsdp, -s - 1))  6.85 us
  transfers between devices with their start and end apart: 35, of which 21 were waited for; matrix products, arithmetic and copies ran while one was open for 2% of the time, Pallas kernels for 15%

profile of v11, /device:TPU:0, one launch (start us, length us, event | category | flops | bytes accessed | tf_op | source)
XLA Modules:
  0.0 147.5 jit_solution(1858471872968780249)
XLA Ops:
  1.2 2.9 %collective-permute-start = (bf16[128,1024]{1,0:T(8,128)(2,1)}, bf16[128,1024]{1,0:T(8,128)(2,1)S(1)}, u32[]{:S(2)}, u32[]{:S(2)}) collective-permute-start(bf16[128,1024]{1,0:T(8,128)(2,1)} %refs_4_.5), channel_id=1, source_target_pairs={{0,1},{1,0},{2,3},{3,2},{4,5},{5,4},{6,7},{7,6},{8,9},{9,8},{10,11... | collective-permute-start | bytes 786440 | tf_op jit(solution)/shard_map/ppermute | solution.py:344
  4.3 3.2 %shard_map.94 = (bf16[128,1024]{1,0:T(8,128)(2,1)S(1)}, bf16[128,1024]{1,0:T(8,128)(2,1)}, bf16[128,1024]{1,0:T(8,128)(2,1)}, bf16[128,1024]{1,0:T(8,128)(2,1)S(...) custom-call(s32[32]{0:T(128)S(1)} %stack.216.starts, ...), custom_call_target="tpu_custom_call" | custom-call | bytes 16777216 | tf_op jit(solution)/shard_map/pallas_call | solution.py:72
  7.7 2.7 %collective-permute-start.3 = (bf16[128,1024]{1,0:T(8,128)(2,1)S(1)}, bf16[128,1024]{1,0:T(8,128)(2,1)S(1)}, u32[]{:S(2)}, u32[]{:S(2)}) collective-permute-start(bf16[128,1024]{1,0:T(8,128)(2,1)S(1)} %get-tuple-element.103), channel_id=1, source_target_pairs={{0,3},{1,2},{2,1},{3,0},{4,7},{5,6},{6,5},{7,4},{8,11},{9,10},{10,... | collective-permute-start | bytes 786440 | tf_op jit(solution)/shard_map/ppermute | solution.py:351
  11.5 4.0 %shard_map.93 = (bf16[128,1024]{1,0:T(8,128)(2,1)}, bf16[128,1024]{1,0:T(8,128)(2,1)}, bf16[128,1024]{1,0:T(8,128)(2,1)}, bf16[128,1024]{1,0:T(8,128)(2,1)}, bf1...) custom-call(s32[32]{0:T(128)S(1)} %stack.215.starts, ...), custom_call_target="tpu_custom_call" | custom-call | bytes 16777216 | tf_op jit(solution)/shard_map/pallas_call | solution.py:72
  17.0 2.2 %collective-permute-start.10 = (bf16[128,1024]{1,0:T(8,128)(2,1)S(1)}, bf16[128,1024]{1,0:T(8,128)(2,1)S(1)}, u32[]{:S(2)}, u32[]{:S(2)}) collective-permute-start(bf16[128,1024]{1,0:T(8,128)(2,1)S(1)} %get-tuple-element.118), channel_id=1, source_target_pairs={{0,1},{1,0},{2,3},{3,2},{4,5},{5,4},{6,7},{7,6},{8,9},{9,8},{10,11... | collective-permute-start | bytes 786440 | tf_op jit(solution)/shard_map/ppermute | solution.py:351
  19.2 3.1 %collective-permute-done.3.refs_3_ = bf16[128,1024]{1,0:T(8,128)(2,1)S(1)} collective-permute-done((bf16[128,1024]{1,0:T(8,128)(2,1)S(1)}, bf16[128,1024]{1,0:T(8,128)(2,1)S(1)}, u32[]{:S(2)}, u32[]{:S(2)}) %collective-permute-start.3) | collective-permute-done | bytes 262176 | tf_op jit(solution)/shard_map/ppermute | solution.py:351
  22.3 1.9 %collective-permute-start.11 = (bf16[128,1024]{1,0:T(8,128)(2,1)S(1)}, bf16[128,1024]{1,0:T(8,128)(2,1)S(1)}, u32[]{:S(2)}, u32[]{:S(2)}) collective-permute-start(bf16[128,1024]{1,0:T(8,128)(2,1)S(1)} %get-tuple-element.119), channel_id=1, source_target_pairs={{0,3},{1,2},{2,1},{3,0},{4,7},{5,6},{6,5},{7,4},{8,11},{9,10},{10,... | collective-permute-start | bytes 786440 | tf_op jit(solution)/shard_map/ppermute | solution.py:351
  24.2 4.0 %shard_map.95 = (bf16[512,512]{1,0:T(8,128)(2,1)S(1)}, f32[512,512]{1,0:T(8,128)S(1)}, bf16[512,512]{1,0:T(8,128)(2,1)S(1)}, f32[512,512]{1,0:T(8,128)S(1)}) custom-call(s32[4]{0:T(128)S(1)} %pad_add_fusion.1.place, bf16[128,1024]{1,0:T(8,128)(2,1)S(1)} %get-tuple-element.100.refs_0_, bf16[128,1024]{1,0:T(8,128)(2,1)S(1)} %collective-permute-done.1.refs_1_, ...), custom_call_target="tpu_custom_call" | custom-call | flops 134217728 | bytes 262144 | tf_op jit(solution)/shard_map/pallas_call | solution.py:135
  31.4 2.4 %convolution_convert_fusion.refs_0_ = bf16[256,4096]{1,0:T(8,128)(2,1)S(1)} fusion(bf16[128,1024]{1,0:T(8,128)(2,1)S(1)} %collective-permute-done.refs_6_, bf16[128,1024]{1,0:T(8,128)(2,1)S(1)} %copy-done, bf16[1,4096,1024]{2,1,0:T(8,128)(2,1)S(1)} %bitcast.49), kind=kOutput, calls=%fused_computation | convolution fusion | flops 2149580800 | bytes 11010048 | tf_op jit(solution)/shard_map/dot_general | solution.py:392
  33.9 7.2 %collective-permute-done.7.from_x = bf16[512,512]{1,0:T(8,128)(2,1)S(1)} collective-permute-done((bf16[512,512]{1,0:T(8,128)(2,1)S(1)}, bf16[512,512]{1,0:T(8,128)(2,1)S(1)}, u32[]{:S(2)}, u32[]{:S(2)}) %collective-permute-start.7) | collective-permute-done | bytes 524320 | tf_op jit(solution)/shard_map/ppermute | solution.py:399
  44.7 3.7 %shard_map.97 = (bf16[512,768]{1,0:T(8,128)(2,1)S(1)}, f32[512,768]{1,0:T(8,128)S(1)}, bf16[512,256]{1,0:T(8,128)(2,1)S(1)}, f32[512,256]{1,0:T(8,128)S(1)}) custom-call(s32[4]{0:T(128)S(1)} %pad_add_fusion.place, bf16[128,1024]{1,0:T(8,128)(2,1)S(1)} %get-tuple-element.116.refs_0_, bf16[128,1024]{1,0:T(8,128)(2,1)S(1)} %collective-permute-done.9.refs_1_, ...), custom_call_target="tpu_custom_call" | custom-call | flops 134217728 | bytes 262144 | tf_op jit(solution)/shard_map/pallas_call | solution.py:135
  49.0 2.3 %collective-permute-done.13.refs_3_ = bf16[256,512]{1,0:T(8,128)(2,1)S(1)} collective-permute-done((bf16[256,512]{1,0:T(8,128)(2,1)S(1)}, bf16[256,512]{1,0:T(8,128)(2,1)S(1)}, u32[]{:S(2)}, u32[]{:S(2)}) %collective-permute-start.13) | collective-permute-done | bytes 262176 | tf_op jit(solution)/shard_map/ppermute | solution.py:368
  52.6 2.7 %collective-permute-start.16 = (bf16[256,1024]{1,0:T(8,128)(2,1)S(1)}, bf16[256,1024]{1,0:T(8,128)(2,1)S(1)}, u32[]{:S(2)}, u32[]{:S(2)}) collective-permute-start(bf16[256,1024]{1,0:T(8,128)(2,1)S(1)} %shard_map.99), channel_id=1, source_target_pairs={{0,16},{8,24},{16,0},{24,8},{1,17},{9,25},{17,1},{25,9},{2,18},{10... | collective-permute-start | bytes 1572872 | tf_op jit(solution)/shard_map/ppermute | solution.py:389
  56.8 4.6 %collective-permute-done.15.from_z = bf16[512,256]{1,0:T(8,128)(2,1)S(1)} collective-permute-done((bf16[512,256]{1,0:T(8,128)(2,1)S(1)}, bf16[512,256]{1,0:T(8,128)(2,1)S(1)}, u32[]{:S(2)}, u32[]{:S(2)}) %collective-permute-start.15) | collective-permute-done | bytes 262176 | tf_op jit(solution)/shard_map/ppermute | solution.py:399
  61.4 7.2 %collective-permute-done.14.from_x = bf16[512,768]{1,0:T(8,128)(2,1)S(1)} collective-permute-done((bf16[512,768]{1,0:T(8,128)(2,1)S(1)}, bf16[512,768]{1,0:T(8,128)(2,1)S(1)}, u32[]{:S(2)}, u32[]{:S(2)}) %collective-permute-start.14) | collective-permute-done | bytes 786464 | tf_op jit(solution)/shard_map/ppermute | solution.py:399
  69.5 4.3 %collective-permute-done.16.refs_0_ = bf16[256,1024]{1,0:T(8,128)(2,1)S(1)} collective-permute-done((bf16[256,1024]{1,0:T(8,128)(2,1)S(1)}, bf16[256,1024]{1,0:T(8,128)(2,1)S(1)}, u32[]{:S(2)}, u32[]{:S(2)}) %collective-permute-start.16) | collective-permute-done | bytes 524320 | tf_op jit(solution)/shard_map/ppermute | solution.py:389
  74.0 5.2 %collective-permute-done.17.refs_1_ = bf16[256,768]{1,0:T(8,128)(2,1)S(1)} collective-permute-done((bf16[256,768]{1,0:T(8,128)(2,1)S(1)}, bf16[256,768]{1,0:T(8,128)(2,1)S(1)}, u32[]{:S(2)}, u32[]{:S(2)}) %collective-permute-start.17) | collective-permute-done | bytes 393248 | tf_op jit(solution)/shard_map/ppermute | solution.py:368
  79.6 6.2 %collective-permute-start.27 = (bf16[256,1024]{1,0:T(8,128)(2,1)S(1)}, bf16[256,1024]{1,0:T(8,128)(2,1)S(1)}, u32[]{:S(2)}, u32[]{:S(2)}) collective-permute-start(bf16[256,1024]{1,0:T(8,128)(2,1)S(1)} %shard_map.101.refs_8_), channel_id=1, source_target_pairs={{0,16},{8,24},{16,0},{24,8},{1,17},{9,25},{17,1},{25,9},{2,18},{10... | collective-permute-start | bytes 1572872 | tf_op jit(solution)/shard_map/ppermute | solution.py:444
  85.8 5.0 %collective-permute-start.19 = (bf16[128,1024]{1,0:T(8,128)(2,1)S(1)}, bf16[128,1024]{1,0:T(8,128)(2,1)S(1)}, u32[]{:S(2)}, u32[]{:S(2)}) collective-permute-start(bf16[128,1024]{1,0:T(8,128)(2,1)S(1)} %copy-done.10), channel_id=1, source_target_pairs={{0,1},{1,0},{2,3},{3,2},{4,5},{5,4},{6,7},{7,6},{8,9},{9,8},{10,11... | collective-permute-start | bytes 786440 | tf_op jit(solution)/shard_map/ppermute | solution.py:340
  91.7 1.9 %shard_map.103 = bf16[128,8192]{1,0:T(8,128)(2,1)} custom-call(s32[2]{0:T(128)S(1)} %pad_add_fusion.2.starts, bf16[256,4096]{1,0:T(8,128)(2,1)S(1)} %convolution_convert_fusion.refs_0_, bf16[128,4096]{1,0:T(8,128)(2,1)S(1)} %collective-permute-done.28.refs_1_), custom_call_target="tpu_custom_call" | custom-call | bytes 4194304 | tf_op jit(solution)/shard_map/pallas_call | solution.py:298
  94.4 7.0 %collective-permute-done.26.refs_9_ = bf16[256,1024]{1,0:T(8,128)(2,1)S(1)} collective-permute-done((bf16[256,1024]{1,0:T(8,128)(2,1)S(1)}, bf16[256,1024]{1,0:T(8,128)(2,1)S(1)}, u32[]{:S(2)}, u32[]{:S(2)}) %collective-permute-start.26) | collective-permute-done | bytes 524320 | tf_op jit(solution)/shard_map/ppermute | solution.py:444
  101.4 1.9 %collective-permute-start.22 = (bf16[128,1024]{1,0:T(8,128)(2,1)S(1)}, bf16[128,1024]{1,0:T(8,128)(2,1)S(1)}, u32[]{:S(2)}, u32[]{:S(2)}) collective-permute-start(bf16[128,1024]{1,0:T(8,128)(2,1)S(1)} %copy-done.7), channel_id=1, source_target_pairs={{0,3},{1,2},{2,1},{3,0},{4,7},{5,6},{6,5},{7,4},{8,11},{9,10},{10,... | collective-permute-start | bytes 786440 | tf_op jit(solution)/shard_map/ppermute | solution.py:340
  103.4 3.6 %collective-permute-start.23 = (bf16[128,1024]{1,0:T(8,128)(2,1)S(1)}, bf16[128,1024]{1,0:T(8,128)(2,1)S(1)}, u32[]{:S(2)}, u32[]{:S(2)}) collective-permute-start(bf16[128,1024]{1,0:T(8,128)(2,1)S(1)} %copy-done.6), channel_id=1, source_target_pairs={{0,6},{1,7},{2,4},{3,5},{4,2},{5,3},{6,0},{7,1},{8,14},{9,15},{10,... | collective-permute-start | bytes 786440 | tf_op jit(solution)/shard_map/ppermute | solution.py:340
  110.0 3.7 %collective-permute-done.23.refs_5_.refs_2_ = bf16[128,1024]{1,0:T(8,128)(2,1)S(1)} collective-permute-done((bf16[128,1024]{1,0:T(8,128)(2,1)S(1)}, bf16[128,1024]{1,0:T(8,128)(2,1)S(1)}, u32[]{:S(2)}, u32[]{:S(2)}) %collective-permute-start.23) | collective-permute-done | bytes 262176 | tf_op jit(solution)/shard_map/ppermute | solution.py:340
  113.6 5.9 %collective-permute-done.24.refs_6_.refs_3_ = bf16[128,1024]{1,0:T(8,128)(2,1)S(1)} collective-permute-done((bf16[128,1024]{1,0:T(8,128)(2,1)S(1)}, bf16[128,1024]{1,0:T(8,128)(2,1)S(1)}, u32[]{:S(2)}, u32[]{:S(2)}) %collective-permute-start.24) | collective-permute-done | bytes 262176 | tf_op jit(solution)/shard_map/ppermute | solution.py:340
  119.6 1.8 %shard_map.102 = (f32[512,1024]{1,0:T(8,128)S(1)}, f32[512,1024]{1,0:T(8,128)S(1)}) custom-call(bf16[128,1024]{1,0:T(8,128)(2,1)S(1)} %copy-done.3, bf16[128,1024]{1,0:T(8,128)(2,1)S(1)} %collective-permute-done.19.refs_1_, bf16[128,1024]{1,0:T(8,128)(2,1)S(1)} %collective-permute-done.20.refs_2_, bf16[128,1024]{1,0:T(8,128)(2,1)S(1)} %collective-permute-done.21.refs_3_, ...), custom_call_target="tpu_custom_call" | custom-call | flops 17179869184 | bytes 524288 | tf_op jit(solution)/shard_map/pallas_call | solution.py:224
  121.4 2.9 %collective-permute-done.29.refs_4_ = bf16[256,1024]{1,0:T(8,128)(2,1)S(1)} collective-permute-done((bf16[256,1024]{1,0:T(8,128)(2,1)S(1)}, bf16[256,1024]{1,0:T(8,128)(2,1)S(1)}, u32[]{:S(2)}, u32[]{:S(2)}) %collective-permute-start.29) | collective-permute-done | bytes 524320 | tf_op jit(solution)/shard_map/ppermute | solution.py:444
  125.3 2.2 %collective-permute-done.30.came = bf16[512,1024]{1,0:T(8,128)(2,1)S(1)} collective-permute-done((bf16[512,1024]{1,0:T(8,128)(2,1)S(1)}, bf16[512,1024]{1,0:T(8,128)(2,1)S(1)}, u32[]{:S(2)}, u32[]{:S(2)}) %collective-permute-start.30) | collective-permute-done | bytes 1048608 | tf_op jit(solution)/shard_map/ppermute | solution.py:456
  128.3 5.1 %collective-permute-start.32 = (bf16[256,512]{1,0:T(8,128)(2,1)S(1)}, bf16[256,512]{1,0:T(8,128)(2,1)S(1)}, u32[]{:S(2)}, u32[]{:S(2)}) collective-permute-start(bf16[256,512]{1,0:T(8,128)(2,1)S(1)} %get-tuple-element.169), channel_id=1, source_target_pairs={{0,1},{1,0},{2,3},{3,2},{4,5},{5,4},{6,7},{7,6},{8,9},{9,8},{10,11... | collective-permute-start | bytes 786440 | tf_op jit(solution)/shard_map/ppermute | solution.py:467
  133.4 2.7 %collective-permute-done.31.refs_2_ = bf16[256,512]{1,0:T(8,128)(2,1)S(1)} collective-permute-done((bf16[256,512]{1,0:T(8,128)(2,1)S(1)}, bf16[256,512]{1,0:T(8,128)(2,1)S(1)}, u32[]{:S(2)}, u32[]{:S(2)}) %collective-permute-start.31) | collective-permute-done | bytes 262176 | tf_op jit(solution)/shard_map/ppermute | solution.py:466
  136.1 3.9 %collective-permute-done.32.refs_3_ = bf16[256,512]{1,0:T(8,128)(2,1)S(1)} collective-permute-done((bf16[256,512]{1,0:T(8,128)(2,1)S(1)}, bf16[256,512]{1,0:T(8,128)(2,1)S(1)}, u32[]{:S(2)}, u32[]{:S(2)}) %collective-permute-start.32) | collective-permute-done | bytes 262176 | tf_op jit(solution)/shard_map/ppermute | solution.py:467
  141.8 1.7 %collective-permute-start.34 = (bf16[128,512]{1,0:T(8,128)(2,1)S(1)}, bf16[128,512]{1,0:T(8,128)(2,1)S(1)}, u32[]{:S(2)}, u32[]{:S(2)}) collective-permute-start(bf16[128,512]{1,0:T(8,128)(2,1)S(1)} %get-tuple-element.173), channel_id=1, source_target_pairs={{0,1},{1,0},{2,3},{3,2},{4,5},{5,4},{6,7},{7,6},{8,9},{9,8},{10,11... | collective-permute-start | bytes 393224 | tf_op jit(solution)/shard_map/ppermute | solution.py:467
  (89 shorter events, 27.3 us)
Async XLA Ops:
  0.6 23.6 %collective-permute-start.6 = (bf16[4096,1024]{1,0:T(8,128)(2,1)}, bf16[4096,1024]{1,0:T(8,128)(2,1)}, u32[]{:S(2)}, u32[]{:S(2)}) collective-permute-start(bf16[4096,1024]{1,0:T(8,128)(2,1)} %bitcast.45), channel_id=1, source_target_pairs={{0,2},{2,0},{1,3},{3,1},{4,6},{6,4},{5,7},{7,5},{8,10},{10,8},{9,1... | collective-permute-start | bytes 25165832 | tf_op jit(solution)/shard_map/ppermute | solution.py:353
  1.1 6.5 %collective-permute-start.4 = (bf16[128,1024]{1,0:T(8,128)(2,1)}, bf16[128,1024]{1,0:T(8,128)(2,1)S(1)}, u32[]{:S(2)}, u32[]{:S(2)}) collective-permute-start(bf16[128,1024]{1,0:T(8,128)(2,1)} %refs_4_.5), channel_id=1, source_target_pairs={{0,2},{2,0},{1,3},{3,1},{4,6},{6,4},{5,7},{7,5},{8,10},{10,8},{9,1... | collective-permute-start | bytes 786440 | tf_op jit(solution)/shard_map/ppermute | solution.py:354
  1.2 9.9 %collective-permute-start = (bf16[128,1024]{1,0:T(8,128)(2,1)}, bf16[128,1024]{1,0:T(8,128)(2,1)S(1)}, u32[]{:S(2)}, u32[]{:S(2)}) collective-permute-start(bf16[128,1024]{1,0:T(8,128)(2,1)} %refs_4_.5), channel_id=1, source_target_pairs={{0,1},{1,0},{2,3},{3,2},{4,5},{5,4},{6,7},{7,6},{8,9},{9,8},{10,11... | collective-permute-start | bytes 786440 | tf_op jit(solution)/shard_map/ppermute | solution.py:344
  7.5 7.9 %collective-permute-start.1 = (bf16[128,1024]{1,0:T(8,128)(2,1)}, bf16[128,1024]{1,0:T(8,128)(2,1)S(1)}, u32[]{:S(2)}, u32[]{:S(2)}) collective-permute-start(bf16[128,1024]{1,0:T(8,128)(2,1)} %get-tuple-element.101), channel_id=1, source_target_pairs={{0,2},{1,3},{2,0},{3,1},{4,6},{5,7},{6,4},{7,5},{8,10},{9,11},{10,... | collective-permute-start | bytes 786440 | tf_op jit(solution)/shard_map/ppermute | solution.py:351
  7.6 9.4 %collective-permute-start.2 = (bf16[128,1024]{1,0:T(8,128)(2,1)}, bf16[128,1024]{1,0:T(8,128)(2,1)S(1)}, u32[]{:S(2)}, u32[]{:S(2)}) collective-permute-start(bf16[128,1024]{1,0:T(8,128)(2,1)} %get-tuple-element.102), channel_id=1, source_target_pairs={{0,1},{1,0},{2,3},{3,2},{4,5},{5,4},{6,7},{7,6},{8,9},{9,8},{10,11... | collective-permute-start | bytes 786440 | tf_op jit(solution)/shard_map/ppermute | solution.py:351
  7.7 14.6 %collective-permute-start.3 = (bf16[128,1024]{1,0:T(8,128)(2,1)S(1)}, bf16[128,1024]{1,0:T(8,128)(2,1)S(1)}, u32[]{:S(2)}, u32[]{:S(2)}) collective-permute-start(bf16[128,1024]{1,0:T(8,128)(2,1)S(1)} %get-tuple-element.103), channel_id=1, source_target_pairs={{0,3},{1,2},{2,1},{3,0},{4,7},{5,6},{6,5},{7,4},{8,11},{9,10},{10,... | collective-permute-start | bytes 786440 | tf_op jit(solution)/shard_map/ppermute | solution.py:351
  11.2 13.0 %collective-permute-start.5 = (bf16[128,1024]{1,0:T(8,128)(2,1)S(1)}, bf16[128,1024]{1,0:T(8,128)(2,1)S(1)}, u32[]{:S(2)}, u32[]{:S(2)}) collective-permute-start(bf16[128,1024]{1,0:T(8,128)(2,1)S(1)} %collective-permute-done.refs_6_), channel_id=1, source_target_pairs={{0,2},{2,0},{1,3},{3,1},{4,6},{6,4},{5,7},{7,5},{8,10},{10,8},{9,1... | collective-permute-start | bytes 786440 | tf_op jit(solution)/shard_map/ppermute | solution.py:356
  15.5 29.2 %collective-permute-start.9 = (bf16[128,1024]{1,0:T(8,128)(2,1)S(1)}, bf16[128,1024]{1,0:T(8,128)(2,1)S(1)}, u32[]{:S(2)}, u32[]{:S(2)}) collective-permute-start(bf16[128,1024]{1,0:T(8,128)(2,1)S(1)} %get-tuple-element.117), channel_id=1, source_target_pairs={{0,2},{1,3},{2,0},{3,1},{4,6},{5,7},{6,4},{7,5},{8,10},{9,11},{10,... | collective-permute-start | bytes 786440 | tf_op jit(solution)/shard_map/ppermute | solution.py:351
  17.0 27.7 %collective-permute-start.10 = (bf16[128,1024]{1,0:T(8,128)(2,1)S(1)}, bf16[128,1024]{1,0:T(8,128)(2,1)S(1)}, u32[]{:S(2)}, u32[]{:S(2)}) collective-permute-start(bf16[128,1024]{1,0:T(8,128)(2,1)S(1)} %get-tuple-element.118), channel_id=1, source_target_pairs={{0,1},{1,0},{2,3},{3,2},{4,5},{5,4},{6,7},{7,6},{8,9},{9,8},{10,11... | collective-permute-start | bytes 786440 | tf_op jit(solution)/shard_map/ppermute | solution.py:351
  22.3 22.4 %collective-permute-start.11 = (bf16[128,1024]{1,0:T(8,128)(2,1)S(1)}, bf16[128,1024]{1,0:T(8,128)(2,1)S(1)}, u32[]{:S(2)}, u32[]{:S(2)}) collective-permute-start(bf16[128,1024]{1,0:T(8,128)(2,1)S(1)} %get-tuple-element.119), channel_id=1, source_target_pairs={{0,3},{1,2},{2,1},{3,0},{4,7},{5,6},{6,5},{7,4},{8,11},{9,10},{10,... | collective-permute-start | bytes 786440 | tf_op jit(solution)/shard_map/ppermute | solution.py:351
  28.3 12.8 %collective-permute-start.7 = (bf16[512,512]{1,0:T(8,128)(2,1)S(1)}, bf16[512,512]{1,0:T(8,128)(2,1)S(1)}, u32[]{:S(2)}, u32[]{:S(2)}) collective-permute-start(bf16[512,512]{1,0:T(8,128)(2,1)S(1)} %get-tuple-element.110), channel_id=1, source_target_pairs={{0,4},{4,0},{1,5},{5,1},{2,6},{6,2},{3,7},{7,3},{8,12},{12,8},{9,1... | collective-permute-start | bytes 1572872 | tf_op jit(solution)/shard_map/ppermute | solution.py:399
  29.8 12.5 %collective-permute-start.8 = (bf16[512,512]{1,0:T(8,128)(2,1)S(1)}, bf16[512,512]{1,0:T(8,128)(2,1)S(1)}, u32[]{:S(2)}, u32[]{:S(2)}) collective-permute-start(bf16[512,512]{1,0:T(8,128)(2,1)S(1)} %get-tuple-element.112), channel_id=1, source_target_pairs={{0,8},{8,0},{16,24},{24,16},{1,9},{9,1},{17,25},{25,17},{2,10},{10... | collective-permute-start | bytes 1572872 | tf_op jit(solution)/shard_map/ppermute | solution.py:399
  42.5 6.4 %collective-permute-start.12 = (bf16[256,512]{1,0:T(8,128)(2,1)S(1)}, bf16[256,512]{1,0:T(8,128)(2,1)S(1)}, u32[]{:S(2)}, u32[]{:S(2)}) collective-permute-start(bf16[256,512]{1,0:T(8,128)(2,1)S(1)} %get-tuple-element.123), channel_id=1, source_target_pairs={{0,8},{8,0},{16,24},{24,16},{1,9},{9,1},{17,25},{25,17},{2,10},{10... | collective-permute-start | bytes 786440 | tf_op jit(solution)/shard_map/ppermute | solution.py:368
  44.2 7.1 %collective-permute-start.13 = (bf16[256,512]{1,0:T(8,128)(2,1)S(1)}, bf16[256,512]{1,0:T(8,128)(2,1)S(1)}, u32[]{:S(2)}, u32[]{:S(2)}) collective-permute-start(bf16[256,512]{1,0:T(8,128)(2,1)S(1)} %get-tuple-element.124), channel_id=1, source_target_pairs={{0,4},{4,0},{1,5},{5,1},{2,6},{6,2},{3,7},{7,3},{8,12},{12,8},{9,1... | collective-permute-start | bytes 786440 | tf_op jit(solution)/shard_map/ppermute | solution.py:368
  51.3 17.3 %collective-permute-start.14 = (bf16[512,768]{1,0:T(8,128)(2,1)S(1)}, bf16[512,768]{1,0:T(8,128)(2,1)S(1)}, u32[]{:S(2)}, u32[]{:S(2)}) collective-permute-start(bf16[512,768]{1,0:T(8,128)(2,1)S(1)} %get-tuple-element.125), channel_id=1, source_target_pairs={{0,4},{4,0},{1,5},{5,1},{2,6},{6,2},{3,7},{7,3},{8,12},{12,8},{9,1... | collective-permute-start | bytes 2359304 | tf_op jit(solution)/shard_map/ppermute | solution.py:399
  51.8 9.6 %collective-permute-start.15 = (bf16[512,256]{1,0:T(8,128)(2,1)S(1)}, bf16[512,256]{1,0:T(8,128)(2,1)S(1)}, u32[]{:S(2)}, u32[]{:S(2)}) collective-permute-start(bf16[512,256]{1,0:T(8,128)(2,1)S(1)} %get-tuple-element.127), channel_id=1, source_target_pairs={{0,8},{8,0},{16,24},{24,16},{1,9},{9,1},{17,25},{25,17},{2,10},{10... | collective-permute-start | bytes 786440 | tf_op jit(solution)/shard_map/ppermute | solution.py:399
  52.6 21.1 %collective-permute-start.16 = (bf16[256,1024]{1,0:T(8,128)(2,1)S(1)}, bf16[256,1024]{1,0:T(8,128)(2,1)S(1)}, u32[]{:S(2)}, u32[]{:S(2)}) collective-permute-start(bf16[256,1024]{1,0:T(8,128)(2,1)S(1)} %shard_map.99), channel_id=1, source_target_pairs={{0,16},{8,24},{16,0},{24,8},{1,17},{9,25},{17,1},{25,9},{2,18},{10... | collective-permute-start | bytes 1572872 | tf_op jit(solution)/shard_map/ppermute | solution.py:389
  55.3 36.4 %collective-permute-start.28 = (bf16[128,4096]{1,0:T(8,128)(2,1)S(1)}, bf16[128,4096]{1,0:T(8,128)(2,1)S(1)}, u32[]{:S(2)}, u32[]{:S(2)}) collective-permute-start(bf16[128,4096]{1,0:T(8,128)(2,1)S(1)} %slice.4), channel_id=1, source_target_pairs={{0,1},{1,0},{2,3},{3,2},{4,5},{5,4},{6,7},{7,6},{8,9},{9,8},{10,11... | collective-permute-start | bytes 3145736 | tf_op jit(solution)/shard_map/ppermute | solution.py:398
  68.8 10.3 %collective-permute-start.17 = (bf16[256,768]{1,0:T(8,128)(2,1)S(1)}, bf16[256,768]{1,0:T(8,128)(2,1)S(1)}, u32[]{:S(2)}, u32[]{:S(2)}) collective-permute-start(bf16[256,768]{1,0:T(8,128)(2,1)S(1)} %get-tuple-element.135), channel_id=1, source_target_pairs={{0,8},{8,0},{16,24},{24,16},{1,9},{9,1},{17,25},{25,17},{2,10},{10... | collective-permute-start | bytes 1179656 | tf_op jit(solution)/shard_map/ppermute | solution.py:368
  79.5 21.9 %collective-permute-start.26 = (bf16[256,1024]{1,0:T(8,128)(2,1)S(1)}, bf16[256,1024]{1,0:T(8,128)(2,1)S(1)}, u32[]{:S(2)}, u32[]{:S(2)}) collective-permute-start(bf16[256,1024]{1,0:T(8,128)(2,1)S(1)} %shard_map.101.refs_8_), channel_id=1, source_target_pairs={{0,8},{8,0},{16,24},{24,16},{1,9},{9,1},{17,25},{25,17},{2,10},{10... | collective-permute-start | bytes 1572872 | tf_op jit(solution)/shard_map/ppermute | solution.py:444
  79.6 28.7 %collective-permute-start.27 = (bf16[256,1024]{1,0:T(8,128)(2,1)S(1)}, bf16[256,1024]{1,0:T(8,128)(2,1)S(1)}, u32[]{:S(2)}, u32[]{:S(2)}) collective-permute-start(bf16[256,1024]{1,0:T(8,128)(2,1)S(1)} %shard_map.101.refs_8_), channel_id=1, source_target_pairs={{0,16},{8,24},{16,0},{24,8},{1,17},{9,25},{17,1},{25,9},{2,18},{10... | collective-permute-start | bytes 1572872 | tf_op jit(solution)/shard_map/ppermute | solution.py:444
  85.8 17.6 %collective-permute-start.19 = (bf16[128,1024]{1,0:T(8,128)(2,1)S(1)}, bf16[128,1024]{1,0:T(8,128)(2,1)S(1)}, u32[]{:S(2)}, u32[]{:S(2)}) collective-permute-start(bf16[128,1024]{1,0:T(8,128)(2,1)S(1)} %copy-done.10), channel_id=1, source_target_pairs={{0,1},{1,0},{2,3},{3,2},{4,5},{5,4},{6,7},{7,6},{8,9},{9,8},{10,11... | collective-permute-start | bytes 786440 | tf_op jit(solution)/shard_map/ppermute | solution.py:340
  90.8 16.2 %collective-permute-start.20 = (bf16[128,1024]{1,0:T(8,128)(2,1)S(1)}, bf16[128,1024]{1,0:T(8,128)(2,1)S(1)}, u32[]{:S(2)}, u32[]{:S(2)}) collective-permute-start(bf16[128,1024]{1,0:T(8,128)(2,1)S(1)} %copy-done.9), channel_id=1, source_target_pairs={{0,4},{1,5},{2,6},{3,7},{4,0},{5,1},{6,2},{7,3},{8,12},{9,13},{10,... | collective-permute-start | bytes 786440 | tf_op jit(solution)/shard_map/ppermute | solution.py:340
  93.6 16.4 %collective-permute-start.21 = (bf16[128,1024]{1,0:T(8,128)(2,1)S(1)}, bf16[128,1024]{1,0:T(8,128)(2,1)S(1)}, u32[]{:S(2)}, u32[]{:S(2)}) collective-permute-start(bf16[128,1024]{1,0:T(8,128)(2,1)S(1)} %copy-done.8), channel_id=1, source_target_pairs={{0,5},{1,4},{2,7},{3,6},{4,1},{5,0},{6,3},{7,2},{8,13},{9,12},{10,... | collective-permute-start | bytes 786440 | tf_op jit(solution)/shard_map/ppermute | solution.py:340
  101.4 8.6 %collective-permute-start.22 = (bf16[128,1024]{1,0:T(8,128)(2,1)S(1)}, bf16[128,1024]{1,0:T(8,128)(2,1)S(1)}, u32[]{:S(2)}, u32[]{:S(2)}) collective-permute-start(bf16[128,1024]{1,0:T(8,128)(2,1)S(1)} %copy-done.7), channel_id=1, source_target_pairs={{0,3},{1,2},{2,1},{3,0},{4,7},{5,6},{6,5},{7,4},{8,11},{9,10},{10,... | collective-permute-start | bytes 786440 | tf_op jit(solution)/shard_map/ppermute | solution.py:340
  103.4 10.3 %collective-permute-start.23 = (bf16[128,1024]{1,0:T(8,128)(2,1)S(1)}, bf16[128,1024]{1,0:T(8,128)(2,1)S(1)}, u32[]{:S(2)}, u32[]{:S(2)}) collective-permute-start(bf16[128,1024]{1,0:T(8,128)(2,1)S(1)} %copy-done.6), channel_id=1, source_target_pairs={{0,6},{1,7},{2,4},{3,5},{4,2},{5,3},{6,0},{7,1},{8,14},{9,15},{10,... | collective-permute-start | bytes 786440 | tf_op jit(solution)/shard_map/ppermute | solution.py:340
  107.0 12.6 %collective-permute-start.24 = (bf16[128,1024]{1,0:T(8,128)(2,1)S(1)}, bf16[128,1024]{1,0:T(8,128)(2,1)S(1)}, u32[]{:S(2)}, u32[]{:S(2)}) collective-permute-start(bf16[128,1024]{1,0:T(8,128)(2,1)S(1)} %copy-done.5), channel_id=1, source_target_pairs={{0,7},{1,6},{2,5},{3,4},{4,3},{5,2},{6,1},{7,0},{8,15},{9,14},{10,... | collective-permute-start | bytes 786440 | tf_op jit(solution)/shard_map/ppermute | solution.py:340
  108.3 11.3 %collective-permute-start.25 = (bf16[128,1024]{1,0:T(8,128)(2,1)S(1)}, bf16[128,1024]{1,0:T(8,128)(2,1)S(1)}, u32[]{:S(2)}, u32[]{:S(2)}) collective-permute-start(bf16[128,1024]{1,0:T(8,128)(2,1)S(1)} %copy-done.4), channel_id=1, source_target_pairs={{0,2},{1,3},{2,0},{3,1},{4,6},{5,7},{6,4},{7,5},{8,10},{9,11},{10,... | collective-permute-start | bytes 786440 | tf_op jit(solution)/shard_map/ppermute | solution.py:340
  110.0 14.3 %collective-permute-start.29 = (bf16[256,1024]{1,0:T(8,128)(2,1)S(1)}, bf16[256,1024]{1,0:T(8,128)(2,1)S(1)}, u32[]{:S(2)}, u32[]{:S(2)}) collective-permute-start(bf16[256,1024]{1,0:T(8,128)(2,1)S(1)} %collective-permute-done.27.refs_10_), channel_id=1, source_target_pairs={{0,8},{8,0},{16,24},{24,16},{1,9},{9,1},{17,25},{25,17},{2,10},{10... | collective-permute-start | bytes 1572872 | tf_op jit(solution)/shard_map/ppermute | solution.py:444
  127.7 8.4 %collective-permute-start.31 = (bf16[256,512]{1,0:T(8,128)(2,1)S(1)}, bf16[256,512]{1,0:T(8,128)(2,1)S(1)}, u32[]{:S(2)}, u32[]{:S(2)}) collective-permute-start(bf16[256,512]{1,0:T(8,128)(2,1)S(1)} %get-tuple-element.168), channel_id=1, source_target_pairs={{0,4},{4,0},{1,5},{5,1},{2,6},{6,2},{3,7},{7,3},{8,12},{12,8},{9,1... | collective-permute-start | bytes 786440 | tf_op jit(solution)/shard_map/ppermute | solution.py:466
  128.3 11.7 %collective-permute-start.32 = (bf16[256,512]{1,0:T(8,128)(2,1)S(1)}, bf16[256,512]{1,0:T(8,128)(2,1)S(1)}, u32[]{:S(2)}, u32[]{:S(2)}) collective-permute-start(bf16[256,512]{1,0:T(8,128)(2,1)S(1)} %get-tuple-element.169), channel_id=1, source_target_pairs={{0,1},{1,0},{2,3},{3,2},{4,5},{5,4},{6,7},{7,6},{8,9},{9,8},{10,11... | collective-permute-start | bytes 786440 | tf_op jit(solution)/shard_map/ppermute | solution.py:467
  140.1 5.1 %collective-permute-start.33 = (bf16[128,512]{1,0:T(8,128)(2,1)S(1)}, bf16[128,512]{1,0:T(8,128)(2,1)S(1)}, u32[]{:S(2)}, u32[]{:S(2)}) collective-permute-start(bf16[128,512]{1,0:T(8,128)(2,1)S(1)} %get-tuple-element.172), channel_id=1, source_target_pairs={{0,4},{4,0},{1,5},{5,1},{2,6},{6,2},{3,7},{7,3},{8,12},{12,8},{9,1... | collective-permute-start | bytes 393224 | tf_op jit(solution)/shard_map/ppermute | solution.py:466
  (16 other events, 180.7 us)

commit v12 on v9

--- a/solution.py
+++ b/solution.py
@@ -326,7 +326,7 @@
     stages = [(m + 1, m) for m in range(nz - 2, -1, -2)]
 
     far = [(i, k, s) for k in range(CORES) for i in range(PAIR) for s in range(fsdp)]
-    early = [(0, 1, 0)]
+    early = [(0, 1, 0), (1, 0, 0)]
     late = [e for e in far if e not in early]
     index = lambda i, k, s: ((i % PAIR) * CORES + k % CORES) * fsdp + s % fsdp
     every = [(i, k, s) for i in range(PAIR) for k in range(CORES) for s in range(fsdp)]

time: 146 us -> 146 us (level)
    ppermute x2, waiting for transfers between devices: 5.64 us -> 0.54 us  [finish(): lax.ppermute(to_z, 'z', across_z)]
    ppermute x2, waiting for transfers between devices: 2.46 us -> 4.65 us  [finish(): lax.ppermute(to_x, 'x', across_x)]
    ppermute x7, waiting for transfers between devices: 3.23 us -> 4.97 us  [send_next(): lax.ppermute(mine[i, k, s], ('x', 'core', 'fsdp'), pairs)]
where the time goes in v12:
time: 146 us
  waiting for transfers between devices  70 us (48%)
  starting transfers between devices  48.7 us (33%)
  Pallas kernels  23.1 us (16%)
  matrix products  2.38 us (2%)
    ppermute x3, waiting for transfers between devices, local(): lax.ppermute(piece, 'z', [(i, i ^ low) for i in range(nz)])  16.1 us
    ppermute x7, starting transfers between devices, send_next(): lax.ppermute(mine[i, k, s], ('x', 'core', 'fsdp'), pairs)  15 us
    ppermute x2, waiting for transfers between devices, local(): lax.ppermute(to_x, 'x', across_x)  13.3 us
    ppermute x2, waiting for transfers between devices, home(): from_x = lax.ppermute(to_x, 'x', ring(PAIR, 1))  10.7 us
    pallas_call x2, Pallas kernels, inner_blocks(): pl.pallas_call(functools.partial(inner_kernel, pieces, share, inner_rate...  7.74 us
    ppermute x6, starting transfers between devices, local(): lax.ppermute(part, ('core', 'fsdp'), pair_ring(k, s))  7.53 us
    pallas_call x2, Pallas kernels, pack(): pl.pallas_call(functools.partial(pack_kernel, plan), out_shape=shapes, in...  7.19 us
    ppermute x3, starting transfers between devices, local(): lax.ppermute(piece, 'z', [(i, i ^ low) for i in range(nz)])  6.5 us
  transfers between devices with their start and end apart: 35, of which 21 were waited for; matrix products, arithmetic and copies ran while one was open for 2% of the time, Pallas kernels for 15%

profile of v12, /device:TPU:0, one launch (start us, length us, event | category | flops | bytes accessed | tf_op | source)
XLA Modules:
  0.0 145.7 jit_solution(3464231673803311507)
XLA Ops:
  1.2 2.9 %collective-permute-start = (bf16[128,1024]{1,0:T(8,128)(2,1)}, bf16[128,1024]{1,0:T(8,128)(2,1)S(1)}, u32[]{:S(2)}, u32[]{:S(2)}) collective-permute-start(bf16[128,1024]{1,0:T(8,128)(2,1)} %refs_4_.4), channel_id=1, source_target_pairs={{0,1},{1,0},{2,3},{3,2},{4,5},{5,4},{6,7},{7,6},{8,9},{9,8},{10,11... | collective-permute-start | bytes 786440 | tf_op jit(solution)/shard_map/ppermute | solution.py:344
  4.3 3.2 %shard_map.94 = (bf16[128,1024]{1,0:T(8,128)(2,1)S(1)}, bf16[128,1024]{1,0:T(8,128)(2,1)}, bf16[128,1024]{1,0:T(8,128)(2,1)}, bf16[128,1024]{1,0:T(8,128)(2,1)S(...) custom-call(s32[32]{0:T(128)S(1)} %stack.216.starts, ...), custom_call_target="tpu_custom_call" | custom-call | bytes 16777216 | tf_op jit(solution)/shard_map/pallas_call | solution.py:72
  7.7 2.7 %collective-permute-start.3 = (bf16[128,1024]{1,0:T(8,128)(2,1)S(1)}, bf16[128,1024]{1,0:T(8,128)(2,1)S(1)}, u32[]{:S(2)}, u32[]{:S(2)}) collective-permute-start(bf16[128,1024]{1,0:T(8,128)(2,1)S(1)} %get-tuple-element.109), channel_id=1, source_target_pairs={{0,3},{1,2},{2,1},{3,0},{4,7},{5,6},{6,5},{7,4},{8,11},{9,10},{10,... | collective-permute-start | bytes 786440 | tf_op jit(solution)/shard_map/ppermute | solution.py:351
  11.5 4.0 %shard_map.93 = (bf16[128,1024]{1,0:T(8,128)(2,1)}, bf16[128,1024]{1,0:T(8,128)(2,1)}, bf16[128,1024]{1,0:T(8,128)(2,1)}, bf16[128,1024]{1,0:T(8,128)(2,1)}, bf1...) custom-call(s32[32]{0:T(128)S(1)} %stack.215.starts, ...), custom_call_target="tpu_custom_call" | custom-call | bytes 16777216 | tf_op jit(solution)/shard_map/pallas_call | solution.py:72
  17.0 2.2 %collective-permute-start.10 = (bf16[128,1024]{1,0:T(8,128)(2,1)S(1)}, bf16[128,1024]{1,0:T(8,128)(2,1)S(1)}, u32[]{:S(2)}, u32[]{:S(2)}) collective-permute-start(bf16[128,1024]{1,0:T(8,128)(2,1)S(1)} %get-tuple-element.124), channel_id=1, source_target_pairs={{0,1},{1,0},{2,3},{3,2},{4,5},{5,4},{6,7},{7,6},{8,9},{9,8},{10,11... | collective-permute-start | bytes 786440 | tf_op jit(solution)/shard_map/ppermute | solution.py:351
  19.2 3.1 %collective-permute-done.3.refs_3_ = bf16[128,1024]{1,0:T(8,128)(2,1)S(1)} collective-permute-done((bf16[128,1024]{1,0:T(8,128)(2,1)S(1)}, bf16[128,1024]{1,0:T(8,128)(2,1)S(1)}, u32[]{:S(2)}, u32[]{:S(2)}) %collective-permute-start.3) | collective-permute-done | bytes 262176 | tf_op jit(solution)/shard_map/ppermute | solution.py:351
  22.3 1.9 %collective-permute-start.11 = (bf16[128,1024]{1,0:T(8,128)(2,1)S(1)}, bf16[128,1024]{1,0:T(8,128)(2,1)S(1)}, u32[]{:S(2)}, u32[]{:S(2)}) collective-permute-start(bf16[128,1024]{1,0:T(8,128)(2,1)S(1)} %get-tuple-element.125), channel_id=1, source_target_pairs={{0,3},{1,2},{2,1},{3,0},{4,7},{5,6},{6,5},{7,4},{8,11},{9,10},{10,... | collective-permute-start | bytes 786440 | tf_op jit(solution)/shard_map/ppermute | solution.py:351
  24.2 4.0 %shard_map.95 = (bf16[512,512]{1,0:T(8,128)(2,1)S(1)}, f32[512,512]{1,0:T(8,128)S(1)}, bf16[512,512]{1,0:T(8,128)(2,1)S(1)}, f32[512,512]{1,0:T(8,128)S(1)}) custom-call(s32[4]{0:T(128)S(1)} %pad_add_fusion.1.place, bf16[128,1024]{1,0:T(8,128)(2,1)S(1)} %get-tuple-element.106.refs_0_, bf16[128,1024]{1,0:T(8,128)(2,1)S(1)} %collective-permute-done.1.refs_1_, ...), custom_call_target="tpu_custom_call" | custom-call | flops 134217728 | bytes 262144 | tf_op jit(solution)/shard_map/pallas_call | solution.py:135
  31.4 2.4 %convolution_convert_fusion.refs_0_ = bf16[256,4096]{1,0:T(8,128)(2,1)S(1)} fusion(bf16[128,1024]{1,0:T(8,128)(2,1)S(1)} %collective-permute-done.refs_6_, bf16[128,1024]{1,0:T(8,128)(2,1)S(1)} %copy-done, bf16[1,4096,1024]{2,1,0:T(8,128)(2,1)S(1)} %bitcast.49), kind=kOutput, calls=%fused_computation | convolution fusion | flops 2149580800 | bytes 11010048 | tf_op jit(solution)/shard_map/dot_general | solution.py:394
  33.9 7.2 %collective-permute-done.7.from_x = bf16[512,512]{1,0:T(8,128)(2,1)S(1)} collective-permute-done((bf16[512,512]{1,0:T(8,128)(2,1)S(1)}, bf16[512,512]{1,0:T(8,128)(2,1)S(1)}, u32[]{:S(2)}, u32[]{:S(2)}) %collective-permute-start.7) | collective-permute-done | bytes 524320 | tf_op jit(solution)/shard_map/ppermute | solution.py:401
  44.7 3.7 %shard_map.97 = (bf16[512,768]{1,0:T(8,128)(2,1)S(1)}, f32[512,768]{1,0:T(8,128)S(1)}, bf16[512,256]{1,0:T(8,128)(2,1)S(1)}, f32[512,256]{1,0:T(8,128)S(1)}) custom-call(s32[4]{0:T(128)S(1)} %pad_add_fusion.place, bf16[128,1024]{1,0:T(8,128)(2,1)S(1)} %get-tuple-element.122.refs_0_, bf16[128,1024]{1,0:T(8,128)(2,1)S(1)} %collective-permute-done.9.refs_1_, ...), custom_call_target="tpu_custom_call" | custom-call | flops 134217728 | bytes 262144 | tf_op jit(solution)/shard_map/pallas_call | solution.py:135
  49.0 2.3 %collective-permute-done.13.refs_3_ = bf16[256,512]{1,0:T(8,128)(2,1)S(1)} collective-permute-done((bf16[256,512]{1,0:T(8,128)(2,1)S(1)}, bf16[256,512]{1,0:T(8,128)(2,1)S(1)}, u32[]{:S(2)}, u32[]{:S(2)}) %collective-permute-start.13) | collective-permute-done | bytes 262176 | tf_op jit(solution)/shard_map/ppermute | solution.py:368
  52.7 2.7 %collective-permute-start.16 = (bf16[256,1024]{1,0:T(8,128)(2,1)S(1)}, bf16[256,1024]{1,0:T(8,128)(2,1)S(1)}, u32[]{:S(2)}, u32[]{:S(2)}) collective-permute-start(bf16[256,1024]{1,0:T(8,128)(2,1)S(1)} %shard_map.99), channel_id=1, source_target_pairs={{0,16},{8,24},{16,0},{24,8},{1,17},{9,25},{17,1},{25,9},{2,18},{10... | collective-permute-start | bytes 1572872 | tf_op jit(solution)/shard_map/ppermute | solution.py:391
  56.8 4.5 %collective-permute-done.15.from_z = bf16[512,256]{1,0:T(8,128)(2,1)S(1)} collective-permute-done((bf16[512,256]{1,0:T(8,128)(2,1)S(1)}, bf16[512,256]{1,0:T(8,128)(2,1)S(1)}, u32[]{:S(2)}, u32[]{:S(2)}) %collective-permute-start.15) | collective-permute-done | bytes 262176 | tf_op jit(solution)/shard_map/ppermute | solution.py:401
  61.3 6.1 %collective-permute-done.14.from_x = bf16[512,768]{1,0:T(8,128)(2,1)S(1)} collective-permute-done((bf16[512,768]{1,0:T(8,128)(2,1)S(1)}, bf16[512,768]{1,0:T(8,128)(2,1)S(1)}, u32[]{:S(2)}, u32[]{:S(2)}) %collective-permute-start.14) | collective-permute-done | bytes 786464 | tf_op jit(solution)/shard_map/ppermute | solution.py:401
  68.7 5.0 %collective-permute-done.16.refs_0_ = bf16[256,1024]{1,0:T(8,128)(2,1)S(1)} collective-permute-done((bf16[256,1024]{1,0:T(8,128)(2,1)S(1)}, bf16[256,1024]{1,0:T(8,128)(2,1)S(1)}, u32[]{:S(2)}, u32[]{:S(2)}) %collective-permute-start.16) | collective-permute-done | bytes 524320 | tf_op jit(solution)/shard_map/ppermute | solution.py:391
  75.4 2.0 %collective-permute-done.18.refs_6_.refs_2_ = bf16[128,1024]{1,0:T(8,128)(2,1)S(1)} collective-permute-done((bf16[128,1024]{1,0:T(8,128)(2,1)S(1)}, bf16[128,1024]{1,0:T(8,128)(2,1)S(1)}, u32[]{:S(2)}, u32[]{:S(2)}) %collective-permute-start.18) | collective-permute-done | bytes 262176 | tf_op jit(solution)/shard_map/ppermute | solution.py:340
  77.3 2.3 %collective-permute-done.20.refs_3_ = bf16[256,256]{1,0:T(8,128)(2,1)S(1)} collective-permute-done((bf16[256,256]{1,0:T(8,128)(2,1)S(1)}, bf16[256,256]{1,0:T(8,128)(2,1)S(1)}, u32[]{:S(2)}, u32[]{:S(2)}) %collective-permute-start.20) | collective-permute-done | bytes 131104 | tf_op jit(solution)/shard_map/ppermute | solution.py:368
  80.1 3.3 %collective-permute-start.27 = (bf16[256,1024]{1,0:T(8,128)(2,1)S(1)}, bf16[256,1024]{1,0:T(8,128)(2,1)S(1)}, u32[]{:S(2)}, u32[]{:S(2)}) collective-permute-start(bf16[256,1024]{1,0:T(8,128)(2,1)S(1)} %shard_map.101.refs_8_), channel_id=1, source_target_pairs={{0,16},{8,24},{16,0},{24,8},{1,17},{9,25},{17,1},{25,9},{2,18},{10... | collective-permute-start | bytes 1572872 | tf_op jit(solution)/shard_map/ppermute | solution.py:445
  83.4 4.4 %collective-permute-start.21 = (bf16[128,1024]{1,0:T(8,128)(2,1)S(1)}, bf16[128,1024]{1,0:T(8,128)(2,1)S(1)}, u32[]{:S(2)}, u32[]{:S(2)}) collective-permute-start(bf16[128,1024]{1,0:T(8,128)(2,1)S(1)} %copy-done.8), channel_id=1, source_target_pairs={{0,3},{1,2},{2,1},{3,0},{4,7},{5,6},{6,5},{7,4},{8,11},{9,10},{10,... | collective-permute-start | bytes 786440 | tf_op jit(solution)/shard_map/ppermute | solution.py:340
  87.9 1.9 %shard_map.103 = bf16[128,8192]{1,0:T(8,128)(2,1)} custom-call(s32[2]{0:T(128)S(1)} %pad_add_fusion.2.starts, bf16[256,4096]{1,0:T(8,128)(2,1)S(1)} %convolution_convert_fusion.refs_0_, bf16[128,4096]{1,0:T(8,128)(2,1)S(1)} %collective-permute-done.28.refs_1_), custom_call_target="tpu_custom_call" | custom-call | bytes 4194304 | tf_op jit(solution)/shard_map/pallas_call | solution.py:296
  89.8 2.5 %collective-permute-start.26 = (bf16[256,1024]{1,0:T(8,128)(2,1)S(1)}, bf16[256,1024]{1,0:T(8,128)(2,1)S(1)}, u32[]{:S(2)}, u32[]{:S(2)}) collective-permute-start(bf16[256,1024]{1,0:T(8,128)(2,1)S(1)} %shard_map.101.refs_8_), channel_id=1, source_target_pairs={{0,8},{8,0},{16,24},{24,16},{1,9},{9,1},{17,25},{25,17},{2,10},{10... | collective-permute-start | bytes 1572872 | tf_op jit(solution)/shard_map/ppermute | solution.py:445
  94.4 2.6 %collective-permute-start.24 = (bf16[128,1024]{1,0:T(8,128)(2,1)S(1)}, bf16[128,1024]{1,0:T(8,128)(2,1)S(1)}, u32[]{:S(2)}, u32[]{:S(2)}) collective-permute-start(bf16[128,1024]{1,0:T(8,128)(2,1)S(1)} %copy-done.5), channel_id=1, source_target_pairs={{0,1},{1,0},{2,3},{3,2},{4,5},{5,4},{6,7},{7,6},{8,9},{9,8},{10,11... | collective-permute-start | bytes 786440 | tf_op jit(solution)/shard_map/ppermute | solution.py:340
  96.9 8.8 %collective-permute-done.27.refs_10_ = bf16[256,1024]{1,0:T(8,128)(2,1)S(1)} collective-permute-done((bf16[256,1024]{1,0:T(8,128)(2,1)S(1)}, bf16[256,1024]{1,0:T(8,128)(2,1)S(1)}, u32[]{:S(2)}, u32[]{:S(2)}) %collective-permute-start.27) | collective-permute-done | bytes 524320 | tf_op jit(solution)/shard_map/ppermute | solution.py:445
  105.8 5.6 %collective-permute-start.25 = (bf16[128,1024]{1,0:T(8,128)(2,1)S(1)}, bf16[128,1024]{1,0:T(8,128)(2,1)S(1)}, u32[]{:S(2)}, u32[]{:S(2)}) collective-permute-start(bf16[128,1024]{1,0:T(8,128)(2,1)S(1)} %copy-done.4), channel_id=1, source_target_pairs={{0,5},{1,4},{2,7},{3,6},{4,1},{5,0},{6,3},{7,2},{8,13},{9,12},{10,... | collective-permute-start | bytes 786440 | tf_op jit(solution)/shard_map/ppermute | solution.py:340
  113.7 2.8 %collective-permute-done.25.refs_7_.refs_3_ = bf16[128,1024]{1,0:T(8,128)(2,1)S(1)} collective-permute-done((bf16[128,1024]{1,0:T(8,128)(2,1)S(1)}, bf16[128,1024]{1,0:T(8,128)(2,1)S(1)}, u32[]{:S(2)}, u32[]{:S(2)}) %collective-permute-start.25) | collective-permute-done | bytes 262176 | tf_op jit(solution)/shard_map/ppermute | solution.py:340
  116.5 1.8 %shard_map.102 = (f32[512,1024]{1,0:T(8,128)S(1)}, f32[512,1024]{1,0:T(8,128)S(1)}) custom-call(bf16[128,1024]{1,0:T(8,128)(2,1)S(1)} %collective-permute-done.17.refs_0_, bf16[128,1024]{1,0:T(8,128)(2,1)S(1)} %collective-permute-done.21.refs_1_, bf16[128,1024]{1,0:T(8,128)(2,1)S(1)} %collective-permute-done.22.refs_2_, ...), custom_call_target="tpu_custom_call" | custom-call | flops 17179869184 | bytes 524288 | tf_op jit(solution)/shard_map/pallas_call | solution.py:222
  118.3 7.3 %collective-permute-done.29.refs_4_ = bf16[256,1024]{1,0:T(8,128)(2,1)S(1)} collective-permute-done((bf16[256,1024]{1,0:T(8,128)(2,1)S(1)}, bf16[256,1024]{1,0:T(8,128)(2,1)S(1)}, u32[]{:S(2)}, u32[]{:S(2)}) %collective-permute-start.29) | collective-permute-done | bytes 524320 | tf_op jit(solution)/shard_map/ppermute | solution.py:445
  126.5 2.2 %collective-permute-done.30.came = bf16[512,1024]{1,0:T(8,128)(2,1)S(1)} collective-permute-done((bf16[512,1024]{1,0:T(8,128)(2,1)S(1)}, bf16[512,1024]{1,0:T(8,128)(2,1)S(1)}, u32[]{:S(2)}, u32[]{:S(2)}) %collective-permute-start.30) | collective-permute-done | bytes 1048608 | tf_op jit(solution)/shard_map/ppermute | solution.py:456
  128.9 2.5 %collective-permute-start.31 = (bf16[256,512]{1,0:T(8,128)(2,1)S(1)}, bf16[256,512]{1,0:T(8,128)(2,1)S(1)}, u32[]{:S(2)}, u32[]{:S(2)}) collective-permute-start(bf16[256,512]{1,0:T(8,128)(2,1)S(1)} %get-tuple-element.180), channel_id=1, source_target_pairs={{0,4},{4,0},{1,5},{5,1},{2,6},{6,2},{3,7},{7,3},{8,12},{12,8},{9,1... | collective-permute-start | bytes 786440 | tf_op jit(solution)/shard_map/ppermute | solution.py:466
  131.4 6.6 %collective-permute-done.31.refs_2_ = bf16[256,512]{1,0:T(8,128)(2,1)S(1)} collective-permute-done((bf16[256,512]{1,0:T(8,128)(2,1)S(1)}, bf16[256,512]{1,0:T(8,128)(2,1)S(1)}, u32[]{:S(2)}, u32[]{:S(2)}) %collective-permute-start.31) | collective-permute-done | bytes 262176 | tf_op jit(solution)/shard_map/ppermute | solution.py:466
  140.4 4.1 %collective-permute-done.33.from_x = bf16[128,512]{1,0:T(8,128)(2,1)S(1)} collective-permute-done((bf16[128,512]{1,0:T(8,128)(2,1)S(1)}, bf16[128,512]{1,0:T(8,128)(2,1)S(1)}, u32[]{:S(2)}, u32[]{:S(2)}) %collective-permute-start.33) | collective-permute-done | bytes 131104 | tf_op jit(solution)/shard_map/ppermute | solution.py:466
  (89 shorter events, 26.1 us)
Async XLA Ops:
  0.6 23.6 %collective-permute-start.6 = (bf16[4096,1024]{1,0:T(8,128)(2,1)}, bf16[4096,1024]{1,0:T(8,128)(2,1)}, u32[]{:S(2)}, u32[]{:S(2)}) collective-permute-start(bf16[4096,1024]{1,0:T(8,128)(2,1)} %bitcast.45), channel_id=1, source_target_pairs={{0,2},{2,0},{1,3},{3,1},{4,6},{6,4},{5,7},{7,5},{8,10},{10,8},{9,1... | collective-permute-start | bytes 25165832 | tf_op jit(solution)/shard_map/ppermute | solution.py:353
  1.1 6.5 %collective-permute-start.4 = (bf16[128,1024]{1,0:T(8,128)(2,1)}, bf16[128,1024]{1,0:T(8,128)(2,1)S(1)}, u32[]{:S(2)}, u32[]{:S(2)}) collective-permute-start(bf16[128,1024]{1,0:T(8,128)(2,1)} %refs_4_.4), channel_id=1, source_target_pairs={{0,2},{2,0},{1,3},{3,1},{4,6},{6,4},{5,7},{7,5},{8,10},{10,8},{9,1... | collective-permute-start | bytes 786440 | tf_op jit(solution)/shard_map/ppermute | solution.py:354
  1.2 9.9 %collective-permute-start = (bf16[128,1024]{1,0:T(8,128)(2,1)}, bf16[128,1024]{1,0:T(8,128)(2,1)S(1)}, u32[]{:S(2)}, u32[]{:S(2)}) collective-permute-start(bf16[128,1024]{1,0:T(8,128)(2,1)} %refs_4_.4), channel_id=1, source_target_pairs={{0,1},{1,0},{2,3},{3,2},{4,5},{5,4},{6,7},{7,6},{8,9},{9,8},{10,11... | collective-permute-start | bytes 786440 | tf_op jit(solution)/shard_map/ppermute | solution.py:344
  7.5 7.9 %collective-permute-start.1 = (bf16[128,1024]{1,0:T(8,128)(2,1)}, bf16[128,1024]{1,0:T(8,128)(2,1)S(1)}, u32[]{:S(2)}, u32[]{:S(2)}) collective-permute-start(bf16[128,1024]{1,0:T(8,128)(2,1)} %get-tuple-element.107), channel_id=1, source_target_pairs={{0,2},{1,3},{2,0},{3,1},{4,6},{5,7},{6,4},{7,5},{8,10},{9,11},{10,... | collective-permute-start | bytes 786440 | tf_op jit(solution)/shard_map/ppermute | solution.py:351
  7.6 9.4 %collective-permute-start.2 = (bf16[128,1024]{1,0:T(8,128)(2,1)}, bf16[128,1024]{1,0:T(8,128)(2,1)S(1)}, u32[]{:S(2)}, u32[]{:S(2)}) collective-permute-start(bf16[128,1024]{1,0:T(8,128)(2,1)} %get-tuple-element.108), channel_id=1, source_target_pairs={{0,1},{1,0},{2,3},{3,2},{4,5},{5,4},{6,7},{7,6},{8,9},{9,8},{10,11... | collective-permute-start | bytes 786440 | tf_op jit(solution)/shard_map/ppermute | solution.py:351
  7.7 14.6 %collective-permute-start.3 = (bf16[128,1024]{1,0:T(8,128)(2,1)S(1)}, bf16[128,1024]{1,0:T(8,128)(2,1)S(1)}, u32[]{:S(2)}, u32[]{:S(2)}) collective-permute-start(bf16[128,1024]{1,0:T(8,128)(2,1)S(1)} %get-tuple-element.109), channel_id=1, source_target_pairs={{0,3},{1,2},{2,1},{3,0},{4,7},{5,6},{6,5},{7,4},{8,11},{9,10},{10,... | collective-permute-start | bytes 786440 | tf_op jit(solution)/shard_map/ppermute | solution.py:351
  11.2 13.0 %collective-permute-start.5 = (bf16[128,1024]{1,0:T(8,128)(2,1)S(1)}, bf16[128,1024]{1,0:T(8,128)(2,1)S(1)}, u32[]{:S(2)}, u32[]{:S(2)}) collective-permute-start(bf16[128,1024]{1,0:T(8,128)(2,1)S(1)} %collective-permute-done.refs_6_), channel_id=1, source_target_pairs={{0,2},{2,0},{1,3},{3,1},{4,6},{6,4},{5,7},{7,5},{8,10},{10,8},{9,1... | collective-permute-start | bytes 786440 | tf_op jit(solution)/shard_map/ppermute | solution.py:356
  15.5 29.3 %collective-permute-start.9 = (bf16[128,1024]{1,0:T(8,128)(2,1)S(1)}, bf16[128,1024]{1,0:T(8,128)(2,1)S(1)}, u32[]{:S(2)}, u32[]{:S(2)}) collective-permute-start(bf16[128,1024]{1,0:T(8,128)(2,1)S(1)} %get-tuple-element.123), channel_id=1, source_target_pairs={{0,2},{1,3},{2,0},{3,1},{4,6},{5,7},{6,4},{7,5},{8,10},{9,11},{10,... | collective-permute-start | bytes 786440 | tf_op jit(solution)/shard_map/ppermute | solution.py:351
  17.0 27.7 %collective-permute-start.10 = (bf16[128,1024]{1,0:T(8,128)(2,1)S(1)}, bf16[128,1024]{1,0:T(8,128)(2,1)S(1)}, u32[]{:S(2)}, u32[]{:S(2)}) collective-permute-start(bf16[128,1024]{1,0:T(8,128)(2,1)S(1)} %get-tuple-element.124), channel_id=1, source_target_pairs={{0,1},{1,0},{2,3},{3,2},{4,5},{5,4},{6,7},{7,6},{8,9},{9,8},{10,11... | collective-permute-start | bytes 786440 | tf_op jit(solution)/shard_map/ppermute | solution.py:351
  22.3 22.4 %collective-permute-start.11 = (bf16[128,1024]{1,0:T(8,128)(2,1)S(1)}, bf16[128,1024]{1,0:T(8,128)(2,1)S(1)}, u32[]{:S(2)}, u32[]{:S(2)}) collective-permute-start(bf16[128,1024]{1,0:T(8,128)(2,1)S(1)} %get-tuple-element.125), channel_id=1, source_target_pairs={{0,3},{1,2},{2,1},{3,0},{4,7},{5,6},{6,5},{7,4},{8,11},{9,10},{10,... | collective-permute-start | bytes 786440 | tf_op jit(solution)/shard_map/ppermute | solution.py:351
  28.3 12.8 %collective-permute-start.7 = (bf16[512,512]{1,0:T(8,128)(2,1)S(1)}, bf16[512,512]{1,0:T(8,128)(2,1)S(1)}, u32[]{:S(2)}, u32[]{:S(2)}) collective-permute-start(bf16[512,512]{1,0:T(8,128)(2,1)S(1)} %get-tuple-element.116), channel_id=1, source_target_pairs={{0,4},{4,0},{1,5},{5,1},{2,6},{6,2},{3,7},{7,3},{8,12},{12,8},{9,1... | collective-permute-start | bytes 1572872 | tf_op jit(solution)/shard_map/ppermute | solution.py:401
  29.8 12.5 %collective-permute-start.8 = (bf16[512,512]{1,0:T(8,128)(2,1)S(1)}, bf16[512,512]{1,0:T(8,128)(2,1)S(1)}, u32[]{:S(2)}, u32[]{:S(2)}) collective-permute-start(bf16[512,512]{1,0:T(8,128)(2,1)S(1)} %get-tuple-element.118), channel_id=1, source_target_pairs={{0,8},{8,0},{16,24},{24,16},{1,9},{9,1},{17,25},{25,17},{2,10},{10... | collective-permute-start | bytes 1572872 | tf_op jit(solution)/shard_map/ppermute | solution.py:401
  42.5 6.4 %collective-permute-start.12 = (bf16[256,512]{1,0:T(8,128)(2,1)S(1)}, bf16[256,512]{1,0:T(8,128)(2,1)S(1)}, u32[]{:S(2)}, u32[]{:S(2)}) collective-permute-start(bf16[256,512]{1,0:T(8,128)(2,1)S(1)} %get-tuple-element.129), channel_id=1, source_target_pairs={{0,8},{8,0},{16,24},{24,16},{1,9},{9,1},{17,25},{25,17},{2,10},{10... | collective-permute-start | bytes 786440 | tf_op jit(solution)/shard_map/ppermute | solution.py:368
  44.2 7.1 %collective-permute-start.13 = (bf16[256,512]{1,0:T(8,128)(2,1)S(1)}, bf16[256,512]{1,0:T(8,128)(2,1)S(1)}, u32[]{:S(2)}, u32[]{:S(2)}) collective-permute-start(bf16[256,512]{1,0:T(8,128)(2,1)S(1)} %get-tuple-element.130), channel_id=1, source_target_pairs={{0,4},{4,0},{1,5},{5,1},{2,6},{6,2},{3,7},{7,3},{8,12},{12,8},{9,1... | collective-permute-start | bytes 786440 | tf_op jit(solution)/shard_map/ppermute | solution.py:368
  51.3 16.1 %collective-permute-start.14 = (bf16[512,768]{1,0:T(8,128)(2,1)S(1)}, bf16[512,768]{1,0:T(8,128)(2,1)S(1)}, u32[]{:S(2)}, u32[]{:S(2)}) collective-permute-start(bf16[512,768]{1,0:T(8,128)(2,1)S(1)} %get-tuple-element.131), channel_id=1, source_target_pairs={{0,4},{4,0},{1,5},{5,1},{2,6},{6,2},{3,7},{7,3},{8,12},{12,8},{9,1... | collective-permute-start | bytes 2359304 | tf_op jit(solution)/shard_map/ppermute | solution.py:401
  51.8 9.5 %collective-permute-start.15 = (bf16[512,256]{1,0:T(8,128)(2,1)S(1)}, bf16[512,256]{1,0:T(8,128)(2,1)S(1)}, u32[]{:S(2)}, u32[]{:S(2)}) collective-permute-start(bf16[512,256]{1,0:T(8,128)(2,1)S(1)} %get-tuple-element.133), channel_id=1, source_target_pairs={{0,8},{8,0},{16,24},{24,16},{1,9},{9,1},{17,25},{25,17},{2,10},{10... | collective-permute-start | bytes 786440 | tf_op jit(solution)/shard_map/ppermute | solution.py:401
  52.7 21.1 %collective-permute-start.16 = (bf16[256,1024]{1,0:T(8,128)(2,1)S(1)}, bf16[256,1024]{1,0:T(8,128)(2,1)S(1)}, u32[]{:S(2)}, u32[]{:S(2)}) collective-permute-start(bf16[256,1024]{1,0:T(8,128)(2,1)S(1)} %shard_map.99), channel_id=1, source_target_pairs={{0,16},{8,24},{16,0},{24,8},{1,17},{9,25},{17,1},{25,9},{2,18},{10... | collective-permute-start | bytes 1572872 | tf_op jit(solution)/shard_map/ppermute | solution.py:391
  55.3 32.5 %collective-permute-start.28 = (bf16[128,4096]{1,0:T(8,128)(2,1)S(1)}, bf16[128,4096]{1,0:T(8,128)(2,1)S(1)}, u32[]{:S(2)}, u32[]{:S(2)}) collective-permute-start(bf16[128,4096]{1,0:T(8,128)(2,1)S(1)} %slice.4), channel_id=1, source_target_pairs={{0,1},{1,0},{2,3},{3,2},{4,5},{5,4},{6,7},{7,6},{8,9},{9,8},{10,11... | collective-permute-start | bytes 3145736 | tf_op jit(solution)/shard_map/ppermute | solution.py:400
  67.6 12.1 %collective-permute-start.19 = (bf16[256,768]{1,0:T(8,128)(2,1)S(1)}, bf16[256,768]{1,0:T(8,128)(2,1)S(1)}, u32[]{:S(2)}, u32[]{:S(2)}) collective-permute-start(bf16[256,768]{1,0:T(8,128)(2,1)S(1)} %get-tuple-element.145), channel_id=1, source_target_pairs={{0,8},{8,0},{16,24},{24,16},{1,9},{9,1},{17,25},{25,17},{2,10},{10... | collective-permute-start | bytes 1179656 | tf_op jit(solution)/shard_map/ppermute | solution.py:368
  68.1 7.2 %collective-permute-start.17 = (bf16[128,1024]{1,0:T(8,128)(2,1)S(1)}, bf16[128,1024]{1,0:T(8,128)(2,1)S(1)}, u32[]{:S(2)}, u32[]{:S(2)}) collective-permute-start(bf16[128,1024]{1,0:T(8,128)(2,1)S(1)} %copy-done.10), channel_id=1, source_target_pairs={{0,2},{1,3},{2,0},{3,1},{4,6},{5,7},{6,4},{7,5},{8,10},{9,11},{10,... | collective-permute-start | bytes 786440 | tf_op jit(solution)/shard_map/ppermute | solution.py:340
  68.1 9.2 %collective-permute-start.18 = (bf16[128,1024]{1,0:T(8,128)(2,1)S(1)}, bf16[128,1024]{1,0:T(8,128)(2,1)S(1)}, u32[]{:S(2)}, u32[]{:S(2)}) collective-permute-start(bf16[128,1024]{1,0:T(8,128)(2,1)S(1)} %copy-done.9), channel_id=1, source_target_pairs={{0,4},{1,5},{2,6},{3,7},{4,0},{5,1},{6,2},{7,3},{8,12},{9,13},{10,... | collective-permute-start | bytes 786440 | tf_op jit(solution)/shard_map/ppermute | solution.py:340
  73.8 5.9 %collective-permute-start.20 = (bf16[256,256]{1,0:T(8,128)(2,1)S(1)}, bf16[256,256]{1,0:T(8,128)(2,1)S(1)}, u32[]{:S(2)}, u32[]{:S(2)}) collective-permute-start(bf16[256,256]{1,0:T(8,128)(2,1)S(1)} %get-tuple-element.147), channel_id=1, source_target_pairs={{0,4},{4,0},{1,5},{5,1},{2,6},{6,2},{3,7},{7,3},{8,12},{12,8},{9,1... | collective-permute-start | bytes 393224 | tf_op jit(solution)/shard_map/ppermute | solution.py:368
  80.1 25.7 %collective-permute-start.27 = (bf16[256,1024]{1,0:T(8,128)(2,1)S(1)}, bf16[256,1024]{1,0:T(8,128)(2,1)S(1)}, u32[]{:S(2)}, u32[]{:S(2)}) collective-permute-start(bf16[256,1024]{1,0:T(8,128)(2,1)S(1)} %shard_map.101.refs_8_), channel_id=1, source_target_pairs={{0,16},{8,24},{16,0},{24,8},{1,17},{9,25},{17,1},{25,9},{2,18},{10... | collective-permute-start | bytes 1572872 | tf_op jit(solution)/shard_map/ppermute | solution.py:445
  83.4 11.0 %collective-permute-start.21 = (bf16[128,1024]{1,0:T(8,128)(2,1)S(1)}, bf16[128,1024]{1,0:T(8,128)(2,1)S(1)}, u32[]{:S(2)}, u32[]{:S(2)}) collective-permute-start(bf16[128,1024]{1,0:T(8,128)(2,1)S(1)} %copy-done.8), channel_id=1, source_target_pairs={{0,3},{1,2},{2,1},{3,0},{4,7},{5,6},{6,5},{7,4},{8,11},{9,10},{10,... | collective-permute-start | bytes 786440 | tf_op jit(solution)/shard_map/ppermute | solution.py:340
  89.8 26.7 %collective-permute-start.26 = (bf16[256,1024]{1,0:T(8,128)(2,1)S(1)}, bf16[256,1024]{1,0:T(8,128)(2,1)S(1)}, u32[]{:S(2)}, u32[]{:S(2)}) collective-permute-start(bf16[256,1024]{1,0:T(8,128)(2,1)S(1)} %shard_map.101.refs_8_), channel_id=1, source_target_pairs={{0,8},{8,0},{16,24},{24,16},{1,9},{9,1},{17,25},{25,17},{2,10},{10... | collective-permute-start | bytes 1572872 | tf_op jit(solution)/shard_map/ppermute | solution.py:445
  92.3 20.7 %collective-permute-start.22 = (bf16[128,1024]{1,0:T(8,128)(2,1)S(1)}, bf16[128,1024]{1,0:T(8,128)(2,1)S(1)}, u32[]{:S(2)}, u32[]{:S(2)}) collective-permute-start(bf16[128,1024]{1,0:T(8,128)(2,1)S(1)} %copy-done.7), channel_id=1, source_target_pairs={{0,6},{1,7},{2,4},{3,5},{4,2},{5,3},{6,0},{7,1},{8,14},{9,15},{10,... | collective-permute-start | bytes 786440 | tf_op jit(solution)/shard_map/ppermute | solution.py:340
  93.1 20.5 %collective-permute-start.23 = (bf16[128,1024]{1,0:T(8,128)(2,1)S(1)}, bf16[128,1024]{1,0:T(8,128)(2,1)S(1)}, u32[]{:S(2)}, u32[]{:S(2)}) collective-permute-start(bf16[128,1024]{1,0:T(8,128)(2,1)S(1)} %copy-done.6), channel_id=1, source_target_pairs={{0,7},{1,6},{2,5},{3,4},{4,3},{5,2},{6,1},{7,0},{8,15},{9,14},{10,... | collective-permute-start | bytes 786440 | tf_op jit(solution)/shard_map/ppermute | solution.py:340
  94.4 19.3 %collective-permute-start.24 = (bf16[128,1024]{1,0:T(8,128)(2,1)S(1)}, bf16[128,1024]{1,0:T(8,128)(2,1)S(1)}, u32[]{:S(2)}, u32[]{:S(2)}) collective-permute-start(bf16[128,1024]{1,0:T(8,128)(2,1)S(1)} %copy-done.5), channel_id=1, source_target_pairs={{0,1},{1,0},{2,3},{3,2},{4,5},{5,4},{6,7},{7,6},{8,9},{9,8},{10,11... | collective-permute-start | bytes 786440 | tf_op jit(solution)/shard_map/ppermute | solution.py:340
  105.8 10.7 %collective-permute-start.25 = (bf16[128,1024]{1,0:T(8,128)(2,1)S(1)}, bf16[128,1024]{1,0:T(8,128)(2,1)S(1)}, u32[]{:S(2)}, u32[]{:S(2)}) collective-permute-start(bf16[128,1024]{1,0:T(8,128)(2,1)S(1)} %copy-done.4), channel_id=1, source_target_pairs={{0,5},{1,4},{2,7},{3,6},{4,1},{5,0},{6,3},{7,2},{8,13},{9,12},{10,... | collective-permute-start | bytes 786440 | tf_op jit(solution)/shard_map/ppermute | solution.py:340
  113.0 12.6 %collective-permute-start.29 = (bf16[256,1024]{1,0:T(8,128)(2,1)S(1)}, bf16[256,1024]{1,0:T(8,128)(2,1)S(1)}, u32[]{:S(2)}, u32[]{:S(2)}) collective-permute-start(bf16[256,1024]{1,0:T(8,128)(2,1)S(1)} %collective-permute-done.27.refs_10_), channel_id=1, source_target_pairs={{0,8},{8,0},{16,24},{24,16},{1,9},{9,1},{17,25},{25,17},{2,10},{10... | collective-permute-start | bytes 1572872 | tf_op jit(solution)/shard_map/ppermute | solution.py:445
  128.9 9.1 %collective-permute-start.31 = (bf16[256,512]{1,0:T(8,128)(2,1)S(1)}, bf16[256,512]{1,0:T(8,128)(2,1)S(1)}, u32[]{:S(2)}, u32[]{:S(2)}) collective-permute-start(bf16[256,512]{1,0:T(8,128)(2,1)S(1)} %get-tuple-element.180), channel_id=1, source_target_pairs={{0,4},{4,0},{1,5},{5,1},{2,6},{6,2},{3,7},{7,3},{8,12},{12,8},{9,1... | collective-permute-start | bytes 786440 | tf_op jit(solution)/shard_map/ppermute | solution.py:466
  131.4 8.1 %collective-permute-start.32 = (bf16[256,512]{1,0:T(8,128)(2,1)S(1)}, bf16[256,512]{1,0:T(8,128)(2,1)S(1)}, u32[]{:S(2)}, u32[]{:S(2)}) collective-permute-start(bf16[256,512]{1,0:T(8,128)(2,1)S(1)} %get-tuple-element.181), channel_id=1, source_target_pairs={{0,1},{1,0},{2,3},{3,2},{4,5},{5,4},{6,7},{7,6},{8,9},{9,8},{10,11... | collective-permute-start | bytes 786440 | tf_op jit(solution)/shard_map/ppermute | solution.py:467
  (16 other events, 180.0 us)
